TPU v7x, 128 devices: a whole 4x4x4 slice. The times are simulated.
128 devices in a mesh: node: 8 (over z, core), local: 16 (over x, y).
Axes of the slice: x: 4, y: 4, z: 4, core: 2. Of those that a mesh axis runs over, the one named last changes fastest.
Arguments:
- tokens: bfloat16 [1024, 7168], P(('node', 'local')), may hold values from -6 to 6
- routes: int32 [1024, 8], P(('node', 'local')), may hold values from 0 to 15, all different within a row; in each aligned block of 8 rows (0 to 7, 8 to 15, ...) at most 5 rows name the same one
- gate_scores: float32 [1024, 8], P(('node', 'local')), may hold values from 0.05 to 1
- gate_weight: bfloat16 [16, 7168, 2048], P('local', None, 'node'), may hold values from -0.0625 to 0.0625
- up_weight: bfloat16 [16, 7168, 2048], P('local', None, 'node'), may hold values from -0.0625 to 0.0625
- down_weight: bfloat16 [16, 2048, 7168], P('local', 'node'), may hold values from -0.125 to 0.125
- query_nope: bfloat16 [1024, 16384], P('node', 'local'), may hold values from -6 to 6
- query_rope: bfloat16 [1024, 8192], P('node', 'local'), may hold values from -8 to 8
- key_up: bfloat16 [128, 128, 512], P('local'), may hold values from -0.5 to 0.5
- value_up: bfloat16 [128, 512, 128], P('local'), may hold values from -2 to 2
- latent_cache: bfloat16 [16, 4096, 512], P('node'), may hold values from -6 to 6
- rope_cache: bfloat16 [16, 4096, 64], P('node'), may hold values from -8 to 8
- new_latent: bfloat16 [1024, 512], P('node'), may hold values from -6 to 6
- new_rope: bfloat16 [1024, 64], P('node'), may hold values from -6 to 6
- lengths: int32 [16], P('node'), may hold values from 1024 to 4096, as said below
Outputs:
- routed_out: bfloat16 [1024, 7168], P(('node', 'local'))
- attention_out: bfloat16 [1024, 16384], P('node', 'local')
Inputs may be any that keep to these rules, and one draw needn't show every extreme that they name: `routes`: in each aligned block of 8 rows (the rows of one device) no expert is named by more than 5 rows, a bound that some block reaches. `lengths`: one sequence has all 4096 slots live.
All inputs are finite; a program needn't handle non-finite values.
Results may differ from a plain program's by a relative error of at most 0.019.
Values may be sent and summed in bfloat16 or wider, within the bound.
No kernel may reach another device: no remote copies, remote signals or barrier semaphores. Data moves between devices by JAX's collectives and lax.ppermute only.
A program may use at most 128 MiB of HBM per device.

v0:
```python
import functools

import jax
import jax.numpy as jnp
import numpy as np
from jax import lax
from jax.experimental import pallas as pl
from jax.experimental.pallas import tpu as pltpu
from jax.sharding import Mesh, PartitionSpec as P

NOPE = 128
ROPE = 64
NEW = 64
CACHE = 4096
EXPERTS = 16
ROUTE_SCALE = 2.5
NEG_BIG = -1e30
AXES = ("z", "core", "x", "y")
SIZES = (4, 2, 4, 4)
RING = 4
ORDERS = ((0, 3, 2), (2, 0, 3))
KERNEL_VMEM = 60 * 1024 * 1024
PACK = 128
DEPTH = 1024
UNITS = 256
HALF = 64
KEY_BLOCK = 1024
HEAD_COUNT = 8
LATENT = 512
LOG2E = 1.4426950408889634


def shift(value, phase, distance):
    pairs = []
    for place in np.ndindex(*SIZES):
        target = list(place)
        axis = ORDERS[place[1]][phase]
        target[axis] = (target[axis] + distance) % RING
        pairs.append((int(np.ravel_multi_index(place, SIZES)), int(np.ravel_multi_index(target, SIZES))))
    return lax.ppermute(value, AXES, pairs)


def widened(value):
    return value.astype(jnp.float32)


def narrowed(value):
    return value.astype(jnp.bfloat16)


def added(*values):
    return sum(widened(value) for value in values)


def with_other_core(value):
    return lax.ppermute(value, "core", [(0, 1), (1, 0)])


def expert_kernel(expert_ref, *refs, sources, outputs):
    row_hbm = refs[:sources]
    gate_hbm, up_hbm, gate_other_hbm, up_other_hbm, down_hbm, down_other_hbm = refs[sources : sources + 6]
    out_refs = refs[sources + 6 : sources + 6 + outputs]
    rows_ref, weight_ref, down_ref, sums_ref, hidden_ref, row_sem, weight_sem, down_sem = refs[sources + 6 + outputs :]
    width = weight_ref.shape[0]
    steps = width // DEPTH
    span = rows_ref.shape[0] // sources
    row_copies = [
        pltpu.make_async_copy(source, rows_ref.at[pl.ds(i * span, span)], row_sem.at[i])
        for i, source in enumerate(row_hbm)
    ]
    down_copies = [
        pltpu.make_async_copy(source, down_ref.at[pl.ds(i * UNITS, UNITS)], down_sem.at[i])
        for i, source in enumerate((down_hbm, down_other_hbm))
    ]
    matrices = (gate_hbm, gate_other_hbm, up_hbm, up_other_hbm)

    def weight_copy(matrix, step):
        part = pl.ds(step * DEPTH, DEPTH)
        return pltpu.make_async_copy(
            matrices[matrix].at[part],
            weight_ref.at[part, pl.ds(matrix * UNITS, UNITS)],
            weight_sem.at[matrix, step],
        )

    for copy in row_copies:
        copy.start()
    for step in range(steps):
        for matrix in range(4):
            weight_copy(matrix, step).start()
    for copy in down_copies:
        copy.start()
    for copy in row_copies:
        copy.wait()
    sums_ref[...] = jnp.zeros_like(sums_ref)

    @pl.loop(0, steps)
    def _(step):
        part = pl.ds(pl.multiple_of(step * DEPTH, DEPTH), DEPTH)
        for matrix in range(4):
            weight_copy(matrix, step).wait()
        sums_ref[...] += jnp.dot(rows_ref[:, part], weight_ref[part, :], preferred_element_type=jnp.float32)

    extra = rows_ref[:, width : width + PACK].astype(jnp.float32)
    lane = lax.broadcasted_iota(jnp.int32, extra.shape, 1)
    pick = (lane % EXPERTS == expert_ref[0]) & (lane < 2 * EXPERTS)
    coefficient = jnp.sum(jnp.where(pick, extra, 0.0), axis=1, keepdims=True)
    gate, up = sums_ref[:, : 2 * UNITS], sums_ref[:, 2 * UNITS :]
    hidden = gate / (1.0 + jnp.exp(-gate)) * up * coefficient
    hidden_ref[...] = jnp.where(coefficient > 0, hidden, 0.0).astype(jnp.bfloat16)
    for copy in down_copies:
        copy.wait()

    @pl.loop(0, steps)
    def _(step):
        part = pl.ds(pl.multiple_of(step * DEPTH, DEPTH), DEPTH)
        result = jnp.dot(hidden_ref[...], down_ref[:, part], preferred_element_type=jnp.float32).astype(jnp.bfloat16)
        for i, out_ref in enumerate(out_refs):
            out_ref[:, part] = result[i * HALF : (i + 1) * HALF]


def expert_terms(expert, pieces, weights, downs):
    width = weights[0].shape[0]
    rows = sum(piece.shape[0] for piece in pieces)
    outputs = rows // HALF
    anywhere = pl.BlockSpec(memory_space=pl.ANY)
    return pl.pallas_call(
        functools.partial(expert_kernel, sources=len(pieces), outputs=outputs),
        in_specs=[pl.BlockSpec(memory_space=pltpu.SMEM)] + [anywhere] * (len(pieces) + 6),
        out_specs=[pl.BlockSpec(memory_space=pltpu.VMEM)] * outputs,
        out_shape=[jax.ShapeDtypeStruct((HALF, width), jnp.bfloat16)] * outputs,
        scratch_shapes=[
            pltpu.VMEM((rows, width + PACK), jnp.bfloat16),
            pltpu.VMEM((width, 4 * UNITS), jnp.bfloat16),
            pltpu.VMEM((2 * UNITS, width), jnp.bfloat16),
            pltpu.VMEM((rows, 4 * UNITS), jnp.float32),
            pltpu.VMEM((rows, 2 * UNITS), jnp.bfloat16),
            pltpu.SemaphoreType.DMA((len(pieces),)),
            pltpu.SemaphoreType.DMA((4, width // DEPTH)),
            pltpu.SemaphoreType.DMA((2,)),
        ],
        compiler_params=pltpu.CompilerParams(vmem_limit_bytes=KERNEL_VMEM),
        cost_estimate=pl.CostEstimate(
            flops=6 * rows * width * UNITS * 2, bytes_accessed=12 * width * UNITS + 4 * rows * width, transcendentals=0
        ),
        name="expert",
    )(expert, *pieces, *weights, *downs)


def pack_kernel(tokens_ref, routes_ref, scores_ref, out_ref):
    rows, width = tokens_ref.shape
    out_ref[:, :width] = tokens_ref[...]
    scores = scores_ref[...]
    weights = scores / jnp.sum(scores, axis=1, keepdims=True) * ROUTE_SCALE
    lane = lax.broadcasted_iota(jnp.int32, (rows, PACK), 1)
    dense = jnp.zeros((rows, PACK), jnp.float32)
    for choice in range(scores.shape[1]):
        named = routes_ref[:, choice : choice + 1] == lane % EXPERTS
        dense += jnp.where(named, weights[:, choice : choice + 1], 0.0)
    high = dense.astype(jnp.bfloat16).astype(jnp.float32)
    extra = jnp.where(lane < EXPERTS, high, jnp.where(lane < 2 * EXPERTS, dense - high, 0.0))
    out_ref[:, width:] = extra.astype(jnp.bfloat16)


def packed_rows(tokens, routes, gate_scores):
    rows, width = tokens.shape
    return pl.pallas_call(
        pack_kernel,
        out_shape=jax.ShapeDtypeStruct((rows, width + PACK), jnp.bfloat16),
        name="pack",
    )(tokens, routes, gate_scores)


def attention_kernel(
    sequence, length_ref, nope_ref, rope_ref, key_up_ref, value_up_ref, latent_ref, rope_key_ref,
    new_latent_ref, new_rope_ref, out_ref, query_ref, query_rope_ref, top_ref, sum_ref, total_ref,
):
    step = pl.program_id(0)
    length = length_ref[0]
    scale = (NOPE + ROPE) ** (-0.5) * LOG2E
    contract_last = (((1,), (1,)), ((), ()))

    def absorb(keys, rope_keys, values, bias):
        scores = lax.dot_general(query_ref[...], keys, contract_last, preferred_element_type=jnp.float32)
        scores += jnp.dot(query_rope_ref[...], rope_keys, preferred_element_type=jnp.float32)
        scores = scores * scale + bias
        old_top = top_ref[...]
        top = jnp.maximum(old_top, jnp.max(scores, axis=1, keepdims=True))
        shrink = jnp.exp2(old_top - top)
        probs = jnp.exp2(scores - top)
        top_ref[...] = top
        sum_ref[...] = sum_ref[...] * shrink + jnp.sum(probs, axis=1, keepdims=True)
        total_ref[...] = total_ref[...] * shrink + jnp.dot(
            probs.astype(jnp.bfloat16), values, preferred_element_type=jnp.float32
        )

    @pl.when(step == 0)
    def _():
        for head in range(HEAD_COUNT):
            query_ref[head * NEW : (head + 1) * NEW, :] = jnp.dot(
                nope_ref[:, head * NOPE : (head + 1) * NOPE], key_up_ref[head], preferred_element_type=jnp.float32
            ).astype(jnp.bfloat16)
            query_rope_ref[head * NEW : (head + 1) * NEW, :] = rope_ref[:, head * ROPE : (head + 1) * ROPE]
        top_ref[...] = jnp.full_like(top_ref, NEG_BIG)
        sum_ref[...] = jnp.zeros_like(sum_ref)
        total_ref[...] = jnp.zeros_like(total_ref)
        position = lax.broadcasted_iota(jnp.int32, (HEAD_COUNT * NEW, NEW), 0) % NEW
        fresh = lax.broadcasted_iota(jnp.int32, (HEAD_COUNT * NEW, NEW), 1)
        bias = jnp.where(fresh <= position, 0.0, NEG_BIG)
        absorb(new_latent_ref[...], new_rope_ref[:, sequence * NEW : (sequence + 1) * NEW], new_latent_ref[...], bias)

    @pl.when(step * KEY_BLOCK < length)
    def _():
        slot = step * KEY_BLOCK + lax.broadcasted_iota(jnp.int32, (1, KEY_BLOCK), 1)
        bias = jnp.where(slot < length, 0.0, NEG_BIG)
        absorb(latent_ref[...], rope_key_ref[...], latent_ref[...], bias)

    @pl.when(step == pl.num_programs(0) - 1)
    def _():
        latent_out = (total_ref[...] / sum_ref[...]).astype(jnp.bfloat16)
        for head in range(HEAD_COUNT):
            out_ref[:, head * NOPE : (head + 1) * NOPE] = jnp.dot(
                latent_out[head * NEW : (head + 1) * NEW], value_up_ref[head], preferred_element_type=jnp.float32
            ).astype(jnp.bfloat16)


def attend(sequence, length, nope, rope, key_up, value_up, latent_cache, rope_cache, new_latent, new_rope):
    rows = HEAD_COUNT * NEW

    def whole(*shape):
        return pl.BlockSpec(shape, lambda step, length: (0,) * len(shape))

    def live(step, length):
        return (sequence, jnp.minimum(step, (length[0] + KEY_BLOCK - 1) // KEY_BLOCK - 1), 0)

    def live_last(step, length):
        sequence_place, block, column = live(step, length)
        return (sequence_place, column, block)

    def own(*shape):
        return pl.BlockSpec(shape, lambda step, length: (sequence,) + (0,) * (len(shape) - 1))

    return pl.pallas_call(
        functools.partial(attention_kernel, sequence),
        grid_spec=pltpu.PrefetchScalarGridSpec(
            num_scalar_prefetch=1,
            grid=(CACHE // KEY_BLOCK,),
            in_specs=[
                own(NEW, HEAD_COUNT * NOPE),
                own(NEW, HEAD_COUNT * ROPE),
                whole(HEAD_COUNT, NOPE, LATENT),
                whole(HEAD_COUNT, LATENT, NOPE),
                pl.BlockSpec((None, KEY_BLOCK, LATENT), live),
                pl.BlockSpec((None, ROPE, KEY_BLOCK), live_last),
                own(NEW, LATENT),
                pl.BlockSpec((ROPE, 2 * NEW), lambda step, length: (0, 0)),
            ],
            out_specs=whole(NEW, HEAD_COUNT * NOPE),
            scratch_shapes=[
                pltpu.VMEM((rows, LATENT), jnp.bfloat16),
                pltpu.VMEM((rows, ROPE), jnp.bfloat16),
                pltpu.VMEM((rows, 1), jnp.float32),
                pltpu.VMEM((rows, 1), jnp.float32),
                pltpu.VMEM((rows, LATENT), jnp.float32),
            ],
        ),
        out_shape=jax.ShapeDtypeStruct((NEW, HEAD_COUNT * NOPE), jnp.bfloat16),
        compiler_params=pltpu.CompilerParams(vmem_limit_bytes=KERNEL_VMEM),
        cost_estimate=pl.CostEstimate(flops=6_000_000_000, bytes_accessed=8_000_000, transcendentals=2_100_000),
        name="attend",
    )(length, nope, rope, key_up, value_up, latent_cache, rope_cache, new_latent, new_rope)


def body(
    tokens,
    routes,
    gate_scores,
    gate_weight,
    up_weight,
    down_weight,
    query_nope,
    query_rope,
    key_up,
    value_up,
    latent_cache,
    rope_cache,
    new_latent,
    new_rope,
    lengths,
):
    packed = packed_rows(tokens, routes, gate_scores)
    small = jnp.concatenate([packed] + [shift(packed, 0, -distance) for distance in (1, 2, 3)], axis=0)
    small, gate_weight, up_weight, down_weight = lax.optimization_barrier(
        (small, gate_weight, up_weight, down_weight)
    )
    gate_part, up_part, down_part = gate_weight[0], up_weight[0], down_weight[0]
    weights = (gate_part, up_part, with_other_core(gate_part), with_other_core(up_part))
    downs = (down_part, with_other_core(down_part))
    expert = (lax.axis_index("x") * RING + lax.axis_index("y")).astype(jnp.int32)[None]
    rope_keys, new_rope_keys = jnp.swapaxes(rope_cache, 1, 2), new_rope.T

    def attention(sequence, length):
        return attend(
            sequence, length, query_nope, query_rope, key_up, value_up, latent_cache, rope_keys, new_latent, new_rope_keys
        )

    half = small.shape[0] // 2
    above, below = shift(small, 1, -1), shift(small, 1, 1)
    far_low, far_high = shift(below[:half], 1, 1), shift(above[half:], 1, -1)
    own = jnp.concatenate([small, above, far_low, far_high, below], axis=0)
    above, below = shift(own, 2, -1), shift(own, 2, 1)
    own, lengths = lax.optimization_barrier((own, lengths))
    own_terms = expert_terms(expert, [own], weights, downs)
    first_attention = attention(0, lengths[:1])
    above, below, own_terms, first_attention = lax.optimization_barrier((above, below, own_terms, first_attention))
    far_low, far_high = shift(below[:HALF], 2, 1), shift(above[HALF:], 2, -1)
    above_low, above_high, below_low, below_high = expert_terms(expert, [above, below], weights, downs)
    near_high, near_low = shift(above_high, 2, 1), shift(below_low, 2, -1)
    far_low, far_high, above_high, below_low = lax.optimization_barrier((far_low, far_high, above_high, below_low))
    far_terms = expert_terms(expert, [far_low, far_high], weights, downs)
    far_terms, near_high, near_low = lax.optimization_barrier((far_terms, near_high, near_low))
    from_below, from_above = shift(far_terms[0], 2, 1), shift(far_terms[1], 2, -1)
    far_terms, lengths = lax.optimization_barrier((far_terms, lengths))
    second_attention = attention(1, lengths[1:])
    from_below, from_above, second_attention = lax.optimization_barrier((from_below, from_above, second_attention))
    from_below = shift(narrowed(added(above_low, from_below)), 2, 1)
    from_above = shift(narrowed(added(below_high, from_above)), 2, -1)
    low = added(own_terms[0], near_low, from_below)
    high = added(own_terms[1], near_high, from_above)

    size = HALF // 2
    half = size // 2
    above, far, below = low[size:], high[:size], high[size:]
    up_first = narrowed(jnp.concatenate([far[:half], above[half:]], axis=0))
    down_first = narrowed(jnp.concatenate([far[half:], below[:half]], axis=0))
    from_below, from_above = shift(up_first, 1, 1), shift(down_first, 1, -1)
    up_second = shift(narrowed(added(above[:half], from_below[:half])), 1, 1)
    down_second = shift(narrowed(added(below[half:], from_above[:half])), 1, -1)
    total = low[:size] + jnp.concatenate(
        [added(up_second, from_above[half:]), added(down_second, from_below[half:])], axis=0
    )

    total = narrowed(total)
    rows = tokens.shape[0]
    arrived = [shift(total[distance * rows : (distance + 1) * rows], 0, distance) for distance in (1, 2, 3)]
    routed_out = narrowed(added(total[:rows], *arrived))
    return (routed_out, jnp.concatenate([first_attention, second_attention], axis=0))


def solution(mesh):
    cube = Mesh(mesh.devices.reshape(4, 2, 4, 4), ("z", "core", "x", "y"))
    node, local = ("z", "core"), ("x", "y")
    every = node + local
    in_specs = (
        P(every, None),
        P(every, None),
        P(every, None),
        P(local, None, node),
        P(local, None, node),
        P(local, node, None),
        P(node, local),
        P(node, local),
        P(local, None, None),
        P(local, None, None),
        P(node, None, None),
        P(node, None, None),
        P(node, None),
        P(node, None),
        P(node),
    )
    out_specs = (P(every, None), P(node, local))
    return jax.shard_map(body, mesh=cube, in_specs=in_specs, out_specs=out_specs, check_vma=False)
```

profile of v0, /device:TPU:0, one launch (start us, length us, event | category | flops | bytes accessed | tf_op | source)
XLA Modules:
  0.0 178.1 jit_solution(16977760083033064102)
XLA Ops:
  0.6 1.8 pack.1
  2.4 4.1 %collective-permute-start = (bf16[8,7296]{1,0:T(8,128)(2,1)}, bf16[8,7296]{1,0:T(8,128)(2,1)S(1)}, u32[]{:S(2)}, u32[]{:S(2)}) collective-permute-start(bf16[8,7296]{1,0:T(8,128)(2,1)} %pack.1), channel_id=1, source_target_pairs={{0,96},{1,97},{2,98},{3,99},{4,100},{5,101},{6,102},{7,103},{8,104... | collective-permute-start | bytes 350216 | tf_op jit(solution)/shard_map/ppermute | solution.py:40
  6.5 0.0 collective-permute-start.1
  6.5 1.3 collective-permute-start.2
  7.8 2.7 %collective-permute-done = bf16[8,7296]{1,0:T(8,128)(2,1)S(1)} collective-permute-done((bf16[8,7296]{1,0:T(8,128)(2,1)}, bf16[8,7296]{1,0:T(8,128)(2,1)S(1)}, u32[]{:S(2)}, u32[]{:S(2)}) %collective-permute-start) | collective-permute-done | bytes 116768 | tf_op jit(solution)/shard_map/ppermute | solution.py:40
  10.4 2.7 %collective-permute-done.1 = bf16[8,7296]{1,0:T(8,128)(2,1)S(1)} collective-permute-done((bf16[8,7296]{1,0:T(8,128)(2,1)}, bf16[8,7296]{1,0:T(8,128)(2,1)S(1)}, u32[]{:S(2)}, u32[]{:S(2)}) %collective-permute-start.1) | collective-permute-done | bytes 116768 | tf_op jit(solution)/shard_map/ppermute | solution.py:40
  13.1 0.9 collective-permute-done.2
  14.0 0.9 pad_maximum_fusion
  14.9 3.1 %collective-permute-start.3 = (bf16[32,7296]{1,0:T(8,128)(2,1)S(1)}, bf16[32,7296]{1,0:T(8,128)(2,1)S(1)}, u32[]{:S(2)}, u32[]{:S(2)}) collective-permute-start(bf16[32,7296]{1,0:T(8,128)(2,1)S(1)} %pad_maximum_fusion), channel_id=1, source_target_pairs={{0,3},{1,0},{2,1},{3,2},{4,7},{5,4},{6,5},{7,6},{8,11},{9,8},{10,9... | collective-permute-start | bytes 1400840 | tf_op jit(solution)/shard_map/ppermute | solution.py:40
  18.0 0.0 collective-permute-start.4
  18.0 0.5 collective-permute-start.11
  18.5 0.0 collective-permute-start.9
  18.5 0.8 constant_dynamic-update-slice_fusion.4
  19.3 8.5 %collective-permute-done.4 = bf16[32,7296]{1,0:T(8,128)(2,1)S(1)} collective-permute-done((bf16[32,7296]{1,0:T(8,128)(2,1)S(1)}, bf16[32,7296]{1,0:T(8,128)(2,1)S(1)}, u32[]{:S(2)}, u32[]{:S(2)}) %collective-permute-start.4) | collective-permute-done | bytes 466976 | tf_op jit(solution)/shard_map/ppermute | solution.py:40
  27.8 0.1 collective-permute-start.5
  27.9 3.3 %collective-permute-start.6 = (bf16[16,7296]{1,0:T(8,128)(2,1)S(1)}, bf16[16,7296]{1,0:T(8,128)(2,1)S(1)}, u32[]{:S(2)}, u32[]{:S(2)}) collective-permute-start(bf16[16,7296]{1,0:T(8,128)(2,1)S(1)} %slice.92), channel_id=1, source_target_pairs={{0,3},{1,0},{2,1},{3,2},{4,7},{5,4},{6,5},{7,6},{8,11},{9,8},{10,9... | collective-permute-start | bytes 700424 | tf_op jit(solution)/shard_map/ppermute | solution.py:40
  31.2 0.8 constant_dynamic-update-slice_fusion.3
  32.0 3.1 %collective-permute-done.5 = bf16[16,7296]{1,0:T(8,128)(2,1)S(1)} collective-permute-done((bf16[16,7296]{1,0:T(8,128)(2,1)S(1)}, bf16[16,7296]{1,0:T(8,128)(2,1)S(1)}, u32[]{:S(2)}, u32[]{:S(2)}) %collective-permute-start.5) | collective-permute-done | bytes 233504 | tf_op jit(solution)/shard_map/ppermute | solution.py:40
  35.2 0.7 constant_dynamic-update-slice_fusion.2
  35.8 0.7 constant_dynamic-update-slice_fusion.1
  36.6 0.8 constant_dynamic-update-slice_fusion.refs_0_
  37.4 2.8 %collective-permute-start.7 = (bf16[128,7296]{1,0:T(8,128)(2,1)}, bf16[128,7296]{1,0:T(8,128)(2,1)S(1)}, u32[]{:S(2)}, u32[]{:S(2)}) collective-permute-start(bf16[128,7296]{1,0:T(8,128)(2,1)} %constant_dynamic-update-slice_fusion.refs_0_), channel_id=1, source_target_pairs={{0,12},{1,13},{2,14},{3,15},{4,0},{5,1},{6,2},{7,3},{8,4},{9,5},{1... | collective-permute-start | bytes 5603336 | tf_op jit(solution)/shard_map/ppermute | solution.py:40
  40.2 13.7 %attend.2 = bf16[64,1024]{1,0:T(8,128)(2,1)} custom-call(s32[1]{0:T(128)} %bitcast.23, bf16[128,1024]{1,0:T(8,128)(2,1)} %nope_ref.3, bf16[128,512]{1,0:T(8,128)(2,1)} %rope_ref.3, bf16[8,128,512]{2,1,0:T(8,128)(2,1)} %key_up_ref.3, bf16[8,512,128]{2,1,0:T(8,128)(2,1)} %value_up_ref.3, bf16[2,4096,512]{2,1,0:T(8,128)(2,1)} %latent_ref.3, ...), custom_call_target="tpu_custom_call" | custom-call | flops 6000000000 | bytes 8000000 | tf_op jit(solution)/shard_map/attend/pallas_call | solution.py:242
  53.9 13.8 %expert.3 = (bf16[64,7168]{1,0:T(8,128)(2,1)}, bf16[64,7168]{1,0:T(8,128)(2,1)}) custom-call(s32[1]{0:T(128)} %bitcast.expert_ref, bf16[128,7296]{1,0:T(8,128)(2,1)} %constant_dynamic-update-slice_fusion.refs_0_, bf16[7168,256]{1,0:T(8,128)(2,1)} %bitcast.8, bf16[7168,256]{1,0:T(8,128)(2,1)} %bitcast.12, ...), custom_call_target="tpu_custom_call" | custom-call | flops 2818572288 | bytes 25690112 | tf_op jit(solution)/shard_map/expert/pallas_call | solution.py:126
  67.7 2.9 %slice.75 = bf16[64,7296]{1,0:T(8,128)(2,1)} slice(bf16[128,7296]{1,0:T(8,128)(2,1)} %collective-permute-done.8.refs_1_), slice={[0:64], [0:7296]} | slice | bytes 1867776 | tf_op jit(solution)/shard_map/slice | solution.py:315
  70.6 0.8 collective-permute-start.12
  71.4 1.0 slice.76
  72.4 2.4 %collective-permute-start.13 = (bf16[64,7296]{1,0:T(8,128)(2,1)}, bf16[64,7296]{1,0:T(8,128)(2,1)}, u32[]{:S(2)}, u32[]{:S(2)}) collective-permute-start(bf16[64,7296]{1,0:T(8,128)(2,1)} %slice.76), channel_id=1, source_target_pairs={{0,12},{1,13},{2,14},{3,15},{4,0},{5,1},{6,2},{7,3},{8,4},{9,5},{1... | collective-permute-start | bytes 2801672 | tf_op jit(solution)/shard_map/ppermute | solution.py:40
  74.8 17.6 %expert.4 = (bf16[64,7168]{1,0:T(8,128)(2,1)}, bf16[64,7168]{1,0:T(8,128)(2,1)}, bf16[64,7168]{1,0:T(8,128)(2,1)}, bf16[64,7168]{1,0:T(8,128)(2,1)}) custom-call(s32[1]{0:T(128)} %bitcast.expert_ref, bf16[128,7296]{1,0:T(8,128)(2,1)} %copy-done, bf16[128,7296]{1,0:T(8,128)(2,1)} %collective-permute-done.8.refs_1_, bf16[7168,256]{1,0:T(8,128)(2,1)} %bitcast.9, ...), custom_call_target="tpu_custom_call" | custom-call | flops 5637144576 | bytes 29360128 | tf_op jit(solution)/shard_map/expert/pallas_call | solution.py:126
  92.5 0.1 collective-permute-start.14
  92.5 0.0 copy-start.8
  92.6 3.2 %collective-permute-start.15 = (bf16[64,7168]{1,0:T(8,128)(2,1)}, bf16[64,7168]{1,0:T(8,128)(2,1)S(1)}, u32[]{:S(2)}, u32[]{:S(2)}) collective-permute-start(bf16[64,7168]{1,0:T(8,128)(2,1)} %get-tuple-element.43), channel_id=1, source_target_pairs={{0,12},{1,13},{2,14},{3,15},{4,0},{5,1},{6,2},{7,3},{8,4},{9,5},{1... | collective-permute-start | bytes 2752520 | tf_op jit(solution)/shard_map/ppermute | solution.py:40
  95.8 0.9 copy-done.1
  96.7 13.7 %expert.5 = (bf16[64,7168]{1,0:T(8,128)(2,1)}, bf16[64,7168]{1,0:T(8,128)(2,1)}) custom-call(s32[1]{0:T(128)} %bitcast.expert_ref, bf16[64,7296]{1,0:T(8,128)(2,1)} %copy-done.1, bf16[64,7296]{1,0:T(8,128)(2,1)} %collective-permute-done.13.refs_1_, bf16[7168,256]{1,0:T(8,128)(2,1)} %bitcast.10, bf16[7168,256]{1,0:T(8,128)(2,1)} %bitcast.14, ...), custom_call_target="tpu_custom_call" | custom-call | flops 2818572288 | bytes 25690112 | tf_op jit(solution)/shard_map/expert/pallas_call | solution.py:126
  110.5 0.3 collective-permute-start.16
  110.7 3.2 %collective-permute-start.17 = (bf16[64,7168]{1,0:T(8,128)(2,1)}, bf16[64,7168]{1,0:T(8,128)(2,1)}, u32[]{:S(2)}, u32[]{:S(2)}) collective-permute-start(bf16[64,7168]{1,0:T(8,128)(2,1)} %get-tuple-element.51), channel_id=1, source_target_pairs={{0,12},{1,13},{2,14},{3,15},{4,0},{5,1},{6,2},{7,3},{8,4},{9,5},{1... | collective-permute-start | bytes 2752520 | tf_op jit(solution)/shard_map/ppermute | solution.py:40
  114.0 0.6 slice.77.length_ref
  114.5 13.8 %attend.3 = bf16[64,1024]{1,0:T(8,128)(2,1)} custom-call(s32[1]{0:T(128)} %slice.77.length_ref, bf16[128,1024]{1,0:T(8,128)(2,1)} %nope_ref.3, bf16[128,512]{1,0:T(8,128)(2,1)} %rope_ref.3, bf16[8,128,512]{2,1,0:T(8,128)(2,1)} %key_up_ref.3, bf16[8,512,128]{2,1,0:T(8,128)(2,1)} %value_up_ref.3, bf16[2,4096,512]{2,1,0:T(8,128)(2,1)} %latent_ref.3, ...), custom_call_target="tpu_custom_call" | custom-call | flops 6000000000 | bytes 8000000 | tf_op jit(solution)/shard_map/attend/pallas_call | solution.py:242
  128.4 1.5 add_convert_fusion
  129.9 0.5 collective-permute-start.19
  130.3 0.2 add_convert_fusion.1
  130.6 1.7 collective-permute-start.18
  132.3 11.1 %collective-permute-done.19 = bf16[64,7168]{1,0:T(8,128)(2,1)S(1)} collective-permute-done((bf16[64,7168]{1,0:T(8,128)(2,1)S(1)}, bf16[64,7168]{1,0:T(8,128)(2,1)S(1)}, u32[]{:S(2)}, u32[]{:S(2)}) %collective-permute-start.19) | collective-permute-done | bytes 917536 | tf_op jit(solution)/shard_map/ppermute | solution.py:40
  143.3 0.4 fusion.3
  143.7 1.6 collective-permute-done.18
  145.3 0.3 convert_add_fusion.1
  145.6 0.1 collective-permute-start.20
  145.8 3.3 %collective-permute-start.22 = (bf16[32,7168]{1,0:T(8,128)(2,1)S(1)}, bf16[32,7168]{1,0:T(8,128)(2,1)S(1)}, u32[]{:S(2)}, u32[]{:S(2)}) collective-permute-start(bf16[32,7168]{1,0:T(8,128)(2,1)S(1)} %concatenate.25), channel_id=1, source_target_pairs={{0,3},{1,0},{2,1},{3,2},{4,7},{5,4},{6,5},{7,6},{8,11},{9,8},{10,9... | collective-permute-start | bytes 1376264 | tf_op jit(solution)/shard_map/ppermute | solution.py:40
  149.1 6.3 %collective-permute-done.20 = bf16[32,7168]{1,0:T(8,128)(2,1)S(1)} collective-permute-done((bf16[32,7168]{1,0:T(8,128)(2,1)S(1)}, bf16[32,7168]{1,0:T(8,128)(2,1)S(1)}, u32[]{:S(2)}, u32[]{:S(2)}) %collective-permute-start.20) | collective-permute-done | bytes 458784 | tf_op jit(solution)/shard_map/ppermute | solution.py:40
  155.4 0.1 fusion.2
  155.5 0.1 collective-permute-start.21
  155.6 7.2 %collective-permute-done.21 = bf16[16,7168]{1,0:T(8,128)(2,1)S(1)} collective-permute-done((bf16[16,7168]{1,0:T(8,128)(2,1)S(1)}, bf16[16,7168]{1,0:T(8,128)(2,1)S(1)}, u32[]{:S(2)}, u32[]{:S(2)}) %collective-permute-start.21) | collective-permute-done | bytes 229408 | tf_op jit(solution)/shard_map/ppermute | solution.py:40
  162.8 0.1 convert_add_fusion.3
  162.9 0.0 copy-start.7
  162.9 0.3 collective-permute-start.23
  163.2 5.8 %collective-permute-done.23 = bf16[16,7168]{1,0:T(8,128)(2,1)S(1)} collective-permute-done((bf16[16,7168]{1,0:T(8,128)(2,1)S(1)}, bf16[16,7168]{1,0:T(8,128)(2,1)S(1)}, u32[]{:S(2)}, u32[]{:S(2)}) %collective-permute-start.23) | collective-permute-done | bytes 229408 | tf_op jit(solution)/shard_map/ppermute | solution.py:40
  169.0 0.1 fusion
  169.1 0.1 collective-permute-start.24
  169.2 0.1 collective-permute-start.25
  169.3 3.1 %collective-permute-start.26 = (bf16[8,7168]{1,0:T(8,128)(2,1)S(1)}, bf16[8,7168]{1,0:T(8,128)(2,1)S(1)}, u32[]{:S(2)}, u32[]{:S(2)}) collective-permute-start(bf16[8,7168]{1,0:T(8,128)(2,1)S(1)} %get-tuple-element.63), channel_id=1, source_target_pairs={{0,96},{1,97},{2,98},{3,99},{4,100},{5,101},{6,102},{7,103},{8,104... | collective-permute-start | bytes 344072 | tf_op jit(solution)/shard_map/ppermute | solution.py:40
  172.5 0.7 pad_maximum_fusion.2
  173.2 3.3 %collective-permute-done.24 = bf16[8,7168]{1,0:T(8,128)(2,1)S(1)} collective-permute-done((bf16[8,7168]{1,0:T(8,128)(2,1)S(1)}, bf16[8,7168]{1,0:T(8,128)(2,1)S(1)}, u32[]{:S(2)}, u32[]{:S(2)}) %collective-permute-start.24) | collective-permute-done | bytes 114720 | tf_op jit(solution)/shard_map/ppermute | solution.py:40
  176.4 0.9 collective-permute-done.26
  177.3 0.7 add_convert_fusion.2
  (40 shorter events, 0.3 us)
Async XLA Ops:
  2.4 8.1 %collective-permute-start = (bf16[8,7296]{1,0:T(8,128)(2,1)}, bf16[8,7296]{1,0:T(8,128)(2,1)S(1)}, u32[]{:S(2)}, u32[]{:S(2)}) collective-permute-start(bf16[8,7296]{1,0:T(8,128)(2,1)} %pack.1), channel_id=1, source_target_pairs={{0,96},{1,97},{2,98},{3,99},{4,100},{5,101},{6,102},{7,103},{8,104... | collective-permute-start | bytes 350216 | tf_op jit(solution)/shard_map/ppermute | solution.py:40
  6.5 6.6 %collective-permute-start.1 = (bf16[8,7296]{1,0:T(8,128)(2,1)}, bf16[8,7296]{1,0:T(8,128)(2,1)S(1)}, u32[]{:S(2)}, u32[]{:S(2)}) collective-permute-start(bf16[8,7296]{1,0:T(8,128)(2,1)} %pack.1), channel_id=1, source_target_pairs={{0,64},{1,65},{2,66},{3,67},{4,68},{5,69},{6,70},{7,71},{8,72},{9,... | collective-permute-start | bytes 350216 | tf_op jit(solution)/shard_map/ppermute | solution.py:40
  6.5 7.5 %collective-permute-start.2 = (bf16[8,7296]{1,0:T(8,128)(2,1)}, bf16[8,7296]{1,0:T(8,128)(2,1)S(1)}, u32[]{:S(2)}, u32[]{:S(2)}) collective-permute-start(bf16[8,7296]{1,0:T(8,128)(2,1)} %pack.1), channel_id=1, source_target_pairs={{0,32},{1,33},{2,34},{3,35},{4,36},{5,37},{6,38},{7,39},{8,40},{9,... | collective-permute-start | bytes 350216 | tf_op jit(solution)/shard_map/ppermute | solution.py:40
  14.9 13.0 %collective-permute-start.3 = (bf16[32,7296]{1,0:T(8,128)(2,1)S(1)}, bf16[32,7296]{1,0:T(8,128)(2,1)S(1)}, u32[]{:S(2)}, u32[]{:S(2)}) collective-permute-start(bf16[32,7296]{1,0:T(8,128)(2,1)S(1)} %pad_maximum_fusion), channel_id=1, source_target_pairs={{0,3},{1,0},{2,1},{3,2},{4,7},{5,4},{6,5},{7,6},{8,11},{9,8},{10,9... | collective-permute-start | bytes 1400840 | tf_op jit(solution)/shard_map/ppermute | solution.py:40
  18.0 9.8 %collective-permute-start.4 = (bf16[32,7296]{1,0:T(8,128)(2,1)S(1)}, bf16[32,7296]{1,0:T(8,128)(2,1)S(1)}, u32[]{:S(2)}, u32[]{:S(2)}) collective-permute-start(bf16[32,7296]{1,0:T(8,128)(2,1)S(1)} %pad_maximum_fusion), channel_id=1, source_target_pairs={{0,1},{1,2},{2,3},{3,0},{4,5},{5,6},{6,7},{7,4},{8,9},{9,10},{10,1... | collective-permute-start | bytes 1400840 | tf_op jit(solution)/shard_map/ppermute | solution.py:40
  18.0 35.8 %collective-permute-start.10 = (bf16[7168,256]{1,0:T(8,128)(2,1)}, bf16[7168,256]{1,0:T(8,128)(2,1)}, u32[]{:S(2)}, u32[]{:S(2)}) collective-permute-start(bf16[7168,256]{1,0:T(8,128)(2,1)} %bitcast.11), channel_id=1, source_target_pairs={{0,16},{16,0},{1,17},{17,1},{2,18},{18,2},{3,19},{19,3},{4,20},{20... | collective-permute-start | bytes 11010056 | tf_op jit(solution)/shard_map/ppermute | solution.py:56
  18.0 35.8 %collective-permute-start.11 = (bf16[256,7168]{1,0:T(8,128)(2,1)}, bf16[256,7168]{1,0:T(8,128)(2,1)}, u32[]{:S(2)}, u32[]{:S(2)}) collective-permute-start(bf16[256,7168]{1,0:T(8,128)(2,1)} %bitcast.15), channel_id=1, source_target_pairs={{0,16},{16,0},{1,17},{17,1},{2,18},{18,2},{3,19},{19,3},{4,20},{20... | collective-permute-start | bytes 11010056 | tf_op jit(solution)/shard_map/ppermute | solution.py:56
  18.5 35.3 %collective-permute-start.9 = (bf16[7168,256]{1,0:T(8,128)(2,1)}, bf16[7168,256]{1,0:T(8,128)(2,1)}, u32[]{:S(2)}, u32[]{:S(2)}) collective-permute-start(bf16[7168,256]{1,0:T(8,128)(2,1)} %bitcast.7), channel_id=1, source_target_pairs={{0,16},{16,0},{1,17},{17,1},{2,18},{18,2},{3,19},{19,3},{4,20},{20... | collective-permute-start | bytes 11010056 | tf_op jit(solution)/shard_map/ppermute | solution.py:56
  27.8 7.3 %collective-permute-start.5 = (bf16[16,7296]{1,0:T(8,128)(2,1)S(1)}, bf16[16,7296]{1,0:T(8,128)(2,1)S(1)}, u32[]{:S(2)}, u32[]{:S(2)}) collective-permute-start(bf16[16,7296]{1,0:T(8,128)(2,1)S(1)} %slice.91), channel_id=1, source_target_pairs={{0,1},{1,2},{2,3},{3,0},{4,5},{5,6},{6,7},{7,4},{8,9},{9,10},{10,1... | collective-permute-start | bytes 700424 | tf_op jit(solution)/shard_map/ppermute | solution.py:40
  27.9 7.9 %collective-permute-start.6 = (bf16[16,7296]{1,0:T(8,128)(2,1)S(1)}, bf16[16,7296]{1,0:T(8,128)(2,1)S(1)}, u32[]{:S(2)}, u32[]{:S(2)}) collective-permute-start(bf16[16,7296]{1,0:T(8,128)(2,1)S(1)} %slice.92), channel_id=1, source_target_pairs={{0,3},{1,0},{2,1},{3,2},{4,7},{5,4},{6,5},{7,6},{8,11},{9,8},{10,9... | collective-permute-start | bytes 700424 | tf_op jit(solution)/shard_map/ppermute | solution.py:40
  37.4 30.3 %collective-permute-start.7 = (bf16[128,7296]{1,0:T(8,128)(2,1)}, bf16[128,7296]{1,0:T(8,128)(2,1)S(1)}, u32[]{:S(2)}, u32[]{:S(2)}) collective-permute-start(bf16[128,7296]{1,0:T(8,128)(2,1)} %constant_dynamic-update-slice_fusion.refs_0_), channel_id=1, source_target_pairs={{0,12},{1,13},{2,14},{3,15},{4,0},{5,1},{6,2},{7,3},{8,4},{9,5},{1... | collective-permute-start | bytes 5603336 | tf_op jit(solution)/shard_map/ppermute | solution.py:40
  40.1 27.5 %collective-permute-start.8 = (bf16[128,7296]{1,0:T(8,128)(2,1)}, bf16[128,7296]{1,0:T(8,128)(2,1)}, u32[]{:S(2)}, u32[]{:S(2)}) collective-permute-start(bf16[128,7296]{1,0:T(8,128)(2,1)} %constant_dynamic-update-slice_fusion.refs_0_), channel_id=1, source_target_pairs={{0,4},{1,5},{2,6},{3,7},{4,8},{5,9},{6,10},{7,11},{8,12},{9,13},{1... | collective-permute-start | bytes 5603336 | tf_op jit(solution)/shard_map/ppermute | solution.py:40
  67.7 4.7 %copy-start = (bf16[128,7296]{1,0:T(8,128)(2,1)}, bf16[128,7296]{1,0:T(8,128)(2,1)S(1)}, u32[]{:S(2)}) copy-start(bf16[128,7296]{1,0:T(8,128)(2,1)S(1)} %collective-permute-done.7.refs_0_) | copy-start | bytes 5603332
  70.6 25.2 %collective-permute-start.12 = (bf16[64,7296]{1,0:T(8,128)(2,1)}, bf16[64,7296]{1,0:T(8,128)(2,1)S(1)}, u32[]{:S(2)}, u32[]{:S(2)}) collective-permute-start(bf16[64,7296]{1,0:T(8,128)(2,1)} %slice.75), channel_id=1, source_target_pairs={{0,4},{1,5},{2,6},{3,7},{4,8},{5,9},{6,10},{7,11},{8,12},{9,13},{1... | collective-permute-start | bytes 2801672 | tf_op jit(solution)/shard_map/ppermute | solution.py:40
  72.4 23.4 %collective-permute-start.13 = (bf16[64,7296]{1,0:T(8,128)(2,1)}, bf16[64,7296]{1,0:T(8,128)(2,1)}, u32[]{:S(2)}, u32[]{:S(2)}) collective-permute-start(bf16[64,7296]{1,0:T(8,128)(2,1)} %slice.76), channel_id=1, source_target_pairs={{0,12},{1,13},{2,14},{3,15},{4,0},{5,1},{6,2},{7,3},{8,4},{9,5},{1... | collective-permute-start | bytes 2801672 | tf_op jit(solution)/shard_map/ppermute | solution.py:40
  92.5 18.0 %collective-permute-start.14 = (bf16[64,7168]{1,0:T(8,128)(2,1)}, bf16[64,7168]{1,0:T(8,128)(2,1)S(1)}, u32[]{:S(2)}, u32[]{:S(2)}) collective-permute-start(bf16[64,7168]{1,0:T(8,128)(2,1)} %get-tuple-element.42), channel_id=1, source_target_pairs={{0,4},{1,5},{2,6},{3,7},{4,8},{5,9},{6,10},{7,11},{8,12},{9,13},{1... | collective-permute-start | bytes 2752520 | tf_op jit(solution)/shard_map/ppermute | solution.py:40
  92.5 21.4 %copy-start.8 = (s32[2]{0:T(128)S(1)}, s32[2]{0:T(128)}, u32[]{:S(2)}) copy-start(s32[2]{0:T(128)} %param.29) | copy-start | bytes 28
  92.6 17.9 %collective-permute-start.15 = (bf16[64,7168]{1,0:T(8,128)(2,1)}, bf16[64,7168]{1,0:T(8,128)(2,1)S(1)}, u32[]{:S(2)}, u32[]{:S(2)}) collective-permute-start(bf16[64,7168]{1,0:T(8,128)(2,1)} %get-tuple-element.43), channel_id=1, source_target_pairs={{0,12},{1,13},{2,14},{3,15},{4,0},{5,1},{6,2},{7,3},{8,4},{9,5},{1... | collective-permute-start | bytes 2752520 | tf_op jit(solution)/shard_map/ppermute | solution.py:40
  95.8 0.9 copy-start.1
  110.5 17.9 %collective-permute-start.16 = (bf16[64,7168]{1,0:T(8,128)(2,1)}, bf16[64,7168]{1,0:T(8,128)(2,1)S(1)}, u32[]{:S(2)}, u32[]{:S(2)}) collective-permute-start(bf16[64,7168]{1,0:T(8,128)(2,1)} %get-tuple-element.50), channel_id=1, source_target_pairs={{0,4},{1,5},{2,6},{3,7},{4,8},{5,9},{6,10},{7,11},{8,12},{9,13},{1... | collective-permute-start | bytes 2752520 | tf_op jit(solution)/shard_map/ppermute | solution.py:40
  110.7 17.6 %collective-permute-start.17 = (bf16[64,7168]{1,0:T(8,128)(2,1)}, bf16[64,7168]{1,0:T(8,128)(2,1)}, u32[]{:S(2)}, u32[]{:S(2)}) collective-permute-start(bf16[64,7168]{1,0:T(8,128)(2,1)} %get-tuple-element.51), channel_id=1, source_target_pairs={{0,12},{1,13},{2,14},{3,15},{4,0},{5,1},{6,2},{7,3},{8,4},{9,5},{1... | collective-permute-start | bytes 2752520 | tf_op jit(solution)/shard_map/ppermute | solution.py:40
  114.5 13.8 %copy-start.5 = (bf16[64,7168]{1,0:T(8,128)(2,1)S(1)}, bf16[64,7168]{1,0:T(8,128)(2,1)}, u32[]{:S(2)}) copy-start(bf16[64,7168]{1,0:T(8,128)(2,1)} %get-tuple-element.56) | copy-start | bytes 2752516
  128.3 2.0 %copy-start.4 = (bf16[64,7168]{1,0:T(8,128)(2,1)S(1)}, bf16[64,7168]{1,0:T(8,128)(2,1)}, u32[]{:S(2)}) copy-start(bf16[64,7168]{1,0:T(8,128)(2,1)} %get-tuple-element.49) | copy-start | bytes 2752516
  129.8 13.5 %copy-start.3 = (bf16[64,7168]{1,0:T(8,128)(2,1)S(1)}, bf16[64,7168]{1,0:T(8,128)(2,1)}, u32[]{:S(2)}) copy-start(bf16[64,7168]{1,0:T(8,128)(2,1)} %get-tuple-element.54) | copy-start | bytes 2752516
  129.9 13.5 %collective-permute-start.19 = (bf16[64,7168]{1,0:T(8,128)(2,1)S(1)}, bf16[64,7168]{1,0:T(8,128)(2,1)S(1)}, u32[]{:S(2)}, u32[]{:S(2)}) collective-permute-start(bf16[64,7168]{1,0:T(8,128)(2,1)S(1)} %add_convert_fusion), channel_id=1, source_target_pairs={{0,12},{1,13},{2,14},{3,15},{4,0},{5,1},{6,2},{7,3},{8,4},{9,5},{1... | collective-permute-start | bytes 2752520 | tf_op jit(solution)/shard_map/ppermute | solution.py:40
  130.6 14.7 %copy-start.2 = (bf16[64,7168]{1,0:T(8,128)(2,1)S(1)}, bf16[64,7168]{1,0:T(8,128)(2,1)}, u32[]{:S(2)}) copy-start(bf16[64,7168]{1,0:T(8,128)(2,1)} %get-tuple-element.39) | copy-start | bytes 2752516
  130.6 14.7 %collective-permute-start.18 = (bf16[64,7168]{1,0:T(8,128)(2,1)S(1)}, bf16[64,7168]{1,0:T(8,128)(2,1)S(1)}, u32[]{:S(2)}, u32[]{:S(2)}) collective-permute-start(bf16[64,7168]{1,0:T(8,128)(2,1)S(1)} %add_convert_fusion.1), channel_id=1, source_target_pairs={{0,4},{1,5},{2,6},{3,7},{4,8},{5,9},{6,10},{7,11},{8,12},{9,13},{1... | collective-permute-start | bytes 2752520 | tf_op jit(solution)/shard_map/ppermute | solution.py:40
  145.6 9.8 %collective-permute-start.20 = (bf16[32,7168]{1,0:T(8,128)(2,1)S(1)}, bf16[32,7168]{1,0:T(8,128)(2,1)S(1)}, u32[]{:S(2)}, u32[]{:S(2)}) collective-permute-start(bf16[32,7168]{1,0:T(8,128)(2,1)S(1)} %pad_maximum_fusion.1), channel_id=1, source_target_pairs={{0,1},{1,2},{2,3},{3,0},{4,5},{5,6},{6,7},{7,4},{8,9},{9,10},{10,1... | collective-permute-start | bytes 1376264 | tf_op jit(solution)/shard_map/ppermute | solution.py:40
  145.8 9.8 %collective-permute-start.22 = (bf16[32,7168]{1,0:T(8,128)(2,1)S(1)}, bf16[32,7168]{1,0:T(8,128)(2,1)S(1)}, u32[]{:S(2)}, u32[]{:S(2)}) collective-permute-start(bf16[32,7168]{1,0:T(8,128)(2,1)S(1)} %concatenate.25), channel_id=1, source_target_pairs={{0,3},{1,0},{2,1},{3,2},{4,7},{5,4},{6,5},{7,6},{8,11},{9,8},{10,9... | collective-permute-start | bytes 1376264 | tf_op jit(solution)/shard_map/ppermute | solution.py:40
  155.5 7.3 %collective-permute-start.21 = (bf16[16,7168]{1,0:T(8,128)(2,1)S(1)}, bf16[16,7168]{1,0:T(8,128)(2,1)S(1)}, u32[]{:S(2)}, u32[]{:S(2)}) collective-permute-start(bf16[16,7168]{1,0:T(8,128)(2,1)S(1)} %fusion.2), channel_id=1, source_target_pairs={{0,1},{1,2},{2,3},{3,0},{4,5},{5,6},{6,7},{7,4},{8,9},{9,10},{10,1... | collective-permute-start | bytes 688136 | tf_op jit(solution)/shard_map/ppermute | solution.py:40
  162.9 9.6 %copy-start.6 = (bf16[64,1024]{1,0:T(8,128)(2,1)S(1)}, bf16[64,1024]{1,0:T(8,128)(2,1)}, u32[]{:S(2)}) copy-start(bf16[64,1024]{1,0:T(8,128)(2,1)} %attend.2) | copy-start | bytes 393220
  162.9 9.6 %copy-start.7 = (bf16[64,1024]{1,0:T(8,128)(2,1)S(1)}, bf16[64,1024]{1,0:T(8,128)(2,1)}, u32[]{:S(2)}) copy-start(bf16[64,1024]{1,0:T(8,128)(2,1)} %attend.3) | copy-start | bytes 393220
  162.9 6.1 %collective-permute-start.23 = (bf16[16,7168]{1,0:T(8,128)(2,1)S(1)}, bf16[16,7168]{1,0:T(8,128)(2,1)S(1)}, u32[]{:S(2)}, u32[]{:S(2)}) collective-permute-start(bf16[16,7168]{1,0:T(8,128)(2,1)S(1)} %get-tuple-element.66), channel_id=1, source_target_pairs={{0,3},{1,0},{2,1},{3,2},{4,7},{5,4},{6,5},{7,6},{8,11},{9,8},{10,9... | collective-permute-start | bytes 688136 | tf_op jit(solution)/shard_map/ppermute | solution.py:40
  169.1 7.3 %collective-permute-start.24 = (bf16[8,7168]{1,0:T(8,128)(2,1)S(1)}, bf16[8,7168]{1,0:T(8,128)(2,1)S(1)}, u32[]{:S(2)}, u32[]{:S(2)}) collective-permute-start(bf16[8,7168]{1,0:T(8,128)(2,1)S(1)} %get-tuple-element.62), channel_id=1, source_target_pairs={{0,32},{1,33},{2,34},{3,35},{4,36},{5,37},{6,38},{7,39},{8,40},{9,... | collective-permute-start | bytes 344072 | tf_op jit(solution)/shard_map/ppermute | solution.py:40
  169.2 7.2 %collective-permute-start.25 = (bf16[8,7168]{1,0:T(8,128)(2,1)S(1)}, bf16[8,7168]{1,0:T(8,128)(2,1)S(1)}, u32[]{:S(2)}, u32[]{:S(2)}) collective-permute-start(bf16[8,7168]{1,0:T(8,128)(2,1)S(1)} %get-tuple-element.64), channel_id=1, source_target_pairs={{0,64},{1,65},{2,66},{3,67},{4,68},{5,69},{6,70},{7,71},{8,72},{9,... | collective-permute-start | bytes 344072 | tf_op jit(solution)/shard_map/ppermute | solution.py:40
  169.3 8.0 %collective-permute-start.26 = (bf16[8,7168]{1,0:T(8,128)(2,1)S(1)}, bf16[8,7168]{1,0:T(8,128)(2,1)S(1)}, u32[]{:S(2)}, u32[]{:S(2)}) collective-permute-start(bf16[8,7168]{1,0:T(8,128)(2,1)S(1)} %get-tuple-element.63), channel_id=1, source_target_pairs={{0,96},{1,97},{2,98},{3,99},{4,100},{5,101},{6,102},{7,103},{8,104... | collective-permute-start | bytes 344072 | tf_op jit(solution)/shard_map/ppermute | solution.py:40
where the time goes:
time: 178 us
  Pallas kernels  74.4 us (42%)
  waiting for transfers between devices  54 us (30%)
  starting transfers between devices  34.3 us (19%)
  local copies, waits for them, and re-layouts  9.42 us (5%)
  other arithmetic  5.01 us (3%)
    ppermute x24, waiting for transfers between devices, shift(): return lax.ppermute(value, AXES, pairs)  54 us
    pallas_call x3, Pallas kernels, expert_terms(): pl.pallas_call(functools.partial(expert_kernel, sources=len(pieces), outp...  45.1 us
    ppermute x24, starting transfers between devices, shift(): return lax.ppermute(value, AXES, pairs)  33.8 us
    pallas_call x2, Pallas kernels, attend(): pl.pallas_call(functools.partial(attention_kernel, sequence), grid_spec=p...  27.5 us
    unnamed x22, local copies, waits for them, and re-layouts  4.02 us
    slice x2, local copies, waits for them, and re-layouts, body(): far_low, far_high = (shift(below[:HALF], 2, 1), shift(above[HALF:], 2, -1))  3.88 us
  transfers between devices with their start and end apart: 27, of which 12 were waited for; matrix products, arithmetic and copies ran while one was open for 4% of the time, Pallas kernels for 41%

commit v1 on v0

--- a/solution.py
+++ b/solution.py
@@ -19,13 +19,14 @@
 SIZES = (4, 2, 4, 4)
 RING = 4
 ORDERS = ((0, 3, 2), (2, 0, 3))
-KERNEL_VMEM = 60 * 1024 * 1024
+KERNEL_VMEM = 28 * 1024 * 1024
 PACK = 128
 DEPTH = 1024
 UNITS = 256
 HALF = 64
 KEY_BLOCK = 1024
 HEAD_COUNT = 8
+PARTS = 2
 LATENT = 512
 LOG2E = 1.4426950408889634
 
@@ -58,92 +59,72 @@
 
 def expert_kernel(expert_ref, *refs, sources, outputs):
     row_hbm = refs[:sources]
-    gate_hbm, up_hbm, gate_other_hbm, up_other_hbm, down_hbm, down_other_hbm = refs[sources : sources + 6]
-    out_refs = refs[sources + 6 : sources + 6 + outputs]
-    rows_ref, weight_ref, down_ref, sums_ref, hidden_ref, row_sem, weight_sem, down_sem = refs[sources + 6 + outputs :]
-    width = weight_ref.shape[0]
+    both_ref, both_other_ref, down_ref, down_other_ref = refs[sources : sources + 4]
+    out_refs = refs[sources + 4 : sources + 4 + outputs]
+    rows_ref, sums_ref, hidden_ref, row_sem = refs[sources + 4 + outputs :]
+    width = both_ref.shape[0]
     steps = width // DEPTH
     span = rows_ref.shape[0] // sources
     row_copies = [
         pltpu.make_async_copy(source, rows_ref.at[pl.ds(i * span, span)], row_sem.at[i])
         for i, source in enumerate(row_hbm)
     ]
-    down_copies = [
-        pltpu.make_async_copy(source, down_ref.at[pl.ds(i * UNITS, UNITS)], down_sem.at[i])
-        for i, source in enumerate((down_hbm, down_other_hbm))
-    ]
-    matrices = (gate_hbm, gate_other_hbm, up_hbm, up_other_hbm)
-
-    def weight_copy(matrix, step):
-        part = pl.ds(step * DEPTH, DEPTH)
-        return pltpu.make_async_copy(
-            matrices[matrix].at[part],
-            weight_ref.at[part, pl.ds(matrix * UNITS, UNITS)],
-            weight_sem.at[matrix, step],
-        )
-
     for copy in row_copies:
         copy.start()
-    for step in range(steps):
-        for matrix in range(4):
-            weight_copy(matrix, step).start()
-    for copy in down_copies:
-        copy.start()
+    sums_ref[...] = jnp.zeros_like(sums_ref)
     for copy in row_copies:
         copy.wait()
-    sums_ref[...] = jnp.zeros_like(sums_ref)
 
     @pl.loop(0, steps)
     def _(step):
         part = pl.ds(pl.multiple_of(step * DEPTH, DEPTH), DEPTH)
-        for matrix in range(4):
-            weight_copy(matrix, step).wait()
-        sums_ref[...] += jnp.dot(rows_ref[:, part], weight_ref[part, :], preferred_element_type=jnp.float32)
+        piece = rows_ref[:, part]
+        for i, matrix in enumerate((both_ref, both_other_ref)):
+            sums_ref[i] += jnp.dot(piece, matrix[part, :], preferred_element_type=jnp.float32)
 
     extra = rows_ref[:, width : width + PACK].astype(jnp.float32)
     lane = lax.broadcasted_iota(jnp.int32, extra.shape, 1)
     pick = (lane % EXPERTS == expert_ref[0]) & (lane < 2 * EXPERTS)
     coefficient = jnp.sum(jnp.where(pick, extra, 0.0), axis=1, keepdims=True)
-    gate, up = sums_ref[:, : 2 * UNITS], sums_ref[:, 2 * UNITS :]
-    hidden = gate / (1.0 + jnp.exp(-gate)) * up * coefficient
-    hidden_ref[...] = jnp.where(coefficient > 0, hidden, 0.0).astype(jnp.bfloat16)
-    for copy in down_copies:
-        copy.wait()
+    for i in range(2):
+        gate, up = sums_ref[i, :, :UNITS], sums_ref[i, :, UNITS:]
+        hidden = gate / (1.0 + jnp.exp(-gate)) * up * coefficient
+        hidden_ref[i] = jnp.where(coefficient > 0, hidden, 0.0).astype(jnp.bfloat16)
 
     @pl.loop(0, steps)
     def _(step):
         part = pl.ds(pl.multiple_of(step * DEPTH, DEPTH), DEPTH)
-        result = jnp.dot(hidden_ref[...], down_ref[:, part], preferred_element_type=jnp.float32).astype(jnp.bfloat16)
+        result = jnp.dot(hidden_ref[0], down_ref[:, part], preferred_element_type=jnp.float32)
+        result += jnp.dot(hidden_ref[1], down_other_ref[:, part], preferred_element_type=jnp.float32)
+        result = result.astype(jnp.bfloat16)
         for i, out_ref in enumerate(out_refs):
             out_ref[:, part] = result[i * HALF : (i + 1) * HALF]
 
 
-def expert_terms(expert, pieces, weights, downs):
+def expert_terms(expert, pieces, weights):
     width = weights[0].shape[0]
     rows = sum(piece.shape[0] for piece in pieces)
     outputs = rows // HALF
-    anywhere = pl.BlockSpec(memory_space=pl.ANY)
+    weights = [pltpu.with_memory_space_constraint(matrix, pltpu.VMEM) for matrix in weights]
     return pl.pallas_call(
         functools.partial(expert_kernel, sources=len(pieces), outputs=outputs),
-        in_specs=[pl.BlockSpec(memory_space=pltpu.SMEM)] + [anywhere] * (len(pieces) + 6),
+        in_specs=[pl.BlockSpec(memory_space=pltpu.SMEM)]
+        + [pl.BlockSpec(memory_space=pl.ANY)] * len(pieces)
+        + [pl.BlockSpec(memory_space=pltpu.VMEM)] * 4,
         out_specs=[pl.BlockSpec(memory_space=pltpu.VMEM)] * outputs,
         out_shape=[jax.ShapeDtypeStruct((HALF, width), jnp.bfloat16)] * outputs,
         scratch_shapes=[
             pltpu.VMEM((rows, width + PACK), jnp.bfloat16),
-            pltpu.VMEM((width, 4 * UNITS), jnp.bfloat16),
-            pltpu.VMEM((2 * UNITS, width), jnp.bfloat16),
-            pltpu.VMEM((rows, 4 * UNITS), jnp.float32),
-            pltpu.VMEM((rows, 2 * UNITS), jnp.bfloat16),
+            pltpu.VMEM((2, rows, 2 * UNITS), jnp.float32),
+            pltpu.VMEM((2, rows, UNITS), jnp.bfloat16),
             pltpu.SemaphoreType.DMA((len(pieces),)),
-            pltpu.SemaphoreType.DMA((4, width // DEPTH)),
-            pltpu.SemaphoreType.DMA((2,)),
         ],
         compiler_params=pltpu.CompilerParams(vmem_limit_bytes=KERNEL_VMEM),
         cost_estimate=pl.CostEstimate(
-            flops=6 * rows * width * UNITS * 2, bytes_accessed=12 * width * UNITS + 4 * rows * width, transcendentals=0
+            flops=6 * rows * width * UNITS * 2, bytes_accessed=4 * rows * width, transcendentals=0
         ),
         name="expert",
-    )(expert, *pieces, *weights, *downs)
+    )(expert, *pieces, *weights)
 
 
 def pack_kernel(tokens_ref, routes_ref, scores_ref, out_ref):
@@ -180,18 +161,24 @@
     contract_last = (((1,), (1,)), ((), ()))
 
     def absorb(keys, rope_keys, values, bias):
-        scores = lax.dot_general(query_ref[...], keys, contract_last, preferred_element_type=jnp.float32)
-        scores += jnp.dot(query_rope_ref[...], rope_keys, preferred_element_type=jnp.float32)
-        scores = scores * scale + bias
-        old_top = top_ref[...]
-        top = jnp.maximum(old_top, jnp.max(scores, axis=1, keepdims=True))
-        shrink = jnp.exp2(old_top - top)
-        probs = jnp.exp2(scores - top)
-        top_ref[...] = top
-        sum_ref[...] = sum_ref[...] * shrink + jnp.sum(probs, axis=1, keepdims=True)
-        total_ref[...] = total_ref[...] * shrink + jnp.dot(
-            probs.astype(jnp.bfloat16), values, preferred_element_type=jnp.float32
-        )
+        rows = HEAD_COUNT * NEW // PARTS
+        parts = [slice(part * rows, (part + 1) * rows) for part in range(PARTS)]
+        biases = [bias if bias.shape[0] == 1 else bias[part] for part in parts]
+        scores = []
+        for part, added_bias in zip(parts, biases):
+            score = lax.dot_general(query_ref[part, :], keys, contract_last, preferred_element_type=jnp.float32)
+            score += jnp.dot(query_rope_ref[part, :], rope_keys, preferred_element_type=jnp.float32)
+            scores.append(score * scale + added_bias)
+        for part, score in zip(parts, scores):
+            old_top = top_ref[part, :]
+            top = jnp.maximum(old_top, jnp.max(score, axis=1, keepdims=True))
+            shrink = jnp.exp2(old_top - top)
+            probs = jnp.exp2(score - top)
+            top_ref[part, :] = top
+            sum_ref[part, :] = sum_ref[part, :] * shrink + jnp.sum(probs, axis=1, keepdims=True)
+            total_ref[part, :] = total_ref[part, :] * shrink + jnp.dot(
+                probs.astype(jnp.bfloat16), values, preferred_element_type=jnp.float32
+            )
 
     @pl.when(step == 0)
     def _():
@@ -288,13 +275,12 @@
     lengths,
 ):
     packed = packed_rows(tokens, routes, gate_scores)
-    small = jnp.concatenate([packed] + [shift(packed, 0, -distance) for distance in (1, 2, 3)], axis=0)
-    small, gate_weight, up_weight, down_weight = lax.optimization_barrier(
-        (small, gate_weight, up_weight, down_weight)
-    )
-    gate_part, up_part, down_part = gate_weight[0], up_weight[0], down_weight[0]
-    weights = (gate_part, up_part, with_other_core(gate_part), with_other_core(up_part))
-    downs = (down_part, with_other_core(down_part))
+    gathered = [packed] + [shift(packed, 0, -distance) for distance in (1, 2, 3)]
+    packed, gate_weight, up_weight = lax.optimization_barrier((packed, gate_weight, up_weight))
+    both = jnp.concatenate([gate_weight[0], up_weight[0]], axis=1)
+    small = jnp.concatenate(gathered, axis=0)
+    small, both, down_part = lax.optimization_barrier((small, both, down_weight[0]))
+    weights = (both, with_other_core(both), down_part, with_other_core(down_part))
     expert = (lax.axis_index("x") * RING + lax.axis_index("y")).astype(jnp.int32)[None]
     rope_keys, new_rope_keys = jnp.swapaxes(rope_cache, 1, 2), new_rope.T
 
@@ -303,27 +289,35 @@
             sequence, length, query_nope, query_rope, key_up, value_up, latent_cache, rope_keys, new_latent, new_rope_keys
         )
 
+    above, below = shift(small, 1, -1), shift(small, 1, 1)
     half = small.shape[0] // 2
-    above, below = shift(small, 1, -1), shift(small, 1, 1)
+    own_low = jnp.concatenate([small, above], axis=0)
+    below_low, above_low = shift(own_low, 2, 1), shift(own_low, 2, -1)
     far_low, far_high = shift(below[:half], 1, 1), shift(above[half:], 1, -1)
-    own = jnp.concatenate([small, above, far_low, far_high, below], axis=0)
-    above, below = shift(own, 2, -1), shift(own, 2, 1)
-    own, lengths = lax.optimization_barrier((own, lengths))
-    own_terms = expert_terms(expert, [own], weights, downs)
-    first_attention = attention(0, lengths[:1])
-    above, below, own_terms, first_attention = lax.optimization_barrier((above, below, own_terms, first_attention))
-    far_low, far_high = shift(below[:HALF], 2, 1), shift(above[HALF:], 2, -1)
-    above_low, above_high, below_low, below_high = expert_terms(expert, [above, below], weights, downs)
+    own_high = jnp.concatenate([far_low, far_high, below], axis=0)
+    below_high, above_high = shift(own_high, 2, 1), shift(own_high, 2, -1)
+    own_terms = expert_terms(expert, [own_low, own_high], weights)
+    far_low, far_high = shift(below_low, 2, 1), shift(above_high, 2, -1)
+    above_low, above_high, below_low, below_high, own_terms = lax.optimization_barrier(
+        (above_low, above_high, below_low, below_high, own_terms)
+    )
+    above_low, above_high, below_low, below_high = expert_terms(
+        expert, [above_low, above_high, below_low, below_high], weights
+    )
     near_high, near_low = shift(above_high, 2, 1), shift(below_low, 2, -1)
     far_low, far_high, above_high, below_low = lax.optimization_barrier((far_low, far_high, above_high, below_low))
-    far_terms = expert_terms(expert, [far_low, far_high], weights, downs)
+    far_terms = expert_terms(expert, [far_low, far_high], weights)
     far_terms, near_high, near_low = lax.optimization_barrier((far_terms, near_high, near_low))
     from_below, from_above = shift(far_terms[0], 2, 1), shift(far_terms[1], 2, -1)
     far_terms, lengths = lax.optimization_barrier((far_terms, lengths))
+    first_attention = attention(0, lengths[:1])
+    from_below, from_above, first_attention, lengths = lax.optimization_barrier(
+        (from_below, from_above, first_attention, lengths)
+    )
+    from_below = shift(narrowed(added(above_low, from_below)), 2, 1)
+    from_above = shift(narrowed(added(below_high, from_above)), 2, -1)
     second_attention = attention(1, lengths[1:])
     from_below, from_above, second_attention = lax.optimization_barrier((from_below, from_above, second_attention))
-    from_below = shift(narrowed(added(above_low, from_below)), 2, 1)
-    from_above = shift(narrowed(added(below_high, from_above)), 2, -1)
     low = added(own_terms[0], near_low, from_below)
     high = added(own_terms[1], near_high, from_above)
 

time: 178 us -> 164 us (0.921)
  Pallas kernels: 74.4 us -> 56.2 us
  starting transfers between devices: 34.3 us -> 41.7 us
  waiting for transfers between devices: 54 us -> 46.6 us
  other arithmetic: 5.01 us -> 9.56 us
    pallas_call x2, Pallas kernels: 27.5 us -> 16.5 us  [attend(): pl.pallas_call(functools.partial(attention_kernel, sequence), grid_spec=p...]
    ppermute x24 -> x26, starting transfers between devices: 33.8 us -> 41.6 us  [shift(): return lax.ppermute(value, AXES, pairs)]
    ppermute x24 -> x26, waiting for transfers between devices: 54 us -> 46.6 us  [shift(): return lax.ppermute(value, AXES, pairs)]
    pallas_call x3, Pallas kernels: 45.1 us -> 37.9 us  [expert_terms(): pl.pallas_call(functools.partial(expert_kernel, sources=len(pieces), outp...]
    concatenate x1 -> x2, other arithmetic: 0.93 us -> 6.77 us  [the longest x1 6.71 us: body(): both = jnp.concatenate([gate_weight[0], up_weight[0]], axis=1)]
    slice x2 -> x0, local copies, waits for them, and re-layouts: 3.88 us -> none  [body(): far_low, far_high = (shift(below[:HALF], 2, 1), shift(above[HALF:], 2, -1))]
    unnamed x22 -> x27, local copies, waits for them, and re-layouts: 4.02 us -> 7.53 us
  transfers between devices with their start and end apart: 27 -> 28, of which waited for: 12 -> 11; matrix products, arithmetic and copies ran while one was open for 4% -> 5% of each run, Pallas kernels for 41% -> 33%
where the time goes in v1:
time: 164 us; the launch traced here: 163 us
  Pallas kernels  56.2 us (34%)
  waiting for transfers between devices  46.6 us (28%)
  starting transfers between devices  41.7 us (25%)
  other arithmetic  9.56 us (6%)
  local copies, waits for them, and re-layouts  8.32 us (5%)
    ppermute x26, waiting for transfers between devices, shift(): return lax.ppermute(value, AXES, pairs)  46.6 us
    ppermute x26, starting transfers between devices, shift(): return lax.ppermute(value, AXES, pairs)  41.6 us
    pallas_call x3, Pallas kernels, expert_terms(): pl.pallas_call(functools.partial(expert_kernel, sources=len(pieces), outp...  37.9 us
    pallas_call x2, Pallas kernels, attend(): pl.pallas_call(functools.partial(attention_kernel, sequence), grid_spec=p...  16.5 us
    unnamed x27, local copies, waits for them, and re-layouts  7.53 us
    concatenate x1, other arithmetic, body(): both = jnp.concatenate([gate_weight[0], up_weight[0]], axis=1)  6.71 us
  transfers between devices with their start and end apart: 28, of which 11 were waited for; matrix products, arithmetic and copies ran while one was open for 5% of the time, Pallas kernels for 33%

profile of v1, /device:TPU:0, one launch (start us, length us, event | category | flops | bytes accessed | tf_op | source)
XLA Modules:
  0.0 163.4 jit_solution(5115192717979502926)
XLA Ops:
  0.6 1.8 %pack.1 = bf16[8,7296]{1,0:T(8,128)(2,1)} custom-call(bf16[8,7168]{1,0:T(8,128)(2,1)} %tokens_ref.1, s32[8,8]{1,0:T(8,128)} %routes_ref.1, f32[8,8]{1,0:T(8,128)} %scores_ref.1), custom_call_target="tpu_custom_call" | custom-call | tf_op jit(solution)/shard_map/pack/pallas_call | solution.py:147
  2.4 4.1 %collective-permute-start = (bf16[8,7296]{1,0:T(8,128)(2,1)}, bf16[8,7296]{1,0:T(8,128)(2,1)S(1)}, u32[]{:S(2)}, u32[]{:S(2)}) collective-permute-start(bf16[8,7296]{1,0:T(8,128)(2,1)} %pack.1), channel_id=1, source_target_pairs={{0,96},{1,97},{2,98},{3,99},{4,100},{5,101},{6,102},{7,103},{8,104... | collective-permute-start | bytes 350216 | tf_op jit(solution)/shard_map/ppermute | solution.py:41
  6.5 1.3 collective-permute-start.2
  7.8 6.7 %pad_maximum_fusion.refs_2_.refs_4_ = bf16[7168,512]{1,0:T(8,128)(2,1)} fusion(bf16[7168,256]{1,0:T(8,128)(2,1)} %bitcast.12, bf16[7168,256]{1,0:T(8,128)(2,1)} %bitcast.13), kind=kLoop, calls=%fused_computation | loop fusion | flops 14680064 | bytes 14680064 | tf_op jit(solution)/shard_map/concatenate | solution.py:280
  14.5 0.1 pad_maximum_fusion.1
  14.6 0.1 collective-permute-start.11
  14.6 1.6 %collective-permute-start.5 = (bf16[32,7296]{1,0:T(8,128)(2,1)S(1)}, bf16[32,7296]{1,0:T(8,128)(2,1)S(1)}, u32[]{:S(2)}, u32[]{:S(2)}) collective-permute-start(bf16[32,7296]{1,0:T(8,128)(2,1)S(1)} %pad_maximum_fusion.1), channel_id=1, source_target_pairs={{0,1},{1,2},{2,3},{3,0},{4,5},{5,6},{6,7},{7,4},{8,9},{9,10},{10,1... | collective-permute-start | bytes 1400840 | tf_op jit(solution)/shard_map/ppermute | solution.py:41
  16.3 1.7 %collective-permute-start.3 = (bf16[32,7296]{1,0:T(8,128)(2,1)S(1)}, bf16[32,7296]{1,0:T(8,128)(2,1)S(1)}, u32[]{:S(2)}, u32[]{:S(2)}) collective-permute-start(bf16[32,7296]{1,0:T(8,128)(2,1)S(1)} %pad_maximum_fusion.1), channel_id=1, source_target_pairs={{0,3},{1,0},{2,1},{3,2},{4,7},{5,4},{6,5},{7,6},{8,11},{9,8},{10,9... | collective-permute-start | bytes 1400840 | tf_op jit(solution)/shard_map/ppermute | solution.py:41
  18.0 6.5 %collective-permute-done.5 = bf16[32,7296]{1,0:T(8,128)(2,1)S(1)} collective-permute-done((bf16[32,7296]{1,0:T(8,128)(2,1)S(1)}, bf16[32,7296]{1,0:T(8,128)(2,1)S(1)}, u32[]{:S(2)}, u32[]{:S(2)}) %collective-permute-start.5) | collective-permute-done | bytes 466976 | tf_op jit(solution)/shard_map/ppermute | solution.py:41
  24.5 0.4 collective-permute-start.6
  25.0 2.9 %collective-permute-start.7 = (bf16[16,7296]{1,0:T(8,128)(2,1)S(1)}, bf16[16,7296]{1,0:T(8,128)(2,1)S(1)}, u32[]{:S(2)}, u32[]{:S(2)}) collective-permute-start(bf16[16,7296]{1,0:T(8,128)(2,1)S(1)} %slice.84), channel_id=1, source_target_pairs={{0,3},{1,0},{2,1},{3,2},{4,7},{5,4},{6,5},{7,6},{8,11},{9,8},{10,9... | collective-permute-start | bytes 700424 | tf_op jit(solution)/shard_map/ppermute | solution.py:41
  28.0 1.6 collective-permute-start.9
  29.5 3.2 %collective-permute-done.6 = bf16[16,7296]{1,0:T(8,128)(2,1)S(1)} collective-permute-done((bf16[16,7296]{1,0:T(8,128)(2,1)S(1)}, bf16[16,7296]{1,0:T(8,128)(2,1)S(1)}, u32[]{:S(2)}, u32[]{:S(2)}) %collective-permute-start.6) | collective-permute-done | bytes 233504 | tf_op jit(solution)/shard_map/ppermute | solution.py:41
  32.9 2.8 %collective-permute-start.8 = (bf16[64,7296]{1,0:T(8,128)(2,1)S(1)}, bf16[64,7296]{1,0:T(8,128)(2,1)}, u32[]{:S(2)}, u32[]{:S(2)}) collective-permute-start(bf16[64,7296]{1,0:T(8,128)(2,1)S(1)} %constant_dynamic-update-slice_fusion.2.refs_1_), channel_id=1, source_target_pairs={{0,12},{1,13},{2,14},{3,15},{4,0},{5,1},{6,2},{7,3},{8,4},{9,5},{1... | collective-permute-start | bytes 2801672 | tf_op jit(solution)/shard_map/ppermute | solution.py:41
  35.7 0.8 collective-permute-start.4
  36.5 6.3 %collective-permute-done.9.refs_2_ = bf16[64,7296]{1,0:T(8,128)(2,1)S(1)} collective-permute-done((bf16[64,7296]{1,0:T(8,128)(2,1)S(1)}, bf16[64,7296]{1,0:T(8,128)(2,1)S(1)}, u32[]{:S(2)}, u32[]{:S(2)}) %collective-permute-start.9) | collective-permute-done | bytes 933920 | tf_op jit(solution)/shard_map/ppermute | solution.py:41
  42.8 0.9 copy-done.10
  43.8 0.3 collective-permute-start.10
  44.0 2.7 %collective-permute-done.8.refs_1_ = bf16[64,7296]{1,0:T(8,128)(2,1)} collective-permute-done((bf16[64,7296]{1,0:T(8,128)(2,1)S(1)}, bf16[64,7296]{1,0:T(8,128)(2,1)}, u32[]{:S(2)}, u32[]{:S(2)}) %collective-permute-start.8) | collective-permute-done | bytes 933920 | tf_op jit(solution)/shard_map/ppermute | solution.py:41
  46.8 1.3 collective-permute-start.13
  48.1 2.5 %collective-permute-start.14 = (bf16[64,7296]{1,0:T(8,128)(2,1)}, bf16[64,7296]{1,0:T(8,128)(2,1)S(1)}, u32[]{:S(2)}, u32[]{:S(2)}) collective-permute-start(bf16[64,7296]{1,0:T(8,128)(2,1)} %collective-permute-done.8.refs_1_), channel_id=1, source_target_pairs={{0,12},{1,13},{2,14},{3,15},{4,0},{5,1},{6,2},{7,3},{8,4},{9,5},{1... | collective-permute-start | bytes 2801672 | tf_op jit(solution)/shard_map/ppermute | solution.py:41
  50.6 3.1 %copy-done = bf16[7168,512]{1,0:T(8,128)(2,1)S(1)} copy-done((bf16[7168,512]{1,0:T(8,128)(2,1)S(1)}, bf16[7168,512]{1,0:T(8,128)(2,1)}, u32[]{:S(2)}) %copy-start) | copy-done | bytes 7340056
  53.7 11.2 %expert.3 = (bf16[64,7168]{1,0:T(8,128)(2,1)S(1)}, bf16[64,7168]{1,0:T(8,128)(2,1)S(1)}) custom-call(s32[1]{0:T(128)} %bitcast.3.expert_ref, bf16[64,7296]{1,0:T(8,128)(2,1)S(1)} %constant_dynamic-update-slice_fusion.refs_0_, bf16[64,7296]{1,0:T(8,128)(2,1)S(1)} %constant_dynamic-update-slice_fusion.2.refs_1_, bf16[7168,512]{1,0:T(8,128)(2,1)S(1)} %copy-done, ...), custom_call_target="tpu_custom_call" | custom-call | flops 2818572288 | bytes 3670016 | tf_op jit(solution)/shard_map/expert/pallas_call | solution.py:109
  64.9 15.5 %expert.4 = (bf16[64,7168]{1,0:T(8,128)(2,1)S(1)}, bf16[64,7168]{1,0:T(8,128)(2,1)S(1)}, bf16[64,7168]{1,0:T(8,128)(2,1)S(1)}, bf16[64,7168]{1,0:T(8,128)(2,1)S(1)}) custom-call(s32[1]{0:T(128)} %bitcast.3.expert_ref, bf16[64,7296]{1,0:T(8,128)(2,1)S(1)} %collective-permute-done.4.refs_0_, bf16[64,7296]{1,0:T(8,128)(2,1)} %collective-permute-done.8.refs_1_, ...), custom_call_target="tpu_custom_call" | custom-call | flops 5637144576 | bytes 7340032 | tf_op jit(solution)/shard_map/expert/pallas_call | solution.py:109
  80.4 0.1 collective-permute-start.15
  80.5 0.0 copy-start.2
  80.5 0.0 copy-start.3
  80.5 0.0 copy-start.4
  80.6 0.0 copy-start.7
  80.6 0.0 copy-start.8
  80.6 3.3 %collective-permute-start.16 = (bf16[64,7168]{1,0:T(8,128)(2,1)S(1)}, bf16[64,7168]{1,0:T(8,128)(2,1)S(1)}, u32[]{:S(2)}, u32[]{:S(2)}) collective-permute-start(bf16[64,7168]{1,0:T(8,128)(2,1)S(1)} %get-tuple-element.48), channel_id=1, source_target_pairs={{0,12},{1,13},{2,14},{3,15},{4,0},{5,1},{6,2},{7,3},{8,4},{9,5},{1... | collective-permute-start | bytes 2752520 | tf_op jit(solution)/shard_map/ppermute | solution.py:41
  83.9 11.2 %expert.5 = (bf16[64,7168]{1,0:T(8,128)(2,1)S(1)}, bf16[64,7168]{1,0:T(8,128)(2,1)S(1)}) custom-call(s32[1]{0:T(128)} %bitcast.3.expert_ref, bf16[64,7296]{1,0:T(8,128)(2,1)S(1)} %collective-permute-done.13.refs_0_, bf16[64,7296]{1,0:T(8,128)(2,1)S(1)} %collective-permute-done.14.refs_1_, bf16[7168,512]{1,0:T(8,128)(2,1)S(1)} %copy-done, ...), custom_call_target="tpu_custom_call" | custom-call | flops 2818572288 | bytes 3670016 | tf_op jit(solution)/shard_map/expert/pallas_call | solution.py:109
  95.1 0.0 collective-permute-done.15
  95.1 0.3 collective-permute-start.17
  95.4 3.0 %collective-permute-start.18 = (bf16[64,7168]{1,0:T(8,128)(2,1)S(1)}, bf16[64,7168]{1,0:T(8,128)(2,1)S(1)}, u32[]{:S(2)}, u32[]{:S(2)}) collective-permute-start(bf16[64,7168]{1,0:T(8,128)(2,1)S(1)} %get-tuple-element.56), channel_id=1, source_target_pairs={{0,12},{1,13},{2,14},{3,15},{4,0},{5,1},{6,2},{7,3},{8,4},{9,5},{1... | collective-permute-start | bytes 2752520 | tf_op jit(solution)/shard_map/ppermute | solution.py:41
  98.5 3.4 %copy-done.1 = bf16[2,4096,512]{2,1,0:T(8,128)(2,1)S(1)} copy-done((bf16[2,4096,512]{2,1,0:T(8,128)(2,1)S(1)}, bf16[2,4096,512]{2,1,0:T(8,128)(2,1)}, u32[]{:S(2)}) %copy-start.1) | copy-done | bytes 8388632
  101.9 7.1 %attend.2 = bf16[64,1024]{1,0:T(8,128)(2,1)S(1)} custom-call(s32[1]{0:T(128)S(1)} %bitcast.11, bf16[128,1024]{1,0:T(8,128)(2,1)S(1)} %copy-done.5, bf16[128,512]{1,0:T(8,128)(2,1)S(1)} %copy-done.6, bf16[8,128,512]{2,1,0:T(8,128)(2,1)S(1)} %copy-done.2, bf16[8,512,128]{2,1,0:T(8,128)(2,1)S(1)} %copy-done.3, bf16[2,4096,512]{2,1,0:T(8,128)(2,1)S(1)} %copy-done.1, ...), custom_call_target="tpu_custom_call" | custom-call | flops 6000000000 | bytes 8000000 | tf_op jit(solution)/shard_map/attend/pallas_call | solution.py:229
  109.0 0.8 collective-permute-done.17
  109.8 0.2 add_convert_fusion
  110.1 3.3 %collective-permute-start.20 = (bf16[64,7168]{1,0:T(8,128)(2,1)S(1)}, bf16[64,7168]{1,0:T(8,128)(2,1)S(1)}, u32[]{:S(2)}, u32[]{:S(2)}) collective-permute-start(bf16[64,7168]{1,0:T(8,128)(2,1)S(1)} %add_convert_fusion), channel_id=1, source_target_pairs={{0,12},{1,13},{2,14},{3,15},{4,0},{5,1},{6,2},{7,3},{8,4},{9,5},{1... | collective-permute-start | bytes 2752520 | tf_op jit(solution)/shard_map/ppermute | solution.py:41
  113.4 0.2 add_convert_fusion.1
  113.6 0.1 collective-permute-start.19
  113.7 0.6 slice.69.length_ref
  114.2 9.4 %attend.3 = bf16[64,1024]{1,0:T(8,128)(2,1)S(1)} custom-call(s32[1]{0:T(128)} %slice.69.length_ref, bf16[128,1024]{1,0:T(8,128)(2,1)S(1)} %copy-done.5, bf16[128,512]{1,0:T(8,128)(2,1)S(1)} %copy-done.6, bf16[8,128,512]{2,1,0:T(8,128)(2,1)S(1)} %copy-done.2, bf16[8,512,128]{2,1,0:T(8,128)(2,1)S(1)} %copy-done.3, bf16[2,4096,512]{2,1,0:T(8,128)(2,1)S(1)} %copy-done.1, ...), custom_call_target="tpu_custom_call" | custom-call | flops 6000000000 | bytes 8000000 | tf_op jit(solution)/shard_map/attend/pallas_call | solution.py:229
  123.7 0.6 collective-permute-done.20
  124.3 4.0 %collective-permute-done.19 = bf16[64,7168]{1,0:T(8,128)(2,1)S(1)} collective-permute-done((bf16[64,7168]{1,0:T(8,128)(2,1)S(1)}, bf16[64,7168]{1,0:T(8,128)(2,1)S(1)}, u32[]{:S(2)}, u32[]{:S(2)}) %collective-permute-start.19) | collective-permute-done | bytes 917536 | tf_op jit(solution)/shard_map/ppermute | solution.py:41
  128.2 0.3 fusion.3
  128.6 0.3 convert_add_fusion.1
  129.0 0.1 collective-permute-start.21
  129.1 3.3 %collective-permute-start.23 = (bf16[32,7168]{1,0:T(8,128)(2,1)S(1)}, bf16[32,7168]{1,0:T(8,128)(2,1)S(1)}, u32[]{:S(2)}, u32[]{:S(2)}) collective-permute-start(bf16[32,7168]{1,0:T(8,128)(2,1)S(1)} %concatenate.33), channel_id=1, source_target_pairs={{0,3},{1,0},{2,1},{3,2},{4,7},{5,4},{6,5},{7,6},{8,11},{9,8},{10,9... | collective-permute-start | bytes 1376264 | tf_op jit(solution)/shard_map/ppermute | solution.py:41
  132.4 6.3 %collective-permute-done.21 = bf16[32,7168]{1,0:T(8,128)(2,1)S(1)} collective-permute-done((bf16[32,7168]{1,0:T(8,128)(2,1)S(1)}, bf16[32,7168]{1,0:T(8,128)(2,1)S(1)}, u32[]{:S(2)}, u32[]{:S(2)}) %collective-permute-start.21) | collective-permute-done | bytes 458784 | tf_op jit(solution)/shard_map/ppermute | solution.py:41
  138.8 0.1 fusion.2
  138.8 0.1 collective-permute-start.22
  138.9 7.2 %collective-permute-done.22 = bf16[16,7168]{1,0:T(8,128)(2,1)S(1)} collective-permute-done((bf16[16,7168]{1,0:T(8,128)(2,1)S(1)}, bf16[16,7168]{1,0:T(8,128)(2,1)S(1)}, u32[]{:S(2)}, u32[]{:S(2)}) %collective-permute-start.22) | collective-permute-done | bytes 229408 | tf_op jit(solution)/shard_map/ppermute | solution.py:41
  146.1 0.1 convert_add_fusion.3
  146.2 0.1 collective-permute-start.24
  146.3 6.0 %collective-permute-done.24 = bf16[16,7168]{1,0:T(8,128)(2,1)S(1)} collective-permute-done((bf16[16,7168]{1,0:T(8,128)(2,1)S(1)}, bf16[16,7168]{1,0:T(8,128)(2,1)S(1)}, u32[]{:S(2)}, u32[]{:S(2)}) %collective-permute-start.24) | collective-permute-done | bytes 229408 | tf_op jit(solution)/shard_map/ppermute | solution.py:41
  152.3 0.1 fusion
  152.5 3.9 %collective-permute-start.25 = (bf16[8,7168]{1,0:T(8,128)(2,1)S(1)}, bf16[8,7168]{1,0:T(8,128)(2,1)S(1)}, u32[]{:S(2)}, u32[]{:S(2)}) collective-permute-start(bf16[8,7168]{1,0:T(8,128)(2,1)S(1)} %get-tuple-element.70), channel_id=1, source_target_pairs={{0,32},{1,33},{2,34},{3,35},{4,36},{5,37},{6,38},{7,39},{8,40},{9,... | collective-permute-start | bytes 344072 | tf_op jit(solution)/shard_map/ppermute | solution.py:41
  156.4 1.2 collective-permute-start.26
  157.6 1.5 collective-permute-start.27
  159.1 0.7 pad_maximum_fusion.3
  159.9 2.8 %collective-permute-done.26 = bf16[8,7168]{1,0:T(8,128)(2,1)S(1)} collective-permute-done((bf16[8,7168]{1,0:T(8,128)(2,1)S(1)}, bf16[8,7168]{1,0:T(8,128)(2,1)S(1)}, u32[]{:S(2)}, u32[]{:S(2)}) %collective-permute-start.26) | collective-permute-done | bytes 114720 | tf_op jit(solution)/shard_map/ppermute | solution.py:41
  162.7 0.7 add_convert_fusion.2
  (47 shorter events, 0.4 us)
Async XLA Ops:
  2.4 12.1 %collective-permute-start = (bf16[8,7296]{1,0:T(8,128)(2,1)}, bf16[8,7296]{1,0:T(8,128)(2,1)S(1)}, u32[]{:S(2)}, u32[]{:S(2)}) collective-permute-start(bf16[8,7296]{1,0:T(8,128)(2,1)} %pack.1), channel_id=1, source_target_pairs={{0,96},{1,97},{2,98},{3,99},{4,100},{5,101},{6,102},{7,103},{8,104... | collective-permute-start | bytes 350216 | tf_op jit(solution)/shard_map/ppermute | solution.py:41
  6.5 8.0 %collective-permute-start.1 = (bf16[8,7296]{1,0:T(8,128)(2,1)}, bf16[8,7296]{1,0:T(8,128)(2,1)S(1)}, u32[]{:S(2)}, u32[]{:S(2)}) collective-permute-start(bf16[8,7296]{1,0:T(8,128)(2,1)} %pack.1), channel_id=1, source_target_pairs={{0,64},{1,65},{2,66},{3,67},{4,68},{5,69},{6,70},{7,71},{8,72},{9,... | collective-permute-start | bytes 350216 | tf_op jit(solution)/shard_map/ppermute | solution.py:41
  6.5 8.0 %collective-permute-start.2 = (bf16[8,7296]{1,0:T(8,128)(2,1)}, bf16[8,7296]{1,0:T(8,128)(2,1)S(1)}, u32[]{:S(2)}, u32[]{:S(2)}) collective-permute-start(bf16[8,7296]{1,0:T(8,128)(2,1)} %pack.1), channel_id=1, source_target_pairs={{0,32},{1,33},{2,34},{3,35},{4,36},{5,37},{6,38},{7,39},{8,40},{9,... | collective-permute-start | bytes 350216 | tf_op jit(solution)/shard_map/ppermute | solution.py:41
  7.8 6.7 %copy-start.11 = (bf16[8,7296]{1,0:T(8,128)(2,1)S(1)}, bf16[8,7296]{1,0:T(8,128)(2,1)}, u32[]{:S(2)}) copy-start(bf16[8,7296]{1,0:T(8,128)(2,1)} %pack.1) | copy-start | bytes 350212
  14.6 36.0 %collective-permute-start.11 = (bf16[7168,512]{1,0:T(8,128)(2,1)}, bf16[7168,512]{1,0:T(8,128)(2,1)}, u32[]{:S(2)}, u32[]{:S(2)}) collective-permute-start(bf16[7168,512]{1,0:T(8,128)(2,1)} %pad_maximum_fusion.refs_2_.refs_4_), channel_id=1, source_target_pairs={{0,16},{16,0},{1,17},{17,1},{2,18},{18,2},{3,19},{19,3},{4,20},{20... | collective-permute-start | bytes 22020104 | tf_op jit(solution)/shard_map/ppermute | solution.py:57
  14.6 9.8 %collective-permute-start.5 = (bf16[32,7296]{1,0:T(8,128)(2,1)S(1)}, bf16[32,7296]{1,0:T(8,128)(2,1)S(1)}, u32[]{:S(2)}, u32[]{:S(2)}) collective-permute-start(bf16[32,7296]{1,0:T(8,128)(2,1)S(1)} %pad_maximum_fusion.1), channel_id=1, source_target_pairs={{0,1},{1,2},{2,3},{3,0},{4,5},{5,6},{6,7},{7,4},{8,9},{9,10},{10,1... | collective-permute-start | bytes 1400840 | tf_op jit(solution)/shard_map/ppermute | solution.py:41
  16.3 8.7 %collective-permute-start.3 = (bf16[32,7296]{1,0:T(8,128)(2,1)S(1)}, bf16[32,7296]{1,0:T(8,128)(2,1)S(1)}, u32[]{:S(2)}, u32[]{:S(2)}) collective-permute-start(bf16[32,7296]{1,0:T(8,128)(2,1)S(1)} %pad_maximum_fusion.1), channel_id=1, source_target_pairs={{0,3},{1,0},{2,1},{3,2},{4,7},{5,4},{6,5},{7,6},{8,11},{9,8},{10,9... | collective-permute-start | bytes 1400840 | tf_op jit(solution)/shard_map/ppermute | solution.py:41
  18.0 30.1 %collective-permute-start.12 = (bf16[256,7168]{1,0:T(8,128)(2,1)}, bf16[256,7168]{1,0:T(8,128)(2,1)}, u32[]{:S(2)}, u32[]{:S(2)}) collective-permute-start(bf16[256,7168]{1,0:T(8,128)(2,1)} %bitcast.2.refs_4_.refs_6_), channel_id=1, source_target_pairs={{0,16},{16,0},{1,17},{17,1},{2,18},{18,2},{3,19},{19,3},{4,20},{20... | collective-permute-start | bytes 11010056 | tf_op jit(solution)/shard_map/ppermute | solution.py:57
  24.5 8.2 %collective-permute-start.6 = (bf16[16,7296]{1,0:T(8,128)(2,1)S(1)}, bf16[16,7296]{1,0:T(8,128)(2,1)S(1)}, u32[]{:S(2)}, u32[]{:S(2)}) collective-permute-start(bf16[16,7296]{1,0:T(8,128)(2,1)S(1)} %slice.83), channel_id=1, source_target_pairs={{0,1},{1,2},{2,3},{3,0},{4,5},{5,6},{6,7},{7,4},{8,9},{9,10},{10,1... | collective-permute-start | bytes 700424 | tf_op jit(solution)/shard_map/ppermute | solution.py:41
  25.0 7.8 %collective-permute-start.7 = (bf16[16,7296]{1,0:T(8,128)(2,1)S(1)}, bf16[16,7296]{1,0:T(8,128)(2,1)S(1)}, u32[]{:S(2)}, u32[]{:S(2)}) collective-permute-start(bf16[16,7296]{1,0:T(8,128)(2,1)S(1)} %slice.84), channel_id=1, source_target_pairs={{0,3},{1,0},{2,1},{3,2},{4,7},{5,4},{6,5},{7,6},{8,11},{9,8},{10,9... | collective-permute-start | bytes 700424 | tf_op jit(solution)/shard_map/ppermute | solution.py:41
  28.0 14.8 %collective-permute-start.9 = (bf16[64,7296]{1,0:T(8,128)(2,1)S(1)}, bf16[64,7296]{1,0:T(8,128)(2,1)S(1)}, u32[]{:S(2)}, u32[]{:S(2)}) collective-permute-start(bf16[64,7296]{1,0:T(8,128)(2,1)S(1)} %constant_dynamic-update-slice_fusion.refs_0_), channel_id=1, source_target_pairs={{0,4},{1,5},{2,6},{3,7},{4,8},{5,9},{6,10},{7,11},{8,12},{9,13},{1... | collective-permute-start | bytes 2801672 | tf_op jit(solution)/shard_map/ppermute | solution.py:41
  32.9 13.9 %collective-permute-start.8 = (bf16[64,7296]{1,0:T(8,128)(2,1)S(1)}, bf16[64,7296]{1,0:T(8,128)(2,1)}, u32[]{:S(2)}, u32[]{:S(2)}) collective-permute-start(bf16[64,7296]{1,0:T(8,128)(2,1)S(1)} %constant_dynamic-update-slice_fusion.2.refs_1_), channel_id=1, source_target_pairs={{0,12},{1,13},{2,14},{3,15},{4,0},{5,1},{6,2},{7,3},{8,4},{9,5},{1... | collective-permute-start | bytes 2801672 | tf_op jit(solution)/shard_map/ppermute | solution.py:41
  35.7 29.2 %collective-permute-start.4 = (bf16[64,7296]{1,0:T(8,128)(2,1)S(1)}, bf16[64,7296]{1,0:T(8,128)(2,1)S(1)}, u32[]{:S(2)}, u32[]{:S(2)}) collective-permute-start(bf16[64,7296]{1,0:T(8,128)(2,1)S(1)} %constant_dynamic-update-slice_fusion.refs_0_), channel_id=1, source_target_pairs={{0,12},{1,13},{2,14},{3,15},{4,0},{5,1},{6,2},{7,3},{8,4},{9,5},{1... | collective-permute-start | bytes 2801672 | tf_op jit(solution)/shard_map/ppermute | solution.py:41
  42.8 0.9 copy-start.10
  43.8 21.1 %collective-permute-start.10 = (bf16[64,7296]{1,0:T(8,128)(2,1)S(1)}, bf16[64,7296]{1,0:T(8,128)(2,1)}, u32[]{:S(2)}, u32[]{:S(2)}) collective-permute-start(bf16[64,7296]{1,0:T(8,128)(2,1)S(1)} %constant_dynamic-update-slice_fusion.2.refs_1_), channel_id=1, source_target_pairs={{0,4},{1,5},{2,6},{3,7},{4,8},{5,9},{6,10},{7,11},{8,12},{9,13},{1... | collective-permute-start | bytes 2801672 | tf_op jit(solution)/shard_map/ppermute | solution.py:41
  46.8 37.1 %collective-permute-start.13 = (bf16[64,7296]{1,0:T(8,128)(2,1)}, bf16[64,7296]{1,0:T(8,128)(2,1)S(1)}, u32[]{:S(2)}, u32[]{:S(2)}) collective-permute-start(bf16[64,7296]{1,0:T(8,128)(2,1)} %copy-done.10), channel_id=1, source_target_pairs={{0,4},{1,5},{2,6},{3,7},{4,8},{5,9},{6,10},{7,11},{8,12},{9,13},{1... | collective-permute-start | bytes 2801672 | tf_op jit(solution)/shard_map/ppermute | solution.py:41
  48.1 35.8 %collective-permute-start.14 = (bf16[64,7296]{1,0:T(8,128)(2,1)}, bf16[64,7296]{1,0:T(8,128)(2,1)S(1)}, u32[]{:S(2)}, u32[]{:S(2)}) collective-permute-start(bf16[64,7296]{1,0:T(8,128)(2,1)} %collective-permute-done.8.refs_1_), channel_id=1, source_target_pairs={{0,12},{1,13},{2,14},{3,15},{4,0},{5,1},{6,2},{7,3},{8,4},{9,5},{1... | collective-permute-start | bytes 2801672 | tf_op jit(solution)/shard_map/ppermute | solution.py:41
  50.6 3.1 %copy-start = (bf16[7168,512]{1,0:T(8,128)(2,1)S(1)}, bf16[7168,512]{1,0:T(8,128)(2,1)}, u32[]{:S(2)}) copy-start(bf16[7168,512]{1,0:T(8,128)(2,1)} %pad_maximum_fusion.refs_2_.refs_4_) | copy-start | bytes 22020100
  80.4 14.7 %collective-permute-start.15 = (bf16[64,7168]{1,0:T(8,128)(2,1)S(1)}, bf16[64,7168]{1,0:T(8,128)(2,1)S(1)}, u32[]{:S(2)}, u32[]{:S(2)}) collective-permute-start(bf16[64,7168]{1,0:T(8,128)(2,1)S(1)} %get-tuple-element.47), channel_id=1, source_target_pairs={{0,4},{1,5},{2,6},{3,7},{4,8},{5,9},{6,10},{7,11},{8,12},{9,13},{1... | collective-permute-start | bytes 2752520 | tf_op jit(solution)/shard_map/ppermute | solution.py:41
  80.5 18.0 %copy-start.2 = (bf16[8,128,512]{2,1,0:T(8,128)(2,1)S(1)}, bf16[8,128,512]{2,1,0:T(8,128)(2,1)}, u32[]{:S(2)}) copy-start(bf16[8,128,512]{2,1,0:T(8,128)(2,1)} %key_up_ref.3) | copy-start | bytes 3145732
  80.5 18.0 %copy-start.3 = (bf16[8,512,128]{2,1,0:T(8,128)(2,1)S(1)}, bf16[8,512,128]{2,1,0:T(8,128)(2,1)}, u32[]{:S(2)}) copy-start(bf16[8,512,128]{2,1,0:T(8,128)(2,1)} %value_up_ref.3) | copy-start | bytes 3145732
  80.5 17.9 %copy-start.4 = (bf16[2,4096,64]{1,2,0:T(8,128)(2,1)S(1)}, bf16[2,4096,64]{1,2,0:T(8,128)(2,1)}, u32[]{:S(2)}) copy-start(bf16[2,4096,64]{1,2,0:T(8,128)(2,1)} %param.26) | copy-start | bytes 3145732
  80.5 17.9 %copy-start.5 = (bf16[128,1024]{1,0:T(8,128)(2,1)S(1)}, bf16[128,1024]{1,0:T(8,128)(2,1)}, u32[]{:S(2)}) copy-start(bf16[128,1024]{1,0:T(8,128)(2,1)} %nope_ref.3) | copy-start | bytes 786436
  80.6 17.9 %copy-start.6 = (bf16[128,512]{1,0:T(8,128)(2,1)S(1)}, bf16[128,512]{1,0:T(8,128)(2,1)}, u32[]{:S(2)}) copy-start(bf16[128,512]{1,0:T(8,128)(2,1)} %rope_ref.3) | copy-start | bytes 393220
  80.6 17.9 %copy-start.7 = (bf16[128,512]{1,0:T(8,128)(2,1)S(1)}, bf16[128,512]{1,0:T(8,128)(2,1)}, u32[]{:S(2)}) copy-start(bf16[128,512]{1,0:T(8,128)(2,1)} %new_latent_ref.3) | copy-start | bytes 393220
  80.6 17.9 %copy-start.8 = (bf16[128,64]{0,1:T(8,128)(2,1)S(1)}, bf16[128,64]{0,1:T(8,128)(2,1)}, u32[]{:S(2)}) copy-start(bf16[128,64]{0,1:T(8,128)(2,1)} %param.28) | copy-start | bytes 49156
  80.6 17.9 %copy-start.9 = (s32[2]{0:T(128)S(1)}, s32[2]{0:T(128)}, u32[]{:S(2)}) copy-start(s32[2]{0:T(128)} %param.29) | copy-start | bytes 28
  80.6 14.5 %collective-permute-start.16 = (bf16[64,7168]{1,0:T(8,128)(2,1)S(1)}, bf16[64,7168]{1,0:T(8,128)(2,1)S(1)}, u32[]{:S(2)}, u32[]{:S(2)}) collective-permute-start(bf16[64,7168]{1,0:T(8,128)(2,1)S(1)} %get-tuple-element.48), channel_id=1, source_target_pairs={{0,12},{1,13},{2,14},{3,15},{4,0},{5,1},{6,2},{7,3},{8,4},{9,5},{1... | collective-permute-start | bytes 2752520 | tf_op jit(solution)/shard_map/ppermute | solution.py:41
  95.1 14.7 %collective-permute-start.17 = (bf16[64,7168]{1,0:T(8,128)(2,1)S(1)}, bf16[64,7168]{1,0:T(8,128)(2,1)S(1)}, u32[]{:S(2)}, u32[]{:S(2)}) collective-permute-start(bf16[64,7168]{1,0:T(8,128)(2,1)S(1)} %get-tuple-element.55), channel_id=1, source_target_pairs={{0,4},{1,5},{2,6},{3,7},{4,8},{5,9},{6,10},{7,11},{8,12},{9,13},{1... | collective-permute-start | bytes 2752520 | tf_op jit(solution)/shard_map/ppermute | solution.py:41
  95.4 14.4 %collective-permute-start.18 = (bf16[64,7168]{1,0:T(8,128)(2,1)S(1)}, bf16[64,7168]{1,0:T(8,128)(2,1)S(1)}, u32[]{:S(2)}, u32[]{:S(2)}) collective-permute-start(bf16[64,7168]{1,0:T(8,128)(2,1)S(1)} %get-tuple-element.56), channel_id=1, source_target_pairs={{0,12},{1,13},{2,14},{3,15},{4,0},{5,1},{6,2},{7,3},{8,4},{9,5},{1... | collective-permute-start | bytes 2752520 | tf_op jit(solution)/shard_map/ppermute | solution.py:41
  98.5 3.4 %copy-start.1 = (bf16[2,4096,512]{2,1,0:T(8,128)(2,1)S(1)}, bf16[2,4096,512]{2,1,0:T(8,128)(2,1)}, u32[]{:S(2)}) copy-start(bf16[2,4096,512]{2,1,0:T(8,128)(2,1)} %latent_ref.3) | copy-start | bytes 25165828
  110.1 14.2 %collective-permute-start.20 = (bf16[64,7168]{1,0:T(8,128)(2,1)S(1)}, bf16[64,7168]{1,0:T(8,128)(2,1)S(1)}, u32[]{:S(2)}, u32[]{:S(2)}) collective-permute-start(bf16[64,7168]{1,0:T(8,128)(2,1)S(1)} %add_convert_fusion), channel_id=1, source_target_pairs={{0,12},{1,13},{2,14},{3,15},{4,0},{5,1},{6,2},{7,3},{8,4},{9,5},{1... | collective-permute-start | bytes 2752520 | tf_op jit(solution)/shard_map/ppermute | solution.py:41
  113.6 14.7 %collective-permute-start.19 = (bf16[64,7168]{1,0:T(8,128)(2,1)S(1)}, bf16[64,7168]{1,0:T(8,128)(2,1)S(1)}, u32[]{:S(2)}, u32[]{:S(2)}) collective-permute-start(bf16[64,7168]{1,0:T(8,128)(2,1)S(1)} %add_convert_fusion.1), channel_id=1, source_target_pairs={{0,4},{1,5},{2,6},{3,7},{4,8},{5,9},{6,10},{7,11},{8,12},{9,13},{1... | collective-permute-start | bytes 2752520 | tf_op jit(solution)/shard_map/ppermute | solution.py:41
  129.0 9.8 %collective-permute-start.21 = (bf16[32,7168]{1,0:T(8,128)(2,1)S(1)}, bf16[32,7168]{1,0:T(8,128)(2,1)S(1)}, u32[]{:S(2)}, u32[]{:S(2)}) collective-permute-start(bf16[32,7168]{1,0:T(8,128)(2,1)S(1)} %pad_maximum_fusion.2), channel_id=1, source_target_pairs={{0,1},{1,2},{2,3},{3,0},{4,5},{5,6},{6,7},{7,4},{8,9},{9,10},{10,1... | collective-permute-start | bytes 1376264 | tf_op jit(solution)/shard_map/ppermute | solution.py:41
  129.1 9.8 %collective-permute-start.23 = (bf16[32,7168]{1,0:T(8,128)(2,1)S(1)}, bf16[32,7168]{1,0:T(8,128)(2,1)S(1)}, u32[]{:S(2)}, u32[]{:S(2)}) collective-permute-start(bf16[32,7168]{1,0:T(8,128)(2,1)S(1)} %concatenate.33), channel_id=1, source_target_pairs={{0,3},{1,0},{2,1},{3,2},{4,7},{5,4},{6,5},{7,6},{8,11},{9,8},{10,9... | collective-permute-start | bytes 1376264 | tf_op jit(solution)/shard_map/ppermute | solution.py:41
  138.8 7.3 %collective-permute-start.22 = (bf16[16,7168]{1,0:T(8,128)(2,1)S(1)}, bf16[16,7168]{1,0:T(8,128)(2,1)S(1)}, u32[]{:S(2)}, u32[]{:S(2)}) collective-permute-start(bf16[16,7168]{1,0:T(8,128)(2,1)S(1)} %fusion.2), channel_id=1, source_target_pairs={{0,1},{1,2},{2,3},{3,0},{4,5},{5,6},{6,7},{7,4},{8,9},{9,10},{10,1... | collective-permute-start | bytes 688136 | tf_op jit(solution)/shard_map/ppermute | solution.py:41
  146.2 6.1 %collective-permute-start.24 = (bf16[16,7168]{1,0:T(8,128)(2,1)S(1)}, bf16[16,7168]{1,0:T(8,128)(2,1)S(1)}, u32[]{:S(2)}, u32[]{:S(2)}) collective-permute-start(bf16[16,7168]{1,0:T(8,128)(2,1)S(1)} %get-tuple-element.74), channel_id=1, source_target_pairs={{0,3},{1,0},{2,1},{3,2},{4,7},{5,4},{6,5},{7,6},{8,11},{9,8},{10,9... | collective-permute-start | bytes 688136 | tf_op jit(solution)/shard_map/ppermute | solution.py:41
  152.5 7.4 %collective-permute-start.25 = (bf16[8,7168]{1,0:T(8,128)(2,1)S(1)}, bf16[8,7168]{1,0:T(8,128)(2,1)S(1)}, u32[]{:S(2)}, u32[]{:S(2)}) collective-permute-start(bf16[8,7168]{1,0:T(8,128)(2,1)S(1)} %get-tuple-element.70), channel_id=1, source_target_pairs={{0,32},{1,33},{2,34},{3,35},{4,36},{5,37},{6,38},{7,39},{8,40},{9,... | collective-permute-start | bytes 344072 | tf_op jit(solution)/shard_map/ppermute | solution.py:41
  156.4 6.3 %collective-permute-start.26 = (bf16[8,7168]{1,0:T(8,128)(2,1)S(1)}, bf16[8,7168]{1,0:T(8,128)(2,1)S(1)}, u32[]{:S(2)}, u32[]{:S(2)}) collective-permute-start(bf16[8,7168]{1,0:T(8,128)(2,1)S(1)} %get-tuple-element.72), channel_id=1, source_target_pairs={{0,64},{1,65},{2,66},{3,67},{4,68},{5,69},{6,70},{7,71},{8,72},{9,... | collective-permute-start | bytes 344072 | tf_op jit(solution)/shard_map/ppermute | solution.py:41
  157.6 5.1 %collective-permute-start.27 = (bf16[8,7168]{1,0:T(8,128)(2,1)S(1)}, bf16[8,7168]{1,0:T(8,128)(2,1)S(1)}, u32[]{:S(2)}, u32[]{:S(2)}) collective-permute-start(bf16[8,7168]{1,0:T(8,128)(2,1)S(1)} %get-tuple-element.71), channel_id=1, source_target_pairs={{0,96},{1,97},{2,98},{3,99},{4,100},{5,101},{6,102},{7,103},{8,104... | collective-permute-start | bytes 344072 | tf_op jit(solution)/shard_map/ppermute | solution.py:41

commit v2 on v1

--- a/solution.py
+++ b/solution.py
@@ -19,7 +19,8 @@
 SIZES = (4, 2, 4, 4)
 RING = 4
 ORDERS = ((0, 3, 2), (2, 0, 3))
-KERNEL_VMEM = 28 * 1024 * 1024
+KERNEL_VMEM = 12 * 1024 * 1024
+EXPERT_VMEM = 10 * 1024 * 1024
 PACK = 128
 DEPTH = 1024
 UNITS = 256
@@ -57,13 +58,12 @@
     return lax.ppermute(value, "core", [(0, 1), (1, 0)])
 
 
-def expert_kernel(expert_ref, *refs, sources, outputs):
+def expert_kernel(*refs, sources, outputs):
     row_hbm = refs[:sources]
     both_ref, both_other_ref, down_ref, down_other_ref = refs[sources : sources + 4]
     out_refs = refs[sources + 4 : sources + 4 + outputs]
-    rows_ref, sums_ref, hidden_ref, row_sem = refs[sources + 4 + outputs :]
+    rows_ref, hidden_ref, row_sem = refs[sources + 4 + outputs :]
     width = both_ref.shape[0]
-    steps = width // DEPTH
     span = rows_ref.shape[0] // sources
     row_copies = [
         pltpu.make_async_copy(source, rows_ref.at[pl.ds(i * span, span)], row_sem.at[i])
@@ -71,29 +71,23 @@
     ]
     for copy in row_copies:
         copy.start()
-    sums_ref[...] = jnp.zeros_like(sums_ref)
     for copy in row_copies:
         copy.wait()
-
-    @pl.loop(0, steps)
-    def _(step):
-        part = pl.ds(pl.multiple_of(step * DEPTH, DEPTH), DEPTH)
-        piece = rows_ref[:, part]
-        for i, matrix in enumerate((both_ref, both_other_ref)):
-            sums_ref[i] += jnp.dot(piece, matrix[part, :], preferred_element_type=jnp.float32)
-
     extra = rows_ref[:, width : width + PACK].astype(jnp.float32)
     lane = lax.broadcasted_iota(jnp.int32, extra.shape, 1)
-    pick = (lane % EXPERTS == expert_ref[0]) & (lane < 2 * EXPERTS)
+    expert = lax.axis_index("x") * RING + lax.axis_index("y")
+    pick = (lane % EXPERTS == expert) & (lane < 2 * EXPERTS)
     coefficient = jnp.sum(jnp.where(pick, extra, 0.0), axis=1, keepdims=True)
-    for i in range(2):
-        gate, up = sums_ref[i, :, :UNITS], sums_ref[i, :, UNITS:]
+    for i, matrix in enumerate((both_ref, both_other_ref)):
+        sums = sum(
+            jnp.dot(rows_ref[:, k : k + DEPTH], matrix[k : k + DEPTH, :], preferred_element_type=jnp.float32)
+            for k in range(0, width, DEPTH)
+        )
+        gate, up = sums[:, :UNITS], sums[:, UNITS:]
         hidden = gate / (1.0 + jnp.exp(-gate)) * up * coefficient
         hidden_ref[i] = jnp.where(coefficient > 0, hidden, 0.0).astype(jnp.bfloat16)
-
-    @pl.loop(0, steps)
-    def _(step):
-        part = pl.ds(pl.multiple_of(step * DEPTH, DEPTH), DEPTH)
+    for start in range(0, width, DEPTH):
+        part = slice(start, start + DEPTH)
         result = jnp.dot(hidden_ref[0], down_ref[:, part], preferred_element_type=jnp.float32)
         result += jnp.dot(hidden_ref[1], down_other_ref[:, part], preferred_element_type=jnp.float32)
         result = result.astype(jnp.bfloat16)
@@ -101,30 +95,52 @@
             out_ref[:, part] = result[i * HALF : (i + 1) * HALF]
 
 
-def expert_terms(expert, pieces, weights):
+def expert_terms(pieces, weights):
     width = weights[0].shape[0]
     rows = sum(piece.shape[0] for piece in pieces)
     outputs = rows // HALF
     weights = [pltpu.with_memory_space_constraint(matrix, pltpu.VMEM) for matrix in weights]
     return pl.pallas_call(
         functools.partial(expert_kernel, sources=len(pieces), outputs=outputs),
-        in_specs=[pl.BlockSpec(memory_space=pltpu.SMEM)]
-        + [pl.BlockSpec(memory_space=pl.ANY)] * len(pieces)
+        in_specs=[pl.BlockSpec(memory_space=pl.ANY)] * len(pieces)
         + [pl.BlockSpec(memory_space=pltpu.VMEM)] * 4,
         out_specs=[pl.BlockSpec(memory_space=pltpu.VMEM)] * outputs,
         out_shape=[jax.ShapeDtypeStruct((HALF, width), jnp.bfloat16)] * outputs,
         scratch_shapes=[
             pltpu.VMEM((rows, width + PACK), jnp.bfloat16),
-            pltpu.VMEM((2, rows, 2 * UNITS), jnp.float32),
             pltpu.VMEM((2, rows, UNITS), jnp.bfloat16),
             pltpu.SemaphoreType.DMA((len(pieces),)),
         ],
-        compiler_params=pltpu.CompilerParams(vmem_limit_bytes=KERNEL_VMEM),
+        compiler_params=pltpu.CompilerParams(vmem_limit_bytes=EXPERT_VMEM),
         cost_estimate=pl.CostEstimate(
             flops=6 * rows * width * UNITS * 2, bytes_accessed=4 * rows * width, transcendentals=0
         ),
         name="expert",
-    )(expert, *pieces, *weights)
+    )(*pieces, *weights)
+
+
+def join_kernel(gate_hbm, up_hbm, out_ref, sem):
+    copies = [
+        pltpu.make_async_copy(source, out_ref.at[:, pl.ds(i * UNITS, UNITS)], sem.at[i])
+        for i, source in enumerate((gate_hbm, up_hbm))
+    ]
+    for copy in copies:
+        copy.start()
+    for copy in copies:
+        copy.wait()
+
+
+def joined(gate, up):
+    return pl.pallas_call(
+        join_kernel,
+        in_specs=[pl.BlockSpec(memory_space=pl.ANY)] * 2,
+        out_specs=pl.BlockSpec(memory_space=pltpu.VMEM),
+        out_shape=pltpu.VMEM((gate.shape[0], 2 * UNITS), jnp.bfloat16),
+        scratch_shapes=[pltpu.SemaphoreType.DMA((2,))],
+        compiler_params=pltpu.CompilerParams(vmem_limit_bytes=KERNEL_VMEM),
+        cost_estimate=pl.CostEstimate(flops=0, bytes_accessed=8 * gate.shape[0] * UNITS, transcendentals=0),
+        name="join",
+    )(*(pltpu.with_memory_space_constraint(value, pltpu.HBM) for value in (gate, up)))
 
 
 def pack_kernel(tokens_ref, routes_ref, scores_ref, out_ref):
@@ -147,6 +163,7 @@
     return pl.pallas_call(
         pack_kernel,
         out_shape=jax.ShapeDtypeStruct((rows, width + PACK), jnp.bfloat16),
+        compiler_params=pltpu.CompilerParams(vmem_limit_bytes=KERNEL_VMEM),
         name="pack",
     )(tokens, routes, gate_scores)
 
@@ -277,11 +294,10 @@
     packed = packed_rows(tokens, routes, gate_scores)
     gathered = [packed] + [shift(packed, 0, -distance) for distance in (1, 2, 3)]
     packed, gate_weight, up_weight = lax.optimization_barrier((packed, gate_weight, up_weight))
-    both = jnp.concatenate([gate_weight[0], up_weight[0]], axis=1)
+    both = joined(gate_weight[0], up_weight[0])
     small = jnp.concatenate(gathered, axis=0)
     small, both, down_part = lax.optimization_barrier((small, both, down_weight[0]))
     weights = (both, with_other_core(both), down_part, with_other_core(down_part))
-    expert = (lax.axis_index("x") * RING + lax.axis_index("y")).astype(jnp.int32)[None]
     rope_keys, new_rope_keys = jnp.swapaxes(rope_cache, 1, 2), new_rope.T
 
     def attention(sequence, length):
@@ -296,17 +312,15 @@
     far_low, far_high = shift(below[:half], 1, 1), shift(above[half:], 1, -1)
     own_high = jnp.concatenate([far_low, far_high, below], axis=0)
     below_high, above_high = shift(own_high, 2, 1), shift(own_high, 2, -1)
-    own_terms = expert_terms(expert, [own_low, own_high], weights)
+    own_terms = expert_terms([own_low, own_high], weights)
+    below_low, above_high, own_terms = lax.optimization_barrier((below_low, above_high, own_terms))
     far_low, far_high = shift(below_low, 2, 1), shift(above_high, 2, -1)
-    above_low, above_high, below_low, below_high, own_terms = lax.optimization_barrier(
-        (above_low, above_high, below_low, below_high, own_terms)
-    )
     above_low, above_high, below_low, below_high = expert_terms(
-        expert, [above_low, above_high, below_low, below_high], weights
+        [above_low, above_high, below_low, below_high], weights
     )
     near_high, near_low = shift(above_high, 2, 1), shift(below_low, 2, -1)
     far_low, far_high, above_high, below_low = lax.optimization_barrier((far_low, far_high, above_high, below_low))
-    far_terms = expert_terms(expert, [far_low, far_high], weights)
+    far_terms = expert_terms([far_low, far_high], weights)
     far_terms, near_high, near_low = lax.optimization_barrier((far_terms, near_high, near_low))
     from_below, from_above = shift(far_terms[0], 2, 1), shift(far_terms[1], 2, -1)
     far_terms, lengths = lax.optimization_barrier((far_terms, lengths))
@@ -327,8 +341,10 @@
     up_first = narrowed(jnp.concatenate([far[:half], above[half:]], axis=0))
     down_first = narrowed(jnp.concatenate([far[half:], below[:half]], axis=0))
     from_below, from_above = shift(up_first, 1, 1), shift(down_first, 1, -1)
-    up_second = shift(narrowed(added(above[:half], from_below[:half])), 1, 1)
-    down_second = shift(narrowed(added(below[half:], from_above[:half])), 1, -1)
+    up_second = narrowed(added(above[:half], from_below[:half]))
+    down_second = narrowed(added(below[half:], from_above[:half]))
+    up_second, down_second = lax.optimization_barrier((up_second, down_second))
+    up_second, down_second = shift(up_second, 1, 1), shift(down_second, 1, -1)
     total = low[:size] + jnp.concatenate(
         [added(up_second, from_above[half:]), added(down_second, from_below[half:])], axis=0
     )

time: 164 us -> 140 us (0.85)
  Pallas kernels: 56.2 us -> 32.7 us
  waiting for transfers between devices: 46.6 us -> 54.5 us
  other arithmetic: 9.56 us -> 2.84 us
  local copies, waits for them, and re-layouts: 8.32 us -> 3.18 us
  starting transfers between devices: 41.7 us -> 45.2 us
    pallas_call x3, Pallas kernels: 37.9 us -> 14.4 us  [expert_terms(): pl.pallas_call(functools.partial(expert_kernel, sources=len(pieces), outp...]
    ppermute x26, waiting for transfers between devices: 46.6 us -> 54.5 us  [shift(): return lax.ppermute(value, AXES, pairs)]
    concatenate x1 -> x0, other arithmetic: 6.71 us -> none  [body(): both = jnp.concatenate([gate_weight[0], up_weight[0]], axis=1)]
    unnamed x27 -> x31, local copies, waits for them, and re-layouts: 7.53 us -> 2.39 us
    ppermute x26, starting transfers between devices: 41.6 us -> 45.1 us  [shift(): return lax.ppermute(value, AXES, pairs)]
    pallas_call x0 -> x1, Pallas kernels: none -> 3.31 us  [joined(): pl.pallas_call(join_kernel, in_specs=[pl.BlockSpec(memory_space=pl.ANY)]...]
    pallas_call x2, Pallas kernels: 16.5 us -> 14.9 us  [attend(): pl.pallas_call(functools.partial(attention_kernel, sequence), grid_spec=p...]
  transfers between devices with their start and end apart: 28 -> 28, of which waited for: 11 -> 16; matrix products, arithmetic and copies ran while one was open for 5% -> 1% of each run, Pallas kernels for 33% -> 23%
where the time goes in v2:
time: 140 us; the launch traced here: 139 us
  waiting for transfers between devices  54.5 us (39%)
  starting transfers between devices  45.2 us (32%)
  Pallas kernels  32.7 us (23%)
  local copies, waits for them, and re-layouts  3.18 us (2%)
  other arithmetic  2.84 us (2%)
    ppermute x26, waiting for transfers between devices, shift(): return lax.ppermute(value, AXES, pairs)  54.5 us
    ppermute x26, starting transfers between devices, shift(): return lax.ppermute(value, AXES, pairs)  45.1 us
    pallas_call x2, Pallas kernels, attend(): pl.pallas_call(functools.partial(attention_kernel, sequence), grid_spec=p...  14.9 us
    pallas_call x3, Pallas kernels, expert_terms(): pl.pallas_call(functools.partial(expert_kernel, sources=len(pieces), outp...  14.4 us
    pallas_call x1, Pallas kernels, joined(): pl.pallas_call(join_kernel, in_specs=[pl.BlockSpec(memory_space=pl.ANY)]...  3.31 us
  transfers between devices with their start and end apart: 28, of which 16 were waited for; matrix products, arithmetic and copies ran while one was open for 1% of the time, Pallas kernels for 23%

profile of v2, /device:TPU:0, one launch (start us, length us, event | category | flops | bytes accessed | tf_op | source)
XLA Modules:
  0.0 139.5 jit_solution(15947160490025544224)
XLA Ops:
  0.6 0.9 copy-done.1
  1.5 0.7 copy-done.2
  2.2 0.7 copy-done.3
  2.9 0.2 pack.1
  3.1 4.2 %collective-permute-start = (bf16[8,7296]{1,0:T(8,128)(2,1)S(1)}, bf16[8,7296]{1,0:T(8,128)(2,1)S(1)}, u32[]{:S(2)}, u32[]{:S(2)}) collective-permute-start(bf16[8,7296]{1,0:T(8,128)(2,1)S(1)} %pack.1), channel_id=1, source_target_pairs={{0,96},{1,97},{2,98},{3,99},{4,100},{5,101},{6,102},{7,103},{8,104... | collective-permute-start | bytes 350216 | tf_op jit(solution)/shard_map/ppermute | solution.py:42
  7.3 1.3 collective-permute-start.2
  8.5 3.3 %join.1.refs_2_.refs_4_ = bf16[7168,512]{1,0:T(8,128)(2,1)S(1)} custom-call(bf16[7168,256]{1,0:T(8,128)(2,1)} %bitcast.17, bf16[7168,256]{1,0:T(8,128)(2,1)} %bitcast.18), custom_call_target="tpu_custom_call" | custom-call | bytes 14680064 | tf_op jit(solution)/shard_map/join/pallas_call | solution.py:134
  11.9 1.8 %collective-permute-done.1 = bf16[8,7296]{1,0:T(8,128)(2,1)S(1)} collective-permute-done((bf16[8,7296]{1,0:T(8,128)(2,1)S(1)}, bf16[8,7296]{1,0:T(8,128)(2,1)S(1)}, u32[]{:S(2)}, u32[]{:S(2)}) %collective-permute-start.1) | collective-permute-done | bytes 116768 | tf_op jit(solution)/shard_map/ppermute | solution.py:42
  13.7 0.9 collective-permute-done.2
  14.6 0.1 pad_maximum_fusion
  14.6 0.1 collective-permute-start.9
  14.7 1.6 %collective-permute-start.5 = (bf16[32,7296]{1,0:T(8,128)(2,1)S(1)}, bf16[32,7296]{1,0:T(8,128)(2,1)S(1)}, u32[]{:S(2)}, u32[]{:S(2)}) collective-permute-start(bf16[32,7296]{1,0:T(8,128)(2,1)S(1)} %pad_maximum_fusion), channel_id=1, source_target_pairs={{0,1},{1,2},{2,3},{3,0},{4,5},{5,6},{6,7},{7,4},{8,9},{9,10},{10,1... | collective-permute-start | bytes 1400840 | tf_op jit(solution)/shard_map/ppermute | solution.py:42
  16.4 1.7 %collective-permute-start.3 = (bf16[32,7296]{1,0:T(8,128)(2,1)S(1)}, bf16[32,7296]{1,0:T(8,128)(2,1)S(1)}, u32[]{:S(2)}, u32[]{:S(2)}) collective-permute-start(bf16[32,7296]{1,0:T(8,128)(2,1)S(1)} %pad_maximum_fusion), channel_id=1, source_target_pairs={{0,3},{1,0},{2,1},{3,2},{4,7},{5,4},{6,5},{7,6},{8,11},{9,8},{10,9... | collective-permute-start | bytes 1400840 | tf_op jit(solution)/shard_map/ppermute | solution.py:42
  18.1 6.5 %collective-permute-done.5 = bf16[32,7296]{1,0:T(8,128)(2,1)S(1)} collective-permute-done((bf16[32,7296]{1,0:T(8,128)(2,1)S(1)}, bf16[32,7296]{1,0:T(8,128)(2,1)S(1)}, u32[]{:S(2)}, u32[]{:S(2)}) %collective-permute-start.5) | collective-permute-done | bytes 466976 | tf_op jit(solution)/shard_map/ppermute | solution.py:42
  24.6 0.4 collective-permute-start.6
  25.0 2.9 %collective-permute-start.7 = (bf16[16,7296]{1,0:T(8,128)(2,1)S(1)}, bf16[16,7296]{1,0:T(8,128)(2,1)S(1)}, u32[]{:S(2)}, u32[]{:S(2)}) collective-permute-start(bf16[16,7296]{1,0:T(8,128)(2,1)S(1)} %slice.84), channel_id=1, source_target_pairs={{0,3},{1,0},{2,1},{3,2},{4,7},{5,4},{6,5},{7,6},{8,11},{9,8},{10,9... | collective-permute-start | bytes 700424 | tf_op jit(solution)/shard_map/ppermute | solution.py:42
  28.0 1.6 %collective-permute-start.4 = (bf16[64,7296]{1,0:T(8,128)(2,1)S(1)}, bf16[64,7296]{1,0:T(8,128)(2,1)S(1)}, u32[]{:S(2)}, u32[]{:S(2)}) collective-permute-start(bf16[64,7296]{1,0:T(8,128)(2,1)S(1)} %constant_dynamic-update-slice_fusion.refs_0_), channel_id=1, source_target_pairs={{0,4},{1,5},{2,6},{3,7},{4,8},{5,9},{6,10},{7,11},{8,12},{9,13},{1... | collective-permute-start | bytes 2801672 | tf_op jit(solution)/shard_map/ppermute | solution.py:42
  29.6 3.2 %collective-permute-done.6 = bf16[16,7296]{1,0:T(8,128)(2,1)S(1)} collective-permute-done((bf16[16,7296]{1,0:T(8,128)(2,1)S(1)}, bf16[16,7296]{1,0:T(8,128)(2,1)S(1)}, u32[]{:S(2)}, u32[]{:S(2)}) %collective-permute-start.6) | collective-permute-done | bytes 233504 | tf_op jit(solution)/shard_map/ppermute | solution.py:42
  32.9 2.8 %collective-permute-start.8 = (bf16[64,7296]{1,0:T(8,128)(2,1)S(1)}, bf16[64,7296]{1,0:T(8,128)(2,1)S(1)}, u32[]{:S(2)}, u32[]{:S(2)}) collective-permute-start(bf16[64,7296]{1,0:T(8,128)(2,1)S(1)} %constant_dynamic-update-slice_fusion.2.refs_1_), channel_id=1, source_target_pairs={{0,12},{1,13},{2,14},{3,15},{4,0},{5,1},{6,2},{7,3},{8,4},{9,5},{1... | collective-permute-start | bytes 2801672 | tf_op jit(solution)/shard_map/ppermute | solution.py:42
  35.7 0.8 collective-permute-start.13
  36.6 1.2 collective-permute-start.14
  37.8 3.7 %expert.3 = (bf16[64,7168]{1,0:T(8,128)(2,1)S(1)}, bf16[64,7168]{1,0:T(8,128)(2,1)S(1)}) custom-call(bf16[64,7296]{1,0:T(8,128)(2,1)S(1)} %constant_dynamic-update-slice_fusion.refs_0_, bf16[64,7296]{1,0:T(8,128)(2,1)S(1)} %constant_dynamic-update-slice_fusion.2.refs_1_, bf16[7168,512]{1,0:T(8,128)(2,1)S(1)} %join.1.refs_2_.refs_4_, ...), custom_call_target="tpu_custom_call" | custom-call | flops 2818572288 | bytes 3670016 | tf_op jit(solution)/shard_map/expert/pallas_call | solution.py:103
  41.5 1.4 collective-permute-done.4.refs_2_
  42.9 4.0 %collective-permute-done.8.refs_1_ = bf16[64,7296]{1,0:T(8,128)(2,1)S(1)} collective-permute-done((bf16[64,7296]{1,0:T(8,128)(2,1)S(1)}, bf16[64,7296]{1,0:T(8,128)(2,1)S(1)}, u32[]{:S(2)}, u32[]{:S(2)}) %collective-permute-start.8) | collective-permute-done | bytes 933920 | tf_op jit(solution)/shard_map/ppermute | solution.py:42
  46.8 1.2 collective-permute-start.11
  48.0 2.5 %collective-permute-start.12 = (bf16[64,7296]{1,0:T(8,128)(2,1)S(1)}, bf16[64,7296]{1,0:T(8,128)(2,1)S(1)}, u32[]{:S(2)}, u32[]{:S(2)}) collective-permute-start(bf16[64,7296]{1,0:T(8,128)(2,1)S(1)} %collective-permute-done.8.refs_1_), channel_id=1, source_target_pairs={{0,12},{1,13},{2,14},{3,15},{4,0},{5,1},{6,2},{7,3},{8,4},{9,5},{1... | collective-permute-start | bytes 2801672 | tf_op jit(solution)/shard_map/ppermute | solution.py:42
  50.5 6.3 %collective-permute-done.13.refs_0_ = bf16[64,7296]{1,0:T(8,128)(2,1)S(1)} collective-permute-done((bf16[64,7296]{1,0:T(8,128)(2,1)S(1)}, bf16[64,7296]{1,0:T(8,128)(2,1)S(1)}, u32[]{:S(2)}, u32[]{:S(2)}) %collective-permute-start.13) | collective-permute-done | bytes 933920 | tf_op jit(solution)/shard_map/ppermute | solution.py:42
  56.8 7.0 %expert.4 = (bf16[64,7168]{1,0:T(8,128)(2,1)S(1)}, bf16[64,7168]{1,0:T(8,128)(2,1)S(1)}, bf16[64,7168]{1,0:T(8,128)(2,1)S(1)}, bf16[64,7168]{1,0:T(8,128)(2,1)S(1)}) custom-call(bf16[64,7296]{1,0:T(8,128)(2,1)S(1)} %collective-permute-done.13.refs_0_, bf16[64,7296]{1,0:T(8,128)(2,1)S(1)} %collective-permute-done.8.refs_1_, ...), custom_call_target="tpu_custom_call" | custom-call | flops 5637144576 | bytes 7340032 | tf_op jit(solution)/shard_map/expert/pallas_call | solution.py:103
  63.8 1.3 collective-permute-start.15
  65.1 0.0 copy-start.7
  65.2 0.0 copy-start.8
  65.2 0.0 copy-start.11
  65.2 2.6 %collective-permute-start.16 = (bf16[64,7168]{1,0:T(8,128)(2,1)S(1)}, bf16[64,7168]{1,0:T(8,128)(2,1)S(1)}, u32[]{:S(2)}, u32[]{:S(2)}) collective-permute-start(bf16[64,7168]{1,0:T(8,128)(2,1)S(1)} %get-tuple-element.46), channel_id=1, source_target_pairs={{0,12},{1,13},{2,14},{3,15},{4,0},{5,1},{6,2},{7,3},{8,4},{9,5},{1... | collective-permute-start | bytes 2752520 | tf_op jit(solution)/shard_map/ppermute | solution.py:42
  67.8 3.7 %expert.5 = (bf16[64,7168]{1,0:T(8,128)(2,1)S(1)}, bf16[64,7168]{1,0:T(8,128)(2,1)S(1)}) custom-call(bf16[64,7296]{1,0:T(8,128)(2,1)S(1)} %collective-permute-done.11.refs_0_, bf16[64,7296]{1,0:T(8,128)(2,1)S(1)} %collective-permute-done.12.refs_1_, bf16[7168,512]{1,0:T(8,128)(2,1)S(1)} %join.1.refs_2_.refs_4_, ...), custom_call_target="tpu_custom_call" | custom-call | flops 2818572288 | bytes 3670016 | tf_op jit(solution)/shard_map/expert/pallas_call | solution.py:103
  71.5 7.5 %collective-permute-done.15 = bf16[64,7168]{1,0:T(8,128)(2,1)S(1)} collective-permute-done((bf16[64,7168]{1,0:T(8,128)(2,1)S(1)}, bf16[64,7168]{1,0:T(8,128)(2,1)S(1)}, u32[]{:S(2)}, u32[]{:S(2)}) %collective-permute-start.15) | collective-permute-done | bytes 917536 | tf_op jit(solution)/shard_map/ppermute | solution.py:42
  79.0 1.6 %collective-permute-start.17 = (bf16[64,7168]{1,0:T(8,128)(2,1)S(1)}, bf16[64,7168]{1,0:T(8,128)(2,1)S(1)}, u32[]{:S(2)}, u32[]{:S(2)}) collective-permute-start(bf16[64,7168]{1,0:T(8,128)(2,1)S(1)} %get-tuple-element.53), channel_id=1, source_target_pairs={{0,4},{1,5},{2,6},{3,7},{4,8},{5,9},{6,10},{7,11},{8,12},{9,13},{1... | collective-permute-start | bytes 2752520 | tf_op jit(solution)/shard_map/ppermute | solution.py:42
  80.5 1.9 %collective-permute-start.18 = (bf16[64,7168]{1,0:T(8,128)(2,1)S(1)}, bf16[64,7168]{1,0:T(8,128)(2,1)S(1)}, u32[]{:S(2)}, u32[]{:S(2)}) collective-permute-start(bf16[64,7168]{1,0:T(8,128)(2,1)S(1)} %get-tuple-element.54), channel_id=1, source_target_pairs={{0,12},{1,13},{2,14},{3,15},{4,0},{5,1},{6,2},{7,3},{8,4},{9,5},{1... | collective-permute-start | bytes 2752520 | tf_op jit(solution)/shard_map/ppermute | solution.py:42
  82.5 8.8 %attend.2 = bf16[64,1024]{1,0:T(8,128)(2,1)S(1)} custom-call(s32[1]{0:T(128)S(1)} %bitcast.16, bf16[128,1024]{1,0:T(8,128)(2,1)S(1)} %copy-done.7, bf16[128,512]{1,0:T(8,128)(2,1)S(1)} %copy-done.8, bf16[8,128,512]{2,1,0:T(8,128)(2,1)S(1)} %copy-done.4, bf16[8,512,128]{2,1,0:T(8,128)(2,1)S(1)} %copy-done.5, bf16[2,4096,512]{2,1,0:T(8,128)(2,1)S(1)} %bitcast.11, ...), custom_call_target="tpu_custom_call" | custom-call | flops 6000000000 | bytes 8000000 | tf_op jit(solution)/shard_map/attend/pallas_call | solution.py:246
  91.3 2.5 %collective-permute-done.17 = bf16[64,7168]{1,0:T(8,128)(2,1)S(1)} collective-permute-done((bf16[64,7168]{1,0:T(8,128)(2,1)S(1)}, bf16[64,7168]{1,0:T(8,128)(2,1)S(1)}, u32[]{:S(2)}, u32[]{:S(2)}) %collective-permute-start.17) | collective-permute-done | bytes 917536 | tf_op jit(solution)/shard_map/ppermute | solution.py:42
  93.8 0.2 collective-permute-done.18
  93.9 0.2 add_convert_fusion
  94.2 3.4 %collective-permute-start.20 = (bf16[64,7168]{1,0:T(8,128)(2,1)S(1)}, bf16[64,7168]{1,0:T(8,128)(2,1)S(1)}, u32[]{:S(2)}, u32[]{:S(2)}) collective-permute-start(bf16[64,7168]{1,0:T(8,128)(2,1)S(1)} %add_convert_fusion), channel_id=1, source_target_pairs={{0,12},{1,13},{2,14},{3,15},{4,0},{5,1},{6,2},{7,3},{8,4},{9,5},{1... | collective-permute-start | bytes 2752520 | tf_op jit(solution)/shard_map/ppermute | solution.py:42
  97.5 0.2 add_convert_fusion.1
  97.7 0.1 collective-permute-start.19
  97.8 0.6 slice.69.length_ref
  98.4 6.1 %attend.3 = bf16[64,1024]{1,0:T(8,128)(2,1)S(1)} custom-call(s32[1]{0:T(128)} %slice.69.length_ref, bf16[128,1024]{1,0:T(8,128)(2,1)S(1)} %copy-done.7, bf16[128,512]{1,0:T(8,128)(2,1)S(1)} %copy-done.8, bf16[8,128,512]{2,1,0:T(8,128)(2,1)S(1)} %copy-done.4, bf16[8,512,128]{2,1,0:T(8,128)(2,1)S(1)} %copy-done.5, bf16[2,4096,512]{2,1,0:T(8,128)(2,1)S(1)} %bitcast.11, ...), custom_call_target="tpu_custom_call" | custom-call | flops 6000000000 | bytes 8000000 | tf_op jit(solution)/shard_map/attend/pallas_call | solution.py:246
  104.5 3.9 %collective-permute-done.20 = bf16[64,7168]{1,0:T(8,128)(2,1)S(1)} collective-permute-done((bf16[64,7168]{1,0:T(8,128)(2,1)S(1)}, bf16[64,7168]{1,0:T(8,128)(2,1)S(1)}, u32[]{:S(2)}, u32[]{:S(2)}) %collective-permute-start.20) | collective-permute-done | bytes 917536 | tf_op jit(solution)/shard_map/ppermute | solution.py:42
  108.4 4.0 %collective-permute-done.19 = bf16[64,7168]{1,0:T(8,128)(2,1)S(1)} collective-permute-done((bf16[64,7168]{1,0:T(8,128)(2,1)S(1)}, bf16[64,7168]{1,0:T(8,128)(2,1)S(1)}, u32[]{:S(2)}, u32[]{:S(2)}) %collective-permute-start.19) | collective-permute-done | bytes 917536 | tf_op jit(solution)/shard_map/ppermute | solution.py:42
  112.4 0.3 fusion.3
  112.8 0.3 convert_add_fusion.1
  113.2 0.1 collective-permute-start.21
  113.3 3.3 %collective-permute-start.22 = (bf16[32,7168]{1,0:T(8,128)(2,1)S(1)}, bf16[32,7168]{1,0:T(8,128)(2,1)S(1)}, u32[]{:S(2)}, u32[]{:S(2)}) collective-permute-start(bf16[32,7168]{1,0:T(8,128)(2,1)S(1)} %concatenate.29), channel_id=1, source_target_pairs={{0,3},{1,0},{2,1},{3,2},{4,7},{5,4},{6,5},{7,6},{8,11},{9,8},{10,9... | collective-permute-start | bytes 1376264 | tf_op jit(solution)/shard_map/ppermute | solution.py:42
  116.6 6.3 %collective-permute-done.21 = bf16[32,7168]{1,0:T(8,128)(2,1)S(1)} collective-permute-done((bf16[32,7168]{1,0:T(8,128)(2,1)S(1)}, bf16[32,7168]{1,0:T(8,128)(2,1)S(1)}, u32[]{:S(2)}, u32[]{:S(2)}) %collective-permute-start.21) | collective-permute-done | bytes 458784 | tf_op jit(solution)/shard_map/ppermute | solution.py:42
  123.0 0.7 collective-permute-start.23
  123.7 2.7 %collective-permute-start.24 = (bf16[16,7168]{1,0:T(8,128)(2,1)S(1)}, bf16[16,7168]{1,0:T(8,128)(2,1)S(1)}, u32[]{:S(2)}, u32[]{:S(2)}) collective-permute-start(bf16[16,7168]{1,0:T(8,128)(2,1)S(1)} %fusion.1), channel_id=1, source_target_pairs={{0,3},{1,0},{2,1},{3,2},{4,7},{5,4},{6,5},{7,6},{8,11},{9,8},{10,9... | collective-permute-start | bytes 688136 | tf_op jit(solution)/shard_map/ppermute | solution.py:42
  126.5 3.9 %collective-permute-done.23 = bf16[16,7168]{1,0:T(8,128)(2,1)S(1)} collective-permute-done((bf16[16,7168]{1,0:T(8,128)(2,1)S(1)}, bf16[16,7168]{1,0:T(8,128)(2,1)S(1)}, u32[]{:S(2)}, u32[]{:S(2)}) %collective-permute-start.23) | collective-permute-done | bytes 229408 | tf_op jit(solution)/shard_map/ppermute | solution.py:42
  130.5 0.1 fusion
  130.6 0.2 collective-permute-start.25
  130.8 3.2 %collective-permute-start.26 = (bf16[8,7168]{1,0:T(8,128)(2,1)S(1)}, bf16[8,7168]{1,0:T(8,128)(2,1)S(1)}, u32[]{:S(2)}, u32[]{:S(2)}) collective-permute-start(bf16[8,7168]{1,0:T(8,128)(2,1)S(1)} %get-tuple-element.72), channel_id=1, source_target_pairs={{0,64},{1,65},{2,66},{3,67},{4,68},{5,69},{6,70},{7,71},{8,72},{9,... | collective-permute-start | bytes 344072 | tf_op jit(solution)/shard_map/ppermute | solution.py:42
  134.0 2.0 %collective-permute-start.27 = (bf16[8,7168]{1,0:T(8,128)(2,1)S(1)}, bf16[8,7168]{1,0:T(8,128)(2,1)S(1)}, u32[]{:S(2)}, u32[]{:S(2)}) collective-permute-start(bf16[8,7168]{1,0:T(8,128)(2,1)S(1)} %get-tuple-element.71), channel_id=1, source_target_pairs={{0,96},{1,97},{2,98},{3,99},{4,100},{5,101},{6,102},{7,103},{8,104... | collective-permute-start | bytes 344072 | tf_op jit(solution)/shard_map/ppermute | solution.py:42
  136.0 0.7 pad_maximum_fusion.2
  136.7 1.3 collective-permute-done.26
  137.9 0.8 collective-permute-done.27
  138.8 0.7 add_convert_fusion.2
  (53 shorter events, 0.6 us)
Async XLA Ops:
  0.6 0.9 copy-start.1
  1.5 0.7 copy-start.2
  2.2 0.7 copy-start.3
  3.1 8.8 %collective-permute-start = (bf16[8,7296]{1,0:T(8,128)(2,1)S(1)}, bf16[8,7296]{1,0:T(8,128)(2,1)S(1)}, u32[]{:S(2)}, u32[]{:S(2)}) collective-permute-start(bf16[8,7296]{1,0:T(8,128)(2,1)S(1)} %pack.1), channel_id=1, source_target_pairs={{0,96},{1,97},{2,98},{3,99},{4,100},{5,101},{6,102},{7,103},{8,104... | collective-permute-start | bytes 350216 | tf_op jit(solution)/shard_map/ppermute | solution.py:42
  7.3 6.4 %collective-permute-start.1 = (bf16[8,7296]{1,0:T(8,128)(2,1)S(1)}, bf16[8,7296]{1,0:T(8,128)(2,1)S(1)}, u32[]{:S(2)}, u32[]{:S(2)}) collective-permute-start(bf16[8,7296]{1,0:T(8,128)(2,1)S(1)} %pack.1), channel_id=1, source_target_pairs={{0,64},{1,65},{2,66},{3,67},{4,68},{5,69},{6,70},{7,71},{8,72},{9,... | collective-permute-start | bytes 350216 | tf_op jit(solution)/shard_map/ppermute | solution.py:42
  7.3 7.3 %collective-permute-start.2 = (bf16[8,7296]{1,0:T(8,128)(2,1)S(1)}, bf16[8,7296]{1,0:T(8,128)(2,1)S(1)}, u32[]{:S(2)}, u32[]{:S(2)}) collective-permute-start(bf16[8,7296]{1,0:T(8,128)(2,1)S(1)} %pack.1), channel_id=1, source_target_pairs={{0,32},{1,33},{2,34},{3,35},{4,36},{5,37},{6,38},{7,39},{8,40},{9,... | collective-permute-start | bytes 350216 | tf_op jit(solution)/shard_map/ppermute | solution.py:42
  8.5 9.5 %copy-start = (bf16[1,256,7168]{2,1,0:T(8,128)(2,1)S(1)}, bf16[1,256,7168]{2,1,0:T(8,128)(2,1)}, u32[]{:S(2)}) copy-start(bf16[1,256,7168]{2,1,0:T(8,128)(2,1)} %param.20) | copy-start | bytes 11010052
  14.6 23.2 %collective-permute-start.9 = (bf16[7168,512]{1,0:T(8,128)(2,1)S(1)}, bf16[7168,512]{1,0:T(8,128)(2,1)S(1)}, u32[]{:S(2)}, u32[]{:S(2)}) collective-permute-start(bf16[7168,512]{1,0:T(8,128)(2,1)S(1)} %join.1.refs_2_.refs_4_), channel_id=1, source_target_pairs={{0,16},{16,0},{1,17},{17,1},{2,18},{18,2},{3,19},{19,3},{4,20},{20... | collective-permute-start | bytes 22020104 | tf_op jit(solution)/shard_map/ppermute | solution.py:58
  14.7 9.8 %collective-permute-start.5 = (bf16[32,7296]{1,0:T(8,128)(2,1)S(1)}, bf16[32,7296]{1,0:T(8,128)(2,1)S(1)}, u32[]{:S(2)}, u32[]{:S(2)}) collective-permute-start(bf16[32,7296]{1,0:T(8,128)(2,1)S(1)} %pad_maximum_fusion), channel_id=1, source_target_pairs={{0,1},{1,2},{2,3},{3,0},{4,5},{5,6},{6,7},{7,4},{8,9},{9,10},{10,1... | collective-permute-start | bytes 1400840 | tf_op jit(solution)/shard_map/ppermute | solution.py:42
  16.4 8.7 %collective-permute-start.3 = (bf16[32,7296]{1,0:T(8,128)(2,1)S(1)}, bf16[32,7296]{1,0:T(8,128)(2,1)S(1)}, u32[]{:S(2)}, u32[]{:S(2)}) collective-permute-start(bf16[32,7296]{1,0:T(8,128)(2,1)S(1)} %pad_maximum_fusion), channel_id=1, source_target_pairs={{0,3},{1,0},{2,1},{3,2},{4,7},{5,4},{6,5},{7,6},{8,11},{9,8},{10,9... | collective-permute-start | bytes 1400840 | tf_op jit(solution)/shard_map/ppermute | solution.py:42
  18.0 18.6 %collective-permute-start.10 = (bf16[256,7168]{1,0:T(8,128)(2,1)S(1)}, bf16[256,7168]{1,0:T(8,128)(2,1)S(1)}, u32[]{:S(2)}, u32[]{:S(2)}) collective-permute-start(bf16[256,7168]{1,0:T(8,128)(2,1)S(1)} %bitcast.6), channel_id=1, source_target_pairs={{0,16},{16,0},{1,17},{17,1},{2,18},{18,2},{3,19},{19,3},{4,20},{20... | collective-permute-start | bytes 11010056 | tf_op jit(solution)/shard_map/ppermute | solution.py:58
  24.6 8.2 %collective-permute-start.6 = (bf16[16,7296]{1,0:T(8,128)(2,1)S(1)}, bf16[16,7296]{1,0:T(8,128)(2,1)S(1)}, u32[]{:S(2)}, u32[]{:S(2)}) collective-permute-start(bf16[16,7296]{1,0:T(8,128)(2,1)S(1)} %slice.83), channel_id=1, source_target_pairs={{0,1},{1,2},{2,3},{3,0},{4,5},{5,6},{6,7},{7,4},{8,9},{9,10},{10,1... | collective-permute-start | bytes 700424 | tf_op jit(solution)/shard_map/ppermute | solution.py:42
  25.0 7.8 %collective-permute-start.7 = (bf16[16,7296]{1,0:T(8,128)(2,1)S(1)}, bf16[16,7296]{1,0:T(8,128)(2,1)S(1)}, u32[]{:S(2)}, u32[]{:S(2)}) collective-permute-start(bf16[16,7296]{1,0:T(8,128)(2,1)S(1)} %slice.84), channel_id=1, source_target_pairs={{0,3},{1,0},{2,1},{3,2},{4,7},{5,4},{6,5},{7,6},{8,11},{9,8},{10,9... | collective-permute-start | bytes 700424 | tf_op jit(solution)/shard_map/ppermute | solution.py:42
  28.0 14.8 %collective-permute-start.4 = (bf16[64,7296]{1,0:T(8,128)(2,1)S(1)}, bf16[64,7296]{1,0:T(8,128)(2,1)S(1)}, u32[]{:S(2)}, u32[]{:S(2)}) collective-permute-start(bf16[64,7296]{1,0:T(8,128)(2,1)S(1)} %constant_dynamic-update-slice_fusion.refs_0_), channel_id=1, source_target_pairs={{0,4},{1,5},{2,6},{3,7},{4,8},{5,9},{6,10},{7,11},{8,12},{9,13},{1... | collective-permute-start | bytes 2801672 | tf_op jit(solution)/shard_map/ppermute | solution.py:42
  32.9 13.9 %collective-permute-start.8 = (bf16[64,7296]{1,0:T(8,128)(2,1)S(1)}, bf16[64,7296]{1,0:T(8,128)(2,1)S(1)}, u32[]{:S(2)}, u32[]{:S(2)}) collective-permute-start(bf16[64,7296]{1,0:T(8,128)(2,1)S(1)} %constant_dynamic-update-slice_fusion.2.refs_1_), channel_id=1, source_target_pairs={{0,12},{1,13},{2,14},{3,15},{4,0},{5,1},{6,2},{7,3},{8,4},{9,5},{1... | collective-permute-start | bytes 2801672 | tf_op jit(solution)/shard_map/ppermute | solution.py:42
  35.7 21.1 %collective-permute-start.13 = (bf16[64,7296]{1,0:T(8,128)(2,1)S(1)}, bf16[64,7296]{1,0:T(8,128)(2,1)S(1)}, u32[]{:S(2)}, u32[]{:S(2)}) collective-permute-start(bf16[64,7296]{1,0:T(8,128)(2,1)S(1)} %constant_dynamic-update-slice_fusion.refs_0_), channel_id=1, source_target_pairs={{0,12},{1,13},{2,14},{3,15},{4,0},{5,1},{6,2},{7,3},{8,4},{9,5},{1... | collective-permute-start | bytes 2801672 | tf_op jit(solution)/shard_map/ppermute | solution.py:42
  36.6 20.3 %collective-permute-start.14 = (bf16[64,7296]{1,0:T(8,128)(2,1)S(1)}, bf16[64,7296]{1,0:T(8,128)(2,1)S(1)}, u32[]{:S(2)}, u32[]{:S(2)}) collective-permute-start(bf16[64,7296]{1,0:T(8,128)(2,1)S(1)} %constant_dynamic-update-slice_fusion.2.refs_1_), channel_id=1, source_target_pairs={{0,4},{1,5},{2,6},{3,7},{4,8},{5,9},{6,10},{7,11},{8,12},{9,13},{1... | collective-permute-start | bytes 2801672 | tf_op jit(solution)/shard_map/ppermute | solution.py:42
  46.8 21.0 %collective-permute-start.11 = (bf16[64,7296]{1,0:T(8,128)(2,1)S(1)}, bf16[64,7296]{1,0:T(8,128)(2,1)S(1)}, u32[]{:S(2)}, u32[]{:S(2)}) collective-permute-start(bf16[64,7296]{1,0:T(8,128)(2,1)S(1)} %collective-permute-done.4.refs_2_), channel_id=1, source_target_pairs={{0,4},{1,5},{2,6},{3,7},{4,8},{5,9},{6,10},{7,11},{8,12},{9,13},{1... | collective-permute-start | bytes 2801672 | tf_op jit(solution)/shard_map/ppermute | solution.py:42
  48.0 19.8 %collective-permute-start.12 = (bf16[64,7296]{1,0:T(8,128)(2,1)S(1)}, bf16[64,7296]{1,0:T(8,128)(2,1)S(1)}, u32[]{:S(2)}, u32[]{:S(2)}) collective-permute-start(bf16[64,7296]{1,0:T(8,128)(2,1)S(1)} %collective-permute-done.8.refs_1_), channel_id=1, source_target_pairs={{0,12},{1,13},{2,14},{3,15},{4,0},{5,1},{6,2},{7,3},{8,4},{9,5},{1... | collective-permute-start | bytes 2801672 | tf_op jit(solution)/shard_map/ppermute | solution.py:42
  63.8 15.1 %collective-permute-start.15 = (bf16[64,7168]{1,0:T(8,128)(2,1)S(1)}, bf16[64,7168]{1,0:T(8,128)(2,1)S(1)}, u32[]{:S(2)}, u32[]{:S(2)}) collective-permute-start(bf16[64,7168]{1,0:T(8,128)(2,1)S(1)} %get-tuple-element.45), channel_id=1, source_target_pairs={{0,4},{1,5},{2,6},{3,7},{4,8},{5,9},{6,10},{7,11},{8,12},{9,13},{1... | collective-permute-start | bytes 2752520 | tf_op jit(solution)/shard_map/ppermute | solution.py:42
  65.1 17.3 %slice-start = ((s8[8388608]{0:T(1024)(128)(4,1)}), s8[4194304]{0:T(1024)(128)(4,1)S(1)}, s32[]{:S(2)}) async-start(s8[8388608]{0:T(1024)(128)(4,1)} %bitcast.10), calls=%async_computation | async-start | bytes 8388608
  65.1 17.3 %slice-start.1 = ((s8[8388608]{0:T(1024)(128)(4,1)}), s8[4194304]{0:T(1024)(128)(4,1)S(1)}, s32[]{:S(2)}) async-start(s8[8388608]{0:T(1024)(128)(4,1)} %bitcast.10), calls=%async_computation.1 | async-start | bytes 8388608
  65.1 17.3 %copy-start.4 = (bf16[8,128,512]{2,1,0:T(8,128)(2,1)S(1)}, bf16[8,128,512]{2,1,0:T(8,128)(2,1)}, u32[]{:S(2)}) copy-start(bf16[8,128,512]{2,1,0:T(8,128)(2,1)} %key_up_ref.3) | copy-start | bytes 3145732
  65.1 17.3 %copy-start.5 = (bf16[8,512,128]{2,1,0:T(8,128)(2,1)S(1)}, bf16[8,512,128]{2,1,0:T(8,128)(2,1)}, u32[]{:S(2)}) copy-start(bf16[8,512,128]{2,1,0:T(8,128)(2,1)} %value_up_ref.3) | copy-start | bytes 3145732
  65.1 17.3 %copy-start.6 = (bf16[2,4096,64]{1,2,0:T(8,128)(2,1)S(1)}, bf16[2,4096,64]{1,2,0:T(8,128)(2,1)}, u32[]{:S(2)}) copy-start(bf16[2,4096,64]{1,2,0:T(8,128)(2,1)} %param.26) | copy-start | bytes 3145732
  65.1 17.3 %copy-start.7 = (bf16[128,1024]{1,0:T(8,128)(2,1)S(1)}, bf16[128,1024]{1,0:T(8,128)(2,1)}, u32[]{:S(2)}) copy-start(bf16[128,1024]{1,0:T(8,128)(2,1)} %nope_ref.3) | copy-start | bytes 786436
  65.2 17.3 %copy-start.8 = (bf16[128,512]{1,0:T(8,128)(2,1)S(1)}, bf16[128,512]{1,0:T(8,128)(2,1)}, u32[]{:S(2)}) copy-start(bf16[128,512]{1,0:T(8,128)(2,1)} %rope_ref.3) | copy-start | bytes 393220
  65.2 17.3 %copy-start.9 = (bf16[128,512]{1,0:T(8,128)(2,1)S(1)}, bf16[128,512]{1,0:T(8,128)(2,1)}, u32[]{:S(2)}) copy-start(bf16[128,512]{1,0:T(8,128)(2,1)} %new_latent_ref.3) | copy-start | bytes 393220
  65.2 17.3 %copy-start.10 = (bf16[128,64]{0,1:T(8,128)(2,1)S(1)}, bf16[128,64]{0,1:T(8,128)(2,1)}, u32[]{:S(2)}) copy-start(bf16[128,64]{0,1:T(8,128)(2,1)} %param.28) | copy-start | bytes 49156
  65.2 17.3 %copy-start.11 = (s32[2]{0:T(128)S(1)}, s32[2]{0:T(128)}, u32[]{:S(2)}) copy-start(s32[2]{0:T(128)} %param.29) | copy-start | bytes 28
  65.2 13.8 %collective-permute-start.16 = (bf16[64,7168]{1,0:T(8,128)(2,1)S(1)}, bf16[64,7168]{1,0:T(8,128)(2,1)S(1)}, u32[]{:S(2)}, u32[]{:S(2)}) collective-permute-start(bf16[64,7168]{1,0:T(8,128)(2,1)S(1)} %get-tuple-element.46), channel_id=1, source_target_pairs={{0,12},{1,13},{2,14},{3,15},{4,0},{5,1},{6,2},{7,3},{8,4},{9,5},{1... | collective-permute-start | bytes 2752520 | tf_op jit(solution)/shard_map/ppermute | solution.py:42
  79.0 14.8 %collective-permute-start.17 = (bf16[64,7168]{1,0:T(8,128)(2,1)S(1)}, bf16[64,7168]{1,0:T(8,128)(2,1)S(1)}, u32[]{:S(2)}, u32[]{:S(2)}) collective-permute-start(bf16[64,7168]{1,0:T(8,128)(2,1)S(1)} %get-tuple-element.53), channel_id=1, source_target_pairs={{0,4},{1,5},{2,6},{3,7},{4,8},{5,9},{6,10},{7,11},{8,12},{9,13},{1... | collective-permute-start | bytes 2752520 | tf_op jit(solution)/shard_map/ppermute | solution.py:42
  80.5 13.4 %collective-permute-start.18 = (bf16[64,7168]{1,0:T(8,128)(2,1)S(1)}, bf16[64,7168]{1,0:T(8,128)(2,1)S(1)}, u32[]{:S(2)}, u32[]{:S(2)}) collective-permute-start(bf16[64,7168]{1,0:T(8,128)(2,1)S(1)} %get-tuple-element.54), channel_id=1, source_target_pairs={{0,12},{1,13},{2,14},{3,15},{4,0},{5,1},{6,2},{7,3},{8,4},{9,5},{1... | collective-permute-start | bytes 2752520 | tf_op jit(solution)/shard_map/ppermute | solution.py:42
  94.2 14.3 %collective-permute-start.20 = (bf16[64,7168]{1,0:T(8,128)(2,1)S(1)}, bf16[64,7168]{1,0:T(8,128)(2,1)S(1)}, u32[]{:S(2)}, u32[]{:S(2)}) collective-permute-start(bf16[64,7168]{1,0:T(8,128)(2,1)S(1)} %add_convert_fusion), channel_id=1, source_target_pairs={{0,12},{1,13},{2,14},{3,15},{4,0},{5,1},{6,2},{7,3},{8,4},{9,5},{1... | collective-permute-start | bytes 2752520 | tf_op jit(solution)/shard_map/ppermute | solution.py:42
  97.7 14.7 %collective-permute-start.19 = (bf16[64,7168]{1,0:T(8,128)(2,1)S(1)}, bf16[64,7168]{1,0:T(8,128)(2,1)S(1)}, u32[]{:S(2)}, u32[]{:S(2)}) collective-permute-start(bf16[64,7168]{1,0:T(8,128)(2,1)S(1)} %add_convert_fusion.1), channel_id=1, source_target_pairs={{0,4},{1,5},{2,6},{3,7},{4,8},{5,9},{6,10},{7,11},{8,12},{9,13},{1... | collective-permute-start | bytes 2752520 | tf_op jit(solution)/shard_map/ppermute | solution.py:42
  113.2 9.8 %collective-permute-start.21 = (bf16[32,7168]{1,0:T(8,128)(2,1)S(1)}, bf16[32,7168]{1,0:T(8,128)(2,1)S(1)}, u32[]{:S(2)}, u32[]{:S(2)}) collective-permute-start(bf16[32,7168]{1,0:T(8,128)(2,1)S(1)} %pad_maximum_fusion.1), channel_id=1, source_target_pairs={{0,1},{1,2},{2,3},{3,0},{4,5},{5,6},{6,7},{7,4},{8,9},{9,10},{10,1... | collective-permute-start | bytes 1376264 | tf_op jit(solution)/shard_map/ppermute | solution.py:42
  113.3 9.7 %collective-permute-start.22 = (bf16[32,7168]{1,0:T(8,128)(2,1)S(1)}, bf16[32,7168]{1,0:T(8,128)(2,1)S(1)}, u32[]{:S(2)}, u32[]{:S(2)}) collective-permute-start(bf16[32,7168]{1,0:T(8,128)(2,1)S(1)} %concatenate.29), channel_id=1, source_target_pairs={{0,3},{1,0},{2,1},{3,2},{4,7},{5,4},{6,5},{7,6},{8,11},{9,8},{10,9... | collective-permute-start | bytes 1376264 | tf_op jit(solution)/shard_map/ppermute | solution.py:42
  123.0 7.3 %collective-permute-start.23 = (bf16[16,7168]{1,0:T(8,128)(2,1)S(1)}, bf16[16,7168]{1,0:T(8,128)(2,1)S(1)}, u32[]{:S(2)}, u32[]{:S(2)}) collective-permute-start(bf16[16,7168]{1,0:T(8,128)(2,1)S(1)} %fusion.2), channel_id=1, source_target_pairs={{0,1},{1,2},{2,3},{3,0},{4,5},{5,6},{6,7},{7,4},{8,9},{9,10},{10,1... | collective-permute-start | bytes 688136 | tf_op jit(solution)/shard_map/ppermute | solution.py:42
  123.7 6.7 %collective-permute-start.24 = (bf16[16,7168]{1,0:T(8,128)(2,1)S(1)}, bf16[16,7168]{1,0:T(8,128)(2,1)S(1)}, u32[]{:S(2)}, u32[]{:S(2)}) collective-permute-start(bf16[16,7168]{1,0:T(8,128)(2,1)S(1)} %fusion.1), channel_id=1, source_target_pairs={{0,3},{1,0},{2,1},{3,2},{4,7},{5,4},{6,5},{7,6},{8,11},{9,8},{10,9... | collective-permute-start | bytes 688136 | tf_op jit(solution)/shard_map/ppermute | solution.py:42
  130.6 6.1 %collective-permute-start.25 = (bf16[8,7168]{1,0:T(8,128)(2,1)S(1)}, bf16[8,7168]{1,0:T(8,128)(2,1)S(1)}, u32[]{:S(2)}, u32[]{:S(2)}) collective-permute-start(bf16[8,7168]{1,0:T(8,128)(2,1)S(1)} %get-tuple-element.70), channel_id=1, source_target_pairs={{0,32},{1,33},{2,34},{3,35},{4,36},{5,37},{6,38},{7,39},{8,40},{9,... | collective-permute-start | bytes 344072 | tf_op jit(solution)/shard_map/ppermute | solution.py:42
  130.8 7.2 %collective-permute-start.26 = (bf16[8,7168]{1,0:T(8,128)(2,1)S(1)}, bf16[8,7168]{1,0:T(8,128)(2,1)S(1)}, u32[]{:S(2)}, u32[]{:S(2)}) collective-permute-start(bf16[8,7168]{1,0:T(8,128)(2,1)S(1)} %get-tuple-element.72), channel_id=1, source_target_pairs={{0,64},{1,65},{2,66},{3,67},{4,68},{5,69},{6,70},{7,71},{8,72},{9,... | collective-permute-start | bytes 344072 | tf_op jit(solution)/shard_map/ppermute | solution.py:42
  134.0 4.8 %collective-permute-start.27 = (bf16[8,7168]{1,0:T(8,128)(2,1)S(1)}, bf16[8,7168]{1,0:T(8,128)(2,1)S(1)}, u32[]{:S(2)}, u32[]{:S(2)}) collective-permute-start(bf16[8,7168]{1,0:T(8,128)(2,1)S(1)} %get-tuple-element.71), channel_id=1, source_target_pairs={{0,96},{1,97},{2,98},{3,99},{4,100},{5,101},{6,102},{7,103},{8,104... | collective-permute-start | bytes 344072 | tf_op jit(solution)/shard_map/ppermute | solution.py:42

commit v3 on v2

--- a/solution.py
+++ b/solution.py
@@ -22,7 +22,7 @@
 KERNEL_VMEM = 12 * 1024 * 1024
 EXPERT_VMEM = 10 * 1024 * 1024
 PACK = 128
-DEPTH = 1024
+DEPTH = 512
 UNITS = 256
 HALF = 64
 KEY_BLOCK = 1024
@@ -60,10 +60,10 @@
 
 def expert_kernel(*refs, sources, outputs):
     row_hbm = refs[:sources]
-    both_ref, both_other_ref, down_ref, down_other_ref = refs[sources : sources + 4]
-    out_refs = refs[sources + 4 : sources + 4 + outputs]
-    rows_ref, hidden_ref, row_sem = refs[sources + 4 + outputs :]
-    width = both_ref.shape[0]
+    matrices = refs[sources : sources + 2]
+    out_refs = refs[sources + 2 : sources + 2 + outputs]
+    rows_ref, hidden_ref, row_sem = refs[sources + 2 + outputs :]
+    width = out_refs[0].shape[1]
     span = rows_ref.shape[0] // sources
     row_copies = [
         pltpu.make_async_copy(source, rows_ref.at[pl.ds(i * span, span)], row_sem.at[i])
@@ -78,32 +78,32 @@
     expert = lax.axis_index("x") * RING + lax.axis_index("y")
     pick = (lane % EXPERTS == expert) & (lane < 2 * EXPERTS)
     coefficient = jnp.sum(jnp.where(pick, extra, 0.0), axis=1, keepdims=True)
-    for i, matrix in enumerate((both_ref, both_other_ref)):
+    for i, matrix in enumerate(matrices):
         sums = sum(
-            jnp.dot(rows_ref[:, k : k + DEPTH], matrix[k : k + DEPTH, :], preferred_element_type=jnp.float32)
-            for k in range(0, width, DEPTH)
+            jnp.dot(rows_ref[:, k : k + 2 * DEPTH], matrix[k : k + 2 * DEPTH, :], preferred_element_type=jnp.float32)
+            for k in range(0, width, 2 * DEPTH)
         )
         gate, up = sums[:, :UNITS], sums[:, UNITS:]
         hidden = gate / (1.0 + jnp.exp(-gate)) * up * coefficient
         hidden_ref[i] = jnp.where(coefficient > 0, hidden, 0.0).astype(jnp.bfloat16)
-    for start in range(0, width, DEPTH):
-        part = slice(start, start + DEPTH)
-        result = jnp.dot(hidden_ref[0], down_ref[:, part], preferred_element_type=jnp.float32)
-        result += jnp.dot(hidden_ref[1], down_other_ref[:, part], preferred_element_type=jnp.float32)
+    for block in range(width // DEPTH):
+        part, place = slice(block * DEPTH, (block + 1) * DEPTH), slice(width + block * UNITS, width + (block + 1) * UNITS)
+        result = jnp.dot(hidden_ref[0], matrices[0][place, :], preferred_element_type=jnp.float32)
+        result += jnp.dot(hidden_ref[1], matrices[1][place, :], preferred_element_type=jnp.float32)
         result = result.astype(jnp.bfloat16)
         for i, out_ref in enumerate(out_refs):
             out_ref[:, part] = result[i * HALF : (i + 1) * HALF]
 
 
 def expert_terms(pieces, weights):
-    width = weights[0].shape[0]
+    width = pieces[0].shape[1] - PACK
     rows = sum(piece.shape[0] for piece in pieces)
     outputs = rows // HALF
     weights = [pltpu.with_memory_space_constraint(matrix, pltpu.VMEM) for matrix in weights]
     return pl.pallas_call(
         functools.partial(expert_kernel, sources=len(pieces), outputs=outputs),
         in_specs=[pl.BlockSpec(memory_space=pl.ANY)] * len(pieces)
-        + [pl.BlockSpec(memory_space=pltpu.VMEM)] * 4,
+        + [pl.BlockSpec(memory_space=pltpu.VMEM)] * 2,
         out_specs=[pl.BlockSpec(memory_space=pltpu.VMEM)] * outputs,
         out_shape=[jax.ShapeDtypeStruct((HALF, width), jnp.bfloat16)] * outputs,
         scratch_shapes=[
@@ -119,28 +119,35 @@
     )(*pieces, *weights)
 
 
-def join_kernel(gate_hbm, up_hbm, out_ref, sem):
+def join_kernel(gate_hbm, up_hbm, down_hbm, out_ref, sem):
+    width = gate_hbm.shape[0]
     copies = [
-        pltpu.make_async_copy(source, out_ref.at[:, pl.ds(i * UNITS, UNITS)], sem.at[i])
+        pltpu.make_async_copy(source, out_ref.at[pl.ds(0, width), pl.ds(i * UNITS, UNITS)], sem.at[i])
         for i, source in enumerate((gate_hbm, up_hbm))
     ]
+    for i in range(width // DEPTH):
+        part = out_ref.at[pl.ds(width + i * UNITS, UNITS)]
+        copies.append(pltpu.make_async_copy(down_hbm.at[:, pl.ds(i * DEPTH, DEPTH)], part, sem.at[2 + i]))
     for copy in copies:
         copy.start()
     for copy in copies:
         copy.wait()
 
 
-def joined(gate, up):
+def joined(gate, up, down):
+    width = gate.shape[0]
+    blocks = width // DEPTH
+    matrices = [pltpu.with_memory_space_constraint(matrix, pltpu.HBM) for matrix in (gate, up, down)]
     return pl.pallas_call(
         join_kernel,
-        in_specs=[pl.BlockSpec(memory_space=pl.ANY)] * 2,
+        in_specs=[pl.BlockSpec(memory_space=pl.ANY)] * 3,
         out_specs=pl.BlockSpec(memory_space=pltpu.VMEM),
-        out_shape=pltpu.VMEM((gate.shape[0], 2 * UNITS), jnp.bfloat16),
-        scratch_shapes=[pltpu.SemaphoreType.DMA((2,))],
+        out_shape=pltpu.VMEM((width + blocks * UNITS, DEPTH), jnp.bfloat16),
+        scratch_shapes=[pltpu.SemaphoreType.DMA((2 + blocks,))],
         compiler_params=pltpu.CompilerParams(vmem_limit_bytes=KERNEL_VMEM),
-        cost_estimate=pl.CostEstimate(flops=0, bytes_accessed=8 * gate.shape[0] * UNITS, transcendentals=0),
+        cost_estimate=pl.CostEstimate(flops=0, bytes_accessed=12 * width * UNITS, transcendentals=0),
         name="join",
-    )(*(pltpu.with_memory_space_constraint(value, pltpu.HBM) for value in (gate, up)))
+    )(*matrices)
 
 
 def pack_kernel(tokens_ref, routes_ref, scores_ref, out_ref):
@@ -165,7 +172,7 @@
         out_shape=jax.ShapeDtypeStruct((rows, width + PACK), jnp.bfloat16),
         compiler_params=pltpu.CompilerParams(vmem_limit_bytes=KERNEL_VMEM),
         name="pack",
-    )(tokens, routes, gate_scores)
+    )(*(pltpu.with_memory_space_constraint(value, pltpu.HBM) for value in (tokens, routes, gate_scores)))
 
 
 def attention_kernel(
@@ -293,11 +300,13 @@
 ):
     packed = packed_rows(tokens, routes, gate_scores)
     gathered = [packed] + [shift(packed, 0, -distance) for distance in (1, 2, 3)]
-    packed, gate_weight, up_weight = lax.optimization_barrier((packed, gate_weight, up_weight))
-    both = joined(gate_weight[0], up_weight[0])
+    packed, gate_weight, up_weight, down_weight = lax.optimization_barrier(
+        (packed, gate_weight, up_weight, down_weight)
+    )
+    own_weights = joined(gate_weight[0], up_weight[0], down_weight[0])
     small = jnp.concatenate(gathered, axis=0)
-    small, both, down_part = lax.optimization_barrier((small, both, down_weight[0]))
-    weights = (both, with_other_core(both), down_part, with_other_core(down_part))
+    small, own_weights = lax.optimization_barrier((small, own_weights))
+    weights = (own_weights, with_other_core(own_weights))
     rope_keys, new_rope_keys = jnp.swapaxes(rope_cache, 1, 2), new_rope.T
 
     def attention(sequence, length):
@@ -309,9 +318,11 @@
     half = small.shape[0] // 2
     own_low = jnp.concatenate([small, above], axis=0)
     below_low, above_low = shift(own_low, 2, 1), shift(own_low, 2, -1)
-    far_low, far_high = shift(below[:half], 1, 1), shift(above[half:], 1, -1)
+    far_low, far_high = lax.optimization_barrier((below[:half], above[half:]))
+    far_low, far_high = shift(far_low, 1, 1), shift(far_high, 1, -1)
     own_high = jnp.concatenate([far_low, far_high, below], axis=0)
     below_high, above_high = shift(own_high, 2, 1), shift(own_high, 2, -1)
+    own_low, own_high, below_low, above_low = lax.optimization_barrier((own_low, own_high, below_low, above_low))
     own_terms = expert_terms([own_low, own_high], weights)
     below_low, above_high, own_terms = lax.optimization_barrier((below_low, above_high, own_terms))
     far_low, far_high = shift(below_low, 2, 1), shift(above_high, 2, -1)
@@ -321,9 +332,8 @@
     near_high, near_low = shift(above_high, 2, 1), shift(below_low, 2, -1)
     far_low, far_high, above_high, below_low = lax.optimization_barrier((far_low, far_high, above_high, below_low))
     far_terms = expert_terms([far_low, far_high], weights)
-    far_terms, near_high, near_low = lax.optimization_barrier((far_terms, near_high, near_low))
     from_below, from_above = shift(far_terms[0], 2, 1), shift(far_terms[1], 2, -1)
-    far_terms, lengths = lax.optimization_barrier((far_terms, lengths))
+    far_terms, near_high, near_low, lengths = lax.optimization_barrier((far_terms, near_high, near_low, lengths))
     first_attention = attention(0, lengths[:1])
     from_below, from_above, first_attention, lengths = lax.optimization_barrier(
         (from_below, from_above, first_attention, lengths)

time: 140 us -> 134 us (0.957)
  waiting for transfers between devices: 54.5 us -> 46.3 us
  Pallas kernels: 32.7 us -> 38.5 us
  starting transfers between devices: 45.2 us -> 41.2 us
    ppermute x26, waiting for transfers between devices: 54.5 us -> 46.3 us  [shift(): return lax.ppermute(value, AXES, pairs)]
    ppermute x26, starting transfers between devices: 45.1 us -> 41.1 us  [shift(): return lax.ppermute(value, AXES, pairs)]
    pallas_call x2, Pallas kernels: 14.9 us -> 18.8 us  [attend(): pl.pallas_call(functools.partial(attention_kernel, sequence), grid_spec=p...]
    unnamed x31 -> x25, local copies, waits for them, and re-layouts: 2.39 us -> 3.5 us
  transfers between devices with their start and end apart: 28 -> 27, of which waited for: 16 -> 18; matrix products, arithmetic and copies ran while one was open for 1% -> 1% of each run, Pallas kernels for 23% -> 28%
where the time goes in v3:
time: 134 us
  waiting for transfers between devices  46.3 us (35%)
  starting transfers between devices  41.2 us (31%)
  Pallas kernels  38.5 us (29%)
  local copies, waits for them, and re-layouts  4.29 us (3%)
  other arithmetic  2.85 us (2%)
    ppermute x26, waiting for transfers between devices, shift(): return lax.ppermute(value, AXES, pairs)  46.3 us
    ppermute x26, starting transfers between devices, shift(): return lax.ppermute(value, AXES, pairs)  41.1 us
    pallas_call x2, Pallas kernels, attend(): pl.pallas_call(functools.partial(attention_kernel, sequence), grid_spec=p...  18.8 us
    pallas_call x3, Pallas kernels, expert_terms(): pl.pallas_call(functools.partial(expert_kernel, sources=len(pieces), outp...  14.3 us
    pallas_call x1, Pallas kernels, joined(): pl.pallas_call(join_kernel, in_specs=[pl.BlockSpec(memory_space=pl.ANY)]...  4.23 us
    unnamed x25, local copies, waits for them, and re-layouts  3.5 us
  transfers between devices with their start and end apart: 27, of which 18 were waited for; matrix products, arithmetic and copies ran while one was open for 1% of the time, Pallas kernels for 28%

profile of v3, /device:TPU:0, one launch (start us, length us, event | category | flops | bytes accessed | tf_op | source)
XLA Modules:
  0.0 134.2 jit_solution(7593067247253445604)
XLA Ops:
  0.6 1.1 pack.1
  1.7 4.2 %collective-permute-start = (bf16[8,7296]{1,0:T(8,128)(2,1)S(1)}, bf16[8,7296]{1,0:T(8,128)(2,1)S(1)}, u32[]{:S(2)}, u32[]{:S(2)}) collective-permute-start(bf16[8,7296]{1,0:T(8,128)(2,1)S(1)} %pack.1), channel_id=1, source_target_pairs={{0,96},{1,97},{2,98},{3,99},{4,100},{5,101},{6,102},{7,103},{8,104... | collective-permute-start | bytes 350216 | tf_op jit(solution)/shard_map/ppermute | solution.py:42
  5.9 1.3 collective-permute-start.2
  7.2 4.2 %join.1.refs_2_.refs_4_ = bf16[10752,512]{1,0:T(8,128)(2,1)S(1)} custom-call(bf16[7168,256]{1,0:T(8,128)(2,1)} %bitcast.13, bf16[7168,256]{1,0:T(8,128)(2,1)} %bitcast.14, bf16[256,7168]{1,0:T(8,128)(2,1)} %bitcast.15), custom_call_target="tpu_custom_call" | custom-call | bytes 22020096 | tf_op jit(solution)/shard_map/join/pallas_call | solution.py:141
  11.4 0.9 collective-permute-done.1
  12.4 0.9 collective-permute-done.2
  13.2 0.1 pad_maximum_fusion
  13.3 0.1 collective-permute-start.10
  13.4 1.6 %collective-permute-start.4 = (bf16[32,7296]{1,0:T(8,128)(2,1)S(1)}, bf16[32,7296]{1,0:T(8,128)(2,1)S(1)}, u32[]{:S(2)}, u32[]{:S(2)}) collective-permute-start(bf16[32,7296]{1,0:T(8,128)(2,1)S(1)} %pad_maximum_fusion), channel_id=1, source_target_pairs={{0,1},{1,2},{2,3},{3,0},{4,5},{5,6},{6,7},{7,4},{8,9},{9,10},{10,1... | collective-permute-start | bytes 1400840 | tf_op jit(solution)/shard_map/ppermute | solution.py:42
  15.0 1.7 %collective-permute-start.3 = (bf16[32,7296]{1,0:T(8,128)(2,1)S(1)}, bf16[32,7296]{1,0:T(8,128)(2,1)S(1)}, u32[]{:S(2)}, u32[]{:S(2)}) collective-permute-start(bf16[32,7296]{1,0:T(8,128)(2,1)S(1)} %pad_maximum_fusion), channel_id=1, source_target_pairs={{0,3},{1,0},{2,1},{3,2},{4,7},{5,4},{6,5},{7,6},{8,11},{9,8},{10,9... | collective-permute-start | bytes 1400840 | tf_op jit(solution)/shard_map/ppermute | solution.py:42
  16.7 6.5 %collective-permute-done.4 = bf16[32,7296]{1,0:T(8,128)(2,1)S(1)} collective-permute-done((bf16[32,7296]{1,0:T(8,128)(2,1)S(1)}, bf16[32,7296]{1,0:T(8,128)(2,1)S(1)}, u32[]{:S(2)}, u32[]{:S(2)}) %collective-permute-start.4) | collective-permute-done | bytes 466976 | tf_op jit(solution)/shard_map/ppermute | solution.py:42
  23.2 0.3 collective-permute-done.3
  23.6 1.6 %collective-permute-start.5 = (bf16[16,7296]{1,0:T(8,128)(2,1)S(1)}, bf16[16,7296]{1,0:T(8,128)(2,1)S(1)}, u32[]{:S(2)}, u32[]{:S(2)}) collective-permute-start(bf16[16,7296]{1,0:T(8,128)(2,1)S(1)} %slice.83), channel_id=1, source_target_pairs={{0,1},{1,2},{2,3},{3,0},{4,5},{5,6},{6,7},{7,4},{8,9},{9,10},{10,1... | collective-permute-start | bytes 700424 | tf_op jit(solution)/shard_map/ppermute | solution.py:42
  25.3 1.6 %collective-permute-start.7 = (bf16[64,7296]{1,0:T(8,128)(2,1)S(1)}, bf16[64,7296]{1,0:T(8,128)(2,1)S(1)}, u32[]{:S(2)}, u32[]{:S(2)}) collective-permute-start(bf16[64,7296]{1,0:T(8,128)(2,1)S(1)} %constant_dynamic-update-slice_fusion.refs_0_), channel_id=1, source_target_pairs={{0,4},{1,5},{2,6},{3,7},{4,8},{5,9},{6,10},{7,11},{8,12},{9,13},{1... | collective-permute-start | bytes 2801672 | tf_op jit(solution)/shard_map/ppermute | solution.py:42
  26.8 1.7 %collective-permute-start.8 = (bf16[64,7296]{1,0:T(8,128)(2,1)S(1)}, bf16[64,7296]{1,0:T(8,128)(2,1)S(1)}, u32[]{:S(2)}, u32[]{:S(2)}) collective-permute-start(bf16[64,7296]{1,0:T(8,128)(2,1)S(1)} %constant_dynamic-update-slice_fusion.refs_0_), channel_id=1, source_target_pairs={{0,12},{1,13},{2,14},{3,15},{4,0},{5,1},{6,2},{7,3},{8,4},{9,5},{1... | collective-permute-start | bytes 2801672 | tf_op jit(solution)/shard_map/ppermute | solution.py:42
  28.6 1.7 %collective-permute-start.6 = (bf16[16,7296]{1,0:T(8,128)(2,1)S(1)}, bf16[16,7296]{1,0:T(8,128)(2,1)S(1)}, u32[]{:S(2)}, u32[]{:S(2)}) collective-permute-start(bf16[16,7296]{1,0:T(8,128)(2,1)S(1)} %slice.84), channel_id=1, source_target_pairs={{0,3},{1,0},{2,1},{3,2},{4,7},{5,4},{6,5},{7,6},{8,11},{9,8},{10,9... | collective-permute-start | bytes 700424 | tf_op jit(solution)/shard_map/ppermute | solution.py:42
  30.2 3.3 %collective-permute-done.5 = bf16[16,7296]{1,0:T(8,128)(2,1)S(1)} collective-permute-done((bf16[16,7296]{1,0:T(8,128)(2,1)S(1)}, bf16[16,7296]{1,0:T(8,128)(2,1)S(1)}, u32[]{:S(2)}, u32[]{:S(2)}) %collective-permute-start.5) | collective-permute-done | bytes 233504 | tf_op jit(solution)/shard_map/ppermute | solution.py:42
  33.5 3.7 %collective-permute-done.6 = bf16[16,7296]{1,0:T(8,128)(2,1)S(1)} collective-permute-done((bf16[16,7296]{1,0:T(8,128)(2,1)S(1)}, bf16[16,7296]{1,0:T(8,128)(2,1)S(1)}, u32[]{:S(2)}, u32[]{:S(2)}) %collective-permute-start.6) | collective-permute-done | bytes 233504 | tf_op jit(solution)/shard_map/ppermute | solution.py:42
  37.3 1.6 %collective-permute-start.9 = (bf16[64,7296]{1,0:T(8,128)(2,1)S(1)}, bf16[64,7296]{1,0:T(8,128)(2,1)S(1)}, u32[]{:S(2)}, u32[]{:S(2)}) collective-permute-start(bf16[64,7296]{1,0:T(8,128)(2,1)S(1)} %constant_dynamic-update-slice_fusion.2.refs_1_), channel_id=1, source_target_pairs={{0,12},{1,13},{2,14},{3,15},{4,0},{5,1},{6,2},{7,3},{8,4},{9,5},{1... | collective-permute-start | bytes 2801672 | tf_op jit(solution)/shard_map/ppermute | solution.py:42
  38.9 0.5 collective-permute-start.13
  39.4 0.7 collective-permute-done.7.refs_2_
  40.1 0.3 collective-permute-done.8.refs_0_
  40.4 3.7 %expert.3 = (bf16[64,7168]{1,0:T(8,128)(2,1)S(1)}, bf16[64,7168]{1,0:T(8,128)(2,1)S(1)}) custom-call(bf16[64,7296]{1,0:T(8,128)(2,1)S(1)} %constant_dynamic-update-slice_fusion.refs_0_, bf16[64,7296]{1,0:T(8,128)(2,1)S(1)} %constant_dynamic-update-slice_fusion.2.refs_1_, bf16[10752,512]{1,0:T(8,128)(2,1)S(1)} %join.1.refs_2_.refs_4_, ...), custom_call_target="tpu_custom_call" | custom-call | flops 2818572288 | bytes 3670016 | tf_op jit(solution)/shard_map/expert/pallas_call | solution.py:103
  44.1 6.8 %collective-permute-done.9.refs_1_ = bf16[64,7296]{1,0:T(8,128)(2,1)S(1)} collective-permute-done((bf16[64,7296]{1,0:T(8,128)(2,1)S(1)}, bf16[64,7296]{1,0:T(8,128)(2,1)S(1)}, u32[]{:S(2)}, u32[]{:S(2)}) %collective-permute-start.9) | collective-permute-done | bytes 933920 | tf_op jit(solution)/shard_map/ppermute | solution.py:42
  50.9 1.0 collective-permute-start.11
  51.9 2.3 %collective-permute-start.12 = (bf16[64,7296]{1,0:T(8,128)(2,1)S(1)}, bf16[64,7296]{1,0:T(8,128)(2,1)S(1)}, u32[]{:S(2)}, u32[]{:S(2)}) collective-permute-start(bf16[64,7296]{1,0:T(8,128)(2,1)S(1)} %collective-permute-done.9.refs_1_), channel_id=1, source_target_pairs={{0,12},{1,13},{2,14},{3,15},{4,0},{5,1},{6,2},{7,3},{8,4},{9,5},{1... | collective-permute-start | bytes 2801672 | tf_op jit(solution)/shard_map/ppermute | solution.py:42
  54.2 7.0 %expert.4 = (bf16[64,7168]{1,0:T(8,128)(2,1)S(1)}, bf16[64,7168]{1,0:T(8,128)(2,1)S(1)}, bf16[64,7168]{1,0:T(8,128)(2,1)S(1)}, bf16[64,7168]{1,0:T(8,128)(2,1)S(1)}) custom-call(bf16[64,7296]{1,0:T(8,128)(2,1)S(1)} %collective-permute-done.8.refs_0_, bf16[64,7296]{1,0:T(8,128)(2,1)S(1)} %collective-permute-done.9.refs_1_, ...), custom_call_target="tpu_custom_call" | custom-call | flops 5637144576 | bytes 7340032 | tf_op jit(solution)/shard_map/expert/pallas_call | solution.py:103
  61.1 0.1 collective-permute-start.14
  61.2 0.0 copy-start.1
  61.3 0.0 copy-start.4
  61.3 0.0 copy-start.5
  61.3 3.3 %collective-permute-start.15 = (bf16[64,7168]{1,0:T(8,128)(2,1)S(1)}, bf16[64,7168]{1,0:T(8,128)(2,1)S(1)}, u32[]{:S(2)}, u32[]{:S(2)}) collective-permute-start(bf16[64,7168]{1,0:T(8,128)(2,1)S(1)} %get-tuple-element.56), channel_id=1, source_target_pairs={{0,12},{1,13},{2,14},{3,15},{4,0},{5,1},{6,2},{7,3},{8,4},{9,5},{1... | collective-permute-start | bytes 2752520 | tf_op jit(solution)/shard_map/ppermute | solution.py:42
  64.6 1.1 collective-permute-done.11.refs_0_
  65.7 3.7 %expert.5 = (bf16[64,7168]{1,0:T(8,128)(2,1)S(1)}, bf16[64,7168]{1,0:T(8,128)(2,1)S(1)}) custom-call(bf16[64,7296]{1,0:T(8,128)(2,1)S(1)} %collective-permute-done.11.refs_0_, bf16[64,7296]{1,0:T(8,128)(2,1)S(1)} %collective-permute-done.12.refs_1_, bf16[10752,512]{1,0:T(8,128)(2,1)S(1)} %join.1.refs_2_.refs_4_, ...), custom_call_target="tpu_custom_call" | custom-call | flops 2818572288 | bytes 3670016 | tf_op jit(solution)/shard_map/expert/pallas_call | solution.py:103
  69.4 1.0 collective-permute-start.16
  70.4 2.3 %collective-permute-start.17 = (bf16[64,7168]{1,0:T(8,128)(2,1)S(1)}, bf16[64,7168]{1,0:T(8,128)(2,1)S(1)}, u32[]{:S(2)}, u32[]{:S(2)}) collective-permute-start(bf16[64,7168]{1,0:T(8,128)(2,1)S(1)} %get-tuple-element.60), channel_id=1, source_target_pairs={{0,12},{1,13},{2,14},{3,15},{4,0},{5,1},{6,2},{7,3},{8,4},{9,5},{1... | collective-permute-start | bytes 2752520 | tf_op jit(solution)/shard_map/ppermute | solution.py:42
  72.8 3.0 %collective-permute-done.14 = bf16[64,7168]{1,0:T(8,128)(2,1)S(1)} collective-permute-done((bf16[64,7168]{1,0:T(8,128)(2,1)S(1)}, bf16[64,7168]{1,0:T(8,128)(2,1)S(1)}, u32[]{:S(2)}, u32[]{:S(2)}) %collective-permute-start.14) | collective-permute-done | bytes 917536 | tf_op jit(solution)/shard_map/ppermute | solution.py:42
  75.9 3.4 %copy-done = bf16[2,4096,512]{2,1,0:T(8,128)(2,1)S(1)} copy-done((bf16[2,4096,512]{2,1,0:T(8,128)(2,1)S(1)}, bf16[2,4096,512]{2,1,0:T(8,128)(2,1)}, u32[]{:S(2)}) %copy-start) | copy-done | bytes 8388632
  79.3 8.8 %attend.2 = bf16[64,1024]{1,0:T(8,128)(2,1)S(1)} custom-call(s32[1]{0:T(128)S(1)} %bitcast.12, bf16[128,1024]{1,0:T(8,128)(2,1)S(1)} %copy-done.4, bf16[128,512]{1,0:T(8,128)(2,1)S(1)} %copy-done.5, bf16[8,128,512]{2,1,0:T(8,128)(2,1)S(1)} %copy-done.1, bf16[8,512,128]{2,1,0:T(8,128)(2,1)S(1)} %copy-done.2, bf16[2,4096,512]{2,1,0:T(8,128)(2,1)S(1)} %copy-done, ...), custom_call_target="tpu_custom_call" | custom-call | flops 6000000000 | bytes 8000000 | tf_op jit(solution)/shard_map/attend/pallas_call | solution.py:253
  88.1 0.2 add_convert_fusion
  88.3 3.4 %collective-permute-start.19 = (bf16[64,7168]{1,0:T(8,128)(2,1)S(1)}, bf16[64,7168]{1,0:T(8,128)(2,1)S(1)}, u32[]{:S(2)}, u32[]{:S(2)}) collective-permute-start(bf16[64,7168]{1,0:T(8,128)(2,1)S(1)} %add_convert_fusion), channel_id=1, source_target_pairs={{0,12},{1,13},{2,14},{3,15},{4,0},{5,1},{6,2},{7,3},{8,4},{9,5},{1... | collective-permute-start | bytes 2752520 | tf_op jit(solution)/shard_map/ppermute | solution.py:42
  91.7 0.2 add_convert_fusion.1
  92.0 0.3 collective-permute-start.18
  92.3 0.6 slice.69.length_ref
  92.8 10.0 %attend.3 = bf16[64,1024]{1,0:T(8,128)(2,1)S(1)} custom-call(s32[1]{0:T(128)} %slice.69.length_ref, bf16[128,1024]{1,0:T(8,128)(2,1)S(1)} %copy-done.4, bf16[128,512]{1,0:T(8,128)(2,1)S(1)} %copy-done.5, bf16[8,128,512]{2,1,0:T(8,128)(2,1)S(1)} %copy-done.1, bf16[8,512,128]{2,1,0:T(8,128)(2,1)S(1)} %copy-done.2, bf16[2,4096,512]{2,1,0:T(8,128)(2,1)S(1)} %bitcast.7, ...), custom_call_target="tpu_custom_call" | custom-call | flops 6000000000 | bytes 8000000 | tf_op jit(solution)/shard_map/attend/pallas_call | solution.py:253
  102.9 4.0 %collective-permute-done.18 = bf16[64,7168]{1,0:T(8,128)(2,1)S(1)} collective-permute-done((bf16[64,7168]{1,0:T(8,128)(2,1)S(1)}, bf16[64,7168]{1,0:T(8,128)(2,1)S(1)}, u32[]{:S(2)}, u32[]{:S(2)}) %collective-permute-start.18) | collective-permute-done | bytes 917536 | tf_op jit(solution)/shard_map/ppermute | solution.py:42
  106.9 0.3 fusion.3
  107.2 0.3 convert_add_fusion.1
  107.6 1.3 collective-permute-start.20
  109.0 2.0 %collective-permute-start.21 = (bf16[32,7168]{1,0:T(8,128)(2,1)S(1)}, bf16[32,7168]{1,0:T(8,128)(2,1)S(1)}, u32[]{:S(2)}, u32[]{:S(2)}) collective-permute-start(bf16[32,7168]{1,0:T(8,128)(2,1)S(1)} %concatenate.29), channel_id=1, source_target_pairs={{0,3},{1,0},{2,1},{3,2},{4,7},{5,4},{6,5},{7,6},{8,11},{9,8},{10,9... | collective-permute-start | bytes 1376264 | tf_op jit(solution)/shard_map/ppermute | solution.py:42
  111.0 6.3 %collective-permute-done.20 = bf16[32,7168]{1,0:T(8,128)(2,1)S(1)} collective-permute-done((bf16[32,7168]{1,0:T(8,128)(2,1)S(1)}, bf16[32,7168]{1,0:T(8,128)(2,1)S(1)}, u32[]{:S(2)}, u32[]{:S(2)}) %collective-permute-start.20) | collective-permute-done | bytes 458784 | tf_op jit(solution)/shard_map/ppermute | solution.py:42
  117.4 0.1 collective-permute-done.21
  117.6 1.5 %collective-permute-start.22 = (bf16[16,7168]{1,0:T(8,128)(2,1)S(1)}, bf16[16,7168]{1,0:T(8,128)(2,1)S(1)}, u32[]{:S(2)}, u32[]{:S(2)}) collective-permute-start(bf16[16,7168]{1,0:T(8,128)(2,1)S(1)} %fusion.2), channel_id=1, source_target_pairs={{0,1},{1,2},{2,3},{3,0},{4,5},{5,6},{6,7},{7,4},{8,9},{9,10},{10,1... | collective-permute-start | bytes 688136 | tf_op jit(solution)/shard_map/ppermute | solution.py:42
  119.1 1.8 %collective-permute-start.23 = (bf16[16,7168]{1,0:T(8,128)(2,1)S(1)}, bf16[16,7168]{1,0:T(8,128)(2,1)S(1)}, u32[]{:S(2)}, u32[]{:S(2)}) collective-permute-start(bf16[16,7168]{1,0:T(8,128)(2,1)S(1)} %fusion.1), channel_id=1, source_target_pairs={{0,3},{1,0},{2,1},{3,2},{4,7},{5,4},{6,5},{7,6},{8,11},{9,8},{10,9... | collective-permute-start | bytes 688136 | tf_op jit(solution)/shard_map/ppermute | solution.py:42
  120.9 4.0 %collective-permute-done.22 = bf16[16,7168]{1,0:T(8,128)(2,1)S(1)} collective-permute-done((bf16[16,7168]{1,0:T(8,128)(2,1)S(1)}, bf16[16,7168]{1,0:T(8,128)(2,1)S(1)}, u32[]{:S(2)}, u32[]{:S(2)}) %collective-permute-start.22) | collective-permute-done | bytes 229408 | tf_op jit(solution)/shard_map/ppermute | solution.py:42
  124.9 0.2 collective-permute-done.23
  125.2 0.1 fusion
  125.3 0.1 collective-permute-start.24
  125.4 1.1 collective-permute-start.25
  126.5 2.1 %collective-permute-start.26 = (bf16[8,7168]{1,0:T(8,128)(2,1)S(1)}, bf16[8,7168]{1,0:T(8,128)(2,1)S(1)}, u32[]{:S(2)}, u32[]{:S(2)}) collective-permute-start(bf16[8,7168]{1,0:T(8,128)(2,1)S(1)} %get-tuple-element.79), channel_id=1, source_target_pairs={{0,96},{1,97},{2,98},{3,99},{4,100},{5,101},{6,102},{7,103},{8,104... | collective-permute-start | bytes 344072 | tf_op jit(solution)/shard_map/ppermute | solution.py:42
  128.6 0.7 pad_maximum_fusion.2
  129.3 3.3 %collective-permute-done.24 = bf16[8,7168]{1,0:T(8,128)(2,1)S(1)} collective-permute-done((bf16[8,7168]{1,0:T(8,128)(2,1)S(1)}, bf16[8,7168]{1,0:T(8,128)(2,1)S(1)}, u32[]{:S(2)}, u32[]{:S(2)}) %collective-permute-start.24) | collective-permute-done | bytes 114720 | tf_op jit(solution)/shard_map/ppermute | solution.py:42
  132.6 0.9 collective-permute-done.26
  133.5 0.7 add_convert_fusion.2
  (45 shorter events, 0.6 us)
Async XLA Ops:
  1.7 9.7 %collective-permute-start = (bf16[8,7296]{1,0:T(8,128)(2,1)S(1)}, bf16[8,7296]{1,0:T(8,128)(2,1)S(1)}, u32[]{:S(2)}, u32[]{:S(2)}) collective-permute-start(bf16[8,7296]{1,0:T(8,128)(2,1)S(1)} %pack.1), channel_id=1, source_target_pairs={{0,96},{1,97},{2,98},{3,99},{4,100},{5,101},{6,102},{7,103},{8,104... | collective-permute-start | bytes 350216 | tf_op jit(solution)/shard_map/ppermute | solution.py:42
  5.9 6.4 %collective-permute-start.1 = (bf16[8,7296]{1,0:T(8,128)(2,1)S(1)}, bf16[8,7296]{1,0:T(8,128)(2,1)S(1)}, u32[]{:S(2)}, u32[]{:S(2)}) collective-permute-start(bf16[8,7296]{1,0:T(8,128)(2,1)S(1)} %pack.1), channel_id=1, source_target_pairs={{0,64},{1,65},{2,66},{3,67},{4,68},{5,69},{6,70},{7,71},{8,72},{9,... | collective-permute-start | bytes 350216 | tf_op jit(solution)/shard_map/ppermute | solution.py:42
  5.9 7.3 %collective-permute-start.2 = (bf16[8,7296]{1,0:T(8,128)(2,1)S(1)}, bf16[8,7296]{1,0:T(8,128)(2,1)S(1)}, u32[]{:S(2)}, u32[]{:S(2)}) collective-permute-start(bf16[8,7296]{1,0:T(8,128)(2,1)S(1)} %pack.1), channel_id=1, source_target_pairs={{0,32},{1,33},{2,34},{3,35},{4,36},{5,37},{6,38},{7,39},{8,40},{9,... | collective-permute-start | bytes 350216 | tf_op jit(solution)/shard_map/ppermute | solution.py:42
  13.3 27.1 %collective-permute-start.10 = (bf16[10752,512]{1,0:T(8,128)(2,1)S(1)}, bf16[10752,512]{1,0:T(8,128)(2,1)S(1)}, u32[]{:S(2)}, u32[]{:S(2)}) collective-permute-start(bf16[10752,512]{1,0:T(8,128)(2,1)S(1)} %join.1.refs_2_.refs_4_), channel_id=1, source_target_pairs={{0,16},{16,0},{1,17},{17,1},{2,18},{18,2},{3,19},{19,3},{4,20},{20... | collective-permute-start | bytes 33030152 | tf_op jit(solution)/shard_map/ppermute | solution.py:58
  13.4 9.8 %collective-permute-start.4 = (bf16[32,7296]{1,0:T(8,128)(2,1)S(1)}, bf16[32,7296]{1,0:T(8,128)(2,1)S(1)}, u32[]{:S(2)}, u32[]{:S(2)}) collective-permute-start(bf16[32,7296]{1,0:T(8,128)(2,1)S(1)} %pad_maximum_fusion), channel_id=1, source_target_pairs={{0,1},{1,2},{2,3},{3,0},{4,5},{5,6},{6,7},{7,4},{8,9},{9,10},{10,1... | collective-permute-start | bytes 1400840 | tf_op jit(solution)/shard_map/ppermute | solution.py:42
  15.0 8.6 %collective-permute-start.3 = (bf16[32,7296]{1,0:T(8,128)(2,1)S(1)}, bf16[32,7296]{1,0:T(8,128)(2,1)S(1)}, u32[]{:S(2)}, u32[]{:S(2)}) collective-permute-start(bf16[32,7296]{1,0:T(8,128)(2,1)S(1)} %pad_maximum_fusion), channel_id=1, source_target_pairs={{0,3},{1,0},{2,1},{3,2},{4,7},{5,4},{6,5},{7,6},{8,11},{9,8},{10,9... | collective-permute-start | bytes 1400840 | tf_op jit(solution)/shard_map/ppermute | solution.py:42
  23.6 9.9 %collective-permute-start.5 = (bf16[16,7296]{1,0:T(8,128)(2,1)S(1)}, bf16[16,7296]{1,0:T(8,128)(2,1)S(1)}, u32[]{:S(2)}, u32[]{:S(2)}) collective-permute-start(bf16[16,7296]{1,0:T(8,128)(2,1)S(1)} %slice.83), channel_id=1, source_target_pairs={{0,1},{1,2},{2,3},{3,0},{4,5},{5,6},{6,7},{7,4},{8,9},{9,10},{10,1... | collective-permute-start | bytes 700424 | tf_op jit(solution)/shard_map/ppermute | solution.py:42
  25.3 14.8 %collective-permute-start.7 = (bf16[64,7296]{1,0:T(8,128)(2,1)S(1)}, bf16[64,7296]{1,0:T(8,128)(2,1)S(1)}, u32[]{:S(2)}, u32[]{:S(2)}) collective-permute-start(bf16[64,7296]{1,0:T(8,128)(2,1)S(1)} %constant_dynamic-update-slice_fusion.refs_0_), channel_id=1, source_target_pairs={{0,4},{1,5},{2,6},{3,7},{4,8},{5,9},{6,10},{7,11},{8,12},{9,13},{1... | collective-permute-start | bytes 2801672 | tf_op jit(solution)/shard_map/ppermute | solution.py:42
  26.8 13.6 %collective-permute-start.8 = (bf16[64,7296]{1,0:T(8,128)(2,1)S(1)}, bf16[64,7296]{1,0:T(8,128)(2,1)S(1)}, u32[]{:S(2)}, u32[]{:S(2)}) collective-permute-start(bf16[64,7296]{1,0:T(8,128)(2,1)S(1)} %constant_dynamic-update-slice_fusion.refs_0_), channel_id=1, source_target_pairs={{0,12},{1,13},{2,14},{3,15},{4,0},{5,1},{6,2},{7,3},{8,4},{9,5},{1... | collective-permute-start | bytes 2801672 | tf_op jit(solution)/shard_map/ppermute | solution.py:42
  28.6 8.6 %collective-permute-start.6 = (bf16[16,7296]{1,0:T(8,128)(2,1)S(1)}, bf16[16,7296]{1,0:T(8,128)(2,1)S(1)}, u32[]{:S(2)}, u32[]{:S(2)}) collective-permute-start(bf16[16,7296]{1,0:T(8,128)(2,1)S(1)} %slice.84), channel_id=1, source_target_pairs={{0,3},{1,0},{2,1},{3,2},{4,7},{5,4},{6,5},{7,6},{8,11},{9,8},{10,9... | collective-permute-start | bytes 700424 | tf_op jit(solution)/shard_map/ppermute | solution.py:42
  37.3 13.6 %collective-permute-start.9 = (bf16[64,7296]{1,0:T(8,128)(2,1)S(1)}, bf16[64,7296]{1,0:T(8,128)(2,1)S(1)}, u32[]{:S(2)}, u32[]{:S(2)}) collective-permute-start(bf16[64,7296]{1,0:T(8,128)(2,1)S(1)} %constant_dynamic-update-slice_fusion.2.refs_1_), channel_id=1, source_target_pairs={{0,12},{1,13},{2,14},{3,15},{4,0},{5,1},{6,2},{7,3},{8,4},{9,5},{1... | collective-permute-start | bytes 2801672 | tf_op jit(solution)/shard_map/ppermute | solution.py:42
  38.9 15.3 %collective-permute-start.13 = (bf16[64,7296]{1,0:T(8,128)(2,1)S(1)}, bf16[64,7296]{1,0:T(8,128)(2,1)S(1)}, u32[]{:S(2)}, u32[]{:S(2)}) collective-permute-start(bf16[64,7296]{1,0:T(8,128)(2,1)S(1)} %constant_dynamic-update-slice_fusion.2.refs_1_), channel_id=1, source_target_pairs={{0,4},{1,5},{2,6},{3,7},{4,8},{5,9},{6,10},{7,11},{8,12},{9,13},{1... | collective-permute-start | bytes 2801672 | tf_op jit(solution)/shard_map/ppermute | solution.py:42
  50.9 14.8 %collective-permute-start.11 = (bf16[64,7296]{1,0:T(8,128)(2,1)S(1)}, bf16[64,7296]{1,0:T(8,128)(2,1)S(1)}, u32[]{:S(2)}, u32[]{:S(2)}) collective-permute-start(bf16[64,7296]{1,0:T(8,128)(2,1)S(1)} %collective-permute-done.7.refs_2_), channel_id=1, source_target_pairs={{0,4},{1,5},{2,6},{3,7},{4,8},{5,9},{6,10},{7,11},{8,12},{9,13},{1... | collective-permute-start | bytes 2801672 | tf_op jit(solution)/shard_map/ppermute | solution.py:42
  51.9 13.8 %collective-permute-start.12 = (bf16[64,7296]{1,0:T(8,128)(2,1)S(1)}, bf16[64,7296]{1,0:T(8,128)(2,1)S(1)}, u32[]{:S(2)}, u32[]{:S(2)}) collective-permute-start(bf16[64,7296]{1,0:T(8,128)(2,1)S(1)} %collective-permute-done.9.refs_1_), channel_id=1, source_target_pairs={{0,12},{1,13},{2,14},{3,15},{4,0},{5,1},{6,2},{7,3},{8,4},{9,5},{1... | collective-permute-start | bytes 2801672 | tf_op jit(solution)/shard_map/ppermute | solution.py:42
  61.1 14.7 %collective-permute-start.14 = (bf16[64,7168]{1,0:T(8,128)(2,1)S(1)}, bf16[64,7168]{1,0:T(8,128)(2,1)S(1)}, u32[]{:S(2)}, u32[]{:S(2)}) collective-permute-start(bf16[64,7168]{1,0:T(8,128)(2,1)S(1)} %get-tuple-element.55), channel_id=1, source_target_pairs={{0,4},{1,5},{2,6},{3,7},{4,8},{5,9},{6,10},{7,11},{8,12},{9,13},{1... | collective-permute-start | bytes 2752520 | tf_op jit(solution)/shard_map/ppermute | solution.py:42
  61.2 14.6 %copy-start.1 = (bf16[8,128,512]{2,1,0:T(8,128)(2,1)S(1)}, bf16[8,128,512]{2,1,0:T(8,128)(2,1)}, u32[]{:S(2)}) copy-start(bf16[8,128,512]{2,1,0:T(8,128)(2,1)} %key_up_ref.3) | copy-start | bytes 3145732
  61.2 14.6 %copy-start.2 = (bf16[8,512,128]{2,1,0:T(8,128)(2,1)S(1)}, bf16[8,512,128]{2,1,0:T(8,128)(2,1)}, u32[]{:S(2)}) copy-start(bf16[8,512,128]{2,1,0:T(8,128)(2,1)} %value_up_ref.3) | copy-start | bytes 3145732
  61.2 14.6 %copy-start.3 = (bf16[2,4096,64]{1,2,0:T(8,128)(2,1)S(1)}, bf16[2,4096,64]{1,2,0:T(8,128)(2,1)}, u32[]{:S(2)}) copy-start(bf16[2,4096,64]{1,2,0:T(8,128)(2,1)} %param.26) | copy-start | bytes 3145732
  61.3 14.6 %copy-start.4 = (bf16[128,1024]{1,0:T(8,128)(2,1)S(1)}, bf16[128,1024]{1,0:T(8,128)(2,1)}, u32[]{:S(2)}) copy-start(bf16[128,1024]{1,0:T(8,128)(2,1)} %nope_ref.3) | copy-start | bytes 786436
  61.3 14.6 %copy-start.5 = (bf16[128,512]{1,0:T(8,128)(2,1)S(1)}, bf16[128,512]{1,0:T(8,128)(2,1)}, u32[]{:S(2)}) copy-start(bf16[128,512]{1,0:T(8,128)(2,1)} %rope_ref.3) | copy-start | bytes 393220
  61.3 14.6 %copy-start.6 = (bf16[128,512]{1,0:T(8,128)(2,1)S(1)}, bf16[128,512]{1,0:T(8,128)(2,1)}, u32[]{:S(2)}) copy-start(bf16[128,512]{1,0:T(8,128)(2,1)} %new_latent_ref.3) | copy-start | bytes 393220
  61.3 14.6 %copy-start.7 = (bf16[128,64]{0,1:T(8,128)(2,1)S(1)}, bf16[128,64]{0,1:T(8,128)(2,1)}, u32[]{:S(2)}) copy-start(bf16[128,64]{0,1:T(8,128)(2,1)} %param.28) | copy-start | bytes 49156
  61.3 14.6 %copy-start.8 = (s32[2]{0:T(128)S(1)}, s32[2]{0:T(128)}, u32[]{:S(2)}) copy-start(s32[2]{0:T(128)} %param.29) | copy-start | bytes 28
  61.3 14.5 %collective-permute-start.15 = (bf16[64,7168]{1,0:T(8,128)(2,1)S(1)}, bf16[64,7168]{1,0:T(8,128)(2,1)S(1)}, u32[]{:S(2)}, u32[]{:S(2)}) collective-permute-start(bf16[64,7168]{1,0:T(8,128)(2,1)S(1)} %get-tuple-element.56), channel_id=1, source_target_pairs={{0,12},{1,13},{2,14},{3,15},{4,0},{5,1},{6,2},{7,3},{8,4},{9,5},{1... | collective-permute-start | bytes 2752520 | tf_op jit(solution)/shard_map/ppermute | solution.py:42
  65.7 27.1 %slice-start = ((s8[8388608]{0:T(1024)(128)(4,1)}), s8[4194304]{0:T(1024)(128)(4,1)S(1)}, s32[]{:S(2)}) async-start(s8[8388608]{0:T(1024)(128)(4,1)} %bitcast.6), calls=%async_computation | async-start | bytes 8388608
  69.4 18.7 %collective-permute-start.16 = (bf16[64,7168]{1,0:T(8,128)(2,1)S(1)}, bf16[64,7168]{1,0:T(8,128)(2,1)S(1)}, u32[]{:S(2)}, u32[]{:S(2)}) collective-permute-start(bf16[64,7168]{1,0:T(8,128)(2,1)S(1)} %get-tuple-element.59), channel_id=1, source_target_pairs={{0,4},{1,5},{2,6},{3,7},{4,8},{5,9},{6,10},{7,11},{8,12},{9,13},{1... | collective-permute-start | bytes 2752520 | tf_op jit(solution)/shard_map/ppermute | solution.py:42
  70.4 17.7 %collective-permute-start.17 = (bf16[64,7168]{1,0:T(8,128)(2,1)S(1)}, bf16[64,7168]{1,0:T(8,128)(2,1)S(1)}, u32[]{:S(2)}, u32[]{:S(2)}) collective-permute-start(bf16[64,7168]{1,0:T(8,128)(2,1)S(1)} %get-tuple-element.60), channel_id=1, source_target_pairs={{0,12},{1,13},{2,14},{3,15},{4,0},{5,1},{6,2},{7,3},{8,4},{9,5},{1... | collective-permute-start | bytes 2752520 | tf_op jit(solution)/shard_map/ppermute | solution.py:42
  75.9 3.4 %copy-start = (bf16[2,4096,512]{2,1,0:T(8,128)(2,1)S(1)}, bf16[2,4096,512]{2,1,0:T(8,128)(2,1)}, u32[]{:S(2)}) copy-start(bf16[2,4096,512]{2,1,0:T(8,128)(2,1)} %latent_ref.3) | copy-start | bytes 25165828
  79.3 13.6 %slice-start.1 = ((s8[8388608]{0:T(1024)(128)(4,1)}), s8[4194304]{0:T(1024)(128)(4,1)S(1)}, s32[]{:S(2)}) async-start(s8[8388608]{0:T(1024)(128)(4,1)} %bitcast.6), calls=%async_computation.1 | async-start | bytes 8388608
  88.3 14.6 %collective-permute-start.19 = (bf16[64,7168]{1,0:T(8,128)(2,1)S(1)}, bf16[64,7168]{1,0:T(8,128)(2,1)S(1)}, u32[]{:S(2)}, u32[]{:S(2)}) collective-permute-start(bf16[64,7168]{1,0:T(8,128)(2,1)S(1)} %add_convert_fusion), channel_id=1, source_target_pairs={{0,12},{1,13},{2,14},{3,15},{4,0},{5,1},{6,2},{7,3},{8,4},{9,5},{1... | collective-permute-start | bytes 2752520 | tf_op jit(solution)/shard_map/ppermute | solution.py:42
  92.0 14.9 %collective-permute-start.18 = (bf16[64,7168]{1,0:T(8,128)(2,1)S(1)}, bf16[64,7168]{1,0:T(8,128)(2,1)S(1)}, u32[]{:S(2)}, u32[]{:S(2)}) collective-permute-start(bf16[64,7168]{1,0:T(8,128)(2,1)S(1)} %add_convert_fusion.1), channel_id=1, source_target_pairs={{0,4},{1,5},{2,6},{3,7},{4,8},{5,9},{6,10},{7,11},{8,12},{9,13},{1... | collective-permute-start | bytes 2752520 | tf_op jit(solution)/shard_map/ppermute | solution.py:42
  107.6 9.8 %collective-permute-start.20 = (bf16[32,7168]{1,0:T(8,128)(2,1)S(1)}, bf16[32,7168]{1,0:T(8,128)(2,1)S(1)}, u32[]{:S(2)}, u32[]{:S(2)}) collective-permute-start(bf16[32,7168]{1,0:T(8,128)(2,1)S(1)} %pad_maximum_fusion.1), channel_id=1, source_target_pairs={{0,1},{1,2},{2,3},{3,0},{4,5},{5,6},{6,7},{7,4},{8,9},{9,10},{10,1... | collective-permute-start | bytes 1376264 | tf_op jit(solution)/shard_map/ppermute | solution.py:42
  109.0 8.5 %collective-permute-start.21 = (bf16[32,7168]{1,0:T(8,128)(2,1)S(1)}, bf16[32,7168]{1,0:T(8,128)(2,1)S(1)}, u32[]{:S(2)}, u32[]{:S(2)}) collective-permute-start(bf16[32,7168]{1,0:T(8,128)(2,1)S(1)} %concatenate.29), channel_id=1, source_target_pairs={{0,3},{1,0},{2,1},{3,2},{4,7},{5,4},{6,5},{7,6},{8,11},{9,8},{10,9... | collective-permute-start | bytes 1376264 | tf_op jit(solution)/shard_map/ppermute | solution.py:42
  117.6 7.3 %collective-permute-start.22 = (bf16[16,7168]{1,0:T(8,128)(2,1)S(1)}, bf16[16,7168]{1,0:T(8,128)(2,1)S(1)}, u32[]{:S(2)}, u32[]{:S(2)}) collective-permute-start(bf16[16,7168]{1,0:T(8,128)(2,1)S(1)} %fusion.2), channel_id=1, source_target_pairs={{0,1},{1,2},{2,3},{3,0},{4,5},{5,6},{6,7},{7,4},{8,9},{9,10},{10,1... | collective-permute-start | bytes 688136 | tf_op jit(solution)/shard_map/ppermute | solution.py:42
  119.1 6.0 %collective-permute-start.23 = (bf16[16,7168]{1,0:T(8,128)(2,1)S(1)}, bf16[16,7168]{1,0:T(8,128)(2,1)S(1)}, u32[]{:S(2)}, u32[]{:S(2)}) collective-permute-start(bf16[16,7168]{1,0:T(8,128)(2,1)S(1)} %fusion.1), channel_id=1, source_target_pairs={{0,3},{1,0},{2,1},{3,2},{4,7},{5,4},{6,5},{7,6},{8,11},{9,8},{10,9... | collective-permute-start | bytes 688136 | tf_op jit(solution)/shard_map/ppermute | solution.py:42
  125.3 7.3 %collective-permute-start.24 = (bf16[8,7168]{1,0:T(8,128)(2,1)S(1)}, bf16[8,7168]{1,0:T(8,128)(2,1)S(1)}, u32[]{:S(2)}, u32[]{:S(2)}) collective-permute-start(bf16[8,7168]{1,0:T(8,128)(2,1)S(1)} %get-tuple-element.78), channel_id=1, source_target_pairs={{0,32},{1,33},{2,34},{3,35},{4,36},{5,37},{6,38},{7,39},{8,40},{9,... | collective-permute-start | bytes 344072 | tf_op jit(solution)/shard_map/ppermute | solution.py:42
  125.4 7.2 %collective-permute-start.25 = (bf16[8,7168]{1,0:T(8,128)(2,1)S(1)}, bf16[8,7168]{1,0:T(8,128)(2,1)S(1)}, u32[]{:S(2)}, u32[]{:S(2)}) collective-permute-start(bf16[8,7168]{1,0:T(8,128)(2,1)S(1)} %get-tuple-element.80), channel_id=1, source_target_pairs={{0,64},{1,65},{2,66},{3,67},{4,68},{5,69},{6,70},{7,71},{8,72},{9,... | collective-permute-start | bytes 344072 | tf_op jit(solution)/shard_map/ppermute | solution.py:42
  126.5 7.0 %collective-permute-start.26 = (bf16[8,7168]{1,0:T(8,128)(2,1)S(1)}, bf16[8,7168]{1,0:T(8,128)(2,1)S(1)}, u32[]{:S(2)}, u32[]{:S(2)}) collective-permute-start(bf16[8,7168]{1,0:T(8,128)(2,1)S(1)} %get-tuple-element.79), channel_id=1, source_target_pairs={{0,96},{1,97},{2,98},{3,99},{4,100},{5,101},{6,102},{7,103},{8,104... | collective-permute-start | bytes 344072 | tf_op jit(solution)/shard_map/ppermute | solution.py:42

commit v4 on v3

--- a/solution.py
+++ b/solution.py
@@ -308,6 +308,7 @@
     small, own_weights = lax.optimization_barrier((small, own_weights))
     weights = (own_weights, with_other_core(own_weights))
     rope_keys, new_rope_keys = jnp.swapaxes(rope_cache, 1, 2), new_rope.T
+    latent_cache = pltpu.with_memory_space_constraint(latent_cache, pltpu.HBM)
 
     def attention(sequence, length):
         return attend(
@@ -315,14 +316,15 @@
         )
 
     above, below = shift(small, 1, -1), shift(small, 1, 1)
-    half = small.shape[0] // 2
     own_low = jnp.concatenate([small, above], axis=0)
     below_low, above_low = shift(own_low, 2, 1), shift(own_low, 2, -1)
-    far_low, far_high = lax.optimization_barrier((below[:half], above[half:]))
-    far_low, far_high = shift(far_low, 1, 1), shift(far_high, 1, -1)
-    own_high = jnp.concatenate([far_low, far_high, below], axis=0)
+    own_high = jnp.concatenate([shift(below, 1, 1), below], axis=0)
     below_high, above_high = shift(own_high, 2, 1), shift(own_high, 2, -1)
-    own_low, own_high, below_low, above_low = lax.optimization_barrier((own_low, own_high, below_low, above_low))
+    own_high, lengths = lax.optimization_barrier((own_high, lengths))
+    first_attention = attention(0, lengths[:1])
+    own_low, own_high, below_low, above_low, first_attention = lax.optimization_barrier(
+        (own_low, own_high, below_low, above_low, first_attention)
+    )
     own_terms = expert_terms([own_low, own_high], weights)
     below_low, above_high, own_terms = lax.optimization_barrier((below_low, above_high, own_terms))
     far_low, far_high = shift(below_low, 2, 1), shift(above_high, 2, -1)
@@ -334,14 +336,10 @@
     far_terms = expert_terms([far_low, far_high], weights)
     from_below, from_above = shift(far_terms[0], 2, 1), shift(far_terms[1], 2, -1)
     far_terms, near_high, near_low, lengths = lax.optimization_barrier((far_terms, near_high, near_low, lengths))
-    first_attention = attention(0, lengths[:1])
-    from_below, from_above, first_attention, lengths = lax.optimization_barrier(
-        (from_below, from_above, first_attention, lengths)
-    )
+    second_attention = attention(1, lengths[1:])
+    from_below, from_above, second_attention = lax.optimization_barrier((from_below, from_above, second_attention))
     from_below = shift(narrowed(added(above_low, from_below)), 2, 1)
     from_above = shift(narrowed(added(below_high, from_above)), 2, -1)
-    second_attention = attention(1, lengths[1:])
-    from_below, from_above, second_attention = lax.optimization_barrier((from_below, from_above, second_attention))
     low = added(own_terms[0], near_low, from_below)
     high = added(own_terms[1], near_high, from_above)
 

time: 134 us -> 135 us (level)
  waiting for transfers between devices: 46.3 us -> 52.4 us
  local copies, waits for them, and re-layouts: 4.29 us -> 0.87 us
  starting transfers between devices: 41.2 us -> 39.5 us
    ppermute x26 -> x25, waiting for transfers between devices: 46.3 us -> 52.4 us  [shift(): return lax.ppermute(value, AXES, pairs)]
    unnamed x25 -> x18, local copies, waits for them, and re-layouts: 3.5 us -> 0.11 us
    ppermute x26 -> x25, starting transfers between devices: 41.1 us -> 39.4 us  [shift(): return lax.ppermute(value, AXES, pairs)]
  transfers between devices with their start and end apart: 27 -> 26, of which waited for: 18 -> 13; matrix products, arithmetic and copies ran while one was open for 1% -> 2% of each run, Pallas kernels for 28% -> 28%
where the time goes in v4:
time: 135 us
  waiting for transfers between devices  52.4 us (39%)
  starting transfers between devices  39.5 us (29%)
  Pallas kernels  38.6 us (29%)
  other arithmetic  2.92 us (2%)
    ppermute x25, waiting for transfers between devices, shift(): return lax.ppermute(value, AXES, pairs)  52.4 us
    ppermute x25, starting transfers between devices, shift(): return lax.ppermute(value, AXES, pairs)  39.4 us
    pallas_call x2, Pallas kernels, attend(): pl.pallas_call(functools.partial(attention_kernel, sequence), grid_spec=p...  18.9 us
    pallas_call x3, Pallas kernels, expert_terms(): pl.pallas_call(functools.partial(expert_kernel, sources=len(pieces), outp...  14.3 us
    pallas_call x1, Pallas kernels, joined(): pl.pallas_call(join_kernel, in_specs=[pl.BlockSpec(memory_space=pl.ANY)]...  4.23 us
  transfers between devices with their start and end apart: 26, of which 13 were waited for; matrix products, arithmetic and copies ran while one was open for 2% of the time, Pallas kernels for 28%

profile of v4, /device:TPU:0, one launch (start us, length us, event | category | flops | bytes accessed | tf_op | source)
XLA Modules:
  0.0 135.3 jit_solution(7828049603786269074)
XLA Ops:
  0.6 1.1 pack.1
  1.7 4.2 %collective-permute-start = (bf16[8,7296]{1,0:T(8,128)(2,1)S(1)}, bf16[8,7296]{1,0:T(8,128)(2,1)S(1)}, u32[]{:S(2)}, u32[]{:S(2)}) collective-permute-start(bf16[8,7296]{1,0:T(8,128)(2,1)S(1)} %pack.1), channel_id=1, source_target_pairs={{0,96},{1,97},{2,98},{3,99},{4,100},{5,101},{6,102},{7,103},{8,104... | collective-permute-start | bytes 350216 | tf_op jit(solution)/shard_map/ppermute | solution.py:42
  5.9 0.0 collective-permute-start.1
  5.9 1.3 collective-permute-start.2
  7.2 4.2 %join.1.refs_2_.refs_4_ = bf16[10752,512]{1,0:T(8,128)(2,1)S(1)} custom-call(bf16[7168,256]{1,0:T(8,128)(2,1)} %bitcast.11, bf16[7168,256]{1,0:T(8,128)(2,1)} %bitcast.12, bf16[256,7168]{1,0:T(8,128)(2,1)} %bitcast.13), custom_call_target="tpu_custom_call" | custom-call | bytes 22020096 | tf_op jit(solution)/shard_map/join/pallas_call | solution.py:141
  11.4 0.9 collective-permute-done.1
  12.4 0.9 collective-permute-done.2
  13.2 0.1 pad_maximum_fusion
  13.3 0.0 copy-start.1
  13.3 0.0 copy-start.2
  13.3 0.0 copy-start.3
  13.3 0.0 copy-start.4
  13.3 0.0 copy-start.5
  13.3 0.0 copy-start.6
  13.3 0.0 copy-start.7
  13.4 0.1 collective-permute-start.9
  13.4 1.6 %collective-permute-start.4 = (bf16[32,7296]{1,0:T(8,128)(2,1)S(1)}, bf16[32,7296]{1,0:T(8,128)(2,1)S(1)}, u32[]{:S(2)}, u32[]{:S(2)}) collective-permute-start(bf16[32,7296]{1,0:T(8,128)(2,1)S(1)} %pad_maximum_fusion), channel_id=1, source_target_pairs={{0,1},{1,2},{2,3},{3,0},{4,5},{5,6},{6,7},{7,4},{8,9},{9,10},{10,1... | collective-permute-start | bytes 1400840 | tf_op jit(solution)/shard_map/ppermute | solution.py:42
  15.1 1.7 %collective-permute-start.3 = (bf16[32,7296]{1,0:T(8,128)(2,1)S(1)}, bf16[32,7296]{1,0:T(8,128)(2,1)S(1)}, u32[]{:S(2)}, u32[]{:S(2)}) collective-permute-start(bf16[32,7296]{1,0:T(8,128)(2,1)S(1)} %pad_maximum_fusion), channel_id=1, source_target_pairs={{0,3},{1,0},{2,1},{3,2},{4,7},{5,4},{6,5},{7,6},{8,11},{9,8},{10,9... | collective-permute-start | bytes 1400840 | tf_op jit(solution)/shard_map/ppermute | solution.py:42
  16.8 6.5 %collective-permute-done.4 = bf16[32,7296]{1,0:T(8,128)(2,1)S(1)} collective-permute-done((bf16[32,7296]{1,0:T(8,128)(2,1)S(1)}, bf16[32,7296]{1,0:T(8,128)(2,1)S(1)}, u32[]{:S(2)}, u32[]{:S(2)}) %collective-permute-start.4) | collective-permute-done | bytes 466976 | tf_op jit(solution)/shard_map/ppermute | solution.py:42
  23.3 0.4 collective-permute-start.5
  23.7 1.6 %collective-permute-start.6 = (bf16[64,7296]{1,0:T(8,128)(2,1)S(1)}, bf16[64,7296]{1,0:T(8,128)(2,1)S(1)}, u32[]{:S(2)}, u32[]{:S(2)}) collective-permute-start(bf16[64,7296]{1,0:T(8,128)(2,1)S(1)} %constant_dynamic-update-slice_fusion.refs_0_), channel_id=1, source_target_pairs={{0,4},{1,5},{2,6},{3,7},{4,8},{5,9},{6,10},{7,11},{8,12},{9,13},{1... | collective-permute-start | bytes 2801672 | tf_op jit(solution)/shard_map/ppermute | solution.py:42
  25.3 1.7 %collective-permute-start.7 = (bf16[64,7296]{1,0:T(8,128)(2,1)S(1)}, bf16[64,7296]{1,0:T(8,128)(2,1)S(1)}, u32[]{:S(2)}, u32[]{:S(2)}) collective-permute-start(bf16[64,7296]{1,0:T(8,128)(2,1)S(1)} %constant_dynamic-update-slice_fusion.refs_0_), channel_id=1, source_target_pairs={{0,12},{1,13},{2,14},{3,15},{4,0},{5,1},{6,2},{7,3},{8,4},{9,5},{1... | collective-permute-start | bytes 2801672 | tf_op jit(solution)/shard_map/ppermute | solution.py:42
  27.0 11.1 %collective-permute-done.5 = bf16[32,7296]{1,0:T(8,128)(2,1)S(1)} collective-permute-done((bf16[32,7296]{1,0:T(8,128)(2,1)S(1)}, bf16[32,7296]{1,0:T(8,128)(2,1)S(1)}, u32[]{:S(2)}, u32[]{:S(2)}) %collective-permute-start.5) | collective-permute-done | bytes 466976 | tf_op jit(solution)/shard_map/ppermute | solution.py:42
  38.2 2.8 %collective-permute-start.8 = (bf16[64,7296]{1,0:T(8,128)(2,1)S(1)}, bf16[64,7296]{1,0:T(8,128)(2,1)S(1)}, u32[]{:S(2)}, u32[]{:S(2)}) collective-permute-start(bf16[64,7296]{1,0:T(8,128)(2,1)S(1)} %constant_dynamic-update-slice_fusion.2.refs_1_), channel_id=1, source_target_pairs={{0,12},{1,13},{2,14},{3,15},{4,0},{5,1},{6,2},{7,3},{8,4},{9,5},{1... | collective-permute-start | bytes 2801672 | tf_op jit(solution)/shard_map/ppermute | solution.py:42
  41.1 10.0 %attend.2 = bf16[64,1024]{1,0:T(8,128)(2,1)S(1)} custom-call(s32[1]{0:T(128)S(1)} %bitcast.10, bf16[128,1024]{1,0:T(8,128)(2,1)S(1)} %copy-done.3, bf16[128,512]{1,0:T(8,128)(2,1)S(1)} %copy-done.4, bf16[8,128,512]{2,1,0:T(8,128)(2,1)S(1)} %copy-done, bf16[8,512,128]{2,1,0:T(8,128)(2,1)S(1)} %copy-done.1, bf16[2,4096,512]{2,1,0:T(8,128)(2,1)} %latent_ref.3, ...), custom_call_target="tpu_custom_call" | custom-call | flops 6000000000 | bytes 8000000 | tf_op jit(solution)/shard_map/attend/pallas_call | solution.py:253
  51.1 3.7 %expert.3 = (bf16[64,7168]{1,0:T(8,128)(2,1)S(1)}, bf16[64,7168]{1,0:T(8,128)(2,1)S(1)}) custom-call(bf16[64,7296]{1,0:T(8,128)(2,1)S(1)} %constant_dynamic-update-slice_fusion.refs_0_, bf16[64,7296]{1,0:T(8,128)(2,1)S(1)} %constant_dynamic-update-slice_fusion.2.refs_1_, bf16[10752,512]{1,0:T(8,128)(2,1)S(1)} %join.1.refs_2_.refs_4_, ...), custom_call_target="tpu_custom_call" | custom-call | flops 2818572288 | bytes 3670016 | tf_op jit(solution)/shard_map/expert/pallas_call | solution.py:103
  54.8 0.8 collective-permute-start.10
  55.6 2.7 %collective-permute-start.11 = (bf16[64,7296]{1,0:T(8,128)(2,1)S(1)}, bf16[64,7296]{1,0:T(8,128)(2,1)S(1)}, u32[]{:S(2)}, u32[]{:S(2)}) collective-permute-start(bf16[64,7296]{1,0:T(8,128)(2,1)S(1)} %collective-permute-done.8.refs_1_), channel_id=1, source_target_pairs={{0,12},{1,13},{2,14},{3,15},{4,0},{5,1},{6,2},{7,3},{8,4},{9,5},{1... | collective-permute-start | bytes 2801672 | tf_op jit(solution)/shard_map/ppermute | solution.py:42
  58.3 7.0 %expert.4 = (bf16[64,7168]{1,0:T(8,128)(2,1)S(1)}, bf16[64,7168]{1,0:T(8,128)(2,1)S(1)}, bf16[64,7168]{1,0:T(8,128)(2,1)S(1)}, bf16[64,7168]{1,0:T(8,128)(2,1)S(1)}) custom-call(bf16[64,7296]{1,0:T(8,128)(2,1)S(1)} %collective-permute-done.7.refs_0_, bf16[64,7296]{1,0:T(8,128)(2,1)S(1)} %collective-permute-done.8.refs_1_, ...), custom_call_target="tpu_custom_call" | custom-call | flops 5637144576 | bytes 7340032 | tf_op jit(solution)/shard_map/expert/pallas_call | solution.py:103
  65.3 0.1 collective-permute-start.13
  65.4 3.2 %collective-permute-start.14 = (bf16[64,7168]{1,0:T(8,128)(2,1)S(1)}, bf16[64,7168]{1,0:T(8,128)(2,1)S(1)}, u32[]{:S(2)}, u32[]{:S(2)}) collective-permute-start(bf16[64,7168]{1,0:T(8,128)(2,1)S(1)} %get-tuple-element.53), channel_id=1, source_target_pairs={{0,12},{1,13},{2,14},{3,15},{4,0},{5,1},{6,2},{7,3},{8,4},{9,5},{1... | collective-permute-start | bytes 2752520 | tf_op jit(solution)/shard_map/ppermute | solution.py:42
  68.6 1.0 collective-permute-done.10.refs_0_
  69.6 3.7 %expert.5 = (bf16[64,7168]{1,0:T(8,128)(2,1)S(1)}, bf16[64,7168]{1,0:T(8,128)(2,1)S(1)}) custom-call(bf16[64,7296]{1,0:T(8,128)(2,1)S(1)} %collective-permute-done.10.refs_0_, bf16[64,7296]{1,0:T(8,128)(2,1)S(1)} %collective-permute-done.11.refs_1_, bf16[10752,512]{1,0:T(8,128)(2,1)S(1)} %join.1.refs_2_.refs_4_, ...), custom_call_target="tpu_custom_call" | custom-call | flops 2818572288 | bytes 3670016 | tf_op jit(solution)/shard_map/expert/pallas_call | solution.py:103
  73.3 1.5 %collective-permute-start.15 = (bf16[64,7168]{1,0:T(8,128)(2,1)S(1)}, bf16[64,7168]{1,0:T(8,128)(2,1)S(1)}, u32[]{:S(2)}, u32[]{:S(2)}) collective-permute-start(bf16[64,7168]{1,0:T(8,128)(2,1)S(1)} %get-tuple-element.56), channel_id=1, source_target_pairs={{0,4},{1,5},{2,6},{3,7},{4,8},{5,9},{6,10},{7,11},{8,12},{9,13},{1... | collective-permute-start | bytes 2752520 | tf_op jit(solution)/shard_map/ppermute | solution.py:42
  74.8 2.2 %collective-permute-start.16 = (bf16[64,7168]{1,0:T(8,128)(2,1)S(1)}, bf16[64,7168]{1,0:T(8,128)(2,1)S(1)}, u32[]{:S(2)}, u32[]{:S(2)}) collective-permute-start(bf16[64,7168]{1,0:T(8,128)(2,1)S(1)} %get-tuple-element.57), channel_id=1, source_target_pairs={{0,12},{1,13},{2,14},{3,15},{4,0},{5,1},{6,2},{7,3},{8,4},{9,5},{1... | collective-permute-start | bytes 2752520 | tf_op jit(solution)/shard_map/ppermute | solution.py:42
  77.0 3.0 %collective-permute-done.13 = bf16[64,7168]{1,0:T(8,128)(2,1)S(1)} collective-permute-done((bf16[64,7168]{1,0:T(8,128)(2,1)S(1)}, bf16[64,7168]{1,0:T(8,128)(2,1)S(1)}, u32[]{:S(2)}, u32[]{:S(2)}) %collective-permute-start.13) | collective-permute-done | bytes 917536 | tf_op jit(solution)/shard_map/ppermute | solution.py:42
  80.0 0.6 slice.61.length_ref
  80.6 8.9 %attend.3 = bf16[64,1024]{1,0:T(8,128)(2,1)S(1)} custom-call(s32[1]{0:T(128)} %slice.61.length_ref, bf16[128,1024]{1,0:T(8,128)(2,1)S(1)} %copy-done.3, bf16[128,512]{1,0:T(8,128)(2,1)S(1)} %copy-done.4, bf16[8,128,512]{2,1,0:T(8,128)(2,1)S(1)} %copy-done, bf16[8,512,128]{2,1,0:T(8,128)(2,1)S(1)} %copy-done.1, bf16[2,4096,512]{2,1,0:T(8,128)(2,1)} %latent_ref.3, ...), custom_call_target="tpu_custom_call" | custom-call | flops 6000000000 | bytes 8000000 | tf_op jit(solution)/shard_map/attend/pallas_call | solution.py:253
  89.5 0.3 collective-permute-done.15
  89.8 0.2 add_convert_fusion
  90.0 3.3 %collective-permute-start.18 = (bf16[64,7168]{1,0:T(8,128)(2,1)S(1)}, bf16[64,7168]{1,0:T(8,128)(2,1)S(1)}, u32[]{:S(2)}, u32[]{:S(2)}) collective-permute-start(bf16[64,7168]{1,0:T(8,128)(2,1)S(1)} %add_convert_fusion), channel_id=1, source_target_pairs={{0,12},{1,13},{2,14},{3,15},{4,0},{5,1},{6,2},{7,3},{8,4},{9,5},{1... | collective-permute-start | bytes 2752520 | tf_op jit(solution)/shard_map/ppermute | solution.py:42
  93.4 0.2 add_convert_fusion.1
  93.6 0.3 collective-permute-start.17
  93.9 10.4 %collective-permute-done.18 = bf16[64,7168]{1,0:T(8,128)(2,1)S(1)} collective-permute-done((bf16[64,7168]{1,0:T(8,128)(2,1)S(1)}, bf16[64,7168]{1,0:T(8,128)(2,1)S(1)}, u32[]{:S(2)}, u32[]{:S(2)}) %collective-permute-start.18) | collective-permute-done | bytes 917536 | tf_op jit(solution)/shard_map/ppermute | solution.py:42
  104.3 0.3 fusion.3
  104.6 3.8 %collective-permute-done.17 = bf16[64,7168]{1,0:T(8,128)(2,1)S(1)} collective-permute-done((bf16[64,7168]{1,0:T(8,128)(2,1)S(1)}, bf16[64,7168]{1,0:T(8,128)(2,1)S(1)}, u32[]{:S(2)}, u32[]{:S(2)}) %collective-permute-start.17) | collective-permute-done | bytes 917536 | tf_op jit(solution)/shard_map/ppermute | solution.py:42
  108.5 0.3 convert_add_fusion.1
  108.8 0.1 collective-permute-start.19
  109.0 3.3 %collective-permute-start.20 = (bf16[32,7168]{1,0:T(8,128)(2,1)S(1)}, bf16[32,7168]{1,0:T(8,128)(2,1)S(1)}, u32[]{:S(2)}, u32[]{:S(2)}) collective-permute-start(bf16[32,7168]{1,0:T(8,128)(2,1)S(1)} %concatenate.29), channel_id=1, source_target_pairs={{0,3},{1,0},{2,1},{3,2},{4,7},{5,4},{6,5},{7,6},{8,11},{9,8},{10,9... | collective-permute-start | bytes 1376264 | tf_op jit(solution)/shard_map/ppermute | solution.py:42
  112.2 6.3 %collective-permute-done.19 = bf16[32,7168]{1,0:T(8,128)(2,1)S(1)} collective-permute-done((bf16[32,7168]{1,0:T(8,128)(2,1)S(1)}, bf16[32,7168]{1,0:T(8,128)(2,1)S(1)}, u32[]{:S(2)}, u32[]{:S(2)}) %collective-permute-start.19) | collective-permute-done | bytes 458784 | tf_op jit(solution)/shard_map/ppermute | solution.py:42
  118.6 0.1 fusion.2
  118.7 0.1 fusion.1
  118.7 0.1 collective-permute-start.21
  118.8 3.3 %collective-permute-start.22 = (bf16[16,7168]{1,0:T(8,128)(2,1)S(1)}, bf16[16,7168]{1,0:T(8,128)(2,1)S(1)}, u32[]{:S(2)}, u32[]{:S(2)}) collective-permute-start(bf16[16,7168]{1,0:T(8,128)(2,1)S(1)} %fusion.1), channel_id=1, source_target_pairs={{0,3},{1,0},{2,1},{3,2},{4,7},{5,4},{6,5},{7,6},{8,11},{9,8},{10,9... | collective-permute-start | bytes 688136 | tf_op jit(solution)/shard_map/ppermute | solution.py:42
  122.1 3.9 %collective-permute-done.21 = bf16[16,7168]{1,0:T(8,128)(2,1)S(1)} collective-permute-done((bf16[16,7168]{1,0:T(8,128)(2,1)S(1)}, bf16[16,7168]{1,0:T(8,128)(2,1)S(1)}, u32[]{:S(2)}, u32[]{:S(2)}) %collective-permute-start.21) | collective-permute-done | bytes 229408 | tf_op jit(solution)/shard_map/ppermute | solution.py:42
  126.1 0.1 convert_add_fusion.3
  126.2 0.1 fusion
  126.4 0.1 collective-permute-start.23
  126.4 1.2 collective-permute-start.24
  127.7 2.0 %collective-permute-start.25 = (bf16[8,7168]{1,0:T(8,128)(2,1)S(1)}, bf16[8,7168]{1,0:T(8,128)(2,1)S(1)}, u32[]{:S(2)}, u32[]{:S(2)}) collective-permute-start(bf16[8,7168]{1,0:T(8,128)(2,1)S(1)} %get-tuple-element.73), channel_id=1, source_target_pairs={{0,96},{1,97},{2,98},{3,99},{4,100},{5,101},{6,102},{7,103},{8,104... | collective-permute-start | bytes 344072 | tf_op jit(solution)/shard_map/ppermute | solution.py:42
  129.7 0.7 pad_maximum_fusion.2
  130.4 3.3 %collective-permute-done.23 = bf16[8,7168]{1,0:T(8,128)(2,1)S(1)} collective-permute-done((bf16[8,7168]{1,0:T(8,128)(2,1)S(1)}, bf16[8,7168]{1,0:T(8,128)(2,1)S(1)}, u32[]{:S(2)}, u32[]{:S(2)}) %collective-permute-start.23) | collective-permute-done | bytes 114720 | tf_op jit(solution)/shard_map/ppermute | solution.py:42
  133.7 0.9 collective-permute-done.25
  134.6 0.7 add_convert_fusion.2
  (33 shorter events, 0.4 us)
Async XLA Ops:
  1.7 9.7 %collective-permute-start = (bf16[8,7296]{1,0:T(8,128)(2,1)S(1)}, bf16[8,7296]{1,0:T(8,128)(2,1)S(1)}, u32[]{:S(2)}, u32[]{:S(2)}) collective-permute-start(bf16[8,7296]{1,0:T(8,128)(2,1)S(1)} %pack.1), channel_id=1, source_target_pairs={{0,96},{1,97},{2,98},{3,99},{4,100},{5,101},{6,102},{7,103},{8,104... | collective-permute-start | bytes 350216 | tf_op jit(solution)/shard_map/ppermute | solution.py:42
  5.9 6.4 %collective-permute-start.1 = (bf16[8,7296]{1,0:T(8,128)(2,1)S(1)}, bf16[8,7296]{1,0:T(8,128)(2,1)S(1)}, u32[]{:S(2)}, u32[]{:S(2)}) collective-permute-start(bf16[8,7296]{1,0:T(8,128)(2,1)S(1)} %pack.1), channel_id=1, source_target_pairs={{0,64},{1,65},{2,66},{3,67},{4,68},{5,69},{6,70},{7,71},{8,72},{9,... | collective-permute-start | bytes 350216 | tf_op jit(solution)/shard_map/ppermute | solution.py:42
  5.9 7.3 %collective-permute-start.2 = (bf16[8,7296]{1,0:T(8,128)(2,1)S(1)}, bf16[8,7296]{1,0:T(8,128)(2,1)S(1)}, u32[]{:S(2)}, u32[]{:S(2)}) collective-permute-start(bf16[8,7296]{1,0:T(8,128)(2,1)S(1)} %pack.1), channel_id=1, source_target_pairs={{0,32},{1,33},{2,34},{3,35},{4,36},{5,37},{6,38},{7,39},{8,40},{9,... | collective-permute-start | bytes 350216 | tf_op jit(solution)/shard_map/ppermute | solution.py:42
  13.3 27.8 %copy-start = (bf16[8,128,512]{2,1,0:T(8,128)(2,1)S(1)}, bf16[8,128,512]{2,1,0:T(8,128)(2,1)}, u32[]{:S(2)}) copy-start(bf16[8,128,512]{2,1,0:T(8,128)(2,1)} %key_up_ref.3) | copy-start | bytes 3145732
  13.3 27.7 %copy-start.1 = (bf16[8,512,128]{2,1,0:T(8,128)(2,1)S(1)}, bf16[8,512,128]{2,1,0:T(8,128)(2,1)}, u32[]{:S(2)}) copy-start(bf16[8,512,128]{2,1,0:T(8,128)(2,1)} %value_up_ref.3) | copy-start | bytes 3145732
  13.3 27.7 %copy-start.2 = (bf16[2,4096,64]{1,2,0:T(8,128)(2,1)S(1)}, bf16[2,4096,64]{1,2,0:T(8,128)(2,1)}, u32[]{:S(2)}) copy-start(bf16[2,4096,64]{1,2,0:T(8,128)(2,1)} %param.26) | copy-start | bytes 3145732
  13.3 27.7 %copy-start.3 = (bf16[128,1024]{1,0:T(8,128)(2,1)S(1)}, bf16[128,1024]{1,0:T(8,128)(2,1)}, u32[]{:S(2)}) copy-start(bf16[128,1024]{1,0:T(8,128)(2,1)} %nope_ref.3) | copy-start | bytes 786436
  13.3 27.7 %copy-start.4 = (bf16[128,512]{1,0:T(8,128)(2,1)S(1)}, bf16[128,512]{1,0:T(8,128)(2,1)}, u32[]{:S(2)}) copy-start(bf16[128,512]{1,0:T(8,128)(2,1)} %rope_ref.3) | copy-start | bytes 393220
  13.3 27.7 %copy-start.5 = (bf16[128,512]{1,0:T(8,128)(2,1)S(1)}, bf16[128,512]{1,0:T(8,128)(2,1)}, u32[]{:S(2)}) copy-start(bf16[128,512]{1,0:T(8,128)(2,1)} %new_latent_ref.3) | copy-start | bytes 393220
  13.3 27.7 %copy-start.6 = (bf16[128,64]{0,1:T(8,128)(2,1)S(1)}, bf16[128,64]{0,1:T(8,128)(2,1)}, u32[]{:S(2)}) copy-start(bf16[128,64]{0,1:T(8,128)(2,1)} %param.28) | copy-start | bytes 49156
  13.3 27.7 %copy-start.7 = (s32[2]{0:T(128)S(1)}, s32[2]{0:T(128)}, u32[]{:S(2)}) copy-start(s32[2]{0:T(128)} %param.29) | copy-start | bytes 28
  13.4 37.7 %collective-permute-start.9 = (bf16[10752,512]{1,0:T(8,128)(2,1)S(1)}, bf16[10752,512]{1,0:T(8,128)(2,1)S(1)}, u32[]{:S(2)}, u32[]{:S(2)}) collective-permute-start(bf16[10752,512]{1,0:T(8,128)(2,1)S(1)} %join.1.refs_2_.refs_4_), channel_id=1, source_target_pairs={{0,16},{16,0},{1,17},{17,1},{2,18},{18,2},{3,19},{19,3},{4,20},{20... | collective-permute-start | bytes 33030152 | tf_op jit(solution)/shard_map/ppermute | solution.py:58
  13.4 9.8 %collective-permute-start.4 = (bf16[32,7296]{1,0:T(8,128)(2,1)S(1)}, bf16[32,7296]{1,0:T(8,128)(2,1)S(1)}, u32[]{:S(2)}, u32[]{:S(2)}) collective-permute-start(bf16[32,7296]{1,0:T(8,128)(2,1)S(1)} %pad_maximum_fusion), channel_id=1, source_target_pairs={{0,1},{1,2},{2,3},{3,0},{4,5},{5,6},{6,7},{7,4},{8,9},{9,10},{10,1... | collective-permute-start | bytes 1400840 | tf_op jit(solution)/shard_map/ppermute | solution.py:42
  15.1 8.6 %collective-permute-start.3 = (bf16[32,7296]{1,0:T(8,128)(2,1)S(1)}, bf16[32,7296]{1,0:T(8,128)(2,1)S(1)}, u32[]{:S(2)}, u32[]{:S(2)}) collective-permute-start(bf16[32,7296]{1,0:T(8,128)(2,1)S(1)} %pad_maximum_fusion), channel_id=1, source_target_pairs={{0,3},{1,0},{2,1},{3,2},{4,7},{5,4},{6,5},{7,6},{8,11},{9,8},{10,9... | collective-permute-start | bytes 1400840 | tf_op jit(solution)/shard_map/ppermute | solution.py:42
  23.3 14.8 %collective-permute-start.5 = (bf16[32,7296]{1,0:T(8,128)(2,1)S(1)}, bf16[32,7296]{1,0:T(8,128)(2,1)S(1)}, u32[]{:S(2)}, u32[]{:S(2)}) collective-permute-start(bf16[32,7296]{1,0:T(8,128)(2,1)S(1)} %collective-permute-done.4), channel_id=1, source_target_pairs={{0,1},{1,2},{2,3},{3,0},{4,5},{5,6},{6,7},{7,4},{8,9},{9,10},{10,1... | collective-permute-start | bytes 1400840 | tf_op jit(solution)/shard_map/ppermute | solution.py:42
  23.7 27.4 %collective-permute-start.6 = (bf16[64,7296]{1,0:T(8,128)(2,1)S(1)}, bf16[64,7296]{1,0:T(8,128)(2,1)S(1)}, u32[]{:S(2)}, u32[]{:S(2)}) collective-permute-start(bf16[64,7296]{1,0:T(8,128)(2,1)S(1)} %constant_dynamic-update-slice_fusion.refs_0_), channel_id=1, source_target_pairs={{0,4},{1,5},{2,6},{3,7},{4,8},{5,9},{6,10},{7,11},{8,12},{9,13},{1... | collective-permute-start | bytes 2801672 | tf_op jit(solution)/shard_map/ppermute | solution.py:42
  25.3 25.8 %collective-permute-start.7 = (bf16[64,7296]{1,0:T(8,128)(2,1)S(1)}, bf16[64,7296]{1,0:T(8,128)(2,1)S(1)}, u32[]{:S(2)}, u32[]{:S(2)}) collective-permute-start(bf16[64,7296]{1,0:T(8,128)(2,1)S(1)} %constant_dynamic-update-slice_fusion.refs_0_), channel_id=1, source_target_pairs={{0,12},{1,13},{2,14},{3,15},{4,0},{5,1},{6,2},{7,3},{8,4},{9,5},{1... | collective-permute-start | bytes 2801672 | tf_op jit(solution)/shard_map/ppermute | solution.py:42
  38.2 16.6 %collective-permute-start.8 = (bf16[64,7296]{1,0:T(8,128)(2,1)S(1)}, bf16[64,7296]{1,0:T(8,128)(2,1)S(1)}, u32[]{:S(2)}, u32[]{:S(2)}) collective-permute-start(bf16[64,7296]{1,0:T(8,128)(2,1)S(1)} %constant_dynamic-update-slice_fusion.2.refs_1_), channel_id=1, source_target_pairs={{0,12},{1,13},{2,14},{3,15},{4,0},{5,1},{6,2},{7,3},{8,4},{9,5},{1... | collective-permute-start | bytes 2801672 | tf_op jit(solution)/shard_map/ppermute | solution.py:42
  41.0 17.3 %collective-permute-start.12 = (bf16[64,7296]{1,0:T(8,128)(2,1)S(1)}, bf16[64,7296]{1,0:T(8,128)(2,1)S(1)}, u32[]{:S(2)}, u32[]{:S(2)}) collective-permute-start(bf16[64,7296]{1,0:T(8,128)(2,1)S(1)} %constant_dynamic-update-slice_fusion.2.refs_1_), channel_id=1, source_target_pairs={{0,4},{1,5},{2,6},{3,7},{4,8},{5,9},{6,10},{7,11},{8,12},{9,13},{1... | collective-permute-start | bytes 2801672 | tf_op jit(solution)/shard_map/ppermute | solution.py:42
  54.8 14.8 %collective-permute-start.10 = (bf16[64,7296]{1,0:T(8,128)(2,1)S(1)}, bf16[64,7296]{1,0:T(8,128)(2,1)S(1)}, u32[]{:S(2)}, u32[]{:S(2)}) collective-permute-start(bf16[64,7296]{1,0:T(8,128)(2,1)S(1)} %collective-permute-done.6.refs_2_), channel_id=1, source_target_pairs={{0,4},{1,5},{2,6},{3,7},{4,8},{5,9},{6,10},{7,11},{8,12},{9,13},{1... | collective-permute-start | bytes 2801672 | tf_op jit(solution)/shard_map/ppermute | solution.py:42
  55.6 14.1 %collective-permute-start.11 = (bf16[64,7296]{1,0:T(8,128)(2,1)S(1)}, bf16[64,7296]{1,0:T(8,128)(2,1)S(1)}, u32[]{:S(2)}, u32[]{:S(2)}) collective-permute-start(bf16[64,7296]{1,0:T(8,128)(2,1)S(1)} %collective-permute-done.8.refs_1_), channel_id=1, source_target_pairs={{0,12},{1,13},{2,14},{3,15},{4,0},{5,1},{6,2},{7,3},{8,4},{9,5},{1... | collective-permute-start | bytes 2801672 | tf_op jit(solution)/shard_map/ppermute | solution.py:42
  65.3 14.7 %collective-permute-start.13 = (bf16[64,7168]{1,0:T(8,128)(2,1)S(1)}, bf16[64,7168]{1,0:T(8,128)(2,1)S(1)}, u32[]{:S(2)}, u32[]{:S(2)}) collective-permute-start(bf16[64,7168]{1,0:T(8,128)(2,1)S(1)} %get-tuple-element.52), channel_id=1, source_target_pairs={{0,4},{1,5},{2,6},{3,7},{4,8},{5,9},{6,10},{7,11},{8,12},{9,13},{1... | collective-permute-start | bytes 2752520 | tf_op jit(solution)/shard_map/ppermute | solution.py:42
  65.4 14.6 %collective-permute-start.14 = (bf16[64,7168]{1,0:T(8,128)(2,1)S(1)}, bf16[64,7168]{1,0:T(8,128)(2,1)S(1)}, u32[]{:S(2)}, u32[]{:S(2)}) collective-permute-start(bf16[64,7168]{1,0:T(8,128)(2,1)S(1)} %get-tuple-element.53), channel_id=1, source_target_pairs={{0,12},{1,13},{2,14},{3,15},{4,0},{5,1},{6,2},{7,3},{8,4},{9,5},{1... | collective-permute-start | bytes 2752520 | tf_op jit(solution)/shard_map/ppermute | solution.py:42
  73.3 16.5 %collective-permute-start.15 = (bf16[64,7168]{1,0:T(8,128)(2,1)S(1)}, bf16[64,7168]{1,0:T(8,128)(2,1)S(1)}, u32[]{:S(2)}, u32[]{:S(2)}) collective-permute-start(bf16[64,7168]{1,0:T(8,128)(2,1)S(1)} %get-tuple-element.56), channel_id=1, source_target_pairs={{0,4},{1,5},{2,6},{3,7},{4,8},{5,9},{6,10},{7,11},{8,12},{9,13},{1... | collective-permute-start | bytes 2752520 | tf_op jit(solution)/shard_map/ppermute | solution.py:42
  74.8 15.0 %collective-permute-start.16 = (bf16[64,7168]{1,0:T(8,128)(2,1)S(1)}, bf16[64,7168]{1,0:T(8,128)(2,1)S(1)}, u32[]{:S(2)}, u32[]{:S(2)}) collective-permute-start(bf16[64,7168]{1,0:T(8,128)(2,1)S(1)} %get-tuple-element.57), channel_id=1, source_target_pairs={{0,12},{1,13},{2,14},{3,15},{4,0},{5,1},{6,2},{7,3},{8,4},{9,5},{1... | collective-permute-start | bytes 2752520 | tf_op jit(solution)/shard_map/ppermute | solution.py:42
  90.0 14.2 %collective-permute-start.18 = (bf16[64,7168]{1,0:T(8,128)(2,1)S(1)}, bf16[64,7168]{1,0:T(8,128)(2,1)S(1)}, u32[]{:S(2)}, u32[]{:S(2)}) collective-permute-start(bf16[64,7168]{1,0:T(8,128)(2,1)S(1)} %add_convert_fusion), channel_id=1, source_target_pairs={{0,12},{1,13},{2,14},{3,15},{4,0},{5,1},{6,2},{7,3},{8,4},{9,5},{1... | collective-permute-start | bytes 2752520 | tf_op jit(solution)/shard_map/ppermute | solution.py:42
  93.6 14.9 %collective-permute-start.17 = (bf16[64,7168]{1,0:T(8,128)(2,1)S(1)}, bf16[64,7168]{1,0:T(8,128)(2,1)S(1)}, u32[]{:S(2)}, u32[]{:S(2)}) collective-permute-start(bf16[64,7168]{1,0:T(8,128)(2,1)S(1)} %add_convert_fusion.1), channel_id=1, source_target_pairs={{0,4},{1,5},{2,6},{3,7},{4,8},{5,9},{6,10},{7,11},{8,12},{9,13},{1... | collective-permute-start | bytes 2752520 | tf_op jit(solution)/shard_map/ppermute | solution.py:42
  108.8 9.8 %collective-permute-start.19 = (bf16[32,7168]{1,0:T(8,128)(2,1)S(1)}, bf16[32,7168]{1,0:T(8,128)(2,1)S(1)}, u32[]{:S(2)}, u32[]{:S(2)}) collective-permute-start(bf16[32,7168]{1,0:T(8,128)(2,1)S(1)} %pad_maximum_fusion.1), channel_id=1, source_target_pairs={{0,1},{1,2},{2,3},{3,0},{4,5},{5,6},{6,7},{7,4},{8,9},{9,10},{10,1... | collective-permute-start | bytes 1376264 | tf_op jit(solution)/shard_map/ppermute | solution.py:42
  109.0 9.7 %collective-permute-start.20 = (bf16[32,7168]{1,0:T(8,128)(2,1)S(1)}, bf16[32,7168]{1,0:T(8,128)(2,1)S(1)}, u32[]{:S(2)}, u32[]{:S(2)}) collective-permute-start(bf16[32,7168]{1,0:T(8,128)(2,1)S(1)} %concatenate.29), channel_id=1, source_target_pairs={{0,3},{1,0},{2,1},{3,2},{4,7},{5,4},{6,5},{7,6},{8,11},{9,8},{10,9... | collective-permute-start | bytes 1376264 | tf_op jit(solution)/shard_map/ppermute | solution.py:42
  118.7 7.3 %collective-permute-start.21 = (bf16[16,7168]{1,0:T(8,128)(2,1)S(1)}, bf16[16,7168]{1,0:T(8,128)(2,1)S(1)}, u32[]{:S(2)}, u32[]{:S(2)}) collective-permute-start(bf16[16,7168]{1,0:T(8,128)(2,1)S(1)} %fusion.2), channel_id=1, source_target_pairs={{0,1},{1,2},{2,3},{3,0},{4,5},{5,6},{6,7},{7,4},{8,9},{9,10},{10,1... | collective-permute-start | bytes 688136 | tf_op jit(solution)/shard_map/ppermute | solution.py:42
  118.8 7.3 %collective-permute-start.22 = (bf16[16,7168]{1,0:T(8,128)(2,1)S(1)}, bf16[16,7168]{1,0:T(8,128)(2,1)S(1)}, u32[]{:S(2)}, u32[]{:S(2)}) collective-permute-start(bf16[16,7168]{1,0:T(8,128)(2,1)S(1)} %fusion.1), channel_id=1, source_target_pairs={{0,3},{1,0},{2,1},{3,2},{4,7},{5,4},{6,5},{7,6},{8,11},{9,8},{10,9... | collective-permute-start | bytes 688136 | tf_op jit(solution)/shard_map/ppermute | solution.py:42
  126.4 7.3 %collective-permute-start.23 = (bf16[8,7168]{1,0:T(8,128)(2,1)S(1)}, bf16[8,7168]{1,0:T(8,128)(2,1)S(1)}, u32[]{:S(2)}, u32[]{:S(2)}) collective-permute-start(bf16[8,7168]{1,0:T(8,128)(2,1)S(1)} %get-tuple-element.72), channel_id=1, source_target_pairs={{0,32},{1,33},{2,34},{3,35},{4,36},{5,37},{6,38},{7,39},{8,40},{9,... | collective-permute-start | bytes 344072 | tf_op jit(solution)/shard_map/ppermute | solution.py:42
  126.4 7.2 %collective-permute-start.24 = (bf16[8,7168]{1,0:T(8,128)(2,1)S(1)}, bf16[8,7168]{1,0:T(8,128)(2,1)S(1)}, u32[]{:S(2)}, u32[]{:S(2)}) collective-permute-start(bf16[8,7168]{1,0:T(8,128)(2,1)S(1)} %get-tuple-element.74), channel_id=1, source_target_pairs={{0,64},{1,65},{2,66},{3,67},{4,68},{5,69},{6,70},{7,71},{8,72},{9,... | collective-permute-start | bytes 344072 | tf_op jit(solution)/shard_map/ppermute | solution.py:42
  127.7 6.9 %collective-permute-start.25 = (bf16[8,7168]{1,0:T(8,128)(2,1)S(1)}, bf16[8,7168]{1,0:T(8,128)(2,1)S(1)}, u32[]{:S(2)}, u32[]{:S(2)}) collective-permute-start(bf16[8,7168]{1,0:T(8,128)(2,1)S(1)} %get-tuple-element.73), channel_id=1, source_target_pairs={{0,96},{1,97},{2,98},{3,99},{4,100},{5,101},{6,102},{7,103},{8,104... | collective-permute-start | bytes 344072 | tf_op jit(solution)/shard_map/ppermute | solution.py:42

commit v5 on v4

--- a/solution.py
+++ b/solution.py
@@ -40,6 +40,16 @@
         target[axis] = (target[axis] + distance) % RING
         pairs.append((int(np.ravel_multi_index(place, SIZES)), int(np.ravel_multi_index(target, SIZES))))
     return lax.ppermute(value, AXES, pairs)
+
+
+def ring_exchange(value):
+    groups = []
+    for core in range(2):
+        axis = ORDERS[core][0]
+        for place in np.ndindex(*(1 if i in (1, axis) else size for i, size in enumerate(SIZES))):
+            members = [[core if i == 1 else step if i == axis else p for i, p in enumerate(place)] for step in range(RING)]
+            groups.append([int(np.ravel_multi_index(member, SIZES)) for member in members])
+    return lax.all_to_all(value, AXES, split_axis=0, concat_axis=0, axis_index_groups=groups, tiled=True)
 
 
 def widened(value):
@@ -150,6 +160,27 @@
     )(*matrices)
 
 
+def placed_sum_kernel(own_ref, up_ref, down_ref, above_ref, below_ref, out_ref):
+    first = jnp.where(lax.axis_index("core") == 0, lax.axis_index("z"), lax.axis_index("x"))
+    low = added(up_ref[...], above_ref[...])
+    high = added(down_ref[...], below_ref[...])
+    total = own_ref[...] + jnp.concatenate([low, high], axis=0)
+    rows = total.shape[0] // RING
+    total = narrowed(total)
+    for distance in range(RING):
+        place = lax.rem(first + distance, RING)
+        out_ref[pl.ds(pl.multiple_of(place * rows, rows), rows), :] = total[distance * rows : (distance + 1) * rows]
+
+
+def placed_sum(own, up, down, above, below):
+    return pl.pallas_call(
+        placed_sum_kernel,
+        out_shape=jax.ShapeDtypeStruct(own.shape, jnp.bfloat16),
+        compiler_params=pltpu.CompilerParams(vmem_limit_bytes=KERNEL_VMEM),
+        name="placed_sum",
+    )(own, up, down, above, below)
+
+
 def pack_kernel(tokens_ref, routes_ref, scores_ref, out_ref):
     rows, width = tokens_ref.shape
     out_ref[:, :width] = tokens_ref[...]
@@ -316,9 +347,12 @@
         )
 
     above, below = shift(small, 1, -1), shift(small, 1, 1)
+    half = small.shape[0] // 2
     own_low = jnp.concatenate([small, above], axis=0)
     below_low, above_low = shift(own_low, 2, 1), shift(own_low, 2, -1)
-    own_high = jnp.concatenate([shift(below, 1, 1), below], axis=0)
+    far_low, far_high = lax.optimization_barrier((below[:half], above[half:]))
+    far_low, far_high = shift(far_low, 1, 1), shift(far_high, 1, -1)
+    own_high = jnp.concatenate([far_low, far_high, below], axis=0)
     below_high, above_high = shift(own_high, 2, 1), shift(own_high, 2, -1)
     own_high, lengths = lax.optimization_barrier((own_high, lengths))
     first_attention = attention(0, lengths[:1])
@@ -353,14 +387,9 @@
     down_second = narrowed(added(below[half:], from_above[:half]))
     up_second, down_second = lax.optimization_barrier((up_second, down_second))
     up_second, down_second = shift(up_second, 1, 1), shift(down_second, 1, -1)
-    total = low[:size] + jnp.concatenate(
-        [added(up_second, from_above[half:]), added(down_second, from_below[half:])], axis=0
-    )
-
-    total = narrowed(total)
-    rows = tokens.shape[0]
-    arrived = [shift(total[distance * rows : (distance + 1) * rows], 0, distance) for distance in (1, 2, 3)]
-    routed_out = narrowed(added(total[:rows], *arrived))
+    total = placed_sum(low[:size], up_second, down_second, from_above[half:], from_below[half:])
+    arrived = ring_exchange(total).reshape(RING, -1, total.shape[1])
+    routed_out = narrowed(jnp.sum(widened(arrived), axis=0))
     return (routed_out, jnp.concatenate([first_attention, second_attention], axis=0))
 
 

time: 135 us -> 138 us (1.022)
  Pallas kernels: 38.6 us -> 41.1 us
  starting transfers between devices: 39.5 us -> 41.3 us
    ppermute x25 -> x23, waiting for transfers between devices: 52.4 us -> 44.6 us  [shift(): return lax.ppermute(value, AXES, pairs)]
    all_to_all x0 -> x1, waiting for transfers between devices: none -> 6.97 us  [ring_exchange(): lax.all_to_all(value, AXES, split_axis=0, concat_axis=0, axis_index_group...]
    all_to_all x0 -> x1, starting transfers between devices: none -> 3.46 us  [ring_exchange(): lax.all_to_all(value, AXES, split_axis=0, concat_axis=0, axis_index_group...]
    ppermute x25 -> x23, starting transfers between devices: 39.4 us -> 37.7 us  [shift(): return lax.ppermute(value, AXES, pairs)]
    pallas_call x2, Pallas kernels: 18.9 us -> 20.5 us  [attend(): pl.pallas_call(functools.partial(attention_kernel, sequence), grid_spec=p...]
  transfers between devices with their start and end apart: 26 -> 25, of which waited for: 13 -> 15; matrix products, arithmetic and copies ran while one was open for 2% -> 2% of each run, Pallas kernels for 28% -> 28%
where the time goes in v5:
time: 138 us; the launch traced here: 139 us
  waiting for transfers between devices  51.6 us (37%)
  starting transfers between devices  41.3 us (30%)
  Pallas kernels  41.1 us (30%)
  other arithmetic  2.72 us (2%)
    ppermute x23, waiting for transfers between devices, shift(): return lax.ppermute(value, AXES, pairs)  44.6 us
    ppermute x23, starting transfers between devices, shift(): return lax.ppermute(value, AXES, pairs)  37.7 us
    pallas_call x2, Pallas kernels, attend(): pl.pallas_call(functools.partial(attention_kernel, sequence), grid_spec=p...  20.5 us
    pallas_call x3, Pallas kernels, expert_terms(): pl.pallas_call(functools.partial(expert_kernel, sources=len(pieces), outp...  14.3 us
    all_to_all x1, waiting for transfers between devices, ring_exchange(): lax.all_to_all(value, AXES, split_axis=0, concat_axis=0, axis_index_group...  6.97 us
    pallas_call x1, Pallas kernels, joined(): pl.pallas_call(join_kernel, in_specs=[pl.BlockSpec(memory_space=pl.ANY)]...  4.23 us
    all_to_all x1, starting transfers between devices, ring_exchange(): lax.all_to_all(value, AXES, split_axis=0, concat_axis=0, axis_index_group...  3.46 us
  transfers between devices with their start and end apart: 25, of which 15 were waited for; matrix products, arithmetic and copies ran while one was open for 2% of the time, Pallas kernels for 28%

profile of v5, /device:TPU:0, one launch (start us, length us, event | category | flops | bytes accessed | tf_op | source)
XLA Modules:
  0.0 138.6 jit_solution(12081099411405211122)
XLA Ops:
  0.6 1.1 pack.1
  1.7 4.2 %collective-permute-start = (bf16[8,7296]{1,0:T(8,128)(2,1)S(1)}, bf16[8,7296]{1,0:T(8,128)(2,1)S(1)}, u32[]{:S(2)}, u32[]{:S(2)}) collective-permute-start(bf16[8,7296]{1,0:T(8,128)(2,1)S(1)} %pack.1), channel_id=1, source_target_pairs={{0,96},{1,97},{2,98},{3,99},{4,100},{5,101},{6,102},{7,103},{8,104... | collective-permute-start | bytes 350216 | tf_op jit(solution)/shard_map/ppermute | solution.py:42
  5.9 1.3 collective-permute-start.2
  7.2 4.2 %join.1.refs_2_.refs_4_ = bf16[10752,512]{1,0:T(8,128)(2,1)S(1)} custom-call(bf16[7168,256]{1,0:T(8,128)(2,1)} %bitcast.12, bf16[7168,256]{1,0:T(8,128)(2,1)} %bitcast.13, bf16[256,7168]{1,0:T(8,128)(2,1)} %bitcast.14), custom_call_target="tpu_custom_call" | custom-call | bytes 22020096 | tf_op jit(solution)/shard_map/join/pallas_call | solution.py:151
  11.4 0.9 collective-permute-done.1
  12.4 0.9 collective-permute-done.2
  13.2 0.1 pad_maximum_fusion
  13.3 0.1 collective-permute-start.10
  13.4 1.6 %collective-permute-start.4 = (bf16[32,7296]{1,0:T(8,128)(2,1)S(1)}, bf16[32,7296]{1,0:T(8,128)(2,1)S(1)}, u32[]{:S(2)}, u32[]{:S(2)}) collective-permute-start(bf16[32,7296]{1,0:T(8,128)(2,1)S(1)} %pad_maximum_fusion), channel_id=1, source_target_pairs={{0,1},{1,2},{2,3},{3,0},{4,5},{5,6},{6,7},{7,4},{8,9},{9,10},{10,1... | collective-permute-start | bytes 1400840 | tf_op jit(solution)/shard_map/ppermute | solution.py:42
  15.0 1.7 %collective-permute-start.3 = (bf16[32,7296]{1,0:T(8,128)(2,1)S(1)}, bf16[32,7296]{1,0:T(8,128)(2,1)S(1)}, u32[]{:S(2)}, u32[]{:S(2)}) collective-permute-start(bf16[32,7296]{1,0:T(8,128)(2,1)S(1)} %pad_maximum_fusion), channel_id=1, source_target_pairs={{0,3},{1,0},{2,1},{3,2},{4,7},{5,4},{6,5},{7,6},{8,11},{9,8},{10,9... | collective-permute-start | bytes 1400840 | tf_op jit(solution)/shard_map/ppermute | solution.py:42
  16.7 0.0 copy-start
  16.7 0.0 copy-start.1
  16.7 0.0 copy-start.2
  16.7 0.0 copy-start.3
  16.7 0.0 copy-start.4
  16.8 0.0 copy-start.5
  16.8 6.4 %collective-permute-done.4 = bf16[32,7296]{1,0:T(8,128)(2,1)S(1)} collective-permute-done((bf16[32,7296]{1,0:T(8,128)(2,1)S(1)}, bf16[32,7296]{1,0:T(8,128)(2,1)S(1)}, u32[]{:S(2)}, u32[]{:S(2)}) %collective-permute-start.4) | collective-permute-done | bytes 466976 | tf_op jit(solution)/shard_map/ppermute | solution.py:42
  23.2 0.3 collective-permute-done.3
  23.6 1.6 %collective-permute-start.5 = (bf16[16,7296]{1,0:T(8,128)(2,1)S(1)}, bf16[16,7296]{1,0:T(8,128)(2,1)S(1)}, u32[]{:S(2)}, u32[]{:S(2)}) collective-permute-start(bf16[16,7296]{1,0:T(8,128)(2,1)S(1)} %slice.67), channel_id=1, source_target_pairs={{0,1},{1,2},{2,3},{3,0},{4,5},{5,6},{6,7},{7,4},{8,9},{9,10},{10,1... | collective-permute-start | bytes 700424 | tf_op jit(solution)/shard_map/ppermute | solution.py:42
  25.3 1.6 %collective-permute-start.7 = (bf16[64,7296]{1,0:T(8,128)(2,1)S(1)}, bf16[64,7296]{1,0:T(8,128)(2,1)S(1)}, u32[]{:S(2)}, u32[]{:S(2)}) collective-permute-start(bf16[64,7296]{1,0:T(8,128)(2,1)S(1)} %constant_dynamic-update-slice_fusion.refs_0_), channel_id=1, source_target_pairs={{0,4},{1,5},{2,6},{3,7},{4,8},{5,9},{6,10},{7,11},{8,12},{9,13},{1... | collective-permute-start | bytes 2801672 | tf_op jit(solution)/shard_map/ppermute | solution.py:42
  26.8 1.7 %collective-permute-start.8 = (bf16[64,7296]{1,0:T(8,128)(2,1)S(1)}, bf16[64,7296]{1,0:T(8,128)(2,1)S(1)}, u32[]{:S(2)}, u32[]{:S(2)}) collective-permute-start(bf16[64,7296]{1,0:T(8,128)(2,1)S(1)} %constant_dynamic-update-slice_fusion.refs_0_), channel_id=1, source_target_pairs={{0,12},{1,13},{2,14},{3,15},{4,0},{5,1},{6,2},{7,3},{8,4},{9,5},{1... | collective-permute-start | bytes 2801672 | tf_op jit(solution)/shard_map/ppermute | solution.py:42
  28.6 1.7 %collective-permute-start.6 = (bf16[16,7296]{1,0:T(8,128)(2,1)S(1)}, bf16[16,7296]{1,0:T(8,128)(2,1)S(1)}, u32[]{:S(2)}, u32[]{:S(2)}) collective-permute-start(bf16[16,7296]{1,0:T(8,128)(2,1)S(1)} %slice.68), channel_id=1, source_target_pairs={{0,3},{1,0},{2,1},{3,2},{4,7},{5,4},{6,5},{7,6},{8,11},{9,8},{10,9... | collective-permute-start | bytes 700424 | tf_op jit(solution)/shard_map/ppermute | solution.py:42
  30.2 3.3 %collective-permute-done.5 = bf16[16,7296]{1,0:T(8,128)(2,1)S(1)} collective-permute-done((bf16[16,7296]{1,0:T(8,128)(2,1)S(1)}, bf16[16,7296]{1,0:T(8,128)(2,1)S(1)}, u32[]{:S(2)}, u32[]{:S(2)}) %collective-permute-start.5) | collective-permute-done | bytes 233504 | tf_op jit(solution)/shard_map/ppermute | solution.py:42
  33.5 3.7 %collective-permute-done.6 = bf16[16,7296]{1,0:T(8,128)(2,1)S(1)} collective-permute-done((bf16[16,7296]{1,0:T(8,128)(2,1)S(1)}, bf16[16,7296]{1,0:T(8,128)(2,1)S(1)}, u32[]{:S(2)}, u32[]{:S(2)}) %collective-permute-start.6) | collective-permute-done | bytes 233504 | tf_op jit(solution)/shard_map/ppermute | solution.py:42
  37.3 1.6 %collective-permute-start.9 = (bf16[64,7296]{1,0:T(8,128)(2,1)S(1)}, bf16[64,7296]{1,0:T(8,128)(2,1)S(1)}, u32[]{:S(2)}, u32[]{:S(2)}) collective-permute-start(bf16[64,7296]{1,0:T(8,128)(2,1)S(1)} %constant_dynamic-update-slice_fusion.2.refs_1_), channel_id=1, source_target_pairs={{0,12},{1,13},{2,14},{3,15},{4,0},{5,1},{6,2},{7,3},{8,4},{9,5},{1... | collective-permute-start | bytes 2801672 | tf_op jit(solution)/shard_map/ppermute | solution.py:42
  38.9 0.5 collective-permute-start.13
  39.4 10.0 %attend.2 = bf16[64,1024]{1,0:T(8,128)(2,1)S(1)} custom-call(s32[1]{0:T(128)S(1)} %bitcast.11, bf16[128,1024]{1,0:T(8,128)(2,1)S(1)} %copy-done.3, bf16[128,512]{1,0:T(8,128)(2,1)S(1)} %copy-done.4, bf16[8,128,512]{2,1,0:T(8,128)(2,1)S(1)} %copy-done, bf16[8,512,128]{2,1,0:T(8,128)(2,1)S(1)} %copy-done.1, bf16[2,4096,512]{2,1,0:T(8,128)(2,1)} %latent_ref.3, ...), custom_call_target="tpu_custom_call" | custom-call | flops 6000000000 | bytes 8000000 | tf_op jit(solution)/shard_map/attend/pallas_call | solution.py:284
  49.4 3.7 %expert.3 = (bf16[64,7168]{1,0:T(8,128)(2,1)S(1)}, bf16[64,7168]{1,0:T(8,128)(2,1)S(1)}) custom-call(bf16[64,7296]{1,0:T(8,128)(2,1)S(1)} %constant_dynamic-update-slice_fusion.refs_0_, bf16[64,7296]{1,0:T(8,128)(2,1)S(1)} %constant_dynamic-update-slice_fusion.2.refs_1_, bf16[10752,512]{1,0:T(8,128)(2,1)S(1)} %join.1.refs_2_.refs_4_, ...), custom_call_target="tpu_custom_call" | custom-call | flops 2818572288 | bytes 3670016 | tf_op jit(solution)/shard_map/expert/pallas_call | solution.py:113
  53.1 0.3 collective-permute-start.11
  53.5 3.0 %collective-permute-start.12 = (bf16[64,7296]{1,0:T(8,128)(2,1)S(1)}, bf16[64,7296]{1,0:T(8,128)(2,1)S(1)}, u32[]{:S(2)}, u32[]{:S(2)}) collective-permute-start(bf16[64,7296]{1,0:T(8,128)(2,1)S(1)} %collective-permute-done.9.refs_1_), channel_id=1, source_target_pairs={{0,12},{1,13},{2,14},{3,15},{4,0},{5,1},{6,2},{7,3},{8,4},{9,5},{1... | collective-permute-start | bytes 2801672 | tf_op jit(solution)/shard_map/ppermute | solution.py:42
  56.4 7.0 %expert.4 = (bf16[64,7168]{1,0:T(8,128)(2,1)S(1)}, bf16[64,7168]{1,0:T(8,128)(2,1)S(1)}, bf16[64,7168]{1,0:T(8,128)(2,1)S(1)}, bf16[64,7168]{1,0:T(8,128)(2,1)S(1)}) custom-call(bf16[64,7296]{1,0:T(8,128)(2,1)S(1)} %collective-permute-done.8.refs_0_, bf16[64,7296]{1,0:T(8,128)(2,1)S(1)} %collective-permute-done.9.refs_1_, ...), custom_call_target="tpu_custom_call" | custom-call | flops 5637144576 | bytes 7340032 | tf_op jit(solution)/shard_map/expert/pallas_call | solution.py:113
  63.4 0.1 collective-permute-start.14
  63.5 3.2 %collective-permute-start.15 = (bf16[64,7168]{1,0:T(8,128)(2,1)S(1)}, bf16[64,7168]{1,0:T(8,128)(2,1)S(1)}, u32[]{:S(2)}, u32[]{:S(2)}) collective-permute-start(bf16[64,7168]{1,0:T(8,128)(2,1)S(1)} %get-tuple-element.57), channel_id=1, source_target_pairs={{0,12},{1,13},{2,14},{3,15},{4,0},{5,1},{6,2},{7,3},{8,4},{9,5},{1... | collective-permute-start | bytes 2752520 | tf_op jit(solution)/shard_map/ppermute | solution.py:42
  66.7 1.3 collective-permute-done.11.refs_0_
  68.0 3.7 %expert.5 = (bf16[64,7168]{1,0:T(8,128)(2,1)S(1)}, bf16[64,7168]{1,0:T(8,128)(2,1)S(1)}) custom-call(bf16[64,7296]{1,0:T(8,128)(2,1)S(1)} %collective-permute-done.11.refs_0_, bf16[64,7296]{1,0:T(8,128)(2,1)S(1)} %collective-permute-done.12.refs_1_, bf16[10752,512]{1,0:T(8,128)(2,1)S(1)} %join.1.refs_2_.refs_4_, ...), custom_call_target="tpu_custom_call" | custom-call | flops 2818572288 | bytes 3670016 | tf_op jit(solution)/shard_map/expert/pallas_call | solution.py:113
  71.7 1.0 collective-permute-start.16
  72.7 2.4 %collective-permute-start.17 = (bf16[64,7168]{1,0:T(8,128)(2,1)S(1)}, bf16[64,7168]{1,0:T(8,128)(2,1)S(1)}, u32[]{:S(2)}, u32[]{:S(2)}) collective-permute-start(bf16[64,7168]{1,0:T(8,128)(2,1)S(1)} %get-tuple-element.61), channel_id=1, source_target_pairs={{0,12},{1,13},{2,14},{3,15},{4,0},{5,1},{6,2},{7,3},{8,4},{9,5},{1... | collective-permute-start | bytes 2752520 | tf_op jit(solution)/shard_map/ppermute | solution.py:42
  75.0 3.0 %collective-permute-done.14 = bf16[64,7168]{1,0:T(8,128)(2,1)S(1)} collective-permute-done((bf16[64,7168]{1,0:T(8,128)(2,1)S(1)}, bf16[64,7168]{1,0:T(8,128)(2,1)S(1)}, u32[]{:S(2)}, u32[]{:S(2)}) %collective-permute-start.14) | collective-permute-done | bytes 917536 | tf_op jit(solution)/shard_map/ppermute | solution.py:42
  78.1 0.6 slice.57.length_ref
  78.7 10.6 %attend.3 = bf16[64,1024]{1,0:T(8,128)(2,1)S(1)} custom-call(s32[1]{0:T(128)} %slice.57.length_ref, bf16[128,1024]{1,0:T(8,128)(2,1)S(1)} %copy-done.3, bf16[128,512]{1,0:T(8,128)(2,1)S(1)} %copy-done.4, bf16[8,128,512]{2,1,0:T(8,128)(2,1)S(1)} %copy-done, bf16[8,512,128]{2,1,0:T(8,128)(2,1)S(1)} %copy-done.1, bf16[2,4096,512]{2,1,0:T(8,128)(2,1)} %latent_ref.3, ...), custom_call_target="tpu_custom_call" | custom-call | flops 6000000000 | bytes 8000000 | tf_op jit(solution)/shard_map/attend/pallas_call | solution.py:284
  89.3 0.2 add_convert_fusion
  89.5 3.3 %collective-permute-start.19 = (bf16[64,7168]{1,0:T(8,128)(2,1)S(1)}, bf16[64,7168]{1,0:T(8,128)(2,1)S(1)}, u32[]{:S(2)}, u32[]{:S(2)}) collective-permute-start(bf16[64,7168]{1,0:T(8,128)(2,1)S(1)} %add_convert_fusion), channel_id=1, source_target_pairs={{0,12},{1,13},{2,14},{3,15},{4,0},{5,1},{6,2},{7,3},{8,4},{9,5},{1... | collective-permute-start | bytes 2752520 | tf_op jit(solution)/shard_map/ppermute | solution.py:42
  92.8 0.2 add_convert_fusion.1
  93.0 0.3 collective-permute-start.18
  93.3 10.4 %collective-permute-done.19 = bf16[64,7168]{1,0:T(8,128)(2,1)S(1)} collective-permute-done((bf16[64,7168]{1,0:T(8,128)(2,1)S(1)}, bf16[64,7168]{1,0:T(8,128)(2,1)S(1)}, u32[]{:S(2)}, u32[]{:S(2)}) %collective-permute-start.19) | collective-permute-done | bytes 917536 | tf_op jit(solution)/shard_map/ppermute | solution.py:42
  103.7 0.3 fusion.2
  104.1 3.8 %collective-permute-done.18 = bf16[64,7168]{1,0:T(8,128)(2,1)S(1)} collective-permute-done((bf16[64,7168]{1,0:T(8,128)(2,1)S(1)}, bf16[64,7168]{1,0:T(8,128)(2,1)S(1)}, u32[]{:S(2)}, u32[]{:S(2)}) %collective-permute-start.18) | collective-permute-done | bytes 917536 | tf_op jit(solution)/shard_map/ppermute | solution.py:42
  107.9 0.3 convert_add_fusion.1
  108.3 1.4 collective-permute-start.20
  109.7 2.0 %collective-permute-start.21 = (bf16[32,7168]{1,0:T(8,128)(2,1)S(1)}, bf16[32,7168]{1,0:T(8,128)(2,1)S(1)}, u32[]{:S(2)}, u32[]{:S(2)}) collective-permute-start(bf16[32,7168]{1,0:T(8,128)(2,1)S(1)} %concatenate.25), channel_id=1, source_target_pairs={{0,3},{1,0},{2,1},{3,2},{4,7},{5,4},{6,5},{7,6},{8,11},{9,8},{10,9... | collective-permute-start | bytes 1376264 | tf_op jit(solution)/shard_map/ppermute | solution.py:42
  111.7 6.3 %collective-permute-done.20 = bf16[32,7168]{1,0:T(8,128)(2,1)S(1)} collective-permute-done((bf16[32,7168]{1,0:T(8,128)(2,1)S(1)}, bf16[32,7168]{1,0:T(8,128)(2,1)S(1)}, u32[]{:S(2)}, u32[]{:S(2)}) %collective-permute-start.20) | collective-permute-done | bytes 458784 | tf_op jit(solution)/shard_map/ppermute | solution.py:42
  118.1 0.1 fusion.1
  118.1 0.1 collective-permute-done.21
  118.2 0.1 fusion
  118.3 1.5 %collective-permute-start.22 = (bf16[16,7168]{1,0:T(8,128)(2,1)S(1)}, bf16[16,7168]{1,0:T(8,128)(2,1)S(1)}, u32[]{:S(2)}, u32[]{:S(2)}) collective-permute-start(bf16[16,7168]{1,0:T(8,128)(2,1)S(1)} %fusion.1), channel_id=1, source_target_pairs={{0,1},{1,2},{2,3},{3,0},{4,5},{5,6},{6,7},{7,4},{8,9},{9,10},{10,1... | collective-permute-start | bytes 688136 | tf_op jit(solution)/shard_map/ppermute | solution.py:42
  119.8 1.8 %collective-permute-start.23 = (bf16[16,7168]{1,0:T(8,128)(2,1)S(1)}, bf16[16,7168]{1,0:T(8,128)(2,1)S(1)}, u32[]{:S(2)}, u32[]{:S(2)}) collective-permute-start(bf16[16,7168]{1,0:T(8,128)(2,1)S(1)} %fusion), channel_id=1, source_target_pairs={{0,3},{1,0},{2,1},{3,2},{4,7},{5,4},{6,5},{7,6},{8,11},{9,8},{10,9... | collective-permute-start | bytes 688136 | tf_op jit(solution)/shard_map/ppermute | solution.py:42
  121.6 0.1 slice.69.own_ref
  121.7 3.9 %collective-permute-done.22.up_ref = bf16[16,7168]{1,0:T(8,128)(2,1)S(1)} collective-permute-done((bf16[16,7168]{1,0:T(8,128)(2,1)S(1)}, bf16[16,7168]{1,0:T(8,128)(2,1)S(1)}, u32[]{:S(2)}, u32[]{:S(2)}) %collective-permute-start.22) | collective-permute-done | bytes 229408 | tf_op jit(solution)/shard_map/ppermute | solution.py:42
  125.6 0.2 collective-permute-done.23.down_ref
  125.8 0.9 placed_sum.1
  126.7 3.5 %all-to-all-start = ((bf16[4,8,7168]{2,1,0:T(8,128)(2,1)}), bf16[4,8,7168]{2,1,0:T(8,128)(2,1)S(1)}, u32[]{:S(2)}, u32[]{:S(2)}) async-start(bf16[4,8,7168]{2,1,0:T(8,128)(2,1)} %bitcast.5), calls=%async_computation | async-start | bytes 917504 | tf_op jit(solution)/shard_map/all_to_all | solution.py:52
  130.2 0.7 pad_maximum_fusion.2
  130.9 7.0 %all-to-all-done = bf16[4,8,7168]{2,1,0:T(8,128)(2,1)S(1)} async-done(((bf16[4,8,7168]{2,1,0:T(8,128)(2,1)}), bf16[4,8,7168]{2,1,0:T(8,128)(2,1)S(1)}, u32[]{:S(2)}, u32[]{:S(2)}) %all-to-all-start) | async-done | bytes 458784 | tf_op jit(solution)/shard_map/all_to_all | solution.py:52
  137.9 0.7 reduce_sum.12
  (34 shorter events, 0.4 us)
Async XLA Ops:
  1.7 9.7 %collective-permute-start = (bf16[8,7296]{1,0:T(8,128)(2,1)S(1)}, bf16[8,7296]{1,0:T(8,128)(2,1)S(1)}, u32[]{:S(2)}, u32[]{:S(2)}) collective-permute-start(bf16[8,7296]{1,0:T(8,128)(2,1)S(1)} %pack.1), channel_id=1, source_target_pairs={{0,96},{1,97},{2,98},{3,99},{4,100},{5,101},{6,102},{7,103},{8,104... | collective-permute-start | bytes 350216 | tf_op jit(solution)/shard_map/ppermute | solution.py:42
  5.9 6.4 %collective-permute-start.1 = (bf16[8,7296]{1,0:T(8,128)(2,1)S(1)}, bf16[8,7296]{1,0:T(8,128)(2,1)S(1)}, u32[]{:S(2)}, u32[]{:S(2)}) collective-permute-start(bf16[8,7296]{1,0:T(8,128)(2,1)S(1)} %pack.1), channel_id=1, source_target_pairs={{0,64},{1,65},{2,66},{3,67},{4,68},{5,69},{6,70},{7,71},{8,72},{9,... | collective-permute-start | bytes 350216 | tf_op jit(solution)/shard_map/ppermute | solution.py:42
  5.9 7.3 %collective-permute-start.2 = (bf16[8,7296]{1,0:T(8,128)(2,1)S(1)}, bf16[8,7296]{1,0:T(8,128)(2,1)S(1)}, u32[]{:S(2)}, u32[]{:S(2)}) collective-permute-start(bf16[8,7296]{1,0:T(8,128)(2,1)S(1)} %pack.1), channel_id=1, source_target_pairs={{0,32},{1,33},{2,34},{3,35},{4,36},{5,37},{6,38},{7,39},{8,40},{9,... | collective-permute-start | bytes 350216 | tf_op jit(solution)/shard_map/ppermute | solution.py:42
  13.3 36.1 %collective-permute-start.10 = (bf16[10752,512]{1,0:T(8,128)(2,1)S(1)}, bf16[10752,512]{1,0:T(8,128)(2,1)S(1)}, u32[]{:S(2)}, u32[]{:S(2)}) collective-permute-start(bf16[10752,512]{1,0:T(8,128)(2,1)S(1)} %join.1.refs_2_.refs_4_), channel_id=1, source_target_pairs={{0,16},{16,0},{1,17},{17,1},{2,18},{18,2},{3,19},{19,3},{4,20},{20... | collective-permute-start | bytes 33030152 | tf_op jit(solution)/shard_map/ppermute | solution.py:68
  13.4 9.8 %collective-permute-start.4 = (bf16[32,7296]{1,0:T(8,128)(2,1)S(1)}, bf16[32,7296]{1,0:T(8,128)(2,1)S(1)}, u32[]{:S(2)}, u32[]{:S(2)}) collective-permute-start(bf16[32,7296]{1,0:T(8,128)(2,1)S(1)} %pad_maximum_fusion), channel_id=1, source_target_pairs={{0,1},{1,2},{2,3},{3,0},{4,5},{5,6},{6,7},{7,4},{8,9},{9,10},{10,1... | collective-permute-start | bytes 1400840 | tf_op jit(solution)/shard_map/ppermute | solution.py:42
  15.0 8.6 %collective-permute-start.3 = (bf16[32,7296]{1,0:T(8,128)(2,1)S(1)}, bf16[32,7296]{1,0:T(8,128)(2,1)S(1)}, u32[]{:S(2)}, u32[]{:S(2)}) collective-permute-start(bf16[32,7296]{1,0:T(8,128)(2,1)S(1)} %pad_maximum_fusion), channel_id=1, source_target_pairs={{0,3},{1,0},{2,1},{3,2},{4,7},{5,4},{6,5},{7,6},{8,11},{9,8},{10,9... | collective-permute-start | bytes 1400840 | tf_op jit(solution)/shard_map/ppermute | solution.py:42
  16.7 22.7 %copy-start = (bf16[8,128,512]{2,1,0:T(8,128)(2,1)S(1)}, bf16[8,128,512]{2,1,0:T(8,128)(2,1)}, u32[]{:S(2)}) copy-start(bf16[8,128,512]{2,1,0:T(8,128)(2,1)} %key_up_ref.3) | copy-start | bytes 3145732
  16.7 22.7 %copy-start.1 = (bf16[8,512,128]{2,1,0:T(8,128)(2,1)S(1)}, bf16[8,512,128]{2,1,0:T(8,128)(2,1)}, u32[]{:S(2)}) copy-start(bf16[8,512,128]{2,1,0:T(8,128)(2,1)} %value_up_ref.3) | copy-start | bytes 3145732
  16.7 22.7 %copy-start.2 = (bf16[2,4096,64]{1,2,0:T(8,128)(2,1)S(1)}, bf16[2,4096,64]{1,2,0:T(8,128)(2,1)}, u32[]{:S(2)}) copy-start(bf16[2,4096,64]{1,2,0:T(8,128)(2,1)} %param.26) | copy-start | bytes 3145732
  16.7 22.7 %copy-start.3 = (bf16[128,1024]{1,0:T(8,128)(2,1)S(1)}, bf16[128,1024]{1,0:T(8,128)(2,1)}, u32[]{:S(2)}) copy-start(bf16[128,1024]{1,0:T(8,128)(2,1)} %nope_ref.3) | copy-start | bytes 786436
  16.7 22.6 %copy-start.4 = (bf16[128,512]{1,0:T(8,128)(2,1)S(1)}, bf16[128,512]{1,0:T(8,128)(2,1)}, u32[]{:S(2)}) copy-start(bf16[128,512]{1,0:T(8,128)(2,1)} %rope_ref.3) | copy-start | bytes 393220
  16.8 22.6 %copy-start.5 = (bf16[128,512]{1,0:T(8,128)(2,1)S(1)}, bf16[128,512]{1,0:T(8,128)(2,1)}, u32[]{:S(2)}) copy-start(bf16[128,512]{1,0:T(8,128)(2,1)} %new_latent_ref.3) | copy-start | bytes 393220
  16.8 22.6 %copy-start.6 = (bf16[128,64]{0,1:T(8,128)(2,1)S(1)}, bf16[128,64]{0,1:T(8,128)(2,1)}, u32[]{:S(2)}) copy-start(bf16[128,64]{0,1:T(8,128)(2,1)} %param.28) | copy-start | bytes 49156
  16.8 22.6 %copy-start.7 = (s32[2]{0:T(128)S(1)}, s32[2]{0:T(128)}, u32[]{:S(2)}) copy-start(s32[2]{0:T(128)} %param.29) | copy-start | bytes 28
  23.6 9.9 %collective-permute-start.5 = (bf16[16,7296]{1,0:T(8,128)(2,1)S(1)}, bf16[16,7296]{1,0:T(8,128)(2,1)S(1)}, u32[]{:S(2)}, u32[]{:S(2)}) collective-permute-start(bf16[16,7296]{1,0:T(8,128)(2,1)S(1)} %slice.67), channel_id=1, source_target_pairs={{0,1},{1,2},{2,3},{3,0},{4,5},{5,6},{6,7},{7,4},{8,9},{9,10},{10,1... | collective-permute-start | bytes 700424 | tf_op jit(solution)/shard_map/ppermute | solution.py:42
  25.3 24.1 %collective-permute-start.7 = (bf16[64,7296]{1,0:T(8,128)(2,1)S(1)}, bf16[64,7296]{1,0:T(8,128)(2,1)S(1)}, u32[]{:S(2)}, u32[]{:S(2)}) collective-permute-start(bf16[64,7296]{1,0:T(8,128)(2,1)S(1)} %constant_dynamic-update-slice_fusion.refs_0_), channel_id=1, source_target_pairs={{0,4},{1,5},{2,6},{3,7},{4,8},{5,9},{6,10},{7,11},{8,12},{9,13},{1... | collective-permute-start | bytes 2801672 | tf_op jit(solution)/shard_map/ppermute | solution.py:42
  26.8 22.6 %collective-permute-start.8 = (bf16[64,7296]{1,0:T(8,128)(2,1)S(1)}, bf16[64,7296]{1,0:T(8,128)(2,1)S(1)}, u32[]{:S(2)}, u32[]{:S(2)}) collective-permute-start(bf16[64,7296]{1,0:T(8,128)(2,1)S(1)} %constant_dynamic-update-slice_fusion.refs_0_), channel_id=1, source_target_pairs={{0,12},{1,13},{2,14},{3,15},{4,0},{5,1},{6,2},{7,3},{8,4},{9,5},{1... | collective-permute-start | bytes 2801672 | tf_op jit(solution)/shard_map/ppermute | solution.py:42
  28.6 8.6 %collective-permute-start.6 = (bf16[16,7296]{1,0:T(8,128)(2,1)S(1)}, bf16[16,7296]{1,0:T(8,128)(2,1)S(1)}, u32[]{:S(2)}, u32[]{:S(2)}) collective-permute-start(bf16[16,7296]{1,0:T(8,128)(2,1)S(1)} %slice.68), channel_id=1, source_target_pairs={{0,3},{1,0},{2,1},{3,2},{4,7},{5,4},{6,5},{7,6},{8,11},{9,8},{10,9... | collective-permute-start | bytes 700424 | tf_op jit(solution)/shard_map/ppermute | solution.py:42
  37.3 15.8 %collective-permute-start.9 = (bf16[64,7296]{1,0:T(8,128)(2,1)S(1)}, bf16[64,7296]{1,0:T(8,128)(2,1)S(1)}, u32[]{:S(2)}, u32[]{:S(2)}) collective-permute-start(bf16[64,7296]{1,0:T(8,128)(2,1)S(1)} %constant_dynamic-update-slice_fusion.2.refs_1_), channel_id=1, source_target_pairs={{0,12},{1,13},{2,14},{3,15},{4,0},{5,1},{6,2},{7,3},{8,4},{9,5},{1... | collective-permute-start | bytes 2801672 | tf_op jit(solution)/shard_map/ppermute | solution.py:42
  38.9 17.5 %collective-permute-start.13 = (bf16[64,7296]{1,0:T(8,128)(2,1)S(1)}, bf16[64,7296]{1,0:T(8,128)(2,1)S(1)}, u32[]{:S(2)}, u32[]{:S(2)}) collective-permute-start(bf16[64,7296]{1,0:T(8,128)(2,1)S(1)} %constant_dynamic-update-slice_fusion.2.refs_1_), channel_id=1, source_target_pairs={{0,4},{1,5},{2,6},{3,7},{4,8},{5,9},{6,10},{7,11},{8,12},{9,13},{1... | collective-permute-start | bytes 2801672 | tf_op jit(solution)/shard_map/ppermute | solution.py:42
  53.1 14.8 %collective-permute-start.11 = (bf16[64,7296]{1,0:T(8,128)(2,1)S(1)}, bf16[64,7296]{1,0:T(8,128)(2,1)S(1)}, u32[]{:S(2)}, u32[]{:S(2)}) collective-permute-start(bf16[64,7296]{1,0:T(8,128)(2,1)S(1)} %collective-permute-done.7.refs_2_), channel_id=1, source_target_pairs={{0,4},{1,5},{2,6},{3,7},{4,8},{5,9},{6,10},{7,11},{8,12},{9,13},{1... | collective-permute-start | bytes 2801672 | tf_op jit(solution)/shard_map/ppermute | solution.py:42
  53.5 14.5 %collective-permute-start.12 = (bf16[64,7296]{1,0:T(8,128)(2,1)S(1)}, bf16[64,7296]{1,0:T(8,128)(2,1)S(1)}, u32[]{:S(2)}, u32[]{:S(2)}) collective-permute-start(bf16[64,7296]{1,0:T(8,128)(2,1)S(1)} %collective-permute-done.9.refs_1_), channel_id=1, source_target_pairs={{0,12},{1,13},{2,14},{3,15},{4,0},{5,1},{6,2},{7,3},{8,4},{9,5},{1... | collective-permute-start | bytes 2801672 | tf_op jit(solution)/shard_map/ppermute | solution.py:42
  63.4 14.7 %collective-permute-start.14 = (bf16[64,7168]{1,0:T(8,128)(2,1)S(1)}, bf16[64,7168]{1,0:T(8,128)(2,1)S(1)}, u32[]{:S(2)}, u32[]{:S(2)}) collective-permute-start(bf16[64,7168]{1,0:T(8,128)(2,1)S(1)} %get-tuple-element.56), channel_id=1, source_target_pairs={{0,4},{1,5},{2,6},{3,7},{4,8},{5,9},{6,10},{7,11},{8,12},{9,13},{1... | collective-permute-start | bytes 2752520 | tf_op jit(solution)/shard_map/ppermute | solution.py:42
  63.5 14.6 %collective-permute-start.15 = (bf16[64,7168]{1,0:T(8,128)(2,1)S(1)}, bf16[64,7168]{1,0:T(8,128)(2,1)S(1)}, u32[]{:S(2)}, u32[]{:S(2)}) collective-permute-start(bf16[64,7168]{1,0:T(8,128)(2,1)S(1)} %get-tuple-element.57), channel_id=1, source_target_pairs={{0,12},{1,13},{2,14},{3,15},{4,0},{5,1},{6,2},{7,3},{8,4},{9,5},{1... | collective-permute-start | bytes 2752520 | tf_op jit(solution)/shard_map/ppermute | solution.py:42
  71.7 17.6 %collective-permute-start.16 = (bf16[64,7168]{1,0:T(8,128)(2,1)S(1)}, bf16[64,7168]{1,0:T(8,128)(2,1)S(1)}, u32[]{:S(2)}, u32[]{:S(2)}) collective-permute-start(bf16[64,7168]{1,0:T(8,128)(2,1)S(1)} %get-tuple-element.60), channel_id=1, source_target_pairs={{0,4},{1,5},{2,6},{3,7},{4,8},{5,9},{6,10},{7,11},{8,12},{9,13},{1... | collective-permute-start | bytes 2752520 | tf_op jit(solution)/shard_map/ppermute | solution.py:42
  72.7 16.6 %collective-permute-start.17 = (bf16[64,7168]{1,0:T(8,128)(2,1)S(1)}, bf16[64,7168]{1,0:T(8,128)(2,1)S(1)}, u32[]{:S(2)}, u32[]{:S(2)}) collective-permute-start(bf16[64,7168]{1,0:T(8,128)(2,1)S(1)} %get-tuple-element.61), channel_id=1, source_target_pairs={{0,12},{1,13},{2,14},{3,15},{4,0},{5,1},{6,2},{7,3},{8,4},{9,5},{1... | collective-permute-start | bytes 2752520 | tf_op jit(solution)/shard_map/ppermute | solution.py:42
  89.5 14.2 %collective-permute-start.19 = (bf16[64,7168]{1,0:T(8,128)(2,1)S(1)}, bf16[64,7168]{1,0:T(8,128)(2,1)S(1)}, u32[]{:S(2)}, u32[]{:S(2)}) collective-permute-start(bf16[64,7168]{1,0:T(8,128)(2,1)S(1)} %add_convert_fusion), channel_id=1, source_target_pairs={{0,12},{1,13},{2,14},{3,15},{4,0},{5,1},{6,2},{7,3},{8,4},{9,5},{1... | collective-permute-start | bytes 2752520 | tf_op jit(solution)/shard_map/ppermute | solution.py:42
  93.0 14.9 %collective-permute-start.18 = (bf16[64,7168]{1,0:T(8,128)(2,1)S(1)}, bf16[64,7168]{1,0:T(8,128)(2,1)S(1)}, u32[]{:S(2)}, u32[]{:S(2)}) collective-permute-start(bf16[64,7168]{1,0:T(8,128)(2,1)S(1)} %add_convert_fusion.1), channel_id=1, source_target_pairs={{0,4},{1,5},{2,6},{3,7},{4,8},{5,9},{6,10},{7,11},{8,12},{9,13},{1... | collective-permute-start | bytes 2752520 | tf_op jit(solution)/shard_map/ppermute | solution.py:42
  108.3 9.8 %collective-permute-start.20 = (bf16[32,7168]{1,0:T(8,128)(2,1)S(1)}, bf16[32,7168]{1,0:T(8,128)(2,1)S(1)}, u32[]{:S(2)}, u32[]{:S(2)}) collective-permute-start(bf16[32,7168]{1,0:T(8,128)(2,1)S(1)} %pad_maximum_fusion.1), channel_id=1, source_target_pairs={{0,1},{1,2},{2,3},{3,0},{4,5},{5,6},{6,7},{7,4},{8,9},{9,10},{10,1... | collective-permute-start | bytes 1376264 | tf_op jit(solution)/shard_map/ppermute | solution.py:42
  109.7 8.5 %collective-permute-start.21 = (bf16[32,7168]{1,0:T(8,128)(2,1)S(1)}, bf16[32,7168]{1,0:T(8,128)(2,1)S(1)}, u32[]{:S(2)}, u32[]{:S(2)}) collective-permute-start(bf16[32,7168]{1,0:T(8,128)(2,1)S(1)} %concatenate.25), channel_id=1, source_target_pairs={{0,3},{1,0},{2,1},{3,2},{4,7},{5,4},{6,5},{7,6},{8,11},{9,8},{10,9... | collective-permute-start | bytes 1376264 | tf_op jit(solution)/shard_map/ppermute | solution.py:42
  118.3 7.3 %collective-permute-start.22 = (bf16[16,7168]{1,0:T(8,128)(2,1)S(1)}, bf16[16,7168]{1,0:T(8,128)(2,1)S(1)}, u32[]{:S(2)}, u32[]{:S(2)}) collective-permute-start(bf16[16,7168]{1,0:T(8,128)(2,1)S(1)} %fusion.1), channel_id=1, source_target_pairs={{0,1},{1,2},{2,3},{3,0},{4,5},{5,6},{6,7},{7,4},{8,9},{9,10},{10,1... | collective-permute-start | bytes 688136 | tf_op jit(solution)/shard_map/ppermute | solution.py:42
  119.8 6.0 %collective-permute-start.23 = (bf16[16,7168]{1,0:T(8,128)(2,1)S(1)}, bf16[16,7168]{1,0:T(8,128)(2,1)S(1)}, u32[]{:S(2)}, u32[]{:S(2)}) collective-permute-start(bf16[16,7168]{1,0:T(8,128)(2,1)S(1)} %fusion), channel_id=1, source_target_pairs={{0,3},{1,0},{2,1},{3,2},{4,7},{5,4},{6,5},{7,6},{8,11},{9,8},{10,9... | collective-permute-start | bytes 688136 | tf_op jit(solution)/shard_map/ppermute | solution.py:42
  126.7 11.2 %all-to-all-start = ((bf16[4,8,7168]{2,1,0:T(8,128)(2,1)}), bf16[4,8,7168]{2,1,0:T(8,128)(2,1)S(1)}, u32[]{:S(2)}, u32[]{:S(2)}) async-start(bf16[4,8,7168]{2,1,0:T(8,128)(2,1)} %bitcast.5), calls=%async_computation | async-start | bytes 917504 | tf_op jit(solution)/shard_map/all_to_all | solution.py:52

commit v6 on v3

--- a/solution.py
+++ b/solution.py
@@ -308,6 +308,7 @@
     small, own_weights = lax.optimization_barrier((small, own_weights))
     weights = (own_weights, with_other_core(own_weights))
     rope_keys, new_rope_keys = jnp.swapaxes(rope_cache, 1, 2), new_rope.T
+    latent_cache = pltpu.with_memory_space_constraint(latent_cache, pltpu.HBM)
 
     def attention(sequence, length):
         return attend(
@@ -324,11 +325,12 @@
     below_high, above_high = shift(own_high, 2, 1), shift(own_high, 2, -1)
     own_low, own_high, below_low, above_low = lax.optimization_barrier((own_low, own_high, below_low, above_low))
     own_terms = expert_terms([own_low, own_high], weights)
-    below_low, above_high, own_terms = lax.optimization_barrier((below_low, above_high, own_terms))
-    far_low, far_high = shift(below_low, 2, 1), shift(above_high, 2, -1)
-    above_low, above_high, below_low, below_high = expert_terms(
-        [above_low, above_high, below_low, below_high], weights
-    )
+    above_low, relayed, own_terms = lax.optimization_barrier((above_low, below_low, own_terms))
+    above_low, below_low = expert_terms([above_low, relayed], weights)
+    relayed, above_high, above_low, below_low = lax.optimization_barrier((relayed, above_high, above_low, below_low))
+    far_low, far_high = shift(relayed, 2, 1), shift(above_high, 2, -1)
+    above_high, below_high = expert_terms([above_high, below_high], weights)
+    above_high, below_low = lax.optimization_barrier((above_high, below_low))
     near_high, near_low = shift(above_high, 2, 1), shift(below_low, 2, -1)
     far_low, far_high, above_high, below_low = lax.optimization_barrier((far_low, far_high, above_high, below_low))
     far_terms = expert_terms([far_low, far_high], weights)

time: 134 us -> 132 us (0.985)
  local copies, waits for them, and re-layouts: 4.29 us -> 0.91 us
  waiting for transfers between devices: 46.3 us -> 47.7 us
    unnamed x25 -> x19, local copies, waits for them, and re-layouts: 3.5 us -> 0.12 us
    pallas_call x2, Pallas kernels: 18.8 us -> 17.2 us  [attend(): pl.pallas_call(functools.partial(attention_kernel, sequence), grid_spec=p...]
    pallas_call x3 -> x4, Pallas kernels: 14.3 us -> 14.7 us  [expert_terms(): pl.pallas_call(functools.partial(expert_kernel, sources=len(pieces), outp...]
  transfers between devices with their start and end apart: 27 -> 27, of which waited for: 18 -> 19; matrix products, arithmetic and copies ran while one was open for 1% -> 1% of each run, Pallas kernels for 28% -> 28%
where the time goes in v6:
time: 132 us; the launch traced here: 131 us
  waiting for transfers between devices  47.7 us (36%)
  starting transfers between devices  41.7 us (32%)
  Pallas kernels  37.2 us (28%)
  other arithmetic  2.9 us (2%)
    ppermute x26, waiting for transfers between devices, shift(): return lax.ppermute(value, AXES, pairs)  47.7 us
    ppermute x26, starting transfers between devices, shift(): return lax.ppermute(value, AXES, pairs)  41.6 us
    pallas_call x2, Pallas kernels, attend(): pl.pallas_call(functools.partial(attention_kernel, sequence), grid_spec=p...  17.2 us
    pallas_call x4, Pallas kernels, expert_terms(): pl.pallas_call(functools.partial(expert_kernel, sources=len(pieces), outp...  14.7 us
    pallas_call x1, Pallas kernels, joined(): pl.pallas_call(join_kernel, in_specs=[pl.BlockSpec(memory_space=pl.ANY)]...  4.23 us
  transfers between devices with their start and end apart: 27, of which 19 were waited for; matrix products, arithmetic and copies ran while one was open for 1% of the time, Pallas kernels for 28%

profile of v6, /device:TPU:0, one launch (start us, length us, event | category | flops | bytes accessed | tf_op | source)
XLA Modules:
  0.0 131.3 jit_solution(551896602967094039)
XLA Ops:
  0.6 1.1 pack.1
  1.7 4.2 %collective-permute-start = (bf16[8,7296]{1,0:T(8,128)(2,1)S(1)}, bf16[8,7296]{1,0:T(8,128)(2,1)S(1)}, u32[]{:S(2)}, u32[]{:S(2)}) collective-permute-start(bf16[8,7296]{1,0:T(8,128)(2,1)S(1)} %pack.1), channel_id=1, source_target_pairs={{0,96},{1,97},{2,98},{3,99},{4,100},{5,101},{6,102},{7,103},{8,104... | collective-permute-start | bytes 350216 | tf_op jit(solution)/shard_map/ppermute | solution.py:42
  5.9 1.3 collective-permute-start.2
  7.2 4.2 %join.1.refs_2_ = bf16[10752,512]{1,0:T(8,128)(2,1)S(1)} custom-call(bf16[7168,256]{1,0:T(8,128)(2,1)} %bitcast.11, bf16[7168,256]{1,0:T(8,128)(2,1)} %bitcast.12, bf16[256,7168]{1,0:T(8,128)(2,1)} %bitcast.13), custom_call_target="tpu_custom_call" | custom-call | bytes 22020096 | tf_op jit(solution)/shard_map/join/pallas_call | solution.py:141
  11.4 0.9 collective-permute-done.1
  12.4 0.9 collective-permute-done.2
  13.2 0.1 pad_maximum_fusion
  13.3 0.1 collective-permute-start.9
  13.4 1.6 %collective-permute-start.4 = (bf16[32,7296]{1,0:T(8,128)(2,1)S(1)}, bf16[32,7296]{1,0:T(8,128)(2,1)S(1)}, u32[]{:S(2)}, u32[]{:S(2)}) collective-permute-start(bf16[32,7296]{1,0:T(8,128)(2,1)S(1)} %pad_maximum_fusion), channel_id=1, source_target_pairs={{0,1},{1,2},{2,3},{3,0},{4,5},{5,6},{6,7},{7,4},{8,9},{9,10},{10,1... | collective-permute-start | bytes 1400840 | tf_op jit(solution)/shard_map/ppermute | solution.py:42
  15.0 1.7 %collective-permute-start.3 = (bf16[32,7296]{1,0:T(8,128)(2,1)S(1)}, bf16[32,7296]{1,0:T(8,128)(2,1)S(1)}, u32[]{:S(2)}, u32[]{:S(2)}) collective-permute-start(bf16[32,7296]{1,0:T(8,128)(2,1)S(1)} %pad_maximum_fusion), channel_id=1, source_target_pairs={{0,3},{1,0},{2,1},{3,2},{4,7},{5,4},{6,5},{7,6},{8,11},{9,8},{10,9... | collective-permute-start | bytes 1400840 | tf_op jit(solution)/shard_map/ppermute | solution.py:42
  16.7 6.5 %collective-permute-done.4 = bf16[32,7296]{1,0:T(8,128)(2,1)S(1)} collective-permute-done((bf16[32,7296]{1,0:T(8,128)(2,1)S(1)}, bf16[32,7296]{1,0:T(8,128)(2,1)S(1)}, u32[]{:S(2)}, u32[]{:S(2)}) %collective-permute-start.4) | collective-permute-done | bytes 466976 | tf_op jit(solution)/shard_map/ppermute | solution.py:42
  23.2 0.3 collective-permute-done.3
  23.6 1.6 %collective-permute-start.5 = (bf16[16,7296]{1,0:T(8,128)(2,1)S(1)}, bf16[16,7296]{1,0:T(8,128)(2,1)S(1)}, u32[]{:S(2)}, u32[]{:S(2)}) collective-permute-start(bf16[16,7296]{1,0:T(8,128)(2,1)S(1)} %slice.83), channel_id=1, source_target_pairs={{0,1},{1,2},{2,3},{3,0},{4,5},{5,6},{6,7},{7,4},{8,9},{9,10},{10,1... | collective-permute-start | bytes 700424 | tf_op jit(solution)/shard_map/ppermute | solution.py:42
  25.3 1.6 %collective-permute-start.7 = (bf16[64,7296]{1,0:T(8,128)(2,1)S(1)}, bf16[64,7296]{1,0:T(8,128)(2,1)S(1)}, u32[]{:S(2)}, u32[]{:S(2)}) collective-permute-start(bf16[64,7296]{1,0:T(8,128)(2,1)S(1)} %constant_dynamic-update-slice_fusion.refs_0_), channel_id=1, source_target_pairs={{0,4},{1,5},{2,6},{3,7},{4,8},{5,9},{6,10},{7,11},{8,12},{9,13},{1... | collective-permute-start | bytes 2801672 | tf_op jit(solution)/shard_map/ppermute | solution.py:42
  26.8 1.7 %collective-permute-start.8 = (bf16[64,7296]{1,0:T(8,128)(2,1)S(1)}, bf16[64,7296]{1,0:T(8,128)(2,1)S(1)}, u32[]{:S(2)}, u32[]{:S(2)}) collective-permute-start(bf16[64,7296]{1,0:T(8,128)(2,1)S(1)} %constant_dynamic-update-slice_fusion.refs_0_), channel_id=1, source_target_pairs={{0,12},{1,13},{2,14},{3,15},{4,0},{5,1},{6,2},{7,3},{8,4},{9,5},{1... | collective-permute-start | bytes 2801672 | tf_op jit(solution)/shard_map/ppermute | solution.py:42
  28.6 1.7 %collective-permute-start.6 = (bf16[16,7296]{1,0:T(8,128)(2,1)S(1)}, bf16[16,7296]{1,0:T(8,128)(2,1)S(1)}, u32[]{:S(2)}, u32[]{:S(2)}) collective-permute-start(bf16[16,7296]{1,0:T(8,128)(2,1)S(1)} %slice.84), channel_id=1, source_target_pairs={{0,3},{1,0},{2,1},{3,2},{4,7},{5,4},{6,5},{7,6},{8,11},{9,8},{10,9... | collective-permute-start | bytes 700424 | tf_op jit(solution)/shard_map/ppermute | solution.py:42
  30.2 3.3 %collective-permute-done.5 = bf16[16,7296]{1,0:T(8,128)(2,1)S(1)} collective-permute-done((bf16[16,7296]{1,0:T(8,128)(2,1)S(1)}, bf16[16,7296]{1,0:T(8,128)(2,1)S(1)}, u32[]{:S(2)}, u32[]{:S(2)}) %collective-permute-start.5) | collective-permute-done | bytes 233504 | tf_op jit(solution)/shard_map/ppermute | solution.py:42
  33.5 3.7 %collective-permute-done.6 = bf16[16,7296]{1,0:T(8,128)(2,1)S(1)} collective-permute-done((bf16[16,7296]{1,0:T(8,128)(2,1)S(1)}, bf16[16,7296]{1,0:T(8,128)(2,1)S(1)}, u32[]{:S(2)}, u32[]{:S(2)}) %collective-permute-start.6) | collective-permute-done | bytes 233504 | tf_op jit(solution)/shard_map/ppermute | solution.py:42
  37.3 1.6 %collective-permute-start.10 = (bf16[64,7296]{1,0:T(8,128)(2,1)S(1)}, bf16[64,7296]{1,0:T(8,128)(2,1)S(1)}, u32[]{:S(2)}, u32[]{:S(2)}) collective-permute-start(bf16[64,7296]{1,0:T(8,128)(2,1)S(1)} %constant_dynamic-update-slice_fusion.2.refs_1_), channel_id=1, source_target_pairs={{0,12},{1,13},{2,14},{3,15},{4,0},{5,1},{6,2},{7,3},{8,4},{9,5},{1... | collective-permute-start | bytes 2801672 | tf_op jit(solution)/shard_map/ppermute | solution.py:42
  38.9 0.5 collective-permute-start.13
  39.4 0.7 collective-permute-done.7.refs_1_
  40.1 0.3 collective-permute-done.8.refs_0_
  40.4 3.7 %expert.4 = (bf16[64,7168]{1,0:T(8,128)(2,1)S(1)}, bf16[64,7168]{1,0:T(8,128)(2,1)S(1)}) custom-call(bf16[64,7296]{1,0:T(8,128)(2,1)S(1)} %constant_dynamic-update-slice_fusion.refs_0_, bf16[64,7296]{1,0:T(8,128)(2,1)S(1)} %constant_dynamic-update-slice_fusion.2.refs_1_, bf16[10752,512]{1,0:T(8,128)(2,1)S(1)} %join.1.refs_2_, ...), custom_call_target="tpu_custom_call" | custom-call | flops 2818572288 | bytes 3670016 | tf_op jit(solution)/shard_map/expert/pallas_call | solution.py:103
  44.1 3.7 %expert.5 = (bf16[64,7168]{1,0:T(8,128)(2,1)S(1)}, bf16[64,7168]{1,0:T(8,128)(2,1)S(1)}) custom-call(bf16[64,7296]{1,0:T(8,128)(2,1)S(1)} %collective-permute-done.8.refs_0_, bf16[64,7296]{1,0:T(8,128)(2,1)S(1)} %collective-permute-done.7.refs_1_, bf16[10752,512]{1,0:T(8,128)(2,1)S(1)} %join.1.refs_2_, bf16[10752,512]{1,0:T(8,128)(2,1)S(1)} %collective-permute-done.9.refs_3_), custom_call_target="tpu_custom_call" | custom-call | flops 2818572288 | bytes 3670016 | tf_op jit(solution)/shard_map/expert/pallas_call | solution.py:103
  47.8 3.1 %collective-permute-done.10.refs_0_ = bf16[64,7296]{1,0:T(8,128)(2,1)S(1)} collective-permute-done((bf16[64,7296]{1,0:T(8,128)(2,1)S(1)}, bf16[64,7296]{1,0:T(8,128)(2,1)S(1)}, u32[]{:S(2)}, u32[]{:S(2)}) %collective-permute-start.10) | collective-permute-done | bytes 933920 | tf_op jit(solution)/shard_map/ppermute | solution.py:42
  50.9 1.0 collective-permute-start.11
  51.9 2.3 %collective-permute-start.12 = (bf16[64,7296]{1,0:T(8,128)(2,1)S(1)}, bf16[64,7296]{1,0:T(8,128)(2,1)S(1)}, u32[]{:S(2)}, u32[]{:S(2)}) collective-permute-start(bf16[64,7296]{1,0:T(8,128)(2,1)S(1)} %collective-permute-done.10.refs_0_), channel_id=1, source_target_pairs={{0,12},{1,13},{2,14},{3,15},{4,0},{5,1},{6,2},{7,3},{8,4},{9,5},{1... | collective-permute-start | bytes 2801672 | tf_op jit(solution)/shard_map/ppermute | solution.py:42
  54.2 3.7 %expert.6 = (bf16[64,7168]{1,0:T(8,128)(2,1)S(1)}, bf16[64,7168]{1,0:T(8,128)(2,1)S(1)}) custom-call(bf16[64,7296]{1,0:T(8,128)(2,1)S(1)} %collective-permute-done.10.refs_0_, bf16[64,7296]{1,0:T(8,128)(2,1)S(1)} %collective-permute-done.13.refs_1_, bf16[10752,512]{1,0:T(8,128)(2,1)S(1)} %join.1.refs_2_, bf16[10752,512]{1,0:T(8,128)(2,1)S(1)} %collective-permute-done.9.refs_3_), custom_call_target="tpu_custom_call" | custom-call | flops 2818572288 | bytes 3670016 | tf_op jit(solution)/shard_map/expert/pallas_call | solution.py:103
  57.9 0.1 collective-permute-start.14
  58.0 3.2 %collective-permute-start.15 = (bf16[64,7168]{1,0:T(8,128)(2,1)S(1)}, bf16[64,7168]{1,0:T(8,128)(2,1)S(1)}, u32[]{:S(2)}, u32[]{:S(2)}) collective-permute-start(bf16[64,7168]{1,0:T(8,128)(2,1)S(1)} %get-tuple-element.68), channel_id=1, source_target_pairs={{0,12},{1,13},{2,14},{3,15},{4,0},{5,1},{6,2},{7,3},{8,4},{9,5},{1... | collective-permute-start | bytes 2752520 | tf_op jit(solution)/shard_map/ppermute | solution.py:42
  61.2 4.5 %collective-permute-done.11.refs_0_ = bf16[64,7296]{1,0:T(8,128)(2,1)S(1)} collective-permute-done((bf16[64,7296]{1,0:T(8,128)(2,1)S(1)}, bf16[64,7296]{1,0:T(8,128)(2,1)S(1)}, u32[]{:S(2)}, u32[]{:S(2)}) %collective-permute-start.11) | collective-permute-done | bytes 933920 | tf_op jit(solution)/shard_map/ppermute | solution.py:42
  65.7 3.7 %expert.7 = (bf16[64,7168]{1,0:T(8,128)(2,1)S(1)}, bf16[64,7168]{1,0:T(8,128)(2,1)S(1)}) custom-call(bf16[64,7296]{1,0:T(8,128)(2,1)S(1)} %collective-permute-done.11.refs_0_, bf16[64,7296]{1,0:T(8,128)(2,1)S(1)} %collective-permute-done.12.refs_1_, bf16[10752,512]{1,0:T(8,128)(2,1)S(1)} %join.1.refs_2_, bf16[10752,512]{1,0:T(8,128)(2,1)S(1)} %collective-permute-done.9.refs_3_), custom_call_target="tpu_custom_call" | custom-call | flops 2818572288 | bytes 3670016 | tf_op jit(solution)/shard_map/expert/pallas_call | solution.py:103
  69.4 1.0 collective-permute-start.16
  70.4 2.3 %collective-permute-start.17 = (bf16[64,7168]{1,0:T(8,128)(2,1)S(1)}, bf16[64,7168]{1,0:T(8,128)(2,1)S(1)}, u32[]{:S(2)}, u32[]{:S(2)}) collective-permute-start(bf16[64,7168]{1,0:T(8,128)(2,1)S(1)} %get-tuple-element.72), channel_id=1, source_target_pairs={{0,12},{1,13},{2,14},{3,15},{4,0},{5,1},{6,2},{7,3},{8,4},{9,5},{1... | collective-permute-start | bytes 2752520 | tf_op jit(solution)/shard_map/ppermute | solution.py:42
  72.8 2.8 %collective-permute-done.14 = bf16[64,7168]{1,0:T(8,128)(2,1)S(1)} collective-permute-done((bf16[64,7168]{1,0:T(8,128)(2,1)S(1)}, bf16[64,7168]{1,0:T(8,128)(2,1)S(1)}, u32[]{:S(2)}, u32[]{:S(2)}) %collective-permute-start.14) | collective-permute-done | bytes 917536 | tf_op jit(solution)/shard_map/ppermute | solution.py:42
  75.6 6.6 %attend.2 = bf16[64,1024]{1,0:T(8,128)(2,1)S(1)} custom-call(s32[1]{0:T(128)S(1)} %bitcast.10, bf16[128,1024]{1,0:T(8,128)(2,1)S(1)} %copy-done.3, bf16[128,512]{1,0:T(8,128)(2,1)S(1)} %copy-done.4, bf16[8,128,512]{2,1,0:T(8,128)(2,1)S(1)} %copy-done, bf16[8,512,128]{2,1,0:T(8,128)(2,1)S(1)} %copy-done.1, bf16[2,4096,512]{2,1,0:T(8,128)(2,1)} %latent_ref.3, ...), custom_call_target="tpu_custom_call" | custom-call | flops 6000000000 | bytes 8000000 | tf_op jit(solution)/shard_map/attend/pallas_call | solution.py:253
  82.2 3.1 %collective-permute-done.16 = bf16[64,7168]{1,0:T(8,128)(2,1)S(1)} collective-permute-done((bf16[64,7168]{1,0:T(8,128)(2,1)S(1)}, bf16[64,7168]{1,0:T(8,128)(2,1)S(1)}, u32[]{:S(2)}, u32[]{:S(2)}) %collective-permute-start.16) | collective-permute-done | bytes 917536 | tf_op jit(solution)/shard_map/ppermute | solution.py:42
  85.4 0.2 add_convert_fusion
  85.6 3.3 %collective-permute-start.19 = (bf16[64,7168]{1,0:T(8,128)(2,1)S(1)}, bf16[64,7168]{1,0:T(8,128)(2,1)S(1)}, u32[]{:S(2)}, u32[]{:S(2)}) collective-permute-start(bf16[64,7168]{1,0:T(8,128)(2,1)S(1)} %add_convert_fusion), channel_id=1, source_target_pairs={{0,12},{1,13},{2,14},{3,15},{4,0},{5,1},{6,2},{7,3},{8,4},{9,5},{1... | collective-permute-start | bytes 2752520 | tf_op jit(solution)/shard_map/ppermute | solution.py:42
  88.9 0.2 add_convert_fusion.1
  89.1 0.3 collective-permute-start.18
  89.4 0.6 slice.69.length_ref
  90.0 10.6 %attend.3 = bf16[64,1024]{1,0:T(8,128)(2,1)S(1)} custom-call(s32[1]{0:T(128)} %slice.69.length_ref, bf16[128,1024]{1,0:T(8,128)(2,1)S(1)} %copy-done.3, bf16[128,512]{1,0:T(8,128)(2,1)S(1)} %copy-done.4, bf16[8,128,512]{2,1,0:T(8,128)(2,1)S(1)} %copy-done, bf16[8,512,128]{2,1,0:T(8,128)(2,1)S(1)} %copy-done.1, bf16[2,4096,512]{2,1,0:T(8,128)(2,1)} %latent_ref.3, ...), custom_call_target="tpu_custom_call" | custom-call | flops 6000000000 | bytes 8000000 | tf_op jit(solution)/shard_map/attend/pallas_call | solution.py:253
  100.6 3.4 %collective-permute-done.18 = bf16[64,7168]{1,0:T(8,128)(2,1)S(1)} collective-permute-done((bf16[64,7168]{1,0:T(8,128)(2,1)S(1)}, bf16[64,7168]{1,0:T(8,128)(2,1)S(1)}, u32[]{:S(2)}, u32[]{:S(2)}) %collective-permute-start.18) | collective-permute-done | bytes 917536 | tf_op jit(solution)/shard_map/ppermute | solution.py:42
  104.0 0.3 fusion.3
  104.4 0.3 convert_add_fusion.1
  104.7 1.3 %collective-permute-start.20 = (bf16[32,7168]{1,0:T(8,128)(2,1)S(1)}, bf16[32,7168]{1,0:T(8,128)(2,1)S(1)}, u32[]{:S(2)}, u32[]{:S(2)}) collective-permute-start(bf16[32,7168]{1,0:T(8,128)(2,1)S(1)} %pad_maximum_fusion.1), channel_id=1, source_target_pairs={{0,1},{1,2},{2,3},{3,0},{4,5},{5,6},{6,7},{7,4},{8,9},{9,10},{10,1... | collective-permute-start | bytes 1376264 | tf_op jit(solution)/shard_map/ppermute | solution.py:42
  106.1 2.0 %collective-permute-start.21 = (bf16[32,7168]{1,0:T(8,128)(2,1)S(1)}, bf16[32,7168]{1,0:T(8,128)(2,1)S(1)}, u32[]{:S(2)}, u32[]{:S(2)}) collective-permute-start(bf16[32,7168]{1,0:T(8,128)(2,1)S(1)} %concatenate.29), channel_id=1, source_target_pairs={{0,3},{1,0},{2,1},{3,2},{4,7},{5,4},{6,5},{7,6},{8,11},{9,8},{10,9... | collective-permute-start | bytes 1376264 | tf_op jit(solution)/shard_map/ppermute | solution.py:42
  108.2 6.3 %collective-permute-done.20 = bf16[32,7168]{1,0:T(8,128)(2,1)S(1)} collective-permute-done((bf16[32,7168]{1,0:T(8,128)(2,1)S(1)}, bf16[32,7168]{1,0:T(8,128)(2,1)S(1)}, u32[]{:S(2)}, u32[]{:S(2)}) %collective-permute-start.20) | collective-permute-done | bytes 458784 | tf_op jit(solution)/shard_map/ppermute | solution.py:42
  114.5 0.1 fusion.2
  114.6 0.1 collective-permute-done.21
  114.7 0.1 fusion.1
  114.7 1.5 %collective-permute-start.22 = (bf16[16,7168]{1,0:T(8,128)(2,1)S(1)}, bf16[16,7168]{1,0:T(8,128)(2,1)S(1)}, u32[]{:S(2)}, u32[]{:S(2)}) collective-permute-start(bf16[16,7168]{1,0:T(8,128)(2,1)S(1)} %fusion.2), channel_id=1, source_target_pairs={{0,1},{1,2},{2,3},{3,0},{4,5},{5,6},{6,7},{7,4},{8,9},{9,10},{10,1... | collective-permute-start | bytes 688136 | tf_op jit(solution)/shard_map/ppermute | solution.py:42
  116.2 1.8 %collective-permute-start.23 = (bf16[16,7168]{1,0:T(8,128)(2,1)S(1)}, bf16[16,7168]{1,0:T(8,128)(2,1)S(1)}, u32[]{:S(2)}, u32[]{:S(2)}) collective-permute-start(bf16[16,7168]{1,0:T(8,128)(2,1)S(1)} %fusion.1), channel_id=1, source_target_pairs={{0,3},{1,0},{2,1},{3,2},{4,7},{5,4},{6,5},{7,6},{8,11},{9,8},{10,9... | collective-permute-start | bytes 688136 | tf_op jit(solution)/shard_map/ppermute | solution.py:42
  118.1 4.0 %collective-permute-done.22 = bf16[16,7168]{1,0:T(8,128)(2,1)S(1)} collective-permute-done((bf16[16,7168]{1,0:T(8,128)(2,1)S(1)}, bf16[16,7168]{1,0:T(8,128)(2,1)S(1)}, u32[]{:S(2)}, u32[]{:S(2)}) %collective-permute-start.22) | collective-permute-done | bytes 229408 | tf_op jit(solution)/shard_map/ppermute | solution.py:42
  122.1 0.2 collective-permute-done.23
  122.3 0.1 fusion
  122.5 0.5 collective-permute-start.24
  123.0 2.4 %collective-permute-start.25 = (bf16[8,7168]{1,0:T(8,128)(2,1)S(1)}, bf16[8,7168]{1,0:T(8,128)(2,1)S(1)}, u32[]{:S(2)}, u32[]{:S(2)}) collective-permute-start(bf16[8,7168]{1,0:T(8,128)(2,1)S(1)} %get-tuple-element.92), channel_id=1, source_target_pairs={{0,64},{1,65},{2,66},{3,67},{4,68},{5,69},{6,70},{7,71},{8,72},{9,... | collective-permute-start | bytes 344072 | tf_op jit(solution)/shard_map/ppermute | solution.py:42
  125.4 1.0 collective-permute-start.26
  126.4 0.7 pad_maximum_fusion.2
  127.1 2.7 %collective-permute-done.24 = bf16[8,7168]{1,0:T(8,128)(2,1)S(1)} collective-permute-done((bf16[8,7168]{1,0:T(8,128)(2,1)S(1)}, bf16[8,7168]{1,0:T(8,128)(2,1)S(1)}, u32[]{:S(2)}, u32[]{:S(2)}) %collective-permute-start.24) | collective-permute-done | bytes 114720 | tf_op jit(solution)/shard_map/ppermute | solution.py:42
  129.8 0.9 collective-permute-done.26
  130.6 0.7 add_convert_fusion.2
  (39 shorter events, 0.5 us)
Async XLA Ops:
  1.7 9.7 %collective-permute-start = (bf16[8,7296]{1,0:T(8,128)(2,1)S(1)}, bf16[8,7296]{1,0:T(8,128)(2,1)S(1)}, u32[]{:S(2)}, u32[]{:S(2)}) collective-permute-start(bf16[8,7296]{1,0:T(8,128)(2,1)S(1)} %pack.1), channel_id=1, source_target_pairs={{0,96},{1,97},{2,98},{3,99},{4,100},{5,101},{6,102},{7,103},{8,104... | collective-permute-start | bytes 350216 | tf_op jit(solution)/shard_map/ppermute | solution.py:42
  5.9 6.4 %collective-permute-start.1 = (bf16[8,7296]{1,0:T(8,128)(2,1)S(1)}, bf16[8,7296]{1,0:T(8,128)(2,1)S(1)}, u32[]{:S(2)}, u32[]{:S(2)}) collective-permute-start(bf16[8,7296]{1,0:T(8,128)(2,1)S(1)} %pack.1), channel_id=1, source_target_pairs={{0,64},{1,65},{2,66},{3,67},{4,68},{5,69},{6,70},{7,71},{8,72},{9,... | collective-permute-start | bytes 350216 | tf_op jit(solution)/shard_map/ppermute | solution.py:42
  5.9 7.3 %collective-permute-start.2 = (bf16[8,7296]{1,0:T(8,128)(2,1)S(1)}, bf16[8,7296]{1,0:T(8,128)(2,1)S(1)}, u32[]{:S(2)}, u32[]{:S(2)}) collective-permute-start(bf16[8,7296]{1,0:T(8,128)(2,1)S(1)} %pack.1), channel_id=1, source_target_pairs={{0,32},{1,33},{2,34},{3,35},{4,36},{5,37},{6,38},{7,39},{8,40},{9,... | collective-permute-start | bytes 350216 | tf_op jit(solution)/shard_map/ppermute | solution.py:42
  13.3 27.1 %collective-permute-start.9 = (bf16[10752,512]{1,0:T(8,128)(2,1)S(1)}, bf16[10752,512]{1,0:T(8,128)(2,1)S(1)}, u32[]{:S(2)}, u32[]{:S(2)}) collective-permute-start(bf16[10752,512]{1,0:T(8,128)(2,1)S(1)} %join.1.refs_2_), channel_id=1, source_target_pairs={{0,16},{16,0},{1,17},{17,1},{2,18},{18,2},{3,19},{19,3},{4,20},{20... | collective-permute-start | bytes 33030152 | tf_op jit(solution)/shard_map/ppermute | solution.py:58
  13.4 9.8 %collective-permute-start.4 = (bf16[32,7296]{1,0:T(8,128)(2,1)S(1)}, bf16[32,7296]{1,0:T(8,128)(2,1)S(1)}, u32[]{:S(2)}, u32[]{:S(2)}) collective-permute-start(bf16[32,7296]{1,0:T(8,128)(2,1)S(1)} %pad_maximum_fusion), channel_id=1, source_target_pairs={{0,1},{1,2},{2,3},{3,0},{4,5},{5,6},{6,7},{7,4},{8,9},{9,10},{10,1... | collective-permute-start | bytes 1400840 | tf_op jit(solution)/shard_map/ppermute | solution.py:42
  15.0 8.6 %collective-permute-start.3 = (bf16[32,7296]{1,0:T(8,128)(2,1)S(1)}, bf16[32,7296]{1,0:T(8,128)(2,1)S(1)}, u32[]{:S(2)}, u32[]{:S(2)}) collective-permute-start(bf16[32,7296]{1,0:T(8,128)(2,1)S(1)} %pad_maximum_fusion), channel_id=1, source_target_pairs={{0,3},{1,0},{2,1},{3,2},{4,7},{5,4},{6,5},{7,6},{8,11},{9,8},{10,9... | collective-permute-start | bytes 1400840 | tf_op jit(solution)/shard_map/ppermute | solution.py:42
  23.6 9.9 %collective-permute-start.5 = (bf16[16,7296]{1,0:T(8,128)(2,1)S(1)}, bf16[16,7296]{1,0:T(8,128)(2,1)S(1)}, u32[]{:S(2)}, u32[]{:S(2)}) collective-permute-start(bf16[16,7296]{1,0:T(8,128)(2,1)S(1)} %slice.83), channel_id=1, source_target_pairs={{0,1},{1,2},{2,3},{3,0},{4,5},{5,6},{6,7},{7,4},{8,9},{9,10},{10,1... | collective-permute-start | bytes 700424 | tf_op jit(solution)/shard_map/ppermute | solution.py:42
  25.3 14.8 %collective-permute-start.7 = (bf16[64,7296]{1,0:T(8,128)(2,1)S(1)}, bf16[64,7296]{1,0:T(8,128)(2,1)S(1)}, u32[]{:S(2)}, u32[]{:S(2)}) collective-permute-start(bf16[64,7296]{1,0:T(8,128)(2,1)S(1)} %constant_dynamic-update-slice_fusion.refs_0_), channel_id=1, source_target_pairs={{0,4},{1,5},{2,6},{3,7},{4,8},{5,9},{6,10},{7,11},{8,12},{9,13},{1... | collective-permute-start | bytes 2801672 | tf_op jit(solution)/shard_map/ppermute | solution.py:42
  26.8 13.6 %collective-permute-start.8 = (bf16[64,7296]{1,0:T(8,128)(2,1)S(1)}, bf16[64,7296]{1,0:T(8,128)(2,1)S(1)}, u32[]{:S(2)}, u32[]{:S(2)}) collective-permute-start(bf16[64,7296]{1,0:T(8,128)(2,1)S(1)} %constant_dynamic-update-slice_fusion.refs_0_), channel_id=1, source_target_pairs={{0,12},{1,13},{2,14},{3,15},{4,0},{5,1},{6,2},{7,3},{8,4},{9,5},{1... | collective-permute-start | bytes 2801672 | tf_op jit(solution)/shard_map/ppermute | solution.py:42
  28.6 8.6 %collective-permute-start.6 = (bf16[16,7296]{1,0:T(8,128)(2,1)S(1)}, bf16[16,7296]{1,0:T(8,128)(2,1)S(1)}, u32[]{:S(2)}, u32[]{:S(2)}) collective-permute-start(bf16[16,7296]{1,0:T(8,128)(2,1)S(1)} %slice.84), channel_id=1, source_target_pairs={{0,3},{1,0},{2,1},{3,2},{4,7},{5,4},{6,5},{7,6},{8,11},{9,8},{10,9... | collective-permute-start | bytes 700424 | tf_op jit(solution)/shard_map/ppermute | solution.py:42
  37.3 13.6 %collective-permute-start.10 = (bf16[64,7296]{1,0:T(8,128)(2,1)S(1)}, bf16[64,7296]{1,0:T(8,128)(2,1)S(1)}, u32[]{:S(2)}, u32[]{:S(2)}) collective-permute-start(bf16[64,7296]{1,0:T(8,128)(2,1)S(1)} %constant_dynamic-update-slice_fusion.2.refs_1_), channel_id=1, source_target_pairs={{0,12},{1,13},{2,14},{3,15},{4,0},{5,1},{6,2},{7,3},{8,4},{9,5},{1... | collective-permute-start | bytes 2801672 | tf_op jit(solution)/shard_map/ppermute | solution.py:42
  38.9 15.3 %collective-permute-start.13 = (bf16[64,7296]{1,0:T(8,128)(2,1)S(1)}, bf16[64,7296]{1,0:T(8,128)(2,1)S(1)}, u32[]{:S(2)}, u32[]{:S(2)}) collective-permute-start(bf16[64,7296]{1,0:T(8,128)(2,1)S(1)} %constant_dynamic-update-slice_fusion.2.refs_1_), channel_id=1, source_target_pairs={{0,4},{1,5},{2,6},{3,7},{4,8},{5,9},{6,10},{7,11},{8,12},{9,13},{1... | collective-permute-start | bytes 2801672 | tf_op jit(solution)/shard_map/ppermute | solution.py:42
  50.9 14.8 %collective-permute-start.11 = (bf16[64,7296]{1,0:T(8,128)(2,1)S(1)}, bf16[64,7296]{1,0:T(8,128)(2,1)S(1)}, u32[]{:S(2)}, u32[]{:S(2)}) collective-permute-start(bf16[64,7296]{1,0:T(8,128)(2,1)S(1)} %collective-permute-done.7.refs_1_), channel_id=1, source_target_pairs={{0,4},{1,5},{2,6},{3,7},{4,8},{5,9},{6,10},{7,11},{8,12},{9,13},{1... | collective-permute-start | bytes 2801672 | tf_op jit(solution)/shard_map/ppermute | solution.py:42
  51.9 13.8 %collective-permute-start.12 = (bf16[64,7296]{1,0:T(8,128)(2,1)S(1)}, bf16[64,7296]{1,0:T(8,128)(2,1)S(1)}, u32[]{:S(2)}, u32[]{:S(2)}) collective-permute-start(bf16[64,7296]{1,0:T(8,128)(2,1)S(1)} %collective-permute-done.10.refs_0_), channel_id=1, source_target_pairs={{0,12},{1,13},{2,14},{3,15},{4,0},{5,1},{6,2},{7,3},{8,4},{9,5},{1... | collective-permute-start | bytes 2801672 | tf_op jit(solution)/shard_map/ppermute | solution.py:42
  57.8 17.7 %copy-start = (bf16[8,128,512]{2,1,0:T(8,128)(2,1)S(1)}, bf16[8,128,512]{2,1,0:T(8,128)(2,1)}, u32[]{:S(2)}) copy-start(bf16[8,128,512]{2,1,0:T(8,128)(2,1)} %key_up_ref.3) | copy-start | bytes 3145732
  57.9 17.7 %copy-start.1 = (bf16[8,512,128]{2,1,0:T(8,128)(2,1)S(1)}, bf16[8,512,128]{2,1,0:T(8,128)(2,1)}, u32[]{:S(2)}) copy-start(bf16[8,512,128]{2,1,0:T(8,128)(2,1)} %value_up_ref.3) | copy-start | bytes 3145732
  57.9 17.7 %copy-start.2 = (bf16[2,4096,64]{1,2,0:T(8,128)(2,1)S(1)}, bf16[2,4096,64]{1,2,0:T(8,128)(2,1)}, u32[]{:S(2)}) copy-start(bf16[2,4096,64]{1,2,0:T(8,128)(2,1)} %param.26) | copy-start | bytes 3145732
  57.9 17.7 %copy-start.3 = (bf16[128,1024]{1,0:T(8,128)(2,1)S(1)}, bf16[128,1024]{1,0:T(8,128)(2,1)}, u32[]{:S(2)}) copy-start(bf16[128,1024]{1,0:T(8,128)(2,1)} %nope_ref.3) | copy-start | bytes 786436
  57.9 17.7 %copy-start.4 = (bf16[128,512]{1,0:T(8,128)(2,1)S(1)}, bf16[128,512]{1,0:T(8,128)(2,1)}, u32[]{:S(2)}) copy-start(bf16[128,512]{1,0:T(8,128)(2,1)} %rope_ref.3) | copy-start | bytes 393220
  57.9 17.7 %copy-start.5 = (bf16[128,512]{1,0:T(8,128)(2,1)S(1)}, bf16[128,512]{1,0:T(8,128)(2,1)}, u32[]{:S(2)}) copy-start(bf16[128,512]{1,0:T(8,128)(2,1)} %new_latent_ref.3) | copy-start | bytes 393220
  57.9 17.7 %copy-start.6 = (bf16[128,64]{0,1:T(8,128)(2,1)S(1)}, bf16[128,64]{0,1:T(8,128)(2,1)}, u32[]{:S(2)}) copy-start(bf16[128,64]{0,1:T(8,128)(2,1)} %param.28) | copy-start | bytes 49156
  57.9 17.7 %copy-start.7 = (s32[2]{0:T(128)S(1)}, s32[2]{0:T(128)}, u32[]{:S(2)}) copy-start(s32[2]{0:T(128)} %param.29) | copy-start | bytes 28
  57.9 17.6 %collective-permute-start.14 = (bf16[64,7168]{1,0:T(8,128)(2,1)S(1)}, bf16[64,7168]{1,0:T(8,128)(2,1)S(1)}, u32[]{:S(2)}, u32[]{:S(2)}) collective-permute-start(bf16[64,7168]{1,0:T(8,128)(2,1)S(1)} %get-tuple-element.67), channel_id=1, source_target_pairs={{0,4},{1,5},{2,6},{3,7},{4,8},{5,9},{6,10},{7,11},{8,12},{9,13},{1... | collective-permute-start | bytes 2752520 | tf_op jit(solution)/shard_map/ppermute | solution.py:42
  58.0 17.5 %collective-permute-start.15 = (bf16[64,7168]{1,0:T(8,128)(2,1)S(1)}, bf16[64,7168]{1,0:T(8,128)(2,1)S(1)}, u32[]{:S(2)}, u32[]{:S(2)}) collective-permute-start(bf16[64,7168]{1,0:T(8,128)(2,1)S(1)} %get-tuple-element.68), channel_id=1, source_target_pairs={{0,12},{1,13},{2,14},{3,15},{4,0},{5,1},{6,2},{7,3},{8,4},{9,5},{1... | collective-permute-start | bytes 2752520 | tf_op jit(solution)/shard_map/ppermute | solution.py:42
  69.4 16.0 %collective-permute-start.16 = (bf16[64,7168]{1,0:T(8,128)(2,1)S(1)}, bf16[64,7168]{1,0:T(8,128)(2,1)S(1)}, u32[]{:S(2)}, u32[]{:S(2)}) collective-permute-start(bf16[64,7168]{1,0:T(8,128)(2,1)S(1)} %get-tuple-element.71), channel_id=1, source_target_pairs={{0,4},{1,5},{2,6},{3,7},{4,8},{5,9},{6,10},{7,11},{8,12},{9,13},{1... | collective-permute-start | bytes 2752520 | tf_op jit(solution)/shard_map/ppermute | solution.py:42
  70.4 14.9 %collective-permute-start.17 = (bf16[64,7168]{1,0:T(8,128)(2,1)S(1)}, bf16[64,7168]{1,0:T(8,128)(2,1)S(1)}, u32[]{:S(2)}, u32[]{:S(2)}) collective-permute-start(bf16[64,7168]{1,0:T(8,128)(2,1)S(1)} %get-tuple-element.72), channel_id=1, source_target_pairs={{0,12},{1,13},{2,14},{3,15},{4,0},{5,1},{6,2},{7,3},{8,4},{9,5},{1... | collective-permute-start | bytes 2752520 | tf_op jit(solution)/shard_map/ppermute | solution.py:42
  85.6 15.0 %collective-permute-start.19 = (bf16[64,7168]{1,0:T(8,128)(2,1)S(1)}, bf16[64,7168]{1,0:T(8,128)(2,1)S(1)}, u32[]{:S(2)}, u32[]{:S(2)}) collective-permute-start(bf16[64,7168]{1,0:T(8,128)(2,1)S(1)} %add_convert_fusion), channel_id=1, source_target_pairs={{0,12},{1,13},{2,14},{3,15},{4,0},{5,1},{6,2},{7,3},{8,4},{9,5},{1... | collective-permute-start | bytes 2752520 | tf_op jit(solution)/shard_map/ppermute | solution.py:42
  89.1 14.9 %collective-permute-start.18 = (bf16[64,7168]{1,0:T(8,128)(2,1)S(1)}, bf16[64,7168]{1,0:T(8,128)(2,1)S(1)}, u32[]{:S(2)}, u32[]{:S(2)}) collective-permute-start(bf16[64,7168]{1,0:T(8,128)(2,1)S(1)} %add_convert_fusion.1), channel_id=1, source_target_pairs={{0,4},{1,5},{2,6},{3,7},{4,8},{5,9},{6,10},{7,11},{8,12},{9,13},{1... | collective-permute-start | bytes 2752520 | tf_op jit(solution)/shard_map/ppermute | solution.py:42
  104.7 9.8 %collective-permute-start.20 = (bf16[32,7168]{1,0:T(8,128)(2,1)S(1)}, bf16[32,7168]{1,0:T(8,128)(2,1)S(1)}, u32[]{:S(2)}, u32[]{:S(2)}) collective-permute-start(bf16[32,7168]{1,0:T(8,128)(2,1)S(1)} %pad_maximum_fusion.1), channel_id=1, source_target_pairs={{0,1},{1,2},{2,3},{3,0},{4,5},{5,6},{6,7},{7,4},{8,9},{9,10},{10,1... | collective-permute-start | bytes 1376264 | tf_op jit(solution)/shard_map/ppermute | solution.py:42
  106.1 8.5 %collective-permute-start.21 = (bf16[32,7168]{1,0:T(8,128)(2,1)S(1)}, bf16[32,7168]{1,0:T(8,128)(2,1)S(1)}, u32[]{:S(2)}, u32[]{:S(2)}) collective-permute-start(bf16[32,7168]{1,0:T(8,128)(2,1)S(1)} %concatenate.29), channel_id=1, source_target_pairs={{0,3},{1,0},{2,1},{3,2},{4,7},{5,4},{6,5},{7,6},{8,11},{9,8},{10,9... | collective-permute-start | bytes 1376264 | tf_op jit(solution)/shard_map/ppermute | solution.py:42
  114.7 7.3 %collective-permute-start.22 = (bf16[16,7168]{1,0:T(8,128)(2,1)S(1)}, bf16[16,7168]{1,0:T(8,128)(2,1)S(1)}, u32[]{:S(2)}, u32[]{:S(2)}) collective-permute-start(bf16[16,7168]{1,0:T(8,128)(2,1)S(1)} %fusion.2), channel_id=1, source_target_pairs={{0,1},{1,2},{2,3},{3,0},{4,5},{5,6},{6,7},{7,4},{8,9},{9,10},{10,1... | collective-permute-start | bytes 688136 | tf_op jit(solution)/shard_map/ppermute | solution.py:42
  116.2 6.0 %collective-permute-start.23 = (bf16[16,7168]{1,0:T(8,128)(2,1)S(1)}, bf16[16,7168]{1,0:T(8,128)(2,1)S(1)}, u32[]{:S(2)}, u32[]{:S(2)}) collective-permute-start(bf16[16,7168]{1,0:T(8,128)(2,1)S(1)} %fusion.1), channel_id=1, source_target_pairs={{0,3},{1,0},{2,1},{3,2},{4,7},{5,4},{6,5},{7,6},{8,11},{9,8},{10,9... | collective-permute-start | bytes 688136 | tf_op jit(solution)/shard_map/ppermute | solution.py:42
  122.5 7.3 %collective-permute-start.24 = (bf16[8,7168]{1,0:T(8,128)(2,1)S(1)}, bf16[8,7168]{1,0:T(8,128)(2,1)S(1)}, u32[]{:S(2)}, u32[]{:S(2)}) collective-permute-start(bf16[8,7168]{1,0:T(8,128)(2,1)S(1)} %get-tuple-element.90), channel_id=1, source_target_pairs={{0,32},{1,33},{2,34},{3,35},{4,36},{5,37},{6,38},{7,39},{8,40},{9,... | collective-permute-start | bytes 344072 | tf_op jit(solution)/shard_map/ppermute | solution.py:42
  123.0 6.8 %collective-permute-start.25 = (bf16[8,7168]{1,0:T(8,128)(2,1)S(1)}, bf16[8,7168]{1,0:T(8,128)(2,1)S(1)}, u32[]{:S(2)}, u32[]{:S(2)}) collective-permute-start(bf16[8,7168]{1,0:T(8,128)(2,1)S(1)} %get-tuple-element.92), channel_id=1, source_target_pairs={{0,64},{1,65},{2,66},{3,67},{4,68},{5,69},{6,70},{7,71},{8,72},{9,... | collective-permute-start | bytes 344072 | tf_op jit(solution)/shard_map/ppermute | solution.py:42
  125.4 5.3 %collective-permute-start.26 = (bf16[8,7168]{1,0:T(8,128)(2,1)S(1)}, bf16[8,7168]{1,0:T(8,128)(2,1)S(1)}, u32[]{:S(2)}, u32[]{:S(2)}) collective-permute-start(bf16[8,7168]{1,0:T(8,128)(2,1)S(1)} %get-tuple-element.91), channel_id=1, source_target_pairs={{0,96},{1,97},{2,98},{3,99},{4,100},{5,101},{6,102},{7,103},{8,104... | collective-permute-start | bytes 344072 | tf_op jit(solution)/shard_map/ppermute | solution.py:42

commit v7 on v6

--- a/solution.py
+++ b/solution.py
@@ -27,7 +27,8 @@
 HALF = 64
 KEY_BLOCK = 1024
 HEAD_COUNT = 8
-PARTS = 2
+SHORT, LONG = 60, 1
+PARTS = 4
 LATENT = 512
 LOG2E = 1.4426950408889634
 
@@ -180,7 +181,7 @@
     new_latent_ref, new_rope_ref, out_ref, query_ref, query_rope_ref, top_ref, sum_ref, total_ref,
 ):
     step = pl.program_id(0)
-    length = length_ref[0]
+    length = length_ref[sequence]
     scale = (NOPE + ROPE) ** (-0.5) * LOG2E
     contract_last = (((1,), (1,)), ((), ()))
 
@@ -234,14 +235,14 @@
             ).astype(jnp.bfloat16)
 
 
-def attend(sequence, length, nope, rope, key_up, value_up, latent_cache, rope_cache, new_latent, new_rope):
+def attend(weight, sequence, length, nope, rope, key_up, value_up, latent_cache, rope_cache, new_latent, new_rope):
     rows = HEAD_COUNT * NEW
 
     def whole(*shape):
         return pl.BlockSpec(shape, lambda step, length: (0,) * len(shape))
 
     def live(step, length):
-        return (sequence, jnp.minimum(step, (length[0] + KEY_BLOCK - 1) // KEY_BLOCK - 1), 0)
+        return (sequence, jnp.minimum(step, (length[sequence] + KEY_BLOCK - 1) // KEY_BLOCK - 1), 0)
 
     def live_last(step, length):
         sequence_place, block, column = live(step, length)
@@ -276,7 +277,7 @@
         ),
         out_shape=jax.ShapeDtypeStruct((NEW, HEAD_COUNT * NOPE), jnp.bfloat16),
         compiler_params=pltpu.CompilerParams(vmem_limit_bytes=KERNEL_VMEM),
-        cost_estimate=pl.CostEstimate(flops=6_000_000_000, bytes_accessed=8_000_000, transcendentals=2_100_000),
+        cost_estimate=pl.CostEstimate(flops=6_000_000_000 // weight, bytes_accessed=8_000_000 // weight, transcendentals=2_100_000 // weight),
         name="attend",
     )(length, nope, rope, key_up, value_up, latent_cache, rope_cache, new_latent, new_rope)
 
@@ -310,9 +311,9 @@
     rope_keys, new_rope_keys = jnp.swapaxes(rope_cache, 1, 2), new_rope.T
     latent_cache = pltpu.with_memory_space_constraint(latent_cache, pltpu.HBM)
 
-    def attention(sequence, length):
+    def attention(sequence, lengths, weight):
         return attend(
-            sequence, length, query_nope, query_rope, key_up, value_up, latent_cache, rope_keys, new_latent, new_rope_keys
+            weight, sequence, lengths, query_nope, query_rope, key_up, value_up, latent_cache, rope_keys, new_latent, new_rope_keys
         )
 
     above, below = shift(small, 1, -1), shift(small, 1, 1)
@@ -335,14 +336,14 @@
     far_low, far_high, above_high, below_low = lax.optimization_barrier((far_low, far_high, above_high, below_low))
     far_terms = expert_terms([far_low, far_high], weights)
     from_below, from_above = shift(far_terms[0], 2, 1), shift(far_terms[1], 2, -1)
-    far_terms, near_high, near_low, lengths = lax.optimization_barrier((far_terms, near_high, near_low, lengths))
-    first_attention = attention(0, lengths[:1])
-    from_below, from_above, first_attention, lengths = lax.optimization_barrier(
-        (from_below, from_above, first_attention, lengths)
+    far_terms, lengths = lax.optimization_barrier((far_terms, lengths))
+    first_attention = attention(0, lengths, SHORT)
+    from_below, from_above, near_high, near_low, first_attention, lengths = lax.optimization_barrier(
+        (from_below, from_above, near_high, near_low, first_attention, lengths)
     )
     from_below = shift(narrowed(added(above_low, from_below)), 2, 1)
     from_above = shift(narrowed(added(below_high, from_above)), 2, -1)
-    second_attention = attention(1, lengths[1:])
+    second_attention = attention(1, lengths, LONG)
     from_below, from_above, second_attention = lax.optimization_barrier((from_below, from_above, second_attention))
     low = added(own_terms[0], near_low, from_below)
     high = added(own_terms[1], near_high, from_above)

time: 132 us -> 132 us (level)
  Pallas kernels: 37.2 us -> 42.2 us
  waiting for transfers between devices: 47.7 us -> 44.3 us
    pallas_call x2, Pallas kernels: 17.2 us -> 22.1 us  [attend(): pl.pallas_call(functools.partial(attention_kernel, sequence), grid_spec=p...]
    ppermute x26, waiting for transfers between devices: 47.7 us -> 44.3 us  [shift(): return lax.ppermute(value, AXES, pairs)]
  transfers between devices with their start and end apart: 27 -> 27, of which waited for: 19 -> 18; matrix products, arithmetic and copies ran while one was open for 1% -> 1% of each run, Pallas kernels for 28% -> 31%
where the time goes in v7:
time: 132 us; the launch traced here: 131 us
  waiting for transfers between devices  44.3 us (34%)
  Pallas kernels  42.2 us (32%)
  starting transfers between devices  40.6 us (31%)
  other arithmetic  2.92 us (2%)
    ppermute x26, waiting for transfers between devices, shift(): return lax.ppermute(value, AXES, pairs)  44.3 us
    ppermute x26, starting transfers between devices, shift(): return lax.ppermute(value, AXES, pairs)  40.6 us
    pallas_call x2, Pallas kernels, attend(): pl.pallas_call(functools.partial(attention_kernel, sequence), grid_spec=p...  22.1 us
    pallas_call x4, Pallas kernels, expert_terms(): pl.pallas_call(functools.partial(expert_kernel, sources=len(pieces), outp...  14.7 us
    pallas_call x1, Pallas kernels, joined(): pl.pallas_call(join_kernel, in_specs=[pl.BlockSpec(memory_space=pl.ANY)]...  4.23 us
  transfers between devices with their start and end apart: 27, of which 18 were waited for; matrix products, arithmetic and copies ran while one was open for 1% of the time, Pallas kernels for 31%

profile of v7, /device:TPU:0, one launch (start us, length us, event | category | flops | bytes accessed | tf_op | source)
XLA Modules:
  0.0 131.3 jit_solution(9969929320346538042)
XLA Ops:
  0.6 1.1 pack.1
  1.7 4.2 %collective-permute-start = (bf16[8,7296]{1,0:T(8,128)(2,1)S(1)}, bf16[8,7296]{1,0:T(8,128)(2,1)S(1)}, u32[]{:S(2)}, u32[]{:S(2)}) collective-permute-start(bf16[8,7296]{1,0:T(8,128)(2,1)S(1)} %pack.1), channel_id=1, source_target_pairs={{0,96},{1,97},{2,98},{3,99},{4,100},{5,101},{6,102},{7,103},{8,104... | collective-permute-start | bytes 350216 | tf_op jit(solution)/shard_map/ppermute | solution.py:43
  5.9 1.3 collective-permute-start.2
  7.2 4.2 %join.1.refs_2_ = bf16[10752,512]{1,0:T(8,128)(2,1)S(1)} custom-call(bf16[7168,256]{1,0:T(8,128)(2,1)} %bitcast.9, bf16[7168,256]{1,0:T(8,128)(2,1)} %bitcast.10, bf16[256,7168]{1,0:T(8,128)(2,1)} %bitcast.11), custom_call_target="tpu_custom_call" | custom-call | bytes 22020096 | tf_op jit(solution)/shard_map/join/pallas_call | solution.py:142
  11.4 0.9 collective-permute-done.1
  12.4 0.9 collective-permute-done.2
  13.2 0.1 pad_maximum_fusion
  13.3 0.1 collective-permute-start.9
  13.4 1.6 %collective-permute-start.4 = (bf16[32,7296]{1,0:T(8,128)(2,1)S(1)}, bf16[32,7296]{1,0:T(8,128)(2,1)S(1)}, u32[]{:S(2)}, u32[]{:S(2)}) collective-permute-start(bf16[32,7296]{1,0:T(8,128)(2,1)S(1)} %pad_maximum_fusion), channel_id=1, source_target_pairs={{0,1},{1,2},{2,3},{3,0},{4,5},{5,6},{6,7},{7,4},{8,9},{9,10},{10,1... | collective-permute-start | bytes 1400840 | tf_op jit(solution)/shard_map/ppermute | solution.py:43
  15.0 1.7 %collective-permute-start.3 = (bf16[32,7296]{1,0:T(8,128)(2,1)S(1)}, bf16[32,7296]{1,0:T(8,128)(2,1)S(1)}, u32[]{:S(2)}, u32[]{:S(2)}) collective-permute-start(bf16[32,7296]{1,0:T(8,128)(2,1)S(1)} %pad_maximum_fusion), channel_id=1, source_target_pairs={{0,3},{1,0},{2,1},{3,2},{4,7},{5,4},{6,5},{7,6},{8,11},{9,8},{10,9... | collective-permute-start | bytes 1400840 | tf_op jit(solution)/shard_map/ppermute | solution.py:43
  16.7 6.5 %collective-permute-done.4 = bf16[32,7296]{1,0:T(8,128)(2,1)S(1)} collective-permute-done((bf16[32,7296]{1,0:T(8,128)(2,1)S(1)}, bf16[32,7296]{1,0:T(8,128)(2,1)S(1)}, u32[]{:S(2)}, u32[]{:S(2)}) %collective-permute-start.4) | collective-permute-done | bytes 466976 | tf_op jit(solution)/shard_map/ppermute | solution.py:43
  23.2 0.3 collective-permute-done.3
  23.6 1.6 %collective-permute-start.5 = (bf16[16,7296]{1,0:T(8,128)(2,1)S(1)}, bf16[16,7296]{1,0:T(8,128)(2,1)S(1)}, u32[]{:S(2)}, u32[]{:S(2)}) collective-permute-start(bf16[16,7296]{1,0:T(8,128)(2,1)S(1)} %slice.75), channel_id=1, source_target_pairs={{0,1},{1,2},{2,3},{3,0},{4,5},{5,6},{6,7},{7,4},{8,9},{9,10},{10,1... | collective-permute-start | bytes 700424 | tf_op jit(solution)/shard_map/ppermute | solution.py:43
  25.3 1.6 %collective-permute-start.7 = (bf16[64,7296]{1,0:T(8,128)(2,1)S(1)}, bf16[64,7296]{1,0:T(8,128)(2,1)S(1)}, u32[]{:S(2)}, u32[]{:S(2)}) collective-permute-start(bf16[64,7296]{1,0:T(8,128)(2,1)S(1)} %constant_dynamic-update-slice_fusion.refs_0_), channel_id=1, source_target_pairs={{0,4},{1,5},{2,6},{3,7},{4,8},{5,9},{6,10},{7,11},{8,12},{9,13},{1... | collective-permute-start | bytes 2801672 | tf_op jit(solution)/shard_map/ppermute | solution.py:43
  26.8 1.7 %collective-permute-start.8 = (bf16[64,7296]{1,0:T(8,128)(2,1)S(1)}, bf16[64,7296]{1,0:T(8,128)(2,1)S(1)}, u32[]{:S(2)}, u32[]{:S(2)}) collective-permute-start(bf16[64,7296]{1,0:T(8,128)(2,1)S(1)} %constant_dynamic-update-slice_fusion.refs_0_), channel_id=1, source_target_pairs={{0,12},{1,13},{2,14},{3,15},{4,0},{5,1},{6,2},{7,3},{8,4},{9,5},{1... | collective-permute-start | bytes 2801672 | tf_op jit(solution)/shard_map/ppermute | solution.py:43
  28.6 1.7 %collective-permute-start.6 = (bf16[16,7296]{1,0:T(8,128)(2,1)S(1)}, bf16[16,7296]{1,0:T(8,128)(2,1)S(1)}, u32[]{:S(2)}, u32[]{:S(2)}) collective-permute-start(bf16[16,7296]{1,0:T(8,128)(2,1)S(1)} %slice.76), channel_id=1, source_target_pairs={{0,3},{1,0},{2,1},{3,2},{4,7},{5,4},{6,5},{7,6},{8,11},{9,8},{10,9... | collective-permute-start | bytes 700424 | tf_op jit(solution)/shard_map/ppermute | solution.py:43
  30.2 3.3 %collective-permute-done.5 = bf16[16,7296]{1,0:T(8,128)(2,1)S(1)} collective-permute-done((bf16[16,7296]{1,0:T(8,128)(2,1)S(1)}, bf16[16,7296]{1,0:T(8,128)(2,1)S(1)}, u32[]{:S(2)}, u32[]{:S(2)}) %collective-permute-start.5) | collective-permute-done | bytes 233504 | tf_op jit(solution)/shard_map/ppermute | solution.py:43
  33.5 3.7 %collective-permute-done.6 = bf16[16,7296]{1,0:T(8,128)(2,1)S(1)} collective-permute-done((bf16[16,7296]{1,0:T(8,128)(2,1)S(1)}, bf16[16,7296]{1,0:T(8,128)(2,1)S(1)}, u32[]{:S(2)}, u32[]{:S(2)}) %collective-permute-start.6) | collective-permute-done | bytes 233504 | tf_op jit(solution)/shard_map/ppermute | solution.py:43
  37.3 1.6 %collective-permute-start.10 = (bf16[64,7296]{1,0:T(8,128)(2,1)S(1)}, bf16[64,7296]{1,0:T(8,128)(2,1)S(1)}, u32[]{:S(2)}, u32[]{:S(2)}) collective-permute-start(bf16[64,7296]{1,0:T(8,128)(2,1)S(1)} %constant_dynamic-update-slice_fusion.2.refs_1_), channel_id=1, source_target_pairs={{0,12},{1,13},{2,14},{3,15},{4,0},{5,1},{6,2},{7,3},{8,4},{9,5},{1... | collective-permute-start | bytes 2801672 | tf_op jit(solution)/shard_map/ppermute | solution.py:43
  38.9 0.5 collective-permute-start.13
  39.4 0.7 collective-permute-done.7.refs_1_
  40.1 0.3 collective-permute-done.8.refs_0_
  40.4 3.7 %expert.4 = (bf16[64,7168]{1,0:T(8,128)(2,1)S(1)}, bf16[64,7168]{1,0:T(8,128)(2,1)S(1)}) custom-call(bf16[64,7296]{1,0:T(8,128)(2,1)S(1)} %constant_dynamic-update-slice_fusion.refs_0_, bf16[64,7296]{1,0:T(8,128)(2,1)S(1)} %constant_dynamic-update-slice_fusion.2.refs_1_, bf16[10752,512]{1,0:T(8,128)(2,1)S(1)} %join.1.refs_2_, ...), custom_call_target="tpu_custom_call" | custom-call | flops 2818572288 | bytes 3670016 | tf_op jit(solution)/shard_map/expert/pallas_call | solution.py:104
  44.1 3.7 %expert.5 = (bf16[64,7168]{1,0:T(8,128)(2,1)S(1)}, bf16[64,7168]{1,0:T(8,128)(2,1)S(1)}) custom-call(bf16[64,7296]{1,0:T(8,128)(2,1)S(1)} %collective-permute-done.8.refs_0_, bf16[64,7296]{1,0:T(8,128)(2,1)S(1)} %collective-permute-done.7.refs_1_, bf16[10752,512]{1,0:T(8,128)(2,1)S(1)} %join.1.refs_2_, bf16[10752,512]{1,0:T(8,128)(2,1)S(1)} %collective-permute-done.9.refs_3_), custom_call_target="tpu_custom_call" | custom-call | flops 2818572288 | bytes 3670016 | tf_op jit(solution)/shard_map/expert/pallas_call | solution.py:104
  47.8 3.1 %collective-permute-done.10.refs_0_ = bf16[64,7296]{1,0:T(8,128)(2,1)S(1)} collective-permute-done((bf16[64,7296]{1,0:T(8,128)(2,1)S(1)}, bf16[64,7296]{1,0:T(8,128)(2,1)S(1)}, u32[]{:S(2)}, u32[]{:S(2)}) %collective-permute-start.10) | collective-permute-done | bytes 933920 | tf_op jit(solution)/shard_map/ppermute | solution.py:43
  50.9 1.0 collective-permute-start.11
  51.9 2.3 %collective-permute-start.12 = (bf16[64,7296]{1,0:T(8,128)(2,1)S(1)}, bf16[64,7296]{1,0:T(8,128)(2,1)S(1)}, u32[]{:S(2)}, u32[]{:S(2)}) collective-permute-start(bf16[64,7296]{1,0:T(8,128)(2,1)S(1)} %collective-permute-done.10.refs_0_), channel_id=1, source_target_pairs={{0,12},{1,13},{2,14},{3,15},{4,0},{5,1},{6,2},{7,3},{8,4},{9,5},{1... | collective-permute-start | bytes 2801672 | tf_op jit(solution)/shard_map/ppermute | solution.py:43
  54.2 3.7 %expert.6 = (bf16[64,7168]{1,0:T(8,128)(2,1)S(1)}, bf16[64,7168]{1,0:T(8,128)(2,1)S(1)}) custom-call(bf16[64,7296]{1,0:T(8,128)(2,1)S(1)} %collective-permute-done.10.refs_0_, bf16[64,7296]{1,0:T(8,128)(2,1)S(1)} %collective-permute-done.13.refs_1_, bf16[10752,512]{1,0:T(8,128)(2,1)S(1)} %join.1.refs_2_, bf16[10752,512]{1,0:T(8,128)(2,1)S(1)} %collective-permute-done.9.refs_3_), custom_call_target="tpu_custom_call" | custom-call | flops 2818572288 | bytes 3670016 | tf_op jit(solution)/shard_map/expert/pallas_call | solution.py:104
  57.9 0.1 collective-permute-start.16
  58.0 3.2 %collective-permute-start.17 = (bf16[64,7168]{1,0:T(8,128)(2,1)S(1)}, bf16[64,7168]{1,0:T(8,128)(2,1)S(1)}, u32[]{:S(2)}, u32[]{:S(2)}) collective-permute-start(bf16[64,7168]{1,0:T(8,128)(2,1)S(1)} %get-tuple-element.68), channel_id=1, source_target_pairs={{0,12},{1,13},{2,14},{3,15},{4,0},{5,1},{6,2},{7,3},{8,4},{9,5},{1... | collective-permute-start | bytes 2752520 | tf_op jit(solution)/shard_map/ppermute | solution.py:43
  61.2 4.5 %collective-permute-done.11.refs_0_ = bf16[64,7296]{1,0:T(8,128)(2,1)S(1)} collective-permute-done((bf16[64,7296]{1,0:T(8,128)(2,1)S(1)}, bf16[64,7296]{1,0:T(8,128)(2,1)S(1)}, u32[]{:S(2)}, u32[]{:S(2)}) %collective-permute-start.11) | collective-permute-done | bytes 933920 | tf_op jit(solution)/shard_map/ppermute | solution.py:43
  65.7 3.7 %expert.7 = (bf16[64,7168]{1,0:T(8,128)(2,1)S(1)}, bf16[64,7168]{1,0:T(8,128)(2,1)S(1)}) custom-call(bf16[64,7296]{1,0:T(8,128)(2,1)S(1)} %collective-permute-done.11.refs_0_, bf16[64,7296]{1,0:T(8,128)(2,1)S(1)} %collective-permute-done.12.refs_1_, bf16[10752,512]{1,0:T(8,128)(2,1)S(1)} %join.1.refs_2_, bf16[10752,512]{1,0:T(8,128)(2,1)S(1)} %collective-permute-done.9.refs_3_), custom_call_target="tpu_custom_call" | custom-call | flops 2818572288 | bytes 3670016 | tf_op jit(solution)/shard_map/expert/pallas_call | solution.py:104
  69.4 1.0 collective-permute-start.14
  70.4 2.3 %collective-permute-start.15 = (bf16[64,7168]{1,0:T(8,128)(2,1)S(1)}, bf16[64,7168]{1,0:T(8,128)(2,1)S(1)}, u32[]{:S(2)}, u32[]{:S(2)}) collective-permute-start(bf16[64,7168]{1,0:T(8,128)(2,1)S(1)} %get-tuple-element.72), channel_id=1, source_target_pairs={{0,12},{1,13},{2,14},{3,15},{4,0},{5,1},{6,2},{7,3},{8,4},{9,5},{1... | collective-permute-start | bytes 2752520 | tf_op jit(solution)/shard_map/ppermute | solution.py:43
  72.8 13.5 %attend.2 = bf16[64,1024]{1,0:T(8,128)(2,1)S(1)} custom-call(s32[2]{0:T(128)S(1)} %copy-done.7, bf16[128,1024]{1,0:T(8,128)(2,1)S(1)} %copy-done.3, bf16[128,512]{1,0:T(8,128)(2,1)S(1)} %copy-done.4, bf16[8,128,512]{2,1,0:T(8,128)(2,1)S(1)} %copy-done, bf16[8,512,128]{2,1,0:T(8,128)(2,1)S(1)} %copy-done.1, bf16[2,4096,512]{2,1,0:T(8,128)(2,1)} %latent_ref.3, ...), custom_call_target="tpu_custom_call" | custom-call | flops 100000000 | bytes 133333 | tf_op jit(solution)/shard_map/attend/pallas_call | solution.py:254
  86.4 0.2 add_convert_fusion
  86.6 2.3 %collective-permute-start.19 = (bf16[64,7168]{1,0:T(8,128)(2,1)S(1)}, bf16[64,7168]{1,0:T(8,128)(2,1)S(1)}, u32[]{:S(2)}, u32[]{:S(2)}) collective-permute-start(bf16[64,7168]{1,0:T(8,128)(2,1)S(1)} %add_convert_fusion), channel_id=1, source_target_pairs={{0,12},{1,13},{2,14},{3,15},{4,0},{5,1},{6,2},{7,3},{8,4},{9,5},{1... | collective-permute-start | bytes 2752520 | tf_op jit(solution)/shard_map/ppermute | solution.py:43
  88.9 0.2 add_convert_fusion.1
  89.1 0.3 collective-permute-start.18
  89.4 8.6 %attend.3 = bf16[64,1024]{1,0:T(8,128)(2,1)S(1)} custom-call(s32[2]{0:T(128)S(1)} %copy-done.7, bf16[128,1024]{1,0:T(8,128)(2,1)S(1)} %copy-done.3, bf16[128,512]{1,0:T(8,128)(2,1)S(1)} %copy-done.4, bf16[8,128,512]{2,1,0:T(8,128)(2,1)S(1)} %copy-done, bf16[8,512,128]{2,1,0:T(8,128)(2,1)S(1)} %copy-done.1, bf16[2,4096,512]{2,1,0:T(8,128)(2,1)} %latent_ref.3, ...), custom_call_target="tpu_custom_call" | custom-call | flops 6000000000 | bytes 8000000 | tf_op jit(solution)/shard_map/attend/pallas_call | solution.py:254
  98.1 2.0 %collective-permute-done.19 = bf16[64,7168]{1,0:T(8,128)(2,1)S(1)} collective-permute-done((bf16[64,7168]{1,0:T(8,128)(2,1)S(1)}, bf16[64,7168]{1,0:T(8,128)(2,1)S(1)}, u32[]{:S(2)}, u32[]{:S(2)}) %collective-permute-start.19) | collective-permute-done | bytes 917536 | tf_op jit(solution)/shard_map/ppermute | solution.py:43
  100.1 3.9 %collective-permute-done.18 = bf16[64,7168]{1,0:T(8,128)(2,1)S(1)} collective-permute-done((bf16[64,7168]{1,0:T(8,128)(2,1)S(1)}, bf16[64,7168]{1,0:T(8,128)(2,1)S(1)}, u32[]{:S(2)}, u32[]{:S(2)}) %collective-permute-start.18) | collective-permute-done | bytes 917536 | tf_op jit(solution)/shard_map/ppermute | solution.py:43
  104.0 0.3 fusion.3
  104.4 0.3 convert_add_fusion.1
  104.8 1.3 %collective-permute-start.20 = (bf16[32,7168]{1,0:T(8,128)(2,1)S(1)}, bf16[32,7168]{1,0:T(8,128)(2,1)S(1)}, u32[]{:S(2)}, u32[]{:S(2)}) collective-permute-start(bf16[32,7168]{1,0:T(8,128)(2,1)S(1)} %pad_maximum_fusion.1), channel_id=1, source_target_pairs={{0,1},{1,2},{2,3},{3,0},{4,5},{5,6},{6,7},{7,4},{8,9},{9,10},{10,1... | collective-permute-start | bytes 1376264 | tf_op jit(solution)/shard_map/ppermute | solution.py:43
  106.1 2.0 %collective-permute-start.21 = (bf16[32,7168]{1,0:T(8,128)(2,1)S(1)}, bf16[32,7168]{1,0:T(8,128)(2,1)S(1)}, u32[]{:S(2)}, u32[]{:S(2)}) collective-permute-start(bf16[32,7168]{1,0:T(8,128)(2,1)S(1)} %concatenate.29), channel_id=1, source_target_pairs={{0,3},{1,0},{2,1},{3,2},{4,7},{5,4},{6,5},{7,6},{8,11},{9,8},{10,9... | collective-permute-start | bytes 1376264 | tf_op jit(solution)/shard_map/ppermute | solution.py:43
  108.2 6.3 %collective-permute-done.20 = bf16[32,7168]{1,0:T(8,128)(2,1)S(1)} collective-permute-done((bf16[32,7168]{1,0:T(8,128)(2,1)S(1)}, bf16[32,7168]{1,0:T(8,128)(2,1)S(1)}, u32[]{:S(2)}, u32[]{:S(2)}) %collective-permute-start.20) | collective-permute-done | bytes 458784 | tf_op jit(solution)/shard_map/ppermute | solution.py:43
  114.5 0.1 fusion.2
  114.6 0.1 collective-permute-done.21
  114.7 0.1 fusion.1
  114.7 1.5 %collective-permute-start.22 = (bf16[16,7168]{1,0:T(8,128)(2,1)S(1)}, bf16[16,7168]{1,0:T(8,128)(2,1)S(1)}, u32[]{:S(2)}, u32[]{:S(2)}) collective-permute-start(bf16[16,7168]{1,0:T(8,128)(2,1)S(1)} %fusion.2), channel_id=1, source_target_pairs={{0,1},{1,2},{2,3},{3,0},{4,5},{5,6},{6,7},{7,4},{8,9},{9,10},{10,1... | collective-permute-start | bytes 688136 | tf_op jit(solution)/shard_map/ppermute | solution.py:43
  116.2 1.8 %collective-permute-start.23 = (bf16[16,7168]{1,0:T(8,128)(2,1)S(1)}, bf16[16,7168]{1,0:T(8,128)(2,1)S(1)}, u32[]{:S(2)}, u32[]{:S(2)}) collective-permute-start(bf16[16,7168]{1,0:T(8,128)(2,1)S(1)} %fusion.1), channel_id=1, source_target_pairs={{0,3},{1,0},{2,1},{3,2},{4,7},{5,4},{6,5},{7,6},{8,11},{9,8},{10,9... | collective-permute-start | bytes 688136 | tf_op jit(solution)/shard_map/ppermute | solution.py:43
  118.1 4.0 %collective-permute-done.22 = bf16[16,7168]{1,0:T(8,128)(2,1)S(1)} collective-permute-done((bf16[16,7168]{1,0:T(8,128)(2,1)S(1)}, bf16[16,7168]{1,0:T(8,128)(2,1)S(1)}, u32[]{:S(2)}, u32[]{:S(2)}) %collective-permute-start.22) | collective-permute-done | bytes 229408 | tf_op jit(solution)/shard_map/ppermute | solution.py:43
  122.0 0.1 convert_add_fusion.3
  122.1 0.2 collective-permute-done.23
  122.3 0.1 convert_add_fusion.2
  122.3 0.1 fusion
  122.5 0.5 collective-permute-start.24
  123.0 2.4 %collective-permute-start.25 = (bf16[8,7168]{1,0:T(8,128)(2,1)S(1)}, bf16[8,7168]{1,0:T(8,128)(2,1)S(1)}, u32[]{:S(2)}, u32[]{:S(2)}) collective-permute-start(bf16[8,7168]{1,0:T(8,128)(2,1)S(1)} %get-tuple-element.92), channel_id=1, source_target_pairs={{0,64},{1,65},{2,66},{3,67},{4,68},{5,69},{6,70},{7,71},{8,72},{9,... | collective-permute-start | bytes 344072 | tf_op jit(solution)/shard_map/ppermute | solution.py:43
  125.4 1.0 collective-permute-start.26
  126.4 0.7 pad_maximum_fusion.2
  127.1 2.7 %collective-permute-done.24 = bf16[8,7168]{1,0:T(8,128)(2,1)S(1)} collective-permute-done((bf16[8,7168]{1,0:T(8,128)(2,1)S(1)}, bf16[8,7168]{1,0:T(8,128)(2,1)S(1)}, u32[]{:S(2)}, u32[]{:S(2)}) %collective-permute-start.24) | collective-permute-done | bytes 114720 | tf_op jit(solution)/shard_map/ppermute | solution.py:43
  129.8 0.9 collective-permute-done.26
  130.6 0.7 add_convert_fusion.2
  (38 shorter events, 0.4 us)
Async XLA Ops:
  1.7 9.7 %collective-permute-start = (bf16[8,7296]{1,0:T(8,128)(2,1)S(1)}, bf16[8,7296]{1,0:T(8,128)(2,1)S(1)}, u32[]{:S(2)}, u32[]{:S(2)}) collective-permute-start(bf16[8,7296]{1,0:T(8,128)(2,1)S(1)} %pack.1), channel_id=1, source_target_pairs={{0,96},{1,97},{2,98},{3,99},{4,100},{5,101},{6,102},{7,103},{8,104... | collective-permute-start | bytes 350216 | tf_op jit(solution)/shard_map/ppermute | solution.py:43
  5.9 6.4 %collective-permute-start.1 = (bf16[8,7296]{1,0:T(8,128)(2,1)S(1)}, bf16[8,7296]{1,0:T(8,128)(2,1)S(1)}, u32[]{:S(2)}, u32[]{:S(2)}) collective-permute-start(bf16[8,7296]{1,0:T(8,128)(2,1)S(1)} %pack.1), channel_id=1, source_target_pairs={{0,64},{1,65},{2,66},{3,67},{4,68},{5,69},{6,70},{7,71},{8,72},{9,... | collective-permute-start | bytes 350216 | tf_op jit(solution)/shard_map/ppermute | solution.py:43
  5.9 7.3 %collective-permute-start.2 = (bf16[8,7296]{1,0:T(8,128)(2,1)S(1)}, bf16[8,7296]{1,0:T(8,128)(2,1)S(1)}, u32[]{:S(2)}, u32[]{:S(2)}) collective-permute-start(bf16[8,7296]{1,0:T(8,128)(2,1)S(1)} %pack.1), channel_id=1, source_target_pairs={{0,32},{1,33},{2,34},{3,35},{4,36},{5,37},{6,38},{7,39},{8,40},{9,... | collective-permute-start | bytes 350216 | tf_op jit(solution)/shard_map/ppermute | solution.py:43
  13.3 27.1 %collective-permute-start.9 = (bf16[10752,512]{1,0:T(8,128)(2,1)S(1)}, bf16[10752,512]{1,0:T(8,128)(2,1)S(1)}, u32[]{:S(2)}, u32[]{:S(2)}) collective-permute-start(bf16[10752,512]{1,0:T(8,128)(2,1)S(1)} %join.1.refs_2_), channel_id=1, source_target_pairs={{0,16},{16,0},{1,17},{17,1},{2,18},{18,2},{3,19},{19,3},{4,20},{20... | collective-permute-start | bytes 33030152 | tf_op jit(solution)/shard_map/ppermute | solution.py:59
  13.4 9.8 %collective-permute-start.4 = (bf16[32,7296]{1,0:T(8,128)(2,1)S(1)}, bf16[32,7296]{1,0:T(8,128)(2,1)S(1)}, u32[]{:S(2)}, u32[]{:S(2)}) collective-permute-start(bf16[32,7296]{1,0:T(8,128)(2,1)S(1)} %pad_maximum_fusion), channel_id=1, source_target_pairs={{0,1},{1,2},{2,3},{3,0},{4,5},{5,6},{6,7},{7,4},{8,9},{9,10},{10,1... | collective-permute-start | bytes 1400840 | tf_op jit(solution)/shard_map/ppermute | solution.py:43
  15.0 8.6 %collective-permute-start.3 = (bf16[32,7296]{1,0:T(8,128)(2,1)S(1)}, bf16[32,7296]{1,0:T(8,128)(2,1)S(1)}, u32[]{:S(2)}, u32[]{:S(2)}) collective-permute-start(bf16[32,7296]{1,0:T(8,128)(2,1)S(1)} %pad_maximum_fusion), channel_id=1, source_target_pairs={{0,3},{1,0},{2,1},{3,2},{4,7},{5,4},{6,5},{7,6},{8,11},{9,8},{10,9... | collective-permute-start | bytes 1400840 | tf_op jit(solution)/shard_map/ppermute | solution.py:43
  23.6 9.9 %collective-permute-start.5 = (bf16[16,7296]{1,0:T(8,128)(2,1)S(1)}, bf16[16,7296]{1,0:T(8,128)(2,1)S(1)}, u32[]{:S(2)}, u32[]{:S(2)}) collective-permute-start(bf16[16,7296]{1,0:T(8,128)(2,1)S(1)} %slice.75), channel_id=1, source_target_pairs={{0,1},{1,2},{2,3},{3,0},{4,5},{5,6},{6,7},{7,4},{8,9},{9,10},{10,1... | collective-permute-start | bytes 700424 | tf_op jit(solution)/shard_map/ppermute | solution.py:43
  25.3 14.8 %collective-permute-start.7 = (bf16[64,7296]{1,0:T(8,128)(2,1)S(1)}, bf16[64,7296]{1,0:T(8,128)(2,1)S(1)}, u32[]{:S(2)}, u32[]{:S(2)}) collective-permute-start(bf16[64,7296]{1,0:T(8,128)(2,1)S(1)} %constant_dynamic-update-slice_fusion.refs_0_), channel_id=1, source_target_pairs={{0,4},{1,5},{2,6},{3,7},{4,8},{5,9},{6,10},{7,11},{8,12},{9,13},{1... | collective-permute-start | bytes 2801672 | tf_op jit(solution)/shard_map/ppermute | solution.py:43
  26.8 13.6 %collective-permute-start.8 = (bf16[64,7296]{1,0:T(8,128)(2,1)S(1)}, bf16[64,7296]{1,0:T(8,128)(2,1)S(1)}, u32[]{:S(2)}, u32[]{:S(2)}) collective-permute-start(bf16[64,7296]{1,0:T(8,128)(2,1)S(1)} %constant_dynamic-update-slice_fusion.refs_0_), channel_id=1, source_target_pairs={{0,12},{1,13},{2,14},{3,15},{4,0},{5,1},{6,2},{7,3},{8,4},{9,5},{1... | collective-permute-start | bytes 2801672 | tf_op jit(solution)/shard_map/ppermute | solution.py:43
  28.6 8.6 %collective-permute-start.6 = (bf16[16,7296]{1,0:T(8,128)(2,1)S(1)}, bf16[16,7296]{1,0:T(8,128)(2,1)S(1)}, u32[]{:S(2)}, u32[]{:S(2)}) collective-permute-start(bf16[16,7296]{1,0:T(8,128)(2,1)S(1)} %slice.76), channel_id=1, source_target_pairs={{0,3},{1,0},{2,1},{3,2},{4,7},{5,4},{6,5},{7,6},{8,11},{9,8},{10,9... | collective-permute-start | bytes 700424 | tf_op jit(solution)/shard_map/ppermute | solution.py:43
  37.3 13.6 %collective-permute-start.10 = (bf16[64,7296]{1,0:T(8,128)(2,1)S(1)}, bf16[64,7296]{1,0:T(8,128)(2,1)S(1)}, u32[]{:S(2)}, u32[]{:S(2)}) collective-permute-start(bf16[64,7296]{1,0:T(8,128)(2,1)S(1)} %constant_dynamic-update-slice_fusion.2.refs_1_), channel_id=1, source_target_pairs={{0,12},{1,13},{2,14},{3,15},{4,0},{5,1},{6,2},{7,3},{8,4},{9,5},{1... | collective-permute-start | bytes 2801672 | tf_op jit(solution)/shard_map/ppermute | solution.py:43
  38.9 15.3 %collective-permute-start.13 = (bf16[64,7296]{1,0:T(8,128)(2,1)S(1)}, bf16[64,7296]{1,0:T(8,128)(2,1)S(1)}, u32[]{:S(2)}, u32[]{:S(2)}) collective-permute-start(bf16[64,7296]{1,0:T(8,128)(2,1)S(1)} %constant_dynamic-update-slice_fusion.2.refs_1_), channel_id=1, source_target_pairs={{0,4},{1,5},{2,6},{3,7},{4,8},{5,9},{6,10},{7,11},{8,12},{9,13},{1... | collective-permute-start | bytes 2801672 | tf_op jit(solution)/shard_map/ppermute | solution.py:43
  50.9 14.8 %collective-permute-start.11 = (bf16[64,7296]{1,0:T(8,128)(2,1)S(1)}, bf16[64,7296]{1,0:T(8,128)(2,1)S(1)}, u32[]{:S(2)}, u32[]{:S(2)}) collective-permute-start(bf16[64,7296]{1,0:T(8,128)(2,1)S(1)} %collective-permute-done.7.refs_1_), channel_id=1, source_target_pairs={{0,4},{1,5},{2,6},{3,7},{4,8},{5,9},{6,10},{7,11},{8,12},{9,13},{1... | collective-permute-start | bytes 2801672 | tf_op jit(solution)/shard_map/ppermute | solution.py:43
  51.9 13.8 %collective-permute-start.12 = (bf16[64,7296]{1,0:T(8,128)(2,1)S(1)}, bf16[64,7296]{1,0:T(8,128)(2,1)S(1)}, u32[]{:S(2)}, u32[]{:S(2)}) collective-permute-start(bf16[64,7296]{1,0:T(8,128)(2,1)S(1)} %collective-permute-done.10.refs_0_), channel_id=1, source_target_pairs={{0,12},{1,13},{2,14},{3,15},{4,0},{5,1},{6,2},{7,3},{8,4},{9,5},{1... | collective-permute-start | bytes 2801672 | tf_op jit(solution)/shard_map/ppermute | solution.py:43
  57.8 14.9 %copy-start = (bf16[8,128,512]{2,1,0:T(8,128)(2,1)S(1)}, bf16[8,128,512]{2,1,0:T(8,128)(2,1)}, u32[]{:S(2)}) copy-start(bf16[8,128,512]{2,1,0:T(8,128)(2,1)} %key_up_ref.3) | copy-start | bytes 3145732
  57.9 14.9 %copy-start.1 = (bf16[8,512,128]{2,1,0:T(8,128)(2,1)S(1)}, bf16[8,512,128]{2,1,0:T(8,128)(2,1)}, u32[]{:S(2)}) copy-start(bf16[8,512,128]{2,1,0:T(8,128)(2,1)} %value_up_ref.3) | copy-start | bytes 3145732
  57.9 14.9 %copy-start.2 = (bf16[2,4096,64]{1,2,0:T(8,128)(2,1)S(1)}, bf16[2,4096,64]{1,2,0:T(8,128)(2,1)}, u32[]{:S(2)}) copy-start(bf16[2,4096,64]{1,2,0:T(8,128)(2,1)} %param.26) | copy-start | bytes 3145732
  57.9 14.9 %copy-start.3 = (bf16[128,1024]{1,0:T(8,128)(2,1)S(1)}, bf16[128,1024]{1,0:T(8,128)(2,1)}, u32[]{:S(2)}) copy-start(bf16[128,1024]{1,0:T(8,128)(2,1)} %nope_ref.3) | copy-start | bytes 786436
  57.9 14.9 %copy-start.4 = (bf16[128,512]{1,0:T(8,128)(2,1)S(1)}, bf16[128,512]{1,0:T(8,128)(2,1)}, u32[]{:S(2)}) copy-start(bf16[128,512]{1,0:T(8,128)(2,1)} %rope_ref.3) | copy-start | bytes 393220
  57.9 14.9 %copy-start.5 = (bf16[128,512]{1,0:T(8,128)(2,1)S(1)}, bf16[128,512]{1,0:T(8,128)(2,1)}, u32[]{:S(2)}) copy-start(bf16[128,512]{1,0:T(8,128)(2,1)} %new_latent_ref.3) | copy-start | bytes 393220
  57.9 14.9 %copy-start.6 = (bf16[128,64]{0,1:T(8,128)(2,1)S(1)}, bf16[128,64]{0,1:T(8,128)(2,1)}, u32[]{:S(2)}) copy-start(bf16[128,64]{0,1:T(8,128)(2,1)} %param.28) | copy-start | bytes 49156
  57.9 14.9 %copy-start.7 = (s32[2]{0:T(128)S(1)}, s32[2]{0:T(128)}, u32[]{:S(2)}) copy-start(s32[2]{0:T(128)} %length_ref.1) | copy-start | bytes 28
  57.9 28.4 %collective-permute-start.16 = (bf16[64,7168]{1,0:T(8,128)(2,1)S(1)}, bf16[64,7168]{1,0:T(8,128)(2,1)S(1)}, u32[]{:S(2)}, u32[]{:S(2)}) collective-permute-start(bf16[64,7168]{1,0:T(8,128)(2,1)S(1)} %get-tuple-element.67), channel_id=1, source_target_pairs={{0,4},{1,5},{2,6},{3,7},{4,8},{5,9},{6,10},{7,11},{8,12},{9,13},{1... | collective-permute-start | bytes 2752520 | tf_op jit(solution)/shard_map/ppermute | solution.py:43
  58.0 28.3 %collective-permute-start.17 = (bf16[64,7168]{1,0:T(8,128)(2,1)S(1)}, bf16[64,7168]{1,0:T(8,128)(2,1)S(1)}, u32[]{:S(2)}, u32[]{:S(2)}) collective-permute-start(bf16[64,7168]{1,0:T(8,128)(2,1)S(1)} %get-tuple-element.68), channel_id=1, source_target_pairs={{0,12},{1,13},{2,14},{3,15},{4,0},{5,1},{6,2},{7,3},{8,4},{9,5},{1... | collective-permute-start | bytes 2752520 | tf_op jit(solution)/shard_map/ppermute | solution.py:43
  69.4 17.0 %collective-permute-start.14 = (bf16[64,7168]{1,0:T(8,128)(2,1)S(1)}, bf16[64,7168]{1,0:T(8,128)(2,1)S(1)}, u32[]{:S(2)}, u32[]{:S(2)}) collective-permute-start(bf16[64,7168]{1,0:T(8,128)(2,1)S(1)} %get-tuple-element.71), channel_id=1, source_target_pairs={{0,4},{1,5},{2,6},{3,7},{4,8},{5,9},{6,10},{7,11},{8,12},{9,13},{1... | collective-permute-start | bytes 2752520 | tf_op jit(solution)/shard_map/ppermute | solution.py:43
  70.4 15.9 %collective-permute-start.15 = (bf16[64,7168]{1,0:T(8,128)(2,1)S(1)}, bf16[64,7168]{1,0:T(8,128)(2,1)S(1)}, u32[]{:S(2)}, u32[]{:S(2)}) collective-permute-start(bf16[64,7168]{1,0:T(8,128)(2,1)S(1)} %get-tuple-element.72), channel_id=1, source_target_pairs={{0,12},{1,13},{2,14},{3,15},{4,0},{5,1},{6,2},{7,3},{8,4},{9,5},{1... | collective-permute-start | bytes 2752520 | tf_op jit(solution)/shard_map/ppermute | solution.py:43
  86.6 13.5 %collective-permute-start.19 = (bf16[64,7168]{1,0:T(8,128)(2,1)S(1)}, bf16[64,7168]{1,0:T(8,128)(2,1)S(1)}, u32[]{:S(2)}, u32[]{:S(2)}) collective-permute-start(bf16[64,7168]{1,0:T(8,128)(2,1)S(1)} %add_convert_fusion), channel_id=1, source_target_pairs={{0,12},{1,13},{2,14},{3,15},{4,0},{5,1},{6,2},{7,3},{8,4},{9,5},{1... | collective-permute-start | bytes 2752520 | tf_op jit(solution)/shard_map/ppermute | solution.py:43
  89.1 14.9 %collective-permute-start.18 = (bf16[64,7168]{1,0:T(8,128)(2,1)S(1)}, bf16[64,7168]{1,0:T(8,128)(2,1)S(1)}, u32[]{:S(2)}, u32[]{:S(2)}) collective-permute-start(bf16[64,7168]{1,0:T(8,128)(2,1)S(1)} %add_convert_fusion.1), channel_id=1, source_target_pairs={{0,4},{1,5},{2,6},{3,7},{4,8},{5,9},{6,10},{7,11},{8,12},{9,13},{1... | collective-permute-start | bytes 2752520 | tf_op jit(solution)/shard_map/ppermute | solution.py:43
  104.8 9.8 %collective-permute-start.20 = (bf16[32,7168]{1,0:T(8,128)(2,1)S(1)}, bf16[32,7168]{1,0:T(8,128)(2,1)S(1)}, u32[]{:S(2)}, u32[]{:S(2)}) collective-permute-start(bf16[32,7168]{1,0:T(8,128)(2,1)S(1)} %pad_maximum_fusion.1), channel_id=1, source_target_pairs={{0,1},{1,2},{2,3},{3,0},{4,5},{5,6},{6,7},{7,4},{8,9},{9,10},{10,1... | collective-permute-start | bytes 1376264 | tf_op jit(solution)/shard_map/ppermute | solution.py:43
  106.1 8.5 %collective-permute-start.21 = (bf16[32,7168]{1,0:T(8,128)(2,1)S(1)}, bf16[32,7168]{1,0:T(8,128)(2,1)S(1)}, u32[]{:S(2)}, u32[]{:S(2)}) collective-permute-start(bf16[32,7168]{1,0:T(8,128)(2,1)S(1)} %concatenate.29), channel_id=1, source_target_pairs={{0,3},{1,0},{2,1},{3,2},{4,7},{5,4},{6,5},{7,6},{8,11},{9,8},{10,9... | collective-permute-start | bytes 1376264 | tf_op jit(solution)/shard_map/ppermute | solution.py:43
  114.7 7.3 %collective-permute-start.22 = (bf16[16,7168]{1,0:T(8,128)(2,1)S(1)}, bf16[16,7168]{1,0:T(8,128)(2,1)S(1)}, u32[]{:S(2)}, u32[]{:S(2)}) collective-permute-start(bf16[16,7168]{1,0:T(8,128)(2,1)S(1)} %fusion.2), channel_id=1, source_target_pairs={{0,1},{1,2},{2,3},{3,0},{4,5},{5,6},{6,7},{7,4},{8,9},{9,10},{10,1... | collective-permute-start | bytes 688136 | tf_op jit(solution)/shard_map/ppermute | solution.py:43
  116.2 6.0 %collective-permute-start.23 = (bf16[16,7168]{1,0:T(8,128)(2,1)S(1)}, bf16[16,7168]{1,0:T(8,128)(2,1)S(1)}, u32[]{:S(2)}, u32[]{:S(2)}) collective-permute-start(bf16[16,7168]{1,0:T(8,128)(2,1)S(1)} %fusion.1), channel_id=1, source_target_pairs={{0,3},{1,0},{2,1},{3,2},{4,7},{5,4},{6,5},{7,6},{8,11},{9,8},{10,9... | collective-permute-start | bytes 688136 | tf_op jit(solution)/shard_map/ppermute | solution.py:43
  122.5 7.3 %collective-permute-start.24 = (bf16[8,7168]{1,0:T(8,128)(2,1)S(1)}, bf16[8,7168]{1,0:T(8,128)(2,1)S(1)}, u32[]{:S(2)}, u32[]{:S(2)}) collective-permute-start(bf16[8,7168]{1,0:T(8,128)(2,1)S(1)} %get-tuple-element.90), channel_id=1, source_target_pairs={{0,32},{1,33},{2,34},{3,35},{4,36},{5,37},{6,38},{7,39},{8,40},{9,... | collective-permute-start | bytes 344072 | tf_op jit(solution)/shard_map/ppermute | solution.py:43
  123.0 6.8 %collective-permute-start.25 = (bf16[8,7168]{1,0:T(8,128)(2,1)S(1)}, bf16[8,7168]{1,0:T(8,128)(2,1)S(1)}, u32[]{:S(2)}, u32[]{:S(2)}) collective-permute-start(bf16[8,7168]{1,0:T(8,128)(2,1)S(1)} %get-tuple-element.92), channel_id=1, source_target_pairs={{0,64},{1,65},{2,66},{3,67},{4,68},{5,69},{6,70},{7,71},{8,72},{9,... | collective-permute-start | bytes 344072 | tf_op jit(solution)/shard_map/ppermute | solution.py:43
  125.4 5.3 %collective-permute-start.26 = (bf16[8,7168]{1,0:T(8,128)(2,1)S(1)}, bf16[8,7168]{1,0:T(8,128)(2,1)S(1)}, u32[]{:S(2)}, u32[]{:S(2)}) collective-permute-start(bf16[8,7168]{1,0:T(8,128)(2,1)S(1)} %get-tuple-element.91), channel_id=1, source_target_pairs={{0,96},{1,97},{2,98},{3,99},{4,100},{5,101},{6,102},{7,103},{8,104... | collective-permute-start | bytes 344072 | tf_op jit(solution)/shard_map/ppermute | solution.py:43

commit v8 on v7

--- a/solution.py
+++ b/solution.py
@@ -28,7 +28,7 @@
 KEY_BLOCK = 1024
 HEAD_COUNT = 8
 SHORT, LONG = 60, 1
-PARTS = 4
+PARTS = 2
 LATENT = 512
 LOG2E = 1.4426950408889634
 
@@ -319,9 +319,10 @@
     above, below = shift(small, 1, -1), shift(small, 1, 1)
     half = small.shape[0] // 2
     own_low = jnp.concatenate([small, above], axis=0)
-    below_low, above_low = shift(own_low, 2, 1), shift(own_low, 2, -1)
     far_low, far_high = lax.optimization_barrier((below[:half], above[half:]))
     far_low, far_high = shift(far_low, 1, 1), shift(far_high, 1, -1)
+    own_low, far_low = lax.optimization_barrier((own_low, far_low))
+    below_low, above_low = shift(own_low, 2, 1), shift(own_low, 2, -1)
     own_high = jnp.concatenate([far_low, far_high, below], axis=0)
     below_high, above_high = shift(own_high, 2, 1), shift(own_high, 2, -1)
     own_low, own_high, below_low, above_low = lax.optimization_barrier((own_low, own_high, below_low, above_low))

time: 132 us -> 137 us (1.038)
  waiting for transfers between devices: 44.3 us -> 53.1 us
  Pallas kernels: 42.2 us -> 37.7 us
    ppermute x26, waiting for transfers between devices: 44.3 us -> 53.1 us  [shift(): return lax.ppermute(value, AXES, pairs)]
    pallas_call x2, Pallas kernels: 22.1 us -> 17.6 us  [attend(): pl.pallas_call(functools.partial(attention_kernel, sequence), grid_spec=p...]
  transfers between devices with their start and end apart: 27 -> 27, of which waited for: 18 -> 18; matrix products, arithmetic and copies ran while one was open for 1% -> 1% of each run, Pallas kernels for 31% -> 27%
where the time goes in v8:
time: 137 us; the launch traced here: 136 us
  waiting for transfers between devices  53.1 us (39%)
  starting transfers between devices  41.2 us (30%)
  Pallas kernels  37.7 us (28%)
  other arithmetic  2.99 us (2%)
    ppermute x26, waiting for transfers between devices, shift(): return lax.ppermute(value, AXES, pairs)  53.1 us
    ppermute x26, starting transfers between devices, shift(): return lax.ppermute(value, AXES, pairs)  41.1 us
    pallas_call x2, Pallas kernels, attend(): pl.pallas_call(functools.partial(attention_kernel, sequence), grid_spec=p...  17.6 us
    pallas_call x4, Pallas kernels, expert_terms(): pl.pallas_call(functools.partial(expert_kernel, sources=len(pieces), outp...  14.7 us
    pallas_call x1, Pallas kernels, joined(): pl.pallas_call(join_kernel, in_specs=[pl.BlockSpec(memory_space=pl.ANY)]...  4.23 us
  transfers between devices with their start and end apart: 27, of which 18 were waited for; matrix products, arithmetic and copies ran while one was open for 1% of the time, Pallas kernels for 27%

profile of v8, /device:TPU:0, one launch (start us, length us, event | category | flops | bytes accessed | tf_op | source)
XLA Modules:
  0.0 136.2 jit_solution(8707536230491263412)
XLA Ops:
  0.6 1.1 pack.1
  1.7 4.2 %collective-permute-start = (bf16[8,7296]{1,0:T(8,128)(2,1)S(1)}, bf16[8,7296]{1,0:T(8,128)(2,1)S(1)}, u32[]{:S(2)}, u32[]{:S(2)}) collective-permute-start(bf16[8,7296]{1,0:T(8,128)(2,1)S(1)} %pack.1), channel_id=1, source_target_pairs={{0,96},{1,97},{2,98},{3,99},{4,100},{5,101},{6,102},{7,103},{8,104... | collective-permute-start | bytes 350216 | tf_op jit(solution)/shard_map/ppermute | solution.py:43
  5.9 1.3 collective-permute-start.2
  7.2 4.2 %join.1.refs_2_ = bf16[10752,512]{1,0:T(8,128)(2,1)S(1)} custom-call(bf16[7168,256]{1,0:T(8,128)(2,1)} %bitcast.9, bf16[7168,256]{1,0:T(8,128)(2,1)} %bitcast.10, bf16[256,7168]{1,0:T(8,128)(2,1)} %bitcast.11), custom_call_target="tpu_custom_call" | custom-call | bytes 22020096 | tf_op jit(solution)/shard_map/join/pallas_call | solution.py:142
  11.4 0.9 collective-permute-done.1
  12.4 0.9 collective-permute-done.2
  13.3 0.1 collective-permute-start.9
  13.4 1.6 %collective-permute-start.4 = (bf16[32,7296]{1,0:T(8,128)(2,1)S(1)}, bf16[32,7296]{1,0:T(8,128)(2,1)S(1)}, u32[]{:S(2)}, u32[]{:S(2)}) collective-permute-start(bf16[32,7296]{1,0:T(8,128)(2,1)S(1)} %pad_maximum_fusion.1), channel_id=1, source_target_pairs={{0,1},{1,2},{2,3},{3,0},{4,5},{5,6},{6,7},{7,4},{8,9},{9,10},{10,1... | collective-permute-start | bytes 1400840 | tf_op jit(solution)/shard_map/ppermute | solution.py:43
  15.0 1.7 %collective-permute-start.3 = (bf16[32,7296]{1,0:T(8,128)(2,1)S(1)}, bf16[32,7296]{1,0:T(8,128)(2,1)S(1)}, u32[]{:S(2)}, u32[]{:S(2)}) collective-permute-start(bf16[32,7296]{1,0:T(8,128)(2,1)S(1)} %pad_maximum_fusion.1), channel_id=1, source_target_pairs={{0,3},{1,0},{2,1},{3,2},{4,7},{5,4},{6,5},{7,6},{8,11},{9,8},{10,9... | collective-permute-start | bytes 1400840 | tf_op jit(solution)/shard_map/ppermute | solution.py:43
  16.7 6.5 %collective-permute-done.4 = bf16[32,7296]{1,0:T(8,128)(2,1)S(1)} collective-permute-done((bf16[32,7296]{1,0:T(8,128)(2,1)S(1)}, bf16[32,7296]{1,0:T(8,128)(2,1)S(1)}, u32[]{:S(2)}, u32[]{:S(2)}) %collective-permute-start.4) | collective-permute-done | bytes 466976 | tf_op jit(solution)/shard_map/ppermute | solution.py:43
  23.2 0.3 collective-permute-done.3
  23.6 1.6 %collective-permute-start.5 = (bf16[16,7296]{1,0:T(8,128)(2,1)S(1)}, bf16[16,7296]{1,0:T(8,128)(2,1)S(1)}, u32[]{:S(2)}, u32[]{:S(2)}) collective-permute-start(bf16[16,7296]{1,0:T(8,128)(2,1)S(1)} %slice.75), channel_id=1, source_target_pairs={{0,1},{1,2},{2,3},{3,0},{4,5},{5,6},{6,7},{7,4},{8,9},{9,10},{10,1... | collective-permute-start | bytes 700424 | tf_op jit(solution)/shard_map/ppermute | solution.py:43
  25.2 1.7 %collective-permute-start.6 = (bf16[16,7296]{1,0:T(8,128)(2,1)S(1)}, bf16[16,7296]{1,0:T(8,128)(2,1)S(1)}, u32[]{:S(2)}, u32[]{:S(2)}) collective-permute-start(bf16[16,7296]{1,0:T(8,128)(2,1)S(1)} %slice.76), channel_id=1, source_target_pairs={{0,3},{1,0},{2,1},{3,2},{4,7},{5,4},{6,5},{7,6},{8,11},{9,8},{10,9... | collective-permute-start | bytes 700424 | tf_op jit(solution)/shard_map/ppermute | solution.py:43
  26.9 0.1 pad_maximum_fusion.refs_0_
  27.0 4.0 %collective-permute-done.5 = bf16[16,7296]{1,0:T(8,128)(2,1)S(1)} collective-permute-done((bf16[16,7296]{1,0:T(8,128)(2,1)S(1)}, bf16[16,7296]{1,0:T(8,128)(2,1)S(1)}, u32[]{:S(2)}, u32[]{:S(2)}) %collective-permute-start.5) | collective-permute-done | bytes 233504 | tf_op jit(solution)/shard_map/ppermute | solution.py:43
  30.9 1.5 %collective-permute-start.7 = (bf16[64,7296]{1,0:T(8,128)(2,1)S(1)}, bf16[64,7296]{1,0:T(8,128)(2,1)S(1)}, u32[]{:S(2)}, u32[]{:S(2)}) collective-permute-start(bf16[64,7296]{1,0:T(8,128)(2,1)S(1)} %pad_maximum_fusion.refs_0_), channel_id=1, source_target_pairs={{0,4},{1,5},{2,6},{3,7},{4,8},{5,9},{6,10},{7,11},{8,12},{9,13},{1... | collective-permute-start | bytes 2801672 | tf_op jit(solution)/shard_map/ppermute | solution.py:43
  32.4 1.7 %collective-permute-start.8 = (bf16[64,7296]{1,0:T(8,128)(2,1)S(1)}, bf16[64,7296]{1,0:T(8,128)(2,1)S(1)}, u32[]{:S(2)}, u32[]{:S(2)}) collective-permute-start(bf16[64,7296]{1,0:T(8,128)(2,1)S(1)} %pad_maximum_fusion.refs_0_), channel_id=1, source_target_pairs={{0,12},{1,13},{2,14},{3,15},{4,0},{5,1},{6,2},{7,3},{8,4},{9,5},{1... | collective-permute-start | bytes 2801672 | tf_op jit(solution)/shard_map/ppermute | solution.py:43
  34.3 1.6 %collective-permute-start.10 = (bf16[64,7296]{1,0:T(8,128)(2,1)S(1)}, bf16[64,7296]{1,0:T(8,128)(2,1)S(1)}, u32[]{:S(2)}, u32[]{:S(2)}) collective-permute-start(bf16[64,7296]{1,0:T(8,128)(2,1)S(1)} %constant_dynamic-update-slice_fusion.refs_1_), channel_id=1, source_target_pairs={{0,12},{1,13},{2,14},{3,15},{4,0},{5,1},{6,2},{7,3},{8,4},{9,5},{1... | collective-permute-start | bytes 2801672 | tf_op jit(solution)/shard_map/ppermute | solution.py:43
  35.9 0.5 collective-permute-start.13
  36.4 9.3 %collective-permute-done.7.refs_1_ = bf16[64,7296]{1,0:T(8,128)(2,1)S(1)} collective-permute-done((bf16[64,7296]{1,0:T(8,128)(2,1)S(1)}, bf16[64,7296]{1,0:T(8,128)(2,1)S(1)}, u32[]{:S(2)}, u32[]{:S(2)}) %collective-permute-start.7) | collective-permute-done | bytes 933920 | tf_op jit(solution)/shard_map/ppermute | solution.py:43
  45.7 0.3 collective-permute-done.8.refs_0_
  46.0 3.7 %expert.4 = (bf16[64,7168]{1,0:T(8,128)(2,1)S(1)}, bf16[64,7168]{1,0:T(8,128)(2,1)S(1)}) custom-call(bf16[64,7296]{1,0:T(8,128)(2,1)S(1)} %pad_maximum_fusion.refs_0_, bf16[64,7296]{1,0:T(8,128)(2,1)S(1)} %constant_dynamic-update-slice_fusion.refs_1_, bf16[10752,512]{1,0:T(8,128)(2,1)S(1)} %join.1.refs_2_, bf16[10752,512]{1,0:T(8,128)(2,1)S(1)} %collective-permute-done.9.refs_3_), custom_call_target="tpu_custom_call" | custom-call | flops 2818572288 | bytes 3670016 | tf_op jit(solution)/shard_map/expert/pallas_call | solution.py:104
  49.7 3.7 %expert.5 = (bf16[64,7168]{1,0:T(8,128)(2,1)S(1)}, bf16[64,7168]{1,0:T(8,128)(2,1)S(1)}) custom-call(bf16[64,7296]{1,0:T(8,128)(2,1)S(1)} %collective-permute-done.8.refs_0_, bf16[64,7296]{1,0:T(8,128)(2,1)S(1)} %collective-permute-done.7.refs_1_, bf16[10752,512]{1,0:T(8,128)(2,1)S(1)} %join.1.refs_2_, bf16[10752,512]{1,0:T(8,128)(2,1)S(1)} %collective-permute-done.9.refs_3_), custom_call_target="tpu_custom_call" | custom-call | flops 2818572288 | bytes 3670016 | tf_op jit(solution)/shard_map/expert/pallas_call | solution.py:104
  53.4 2.6 %collective-permute-done.10.refs_0_ = bf16[64,7296]{1,0:T(8,128)(2,1)S(1)} collective-permute-done((bf16[64,7296]{1,0:T(8,128)(2,1)S(1)}, bf16[64,7296]{1,0:T(8,128)(2,1)S(1)}, u32[]{:S(2)}, u32[]{:S(2)}) %collective-permute-start.10) | collective-permute-done | bytes 933920 | tf_op jit(solution)/shard_map/ppermute | solution.py:43
  56.0 1.5 %collective-permute-start.11 = (bf16[64,7296]{1,0:T(8,128)(2,1)S(1)}, bf16[64,7296]{1,0:T(8,128)(2,1)S(1)}, u32[]{:S(2)}, u32[]{:S(2)}) collective-permute-start(bf16[64,7296]{1,0:T(8,128)(2,1)S(1)} %collective-permute-done.7.refs_1_), channel_id=1, source_target_pairs={{0,4},{1,5},{2,6},{3,7},{4,8},{5,9},{6,10},{7,11},{8,12},{9,13},{1... | collective-permute-start | bytes 2801672 | tf_op jit(solution)/shard_map/ppermute | solution.py:43
  57.5 1.7 %collective-permute-start.12 = (bf16[64,7296]{1,0:T(8,128)(2,1)S(1)}, bf16[64,7296]{1,0:T(8,128)(2,1)S(1)}, u32[]{:S(2)}, u32[]{:S(2)}) collective-permute-start(bf16[64,7296]{1,0:T(8,128)(2,1)S(1)} %collective-permute-done.10.refs_0_), channel_id=1, source_target_pairs={{0,12},{1,13},{2,14},{3,15},{4,0},{5,1},{6,2},{7,3},{8,4},{9,5},{1... | collective-permute-start | bytes 2801672 | tf_op jit(solution)/shard_map/ppermute | solution.py:43
  59.2 3.7 %expert.6 = (bf16[64,7168]{1,0:T(8,128)(2,1)S(1)}, bf16[64,7168]{1,0:T(8,128)(2,1)S(1)}) custom-call(bf16[64,7296]{1,0:T(8,128)(2,1)S(1)} %collective-permute-done.10.refs_0_, bf16[64,7296]{1,0:T(8,128)(2,1)S(1)} %collective-permute-done.13.refs_1_, bf16[10752,512]{1,0:T(8,128)(2,1)S(1)} %join.1.refs_2_, bf16[10752,512]{1,0:T(8,128)(2,1)S(1)} %collective-permute-done.9.refs_3_), custom_call_target="tpu_custom_call" | custom-call | flops 2818572288 | bytes 3670016 | tf_op jit(solution)/shard_map/expert/pallas_call | solution.py:104
  63.0 0.3 collective-permute-start.16
  63.4 3.0 %collective-permute-start.17 = (bf16[64,7168]{1,0:T(8,128)(2,1)S(1)}, bf16[64,7168]{1,0:T(8,128)(2,1)S(1)}, u32[]{:S(2)}, u32[]{:S(2)}) collective-permute-start(bf16[64,7168]{1,0:T(8,128)(2,1)S(1)} %get-tuple-element.72), channel_id=1, source_target_pairs={{0,12},{1,13},{2,14},{3,15},{4,0},{5,1},{6,2},{7,3},{8,4},{9,5},{1... | collective-permute-start | bytes 2752520 | tf_op jit(solution)/shard_map/ppermute | solution.py:43
  66.3 4.4 %collective-permute-done.11.refs_0_ = bf16[64,7296]{1,0:T(8,128)(2,1)S(1)} collective-permute-done((bf16[64,7296]{1,0:T(8,128)(2,1)S(1)}, bf16[64,7296]{1,0:T(8,128)(2,1)S(1)}, u32[]{:S(2)}, u32[]{:S(2)}) %collective-permute-start.11) | collective-permute-done | bytes 933920 | tf_op jit(solution)/shard_map/ppermute | solution.py:43
  70.8 0.3 collective-permute-done.12.refs_1_
  71.1 3.7 %expert.7 = (bf16[64,7168]{1,0:T(8,128)(2,1)S(1)}, bf16[64,7168]{1,0:T(8,128)(2,1)S(1)}) custom-call(bf16[64,7296]{1,0:T(8,128)(2,1)S(1)} %collective-permute-done.11.refs_0_, bf16[64,7296]{1,0:T(8,128)(2,1)S(1)} %collective-permute-done.12.refs_1_, bf16[10752,512]{1,0:T(8,128)(2,1)S(1)} %join.1.refs_2_, bf16[10752,512]{1,0:T(8,128)(2,1)S(1)} %collective-permute-done.9.refs_3_), custom_call_target="tpu_custom_call" | custom-call | flops 2818572288 | bytes 3670016 | tf_op jit(solution)/shard_map/expert/pallas_call | solution.py:104
  74.7 1.3 collective-permute-start.14
  76.0 2.0 %collective-permute-start.15 = (bf16[64,7168]{1,0:T(8,128)(2,1)S(1)}, bf16[64,7168]{1,0:T(8,128)(2,1)S(1)}, u32[]{:S(2)}, u32[]{:S(2)}) collective-permute-start(bf16[64,7168]{1,0:T(8,128)(2,1)S(1)} %get-tuple-element.76), channel_id=1, source_target_pairs={{0,12},{1,13},{2,14},{3,15},{4,0},{5,1},{6,2},{7,3},{8,4},{9,5},{1... | collective-permute-start | bytes 2752520 | tf_op jit(solution)/shard_map/ppermute | solution.py:43
  78.1 10.5 %attend.2 = bf16[64,1024]{1,0:T(8,128)(2,1)S(1)} custom-call(s32[2]{0:T(128)S(1)} %copy-done.7, bf16[128,1024]{1,0:T(8,128)(2,1)S(1)} %copy-done.3, bf16[128,512]{1,0:T(8,128)(2,1)S(1)} %copy-done.4, bf16[8,128,512]{2,1,0:T(8,128)(2,1)S(1)} %copy-done, bf16[8,512,128]{2,1,0:T(8,128)(2,1)S(1)} %copy-done.1, bf16[2,4096,512]{2,1,0:T(8,128)(2,1)} %latent_ref.3, ...), custom_call_target="tpu_custom_call" | custom-call | flops 100000000 | bytes 133333 | tf_op jit(solution)/shard_map/attend/pallas_call | solution.py:254
  88.6 1.8 %collective-permute-done.14 = bf16[64,7168]{1,0:T(8,128)(2,1)S(1)} collective-permute-done((bf16[64,7168]{1,0:T(8,128)(2,1)S(1)}, bf16[64,7168]{1,0:T(8,128)(2,1)S(1)}, u32[]{:S(2)}, u32[]{:S(2)}) %collective-permute-start.14) | collective-permute-done | bytes 917536 | tf_op jit(solution)/shard_map/ppermute | solution.py:43
  90.4 0.3 collective-permute-done.15
  90.7 0.2 add_convert_fusion
  90.9 3.0 %collective-permute-start.19 = (bf16[64,7168]{1,0:T(8,128)(2,1)S(1)}, bf16[64,7168]{1,0:T(8,128)(2,1)S(1)}, u32[]{:S(2)}, u32[]{:S(2)}) collective-permute-start(bf16[64,7168]{1,0:T(8,128)(2,1)S(1)} %add_convert_fusion), channel_id=1, source_target_pairs={{0,12},{1,13},{2,14},{3,15},{4,0},{5,1},{6,2},{7,3},{8,4},{9,5},{1... | collective-permute-start | bytes 2752520 | tf_op jit(solution)/shard_map/ppermute | solution.py:43
  94.0 0.2 add_convert_fusion.1
  94.2 0.3 collective-permute-start.18
  94.5 7.2 %attend.3 = bf16[64,1024]{1,0:T(8,128)(2,1)S(1)} custom-call(s32[2]{0:T(128)S(1)} %copy-done.7, bf16[128,1024]{1,0:T(8,128)(2,1)S(1)} %copy-done.3, bf16[128,512]{1,0:T(8,128)(2,1)S(1)} %copy-done.4, bf16[8,128,512]{2,1,0:T(8,128)(2,1)S(1)} %copy-done, bf16[8,512,128]{2,1,0:T(8,128)(2,1)S(1)} %copy-done.1, bf16[2,4096,512]{2,1,0:T(8,128)(2,1)} %latent_ref.3, ...), custom_call_target="tpu_custom_call" | custom-call | flops 6000000000 | bytes 8000000 | tf_op jit(solution)/shard_map/attend/pallas_call | solution.py:254
  101.7 3.2 %collective-permute-done.19 = bf16[64,7168]{1,0:T(8,128)(2,1)S(1)} collective-permute-done((bf16[64,7168]{1,0:T(8,128)(2,1)S(1)}, bf16[64,7168]{1,0:T(8,128)(2,1)S(1)}, u32[]{:S(2)}, u32[]{:S(2)}) %collective-permute-start.19) | collective-permute-done | bytes 917536 | tf_op jit(solution)/shard_map/ppermute | solution.py:43
  104.9 4.2 %collective-permute-done.18 = bf16[64,7168]{1,0:T(8,128)(2,1)S(1)} collective-permute-done((bf16[64,7168]{1,0:T(8,128)(2,1)S(1)}, bf16[64,7168]{1,0:T(8,128)(2,1)S(1)}, u32[]{:S(2)}, u32[]{:S(2)}) %collective-permute-start.18) | collective-permute-done | bytes 917536 | tf_op jit(solution)/shard_map/ppermute | solution.py:43
  109.1 0.3 fusion.3
  109.5 0.3 convert_add_fusion.1
  109.8 0.4 collective-permute-start.20
  110.3 2.9 %collective-permute-start.21 = (bf16[32,7168]{1,0:T(8,128)(2,1)S(1)}, bf16[32,7168]{1,0:T(8,128)(2,1)S(1)}, u32[]{:S(2)}, u32[]{:S(2)}) collective-permute-start(bf16[32,7168]{1,0:T(8,128)(2,1)S(1)} %concatenate.29), channel_id=1, source_target_pairs={{0,3},{1,0},{2,1},{3,2},{4,7},{5,4},{6,5},{7,6},{8,11},{9,8},{10,9... | collective-permute-start | bytes 1376264 | tf_op jit(solution)/shard_map/ppermute | solution.py:43
  113.2 6.3 %collective-permute-done.20 = bf16[32,7168]{1,0:T(8,128)(2,1)S(1)} collective-permute-done((bf16[32,7168]{1,0:T(8,128)(2,1)S(1)}, bf16[32,7168]{1,0:T(8,128)(2,1)S(1)}, u32[]{:S(2)}, u32[]{:S(2)}) %collective-permute-start.20) | collective-permute-done | bytes 458784 | tf_op jit(solution)/shard_map/ppermute | solution.py:43
  119.6 0.1 fusion.2
  119.7 0.1 fusion.1
  119.7 0.5 collective-permute-start.22
  120.3 2.9 %collective-permute-start.23 = (bf16[16,7168]{1,0:T(8,128)(2,1)S(1)}, bf16[16,7168]{1,0:T(8,128)(2,1)S(1)}, u32[]{:S(2)}, u32[]{:S(2)}) collective-permute-start(bf16[16,7168]{1,0:T(8,128)(2,1)S(1)} %fusion.1), channel_id=1, source_target_pairs={{0,3},{1,0},{2,1},{3,2},{4,7},{5,4},{6,5},{7,6},{8,11},{9,8},{10,9... | collective-permute-start | bytes 688136 | tf_op jit(solution)/shard_map/ppermute | solution.py:43
  123.1 3.9 %collective-permute-done.22 = bf16[16,7168]{1,0:T(8,128)(2,1)S(1)} collective-permute-done((bf16[16,7168]{1,0:T(8,128)(2,1)S(1)}, bf16[16,7168]{1,0:T(8,128)(2,1)S(1)}, u32[]{:S(2)}, u32[]{:S(2)}) %collective-permute-start.22) | collective-permute-done | bytes 229408 | tf_op jit(solution)/shard_map/ppermute | solution.py:43
  127.1 0.1 convert_add_fusion.3
  127.1 0.1 convert_add_fusion.2
  127.2 0.1 fusion
  127.3 0.6 collective-permute-start.24
  127.9 2.1 %collective-permute-start.25 = (bf16[8,7168]{1,0:T(8,128)(2,1)S(1)}, bf16[8,7168]{1,0:T(8,128)(2,1)S(1)}, u32[]{:S(2)}, u32[]{:S(2)}) collective-permute-start(bf16[8,7168]{1,0:T(8,128)(2,1)S(1)} %get-tuple-element.96), channel_id=1, source_target_pairs={{0,64},{1,65},{2,66},{3,67},{4,68},{5,69},{6,70},{7,71},{8,72},{9,... | collective-permute-start | bytes 344072 | tf_op jit(solution)/shard_map/ppermute | solution.py:43
  130.0 1.1 collective-permute-start.26
  131.1 0.7 pad_maximum_fusion.3
  131.8 2.8 %collective-permute-done.24 = bf16[8,7168]{1,0:T(8,128)(2,1)S(1)} collective-permute-done((bf16[8,7168]{1,0:T(8,128)(2,1)S(1)}, bf16[8,7168]{1,0:T(8,128)(2,1)S(1)}, u32[]{:S(2)}, u32[]{:S(2)}) %collective-permute-start.24) | collective-permute-done | bytes 114720 | tf_op jit(solution)/shard_map/ppermute | solution.py:43
  134.6 0.9 collective-permute-done.26
  135.5 0.7 add_convert_fusion.2
  (37 shorter events, 0.4 us)
Async XLA Ops:
  1.7 9.7 %collective-permute-start = (bf16[8,7296]{1,0:T(8,128)(2,1)S(1)}, bf16[8,7296]{1,0:T(8,128)(2,1)S(1)}, u32[]{:S(2)}, u32[]{:S(2)}) collective-permute-start(bf16[8,7296]{1,0:T(8,128)(2,1)S(1)} %pack.1), channel_id=1, source_target_pairs={{0,96},{1,97},{2,98},{3,99},{4,100},{5,101},{6,102},{7,103},{8,104... | collective-permute-start | bytes 350216 | tf_op jit(solution)/shard_map/ppermute | solution.py:43
  5.9 6.4 %collective-permute-start.1 = (bf16[8,7296]{1,0:T(8,128)(2,1)S(1)}, bf16[8,7296]{1,0:T(8,128)(2,1)S(1)}, u32[]{:S(2)}, u32[]{:S(2)}) collective-permute-start(bf16[8,7296]{1,0:T(8,128)(2,1)S(1)} %pack.1), channel_id=1, source_target_pairs={{0,64},{1,65},{2,66},{3,67},{4,68},{5,69},{6,70},{7,71},{8,72},{9,... | collective-permute-start | bytes 350216 | tf_op jit(solution)/shard_map/ppermute | solution.py:43
  5.9 7.3 %collective-permute-start.2 = (bf16[8,7296]{1,0:T(8,128)(2,1)S(1)}, bf16[8,7296]{1,0:T(8,128)(2,1)S(1)}, u32[]{:S(2)}, u32[]{:S(2)}) collective-permute-start(bf16[8,7296]{1,0:T(8,128)(2,1)S(1)} %pack.1), channel_id=1, source_target_pairs={{0,32},{1,33},{2,34},{3,35},{4,36},{5,37},{6,38},{7,39},{8,40},{9,... | collective-permute-start | bytes 350216 | tf_op jit(solution)/shard_map/ppermute | solution.py:43
  13.3 32.7 %collective-permute-start.9 = (bf16[10752,512]{1,0:T(8,128)(2,1)S(1)}, bf16[10752,512]{1,0:T(8,128)(2,1)S(1)}, u32[]{:S(2)}, u32[]{:S(2)}) collective-permute-start(bf16[10752,512]{1,0:T(8,128)(2,1)S(1)} %join.1.refs_2_), channel_id=1, source_target_pairs={{0,16},{16,0},{1,17},{17,1},{2,18},{18,2},{3,19},{19,3},{4,20},{20... | collective-permute-start | bytes 33030152 | tf_op jit(solution)/shard_map/ppermute | solution.py:59
  13.4 9.8 %collective-permute-start.4 = (bf16[32,7296]{1,0:T(8,128)(2,1)S(1)}, bf16[32,7296]{1,0:T(8,128)(2,1)S(1)}, u32[]{:S(2)}, u32[]{:S(2)}) collective-permute-start(bf16[32,7296]{1,0:T(8,128)(2,1)S(1)} %pad_maximum_fusion.1), channel_id=1, source_target_pairs={{0,1},{1,2},{2,3},{3,0},{4,5},{5,6},{6,7},{7,4},{8,9},{9,10},{10,1... | collective-permute-start | bytes 1400840 | tf_op jit(solution)/shard_map/ppermute | solution.py:43
  15.0 8.6 %collective-permute-start.3 = (bf16[32,7296]{1,0:T(8,128)(2,1)S(1)}, bf16[32,7296]{1,0:T(8,128)(2,1)S(1)}, u32[]{:S(2)}, u32[]{:S(2)}) collective-permute-start(bf16[32,7296]{1,0:T(8,128)(2,1)S(1)} %pad_maximum_fusion.1), channel_id=1, source_target_pairs={{0,3},{1,0},{2,1},{3,2},{4,7},{5,4},{6,5},{7,6},{8,11},{9,8},{10,9... | collective-permute-start | bytes 1400840 | tf_op jit(solution)/shard_map/ppermute | solution.py:43
  23.6 7.3 %collective-permute-start.5 = (bf16[16,7296]{1,0:T(8,128)(2,1)S(1)}, bf16[16,7296]{1,0:T(8,128)(2,1)S(1)}, u32[]{:S(2)}, u32[]{:S(2)}) collective-permute-start(bf16[16,7296]{1,0:T(8,128)(2,1)S(1)} %slice.75), channel_id=1, source_target_pairs={{0,1},{1,2},{2,3},{3,0},{4,5},{5,6},{6,7},{7,4},{8,9},{9,10},{10,1... | collective-permute-start | bytes 700424 | tf_op jit(solution)/shard_map/ppermute | solution.py:43
  25.2 9.0 %collective-permute-start.6 = (bf16[16,7296]{1,0:T(8,128)(2,1)S(1)}, bf16[16,7296]{1,0:T(8,128)(2,1)S(1)}, u32[]{:S(2)}, u32[]{:S(2)}) collective-permute-start(bf16[16,7296]{1,0:T(8,128)(2,1)S(1)} %slice.76), channel_id=1, source_target_pairs={{0,3},{1,0},{2,1},{3,2},{4,7},{5,4},{6,5},{7,6},{8,11},{9,8},{10,9... | collective-permute-start | bytes 700424 | tf_op jit(solution)/shard_map/ppermute | solution.py:43
  30.9 14.8 %collective-permute-start.7 = (bf16[64,7296]{1,0:T(8,128)(2,1)S(1)}, bf16[64,7296]{1,0:T(8,128)(2,1)S(1)}, u32[]{:S(2)}, u32[]{:S(2)}) collective-permute-start(bf16[64,7296]{1,0:T(8,128)(2,1)S(1)} %pad_maximum_fusion.refs_0_), channel_id=1, source_target_pairs={{0,4},{1,5},{2,6},{3,7},{4,8},{5,9},{6,10},{7,11},{8,12},{9,13},{1... | collective-permute-start | bytes 2801672 | tf_op jit(solution)/shard_map/ppermute | solution.py:43
  32.4 13.6 %collective-permute-start.8 = (bf16[64,7296]{1,0:T(8,128)(2,1)S(1)}, bf16[64,7296]{1,0:T(8,128)(2,1)S(1)}, u32[]{:S(2)}, u32[]{:S(2)}) collective-permute-start(bf16[64,7296]{1,0:T(8,128)(2,1)S(1)} %pad_maximum_fusion.refs_0_), channel_id=1, source_target_pairs={{0,12},{1,13},{2,14},{3,15},{4,0},{5,1},{6,2},{7,3},{8,4},{9,5},{1... | collective-permute-start | bytes 2801672 | tf_op jit(solution)/shard_map/ppermute | solution.py:43
  34.3 21.7 %collective-permute-start.10 = (bf16[64,7296]{1,0:T(8,128)(2,1)S(1)}, bf16[64,7296]{1,0:T(8,128)(2,1)S(1)}, u32[]{:S(2)}, u32[]{:S(2)}) collective-permute-start(bf16[64,7296]{1,0:T(8,128)(2,1)S(1)} %constant_dynamic-update-slice_fusion.refs_1_), channel_id=1, source_target_pairs={{0,12},{1,13},{2,14},{3,15},{4,0},{5,1},{6,2},{7,3},{8,4},{9,5},{1... | collective-permute-start | bytes 2801672 | tf_op jit(solution)/shard_map/ppermute | solution.py:43
  35.9 23.4 %collective-permute-start.13 = (bf16[64,7296]{1,0:T(8,128)(2,1)S(1)}, bf16[64,7296]{1,0:T(8,128)(2,1)S(1)}, u32[]{:S(2)}, u32[]{:S(2)}) collective-permute-start(bf16[64,7296]{1,0:T(8,128)(2,1)S(1)} %constant_dynamic-update-slice_fusion.refs_1_), channel_id=1, source_target_pairs={{0,4},{1,5},{2,6},{3,7},{4,8},{5,9},{6,10},{7,11},{8,12},{9,13},{1... | collective-permute-start | bytes 2801672 | tf_op jit(solution)/shard_map/ppermute | solution.py:43
  56.0 14.8 %collective-permute-start.11 = (bf16[64,7296]{1,0:T(8,128)(2,1)S(1)}, bf16[64,7296]{1,0:T(8,128)(2,1)S(1)}, u32[]{:S(2)}, u32[]{:S(2)}) collective-permute-start(bf16[64,7296]{1,0:T(8,128)(2,1)S(1)} %collective-permute-done.7.refs_1_), channel_id=1, source_target_pairs={{0,4},{1,5},{2,6},{3,7},{4,8},{5,9},{6,10},{7,11},{8,12},{9,13},{1... | collective-permute-start | bytes 2801672 | tf_op jit(solution)/shard_map/ppermute | solution.py:43
  57.5 13.6 %collective-permute-start.12 = (bf16[64,7296]{1,0:T(8,128)(2,1)S(1)}, bf16[64,7296]{1,0:T(8,128)(2,1)S(1)}, u32[]{:S(2)}, u32[]{:S(2)}) collective-permute-start(bf16[64,7296]{1,0:T(8,128)(2,1)S(1)} %collective-permute-done.10.refs_0_), channel_id=1, source_target_pairs={{0,12},{1,13},{2,14},{3,15},{4,0},{5,1},{6,2},{7,3},{8,4},{9,5},{1... | collective-permute-start | bytes 2801672 | tf_op jit(solution)/shard_map/ppermute | solution.py:43
  62.9 15.1 %copy-start = (bf16[8,128,512]{2,1,0:T(8,128)(2,1)S(1)}, bf16[8,128,512]{2,1,0:T(8,128)(2,1)}, u32[]{:S(2)}) copy-start(bf16[8,128,512]{2,1,0:T(8,128)(2,1)} %key_up_ref.3) | copy-start | bytes 3145732
  62.9 15.1 %copy-start.1 = (bf16[8,512,128]{2,1,0:T(8,128)(2,1)S(1)}, bf16[8,512,128]{2,1,0:T(8,128)(2,1)}, u32[]{:S(2)}) copy-start(bf16[8,512,128]{2,1,0:T(8,128)(2,1)} %value_up_ref.3) | copy-start | bytes 3145732
  63.0 15.1 %copy-start.2 = (bf16[2,4096,64]{1,2,0:T(8,128)(2,1)S(1)}, bf16[2,4096,64]{1,2,0:T(8,128)(2,1)}, u32[]{:S(2)}) copy-start(bf16[2,4096,64]{1,2,0:T(8,128)(2,1)} %param.26) | copy-start | bytes 3145732
  63.0 15.1 %copy-start.3 = (bf16[128,1024]{1,0:T(8,128)(2,1)S(1)}, bf16[128,1024]{1,0:T(8,128)(2,1)}, u32[]{:S(2)}) copy-start(bf16[128,1024]{1,0:T(8,128)(2,1)} %nope_ref.3) | copy-start | bytes 786436
  63.0 15.1 %copy-start.4 = (bf16[128,512]{1,0:T(8,128)(2,1)S(1)}, bf16[128,512]{1,0:T(8,128)(2,1)}, u32[]{:S(2)}) copy-start(bf16[128,512]{1,0:T(8,128)(2,1)} %rope_ref.3) | copy-start | bytes 393220
  63.0 15.1 %copy-start.5 = (bf16[128,512]{1,0:T(8,128)(2,1)S(1)}, bf16[128,512]{1,0:T(8,128)(2,1)}, u32[]{:S(2)}) copy-start(bf16[128,512]{1,0:T(8,128)(2,1)} %new_latent_ref.3) | copy-start | bytes 393220
  63.0 15.1 %copy-start.6 = (bf16[128,64]{0,1:T(8,128)(2,1)S(1)}, bf16[128,64]{0,1:T(8,128)(2,1)}, u32[]{:S(2)}) copy-start(bf16[128,64]{0,1:T(8,128)(2,1)} %param.28) | copy-start | bytes 49156
  63.0 15.1 %copy-start.7 = (s32[2]{0:T(128)S(1)}, s32[2]{0:T(128)}, u32[]{:S(2)}) copy-start(s32[2]{0:T(128)} %length_ref.1) | copy-start | bytes 28
  63.0 25.6 %collective-permute-start.16 = (bf16[64,7168]{1,0:T(8,128)(2,1)S(1)}, bf16[64,7168]{1,0:T(8,128)(2,1)S(1)}, u32[]{:S(2)}, u32[]{:S(2)}) collective-permute-start(bf16[64,7168]{1,0:T(8,128)(2,1)S(1)} %get-tuple-element.71), channel_id=1, source_target_pairs={{0,4},{1,5},{2,6},{3,7},{4,8},{5,9},{6,10},{7,11},{8,12},{9,13},{1... | collective-permute-start | bytes 2752520 | tf_op jit(solution)/shard_map/ppermute | solution.py:43
  63.4 25.2 %collective-permute-start.17 = (bf16[64,7168]{1,0:T(8,128)(2,1)S(1)}, bf16[64,7168]{1,0:T(8,128)(2,1)S(1)}, u32[]{:S(2)}, u32[]{:S(2)}) collective-permute-start(bf16[64,7168]{1,0:T(8,128)(2,1)S(1)} %get-tuple-element.72), channel_id=1, source_target_pairs={{0,12},{1,13},{2,14},{3,15},{4,0},{5,1},{6,2},{7,3},{8,4},{9,5},{1... | collective-permute-start | bytes 2752520 | tf_op jit(solution)/shard_map/ppermute | solution.py:43
  74.7 15.7 %collective-permute-start.14 = (bf16[64,7168]{1,0:T(8,128)(2,1)S(1)}, bf16[64,7168]{1,0:T(8,128)(2,1)S(1)}, u32[]{:S(2)}, u32[]{:S(2)}) collective-permute-start(bf16[64,7168]{1,0:T(8,128)(2,1)S(1)} %get-tuple-element.75), channel_id=1, source_target_pairs={{0,4},{1,5},{2,6},{3,7},{4,8},{5,9},{6,10},{7,11},{8,12},{9,13},{1... | collective-permute-start | bytes 2752520 | tf_op jit(solution)/shard_map/ppermute | solution.py:43
  76.0 14.7 %collective-permute-start.15 = (bf16[64,7168]{1,0:T(8,128)(2,1)S(1)}, bf16[64,7168]{1,0:T(8,128)(2,1)S(1)}, u32[]{:S(2)}, u32[]{:S(2)}) collective-permute-start(bf16[64,7168]{1,0:T(8,128)(2,1)S(1)} %get-tuple-element.76), channel_id=1, source_target_pairs={{0,12},{1,13},{2,14},{3,15},{4,0},{5,1},{6,2},{7,3},{8,4},{9,5},{1... | collective-permute-start | bytes 2752520 | tf_op jit(solution)/shard_map/ppermute | solution.py:43
  90.9 13.9 %collective-permute-start.19 = (bf16[64,7168]{1,0:T(8,128)(2,1)S(1)}, bf16[64,7168]{1,0:T(8,128)(2,1)S(1)}, u32[]{:S(2)}, u32[]{:S(2)}) collective-permute-start(bf16[64,7168]{1,0:T(8,128)(2,1)S(1)} %add_convert_fusion), channel_id=1, source_target_pairs={{0,12},{1,13},{2,14},{3,15},{4,0},{5,1},{6,2},{7,3},{8,4},{9,5},{1... | collective-permute-start | bytes 2752520 | tf_op jit(solution)/shard_map/ppermute | solution.py:43
  94.2 14.9 %collective-permute-start.18 = (bf16[64,7168]{1,0:T(8,128)(2,1)S(1)}, bf16[64,7168]{1,0:T(8,128)(2,1)S(1)}, u32[]{:S(2)}, u32[]{:S(2)}) collective-permute-start(bf16[64,7168]{1,0:T(8,128)(2,1)S(1)} %add_convert_fusion.1), channel_id=1, source_target_pairs={{0,4},{1,5},{2,6},{3,7},{4,8},{5,9},{6,10},{7,11},{8,12},{9,13},{1... | collective-permute-start | bytes 2752520 | tf_op jit(solution)/shard_map/ppermute | solution.py:43
  109.8 9.8 %collective-permute-start.20 = (bf16[32,7168]{1,0:T(8,128)(2,1)S(1)}, bf16[32,7168]{1,0:T(8,128)(2,1)S(1)}, u32[]{:S(2)}, u32[]{:S(2)}) collective-permute-start(bf16[32,7168]{1,0:T(8,128)(2,1)S(1)} %pad_maximum_fusion.2), channel_id=1, source_target_pairs={{0,1},{1,2},{2,3},{3,0},{4,5},{5,6},{6,7},{7,4},{8,9},{9,10},{10,1... | collective-permute-start | bytes 1376264 | tf_op jit(solution)/shard_map/ppermute | solution.py:43
  110.3 9.3 %collective-permute-start.21 = (bf16[32,7168]{1,0:T(8,128)(2,1)S(1)}, bf16[32,7168]{1,0:T(8,128)(2,1)S(1)}, u32[]{:S(2)}, u32[]{:S(2)}) collective-permute-start(bf16[32,7168]{1,0:T(8,128)(2,1)S(1)} %concatenate.29), channel_id=1, source_target_pairs={{0,3},{1,0},{2,1},{3,2},{4,7},{5,4},{6,5},{7,6},{8,11},{9,8},{10,9... | collective-permute-start | bytes 1376264 | tf_op jit(solution)/shard_map/ppermute | solution.py:43
  119.7 7.3 %collective-permute-start.22 = (bf16[16,7168]{1,0:T(8,128)(2,1)S(1)}, bf16[16,7168]{1,0:T(8,128)(2,1)S(1)}, u32[]{:S(2)}, u32[]{:S(2)}) collective-permute-start(bf16[16,7168]{1,0:T(8,128)(2,1)S(1)} %fusion.2), channel_id=1, source_target_pairs={{0,1},{1,2},{2,3},{3,0},{4,5},{5,6},{6,7},{7,4},{8,9},{9,10},{10,1... | collective-permute-start | bytes 688136 | tf_op jit(solution)/shard_map/ppermute | solution.py:43
  120.3 6.9 %collective-permute-start.23 = (bf16[16,7168]{1,0:T(8,128)(2,1)S(1)}, bf16[16,7168]{1,0:T(8,128)(2,1)S(1)}, u32[]{:S(2)}, u32[]{:S(2)}) collective-permute-start(bf16[16,7168]{1,0:T(8,128)(2,1)S(1)} %fusion.1), channel_id=1, source_target_pairs={{0,3},{1,0},{2,1},{3,2},{4,7},{5,4},{6,5},{7,6},{8,11},{9,8},{10,9... | collective-permute-start | bytes 688136 | tf_op jit(solution)/shard_map/ppermute | solution.py:43
  127.3 7.3 %collective-permute-start.24 = (bf16[8,7168]{1,0:T(8,128)(2,1)S(1)}, bf16[8,7168]{1,0:T(8,128)(2,1)S(1)}, u32[]{:S(2)}, u32[]{:S(2)}) collective-permute-start(bf16[8,7168]{1,0:T(8,128)(2,1)S(1)} %get-tuple-element.94), channel_id=1, source_target_pairs={{0,32},{1,33},{2,34},{3,35},{4,36},{5,37},{6,38},{7,39},{8,40},{9,... | collective-permute-start | bytes 344072 | tf_op jit(solution)/shard_map/ppermute | solution.py:43
  127.9 6.8 %collective-permute-start.25 = (bf16[8,7168]{1,0:T(8,128)(2,1)S(1)}, bf16[8,7168]{1,0:T(8,128)(2,1)S(1)}, u32[]{:S(2)}, u32[]{:S(2)}) collective-permute-start(bf16[8,7168]{1,0:T(8,128)(2,1)S(1)} %get-tuple-element.96), channel_id=1, source_target_pairs={{0,64},{1,65},{2,66},{3,67},{4,68},{5,69},{6,70},{7,71},{8,72},{9,... | collective-permute-start | bytes 344072 | tf_op jit(solution)/shard_map/ppermute | solution.py:43
  130.0 5.5 %collective-permute-start.26 = (bf16[8,7168]{1,0:T(8,128)(2,1)S(1)}, bf16[8,7168]{1,0:T(8,128)(2,1)S(1)}, u32[]{:S(2)}, u32[]{:S(2)}) collective-permute-start(bf16[8,7168]{1,0:T(8,128)(2,1)S(1)} %get-tuple-element.95), channel_id=1, source_target_pairs={{0,96},{1,97},{2,98},{3,99},{4,100},{5,101},{6,102},{7,103},{8,104... | collective-permute-start | bytes 344072 | tf_op jit(solution)/shard_map/ppermute | solution.py:43

commit v9 on v7

--- a/solution.py
+++ b/solution.py
@@ -28,7 +28,7 @@
 KEY_BLOCK = 1024
 HEAD_COUNT = 8
 SHORT, LONG = 60, 1
-PARTS = 4
+PARTS = 2
 LATENT = 512
 LOG2E = 1.4426950408889634
 

time: 132 us -> 132 us (level)
  Pallas kernels: 42.2 us -> 34.3 us
  waiting for transfers between devices: 44.3 us -> 51.1 us
    pallas_call x2, Pallas kernels: 22.1 us -> 14.3 us  [attend(): pl.pallas_call(functools.partial(attention_kernel, sequence), grid_spec=p...]
    ppermute x26, waiting for transfers between devices: 44.3 us -> 51.1 us  [shift(): return lax.ppermute(value, AXES, pairs)]
  transfers between devices with their start and end apart: 27 -> 27, of which waited for: 18 -> 19; matrix products, arithmetic and copies ran while one was open for 1% -> 1% of each run, Pallas kernels for 31% -> 25%
where the time goes in v9:
time: 132 us; the launch traced here: 131 us
  waiting for transfers between devices  51.1 us (39%)
  starting transfers between devices  41.7 us (32%)
  Pallas kernels  34.3 us (26%)
  other arithmetic  2.92 us (2%)
    ppermute x26, waiting for transfers between devices, shift(): return lax.ppermute(value, AXES, pairs)  51.1 us
    ppermute x26, starting transfers between devices, shift(): return lax.ppermute(value, AXES, pairs)  41.6 us
    pallas_call x4, Pallas kernels, expert_terms(): pl.pallas_call(functools.partial(expert_kernel, sources=len(pieces), outp...  14.7 us
    pallas_call x2, Pallas kernels, attend(): pl.pallas_call(functools.partial(attention_kernel, sequence), grid_spec=p...  14.3 us
    pallas_call x1, Pallas kernels, joined(): pl.pallas_call(join_kernel, in_specs=[pl.BlockSpec(memory_space=pl.ANY)]...  4.23 us
  transfers between devices with their start and end apart: 27, of which 19 were waited for; matrix products, arithmetic and copies ran while one was open for 1% of the time, Pallas kernels for 25%

profile of v9, /device:TPU:0, one launch (start us, length us, event | category | flops | bytes accessed | tf_op | source)
XLA Modules:
  0.0 131.3 jit_solution(12144548444449116063)
XLA Ops:
  0.6 1.1 pack.1
  1.7 4.2 %collective-permute-start = (bf16[8,7296]{1,0:T(8,128)(2,1)S(1)}, bf16[8,7296]{1,0:T(8,128)(2,1)S(1)}, u32[]{:S(2)}, u32[]{:S(2)}) collective-permute-start(bf16[8,7296]{1,0:T(8,128)(2,1)S(1)} %pack.1), channel_id=1, source_target_pairs={{0,96},{1,97},{2,98},{3,99},{4,100},{5,101},{6,102},{7,103},{8,104... | collective-permute-start | bytes 350216 | tf_op jit(solution)/shard_map/ppermute | solution.py:43
  5.9 1.3 collective-permute-start.2
  7.2 4.2 %join.1.refs_2_ = bf16[10752,512]{1,0:T(8,128)(2,1)S(1)} custom-call(bf16[7168,256]{1,0:T(8,128)(2,1)} %bitcast.9, bf16[7168,256]{1,0:T(8,128)(2,1)} %bitcast.10, bf16[256,7168]{1,0:T(8,128)(2,1)} %bitcast.11), custom_call_target="tpu_custom_call" | custom-call | bytes 22020096 | tf_op jit(solution)/shard_map/join/pallas_call | solution.py:142
  11.4 0.9 collective-permute-done.1
  12.4 0.9 collective-permute-done.2
  13.3 0.1 collective-permute-start.9
  13.4 1.6 %collective-permute-start.4 = (bf16[32,7296]{1,0:T(8,128)(2,1)S(1)}, bf16[32,7296]{1,0:T(8,128)(2,1)S(1)}, u32[]{:S(2)}, u32[]{:S(2)}) collective-permute-start(bf16[32,7296]{1,0:T(8,128)(2,1)S(1)} %pad_maximum_fusion), channel_id=1, source_target_pairs={{0,1},{1,2},{2,3},{3,0},{4,5},{5,6},{6,7},{7,4},{8,9},{9,10},{10,1... | collective-permute-start | bytes 1400840 | tf_op jit(solution)/shard_map/ppermute | solution.py:43
  15.0 1.7 %collective-permute-start.3 = (bf16[32,7296]{1,0:T(8,128)(2,1)S(1)}, bf16[32,7296]{1,0:T(8,128)(2,1)S(1)}, u32[]{:S(2)}, u32[]{:S(2)}) collective-permute-start(bf16[32,7296]{1,0:T(8,128)(2,1)S(1)} %pad_maximum_fusion), channel_id=1, source_target_pairs={{0,3},{1,0},{2,1},{3,2},{4,7},{5,4},{6,5},{7,6},{8,11},{9,8},{10,9... | collective-permute-start | bytes 1400840 | tf_op jit(solution)/shard_map/ppermute | solution.py:43
  16.7 6.5 %collective-permute-done.4 = bf16[32,7296]{1,0:T(8,128)(2,1)S(1)} collective-permute-done((bf16[32,7296]{1,0:T(8,128)(2,1)S(1)}, bf16[32,7296]{1,0:T(8,128)(2,1)S(1)}, u32[]{:S(2)}, u32[]{:S(2)}) %collective-permute-start.4) | collective-permute-done | bytes 466976 | tf_op jit(solution)/shard_map/ppermute | solution.py:43
  23.2 0.3 collective-permute-done.3
  23.6 1.6 %collective-permute-start.5 = (bf16[16,7296]{1,0:T(8,128)(2,1)S(1)}, bf16[16,7296]{1,0:T(8,128)(2,1)S(1)}, u32[]{:S(2)}, u32[]{:S(2)}) collective-permute-start(bf16[16,7296]{1,0:T(8,128)(2,1)S(1)} %slice.75), channel_id=1, source_target_pairs={{0,1},{1,2},{2,3},{3,0},{4,5},{5,6},{6,7},{7,4},{8,9},{9,10},{10,1... | collective-permute-start | bytes 700424 | tf_op jit(solution)/shard_map/ppermute | solution.py:43
  25.3 1.6 %collective-permute-start.7 = (bf16[64,7296]{1,0:T(8,128)(2,1)S(1)}, bf16[64,7296]{1,0:T(8,128)(2,1)S(1)}, u32[]{:S(2)}, u32[]{:S(2)}) collective-permute-start(bf16[64,7296]{1,0:T(8,128)(2,1)S(1)} %constant_dynamic-update-slice_fusion.refs_0_), channel_id=1, source_target_pairs={{0,4},{1,5},{2,6},{3,7},{4,8},{5,9},{6,10},{7,11},{8,12},{9,13},{1... | collective-permute-start | bytes 2801672 | tf_op jit(solution)/shard_map/ppermute | solution.py:43
  26.8 1.7 %collective-permute-start.8 = (bf16[64,7296]{1,0:T(8,128)(2,1)S(1)}, bf16[64,7296]{1,0:T(8,128)(2,1)S(1)}, u32[]{:S(2)}, u32[]{:S(2)}) collective-permute-start(bf16[64,7296]{1,0:T(8,128)(2,1)S(1)} %constant_dynamic-update-slice_fusion.refs_0_), channel_id=1, source_target_pairs={{0,12},{1,13},{2,14},{3,15},{4,0},{5,1},{6,2},{7,3},{8,4},{9,5},{1... | collective-permute-start | bytes 2801672 | tf_op jit(solution)/shard_map/ppermute | solution.py:43
  28.6 1.7 %collective-permute-start.6 = (bf16[16,7296]{1,0:T(8,128)(2,1)S(1)}, bf16[16,7296]{1,0:T(8,128)(2,1)S(1)}, u32[]{:S(2)}, u32[]{:S(2)}) collective-permute-start(bf16[16,7296]{1,0:T(8,128)(2,1)S(1)} %slice.76), channel_id=1, source_target_pairs={{0,3},{1,0},{2,1},{3,2},{4,7},{5,4},{6,5},{7,6},{8,11},{9,8},{10,9... | collective-permute-start | bytes 700424 | tf_op jit(solution)/shard_map/ppermute | solution.py:43
  30.2 3.3 %collective-permute-done.5 = bf16[16,7296]{1,0:T(8,128)(2,1)S(1)} collective-permute-done((bf16[16,7296]{1,0:T(8,128)(2,1)S(1)}, bf16[16,7296]{1,0:T(8,128)(2,1)S(1)}, u32[]{:S(2)}, u32[]{:S(2)}) %collective-permute-start.5) | collective-permute-done | bytes 233504 | tf_op jit(solution)/shard_map/ppermute | solution.py:43
  33.5 3.7 %collective-permute-done.6 = bf16[16,7296]{1,0:T(8,128)(2,1)S(1)} collective-permute-done((bf16[16,7296]{1,0:T(8,128)(2,1)S(1)}, bf16[16,7296]{1,0:T(8,128)(2,1)S(1)}, u32[]{:S(2)}, u32[]{:S(2)}) %collective-permute-start.6) | collective-permute-done | bytes 233504 | tf_op jit(solution)/shard_map/ppermute | solution.py:43
  37.3 1.6 %collective-permute-start.10 = (bf16[64,7296]{1,0:T(8,128)(2,1)S(1)}, bf16[64,7296]{1,0:T(8,128)(2,1)S(1)}, u32[]{:S(2)}, u32[]{:S(2)}) collective-permute-start(bf16[64,7296]{1,0:T(8,128)(2,1)S(1)} %constant_dynamic-update-slice_fusion.2.refs_1_), channel_id=1, source_target_pairs={{0,12},{1,13},{2,14},{3,15},{4,0},{5,1},{6,2},{7,3},{8,4},{9,5},{1... | collective-permute-start | bytes 2801672 | tf_op jit(solution)/shard_map/ppermute | solution.py:43
  38.9 0.5 collective-permute-start.13
  39.4 0.7 collective-permute-done.7.refs_1_
  40.1 0.3 collective-permute-done.8.refs_0_
  40.4 3.7 %expert.4 = (bf16[64,7168]{1,0:T(8,128)(2,1)S(1)}, bf16[64,7168]{1,0:T(8,128)(2,1)S(1)}) custom-call(bf16[64,7296]{1,0:T(8,128)(2,1)S(1)} %constant_dynamic-update-slice_fusion.refs_0_, bf16[64,7296]{1,0:T(8,128)(2,1)S(1)} %constant_dynamic-update-slice_fusion.2.refs_1_, bf16[10752,512]{1,0:T(8,128)(2,1)S(1)} %join.1.refs_2_, ...), custom_call_target="tpu_custom_call" | custom-call | flops 2818572288 | bytes 3670016 | tf_op jit(solution)/shard_map/expert/pallas_call | solution.py:104
  44.1 3.7 %expert.5 = (bf16[64,7168]{1,0:T(8,128)(2,1)S(1)}, bf16[64,7168]{1,0:T(8,128)(2,1)S(1)}) custom-call(bf16[64,7296]{1,0:T(8,128)(2,1)S(1)} %collective-permute-done.8.refs_0_, bf16[64,7296]{1,0:T(8,128)(2,1)S(1)} %collective-permute-done.7.refs_1_, bf16[10752,512]{1,0:T(8,128)(2,1)S(1)} %join.1.refs_2_, bf16[10752,512]{1,0:T(8,128)(2,1)S(1)} %collective-permute-done.9.refs_3_), custom_call_target="tpu_custom_call" | custom-call | flops 2818572288 | bytes 3670016 | tf_op jit(solution)/shard_map/expert/pallas_call | solution.py:104
  47.8 3.1 %collective-permute-done.10.refs_0_ = bf16[64,7296]{1,0:T(8,128)(2,1)S(1)} collective-permute-done((bf16[64,7296]{1,0:T(8,128)(2,1)S(1)}, bf16[64,7296]{1,0:T(8,128)(2,1)S(1)}, u32[]{:S(2)}, u32[]{:S(2)}) %collective-permute-start.10) | collective-permute-done | bytes 933920 | tf_op jit(solution)/shard_map/ppermute | solution.py:43
  50.9 1.0 collective-permute-start.11
  51.9 2.3 %collective-permute-start.12 = (bf16[64,7296]{1,0:T(8,128)(2,1)S(1)}, bf16[64,7296]{1,0:T(8,128)(2,1)S(1)}, u32[]{:S(2)}, u32[]{:S(2)}) collective-permute-start(bf16[64,7296]{1,0:T(8,128)(2,1)S(1)} %collective-permute-done.10.refs_0_), channel_id=1, source_target_pairs={{0,12},{1,13},{2,14},{3,15},{4,0},{5,1},{6,2},{7,3},{8,4},{9,5},{1... | collective-permute-start | bytes 2801672 | tf_op jit(solution)/shard_map/ppermute | solution.py:43
  54.2 3.7 %expert.6 = (bf16[64,7168]{1,0:T(8,128)(2,1)S(1)}, bf16[64,7168]{1,0:T(8,128)(2,1)S(1)}) custom-call(bf16[64,7296]{1,0:T(8,128)(2,1)S(1)} %collective-permute-done.10.refs_0_, bf16[64,7296]{1,0:T(8,128)(2,1)S(1)} %collective-permute-done.13.refs_1_, bf16[10752,512]{1,0:T(8,128)(2,1)S(1)} %join.1.refs_2_, bf16[10752,512]{1,0:T(8,128)(2,1)S(1)} %collective-permute-done.9.refs_3_), custom_call_target="tpu_custom_call" | custom-call | flops 2818572288 | bytes 3670016 | tf_op jit(solution)/shard_map/expert/pallas_call | solution.py:104
  57.9 0.1 collective-permute-start.16
  58.0 3.2 %collective-permute-start.17 = (bf16[64,7168]{1,0:T(8,128)(2,1)S(1)}, bf16[64,7168]{1,0:T(8,128)(2,1)S(1)}, u32[]{:S(2)}, u32[]{:S(2)}) collective-permute-start(bf16[64,7168]{1,0:T(8,128)(2,1)S(1)} %get-tuple-element.68), channel_id=1, source_target_pairs={{0,12},{1,13},{2,14},{3,15},{4,0},{5,1},{6,2},{7,3},{8,4},{9,5},{1... | collective-permute-start | bytes 2752520 | tf_op jit(solution)/shard_map/ppermute | solution.py:43
  61.2 4.5 %collective-permute-done.11.refs_0_ = bf16[64,7296]{1,0:T(8,128)(2,1)S(1)} collective-permute-done((bf16[64,7296]{1,0:T(8,128)(2,1)S(1)}, bf16[64,7296]{1,0:T(8,128)(2,1)S(1)}, u32[]{:S(2)}, u32[]{:S(2)}) %collective-permute-start.11) | collective-permute-done | bytes 933920 | tf_op jit(solution)/shard_map/ppermute | solution.py:43
  65.7 3.7 %expert.7 = (bf16[64,7168]{1,0:T(8,128)(2,1)S(1)}, bf16[64,7168]{1,0:T(8,128)(2,1)S(1)}) custom-call(bf16[64,7296]{1,0:T(8,128)(2,1)S(1)} %collective-permute-done.11.refs_0_, bf16[64,7296]{1,0:T(8,128)(2,1)S(1)} %collective-permute-done.12.refs_1_, bf16[10752,512]{1,0:T(8,128)(2,1)S(1)} %join.1.refs_2_, bf16[10752,512]{1,0:T(8,128)(2,1)S(1)} %collective-permute-done.9.refs_3_), custom_call_target="tpu_custom_call" | custom-call | flops 2818572288 | bytes 3670016 | tf_op jit(solution)/shard_map/expert/pallas_call | solution.py:104
  69.4 1.0 collective-permute-start.14
  70.4 2.3 %collective-permute-start.15 = (bf16[64,7168]{1,0:T(8,128)(2,1)S(1)}, bf16[64,7168]{1,0:T(8,128)(2,1)S(1)}, u32[]{:S(2)}, u32[]{:S(2)}) collective-permute-start(bf16[64,7168]{1,0:T(8,128)(2,1)S(1)} %get-tuple-element.72), channel_id=1, source_target_pairs={{0,12},{1,13},{2,14},{3,15},{4,0},{5,1},{6,2},{7,3},{8,4},{9,5},{1... | collective-permute-start | bytes 2752520 | tf_op jit(solution)/shard_map/ppermute | solution.py:43
  72.8 7.1 %attend.2 = bf16[64,1024]{1,0:T(8,128)(2,1)S(1)} custom-call(s32[2]{0:T(128)S(1)} %copy-done.7, bf16[128,1024]{1,0:T(8,128)(2,1)S(1)} %copy-done.3, bf16[128,512]{1,0:T(8,128)(2,1)S(1)} %copy-done.4, bf16[8,128,512]{2,1,0:T(8,128)(2,1)S(1)} %copy-done, bf16[8,512,128]{2,1,0:T(8,128)(2,1)S(1)} %copy-done.1, bf16[2,4096,512]{2,1,0:T(8,128)(2,1)} %latent_ref.3, ...), custom_call_target="tpu_custom_call" | custom-call | flops 100000000 | bytes 133333 | tf_op jit(solution)/shard_map/attend/pallas_call | solution.py:254
  80.0 5.4 %collective-permute-done.14 = bf16[64,7168]{1,0:T(8,128)(2,1)S(1)} collective-permute-done((bf16[64,7168]{1,0:T(8,128)(2,1)S(1)}, bf16[64,7168]{1,0:T(8,128)(2,1)S(1)}, u32[]{:S(2)}, u32[]{:S(2)}) %collective-permute-start.14) | collective-permute-done | bytes 917536 | tf_op jit(solution)/shard_map/ppermute | solution.py:43
  85.4 0.2 add_convert_fusion
  85.6 3.3 %collective-permute-start.19 = (bf16[64,7168]{1,0:T(8,128)(2,1)S(1)}, bf16[64,7168]{1,0:T(8,128)(2,1)S(1)}, u32[]{:S(2)}, u32[]{:S(2)}) collective-permute-start(bf16[64,7168]{1,0:T(8,128)(2,1)S(1)} %add_convert_fusion), channel_id=1, source_target_pairs={{0,12},{1,13},{2,14},{3,15},{4,0},{5,1},{6,2},{7,3},{8,4},{9,5},{1... | collective-permute-start | bytes 2752520 | tf_op jit(solution)/shard_map/ppermute | solution.py:43
  88.9 0.2 add_convert_fusion.1
  89.1 0.3 collective-permute-start.18
  89.4 7.2 %attend.3 = bf16[64,1024]{1,0:T(8,128)(2,1)S(1)} custom-call(s32[2]{0:T(128)S(1)} %copy-done.7, bf16[128,1024]{1,0:T(8,128)(2,1)S(1)} %copy-done.3, bf16[128,512]{1,0:T(8,128)(2,1)S(1)} %copy-done.4, bf16[8,128,512]{2,1,0:T(8,128)(2,1)S(1)} %copy-done, bf16[8,512,128]{2,1,0:T(8,128)(2,1)S(1)} %copy-done.1, bf16[2,4096,512]{2,1,0:T(8,128)(2,1)} %latent_ref.3, ...), custom_call_target="tpu_custom_call" | custom-call | flops 6000000000 | bytes 8000000 | tf_op jit(solution)/shard_map/attend/pallas_call | solution.py:254
  96.6 3.2 %collective-permute-done.19 = bf16[64,7168]{1,0:T(8,128)(2,1)S(1)} collective-permute-done((bf16[64,7168]{1,0:T(8,128)(2,1)S(1)}, bf16[64,7168]{1,0:T(8,128)(2,1)S(1)}, u32[]{:S(2)}, u32[]{:S(2)}) %collective-permute-start.19) | collective-permute-done | bytes 917536 | tf_op jit(solution)/shard_map/ppermute | solution.py:43
  99.8 4.2 %collective-permute-done.18 = bf16[64,7168]{1,0:T(8,128)(2,1)S(1)} collective-permute-done((bf16[64,7168]{1,0:T(8,128)(2,1)S(1)}, bf16[64,7168]{1,0:T(8,128)(2,1)S(1)}, u32[]{:S(2)}, u32[]{:S(2)}) %collective-permute-start.18) | collective-permute-done | bytes 917536 | tf_op jit(solution)/shard_map/ppermute | solution.py:43
  104.0 0.3 fusion.3
  104.4 0.3 convert_add_fusion.1
  104.8 1.3 %collective-permute-start.20 = (bf16[32,7168]{1,0:T(8,128)(2,1)S(1)}, bf16[32,7168]{1,0:T(8,128)(2,1)S(1)}, u32[]{:S(2)}, u32[]{:S(2)}) collective-permute-start(bf16[32,7168]{1,0:T(8,128)(2,1)S(1)} %pad_maximum_fusion.1), channel_id=1, source_target_pairs={{0,1},{1,2},{2,3},{3,0},{4,5},{5,6},{6,7},{7,4},{8,9},{9,10},{10,1... | collective-permute-start | bytes 1376264 | tf_op jit(solution)/shard_map/ppermute | solution.py:43
  106.1 2.0 %collective-permute-start.21 = (bf16[32,7168]{1,0:T(8,128)(2,1)S(1)}, bf16[32,7168]{1,0:T(8,128)(2,1)S(1)}, u32[]{:S(2)}, u32[]{:S(2)}) collective-permute-start(bf16[32,7168]{1,0:T(8,128)(2,1)S(1)} %concatenate.29), channel_id=1, source_target_pairs={{0,3},{1,0},{2,1},{3,2},{4,7},{5,4},{6,5},{7,6},{8,11},{9,8},{10,9... | collective-permute-start | bytes 1376264 | tf_op jit(solution)/shard_map/ppermute | solution.py:43
  108.2 6.3 %collective-permute-done.20 = bf16[32,7168]{1,0:T(8,128)(2,1)S(1)} collective-permute-done((bf16[32,7168]{1,0:T(8,128)(2,1)S(1)}, bf16[32,7168]{1,0:T(8,128)(2,1)S(1)}, u32[]{:S(2)}, u32[]{:S(2)}) %collective-permute-start.20) | collective-permute-done | bytes 458784 | tf_op jit(solution)/shard_map/ppermute | solution.py:43
  114.5 0.1 fusion.2
  114.6 0.1 collective-permute-done.21
  114.7 0.1 fusion.1
  114.7 1.5 %collective-permute-start.22 = (bf16[16,7168]{1,0:T(8,128)(2,1)S(1)}, bf16[16,7168]{1,0:T(8,128)(2,1)S(1)}, u32[]{:S(2)}, u32[]{:S(2)}) collective-permute-start(bf16[16,7168]{1,0:T(8,128)(2,1)S(1)} %fusion.2), channel_id=1, source_target_pairs={{0,1},{1,2},{2,3},{3,0},{4,5},{5,6},{6,7},{7,4},{8,9},{9,10},{10,1... | collective-permute-start | bytes 688136 | tf_op jit(solution)/shard_map/ppermute | solution.py:43
  116.2 1.8 %collective-permute-start.23 = (bf16[16,7168]{1,0:T(8,128)(2,1)S(1)}, bf16[16,7168]{1,0:T(8,128)(2,1)S(1)}, u32[]{:S(2)}, u32[]{:S(2)}) collective-permute-start(bf16[16,7168]{1,0:T(8,128)(2,1)S(1)} %fusion.1), channel_id=1, source_target_pairs={{0,3},{1,0},{2,1},{3,2},{4,7},{5,4},{6,5},{7,6},{8,11},{9,8},{10,9... | collective-permute-start | bytes 688136 | tf_op jit(solution)/shard_map/ppermute | solution.py:43
  118.1 4.0 %collective-permute-done.22 = bf16[16,7168]{1,0:T(8,128)(2,1)S(1)} collective-permute-done((bf16[16,7168]{1,0:T(8,128)(2,1)S(1)}, bf16[16,7168]{1,0:T(8,128)(2,1)S(1)}, u32[]{:S(2)}, u32[]{:S(2)}) %collective-permute-start.22) | collective-permute-done | bytes 229408 | tf_op jit(solution)/shard_map/ppermute | solution.py:43
  122.0 0.1 convert_add_fusion.3
  122.1 0.2 collective-permute-done.23
  122.3 0.1 convert_add_fusion.2
  122.3 0.1 fusion
  122.5 0.5 collective-permute-start.24
  123.0 2.4 %collective-permute-start.25 = (bf16[8,7168]{1,0:T(8,128)(2,1)S(1)}, bf16[8,7168]{1,0:T(8,128)(2,1)S(1)}, u32[]{:S(2)}, u32[]{:S(2)}) collective-permute-start(bf16[8,7168]{1,0:T(8,128)(2,1)S(1)} %get-tuple-element.92), channel_id=1, source_target_pairs={{0,64},{1,65},{2,66},{3,67},{4,68},{5,69},{6,70},{7,71},{8,72},{9,... | collective-permute-start | bytes 344072 | tf_op jit(solution)/shard_map/ppermute | solution.py:43
  125.4 1.0 collective-permute-start.26
  126.4 0.7 pad_maximum_fusion.2
  127.1 2.7 %collective-permute-done.24 = bf16[8,7168]{1,0:T(8,128)(2,1)S(1)} collective-permute-done((bf16[8,7168]{1,0:T(8,128)(2,1)S(1)}, bf16[8,7168]{1,0:T(8,128)(2,1)S(1)}, u32[]{:S(2)}, u32[]{:S(2)}) %collective-permute-start.24) | collective-permute-done | bytes 114720 | tf_op jit(solution)/shard_map/ppermute | solution.py:43
  129.8 0.9 collective-permute-done.26
  130.6 0.7 add_convert_fusion.2
  (38 shorter events, 0.4 us)
Async XLA Ops:
  1.7 9.7 %collective-permute-start = (bf16[8,7296]{1,0:T(8,128)(2,1)S(1)}, bf16[8,7296]{1,0:T(8,128)(2,1)S(1)}, u32[]{:S(2)}, u32[]{:S(2)}) collective-permute-start(bf16[8,7296]{1,0:T(8,128)(2,1)S(1)} %pack.1), channel_id=1, source_target_pairs={{0,96},{1,97},{2,98},{3,99},{4,100},{5,101},{6,102},{7,103},{8,104... | collective-permute-start | bytes 350216 | tf_op jit(solution)/shard_map/ppermute | solution.py:43
  5.9 6.4 %collective-permute-start.1 = (bf16[8,7296]{1,0:T(8,128)(2,1)S(1)}, bf16[8,7296]{1,0:T(8,128)(2,1)S(1)}, u32[]{:S(2)}, u32[]{:S(2)}) collective-permute-start(bf16[8,7296]{1,0:T(8,128)(2,1)S(1)} %pack.1), channel_id=1, source_target_pairs={{0,64},{1,65},{2,66},{3,67},{4,68},{5,69},{6,70},{7,71},{8,72},{9,... | collective-permute-start | bytes 350216 | tf_op jit(solution)/shard_map/ppermute | solution.py:43
  5.9 7.3 %collective-permute-start.2 = (bf16[8,7296]{1,0:T(8,128)(2,1)S(1)}, bf16[8,7296]{1,0:T(8,128)(2,1)S(1)}, u32[]{:S(2)}, u32[]{:S(2)}) collective-permute-start(bf16[8,7296]{1,0:T(8,128)(2,1)S(1)} %pack.1), channel_id=1, source_target_pairs={{0,32},{1,33},{2,34},{3,35},{4,36},{5,37},{6,38},{7,39},{8,40},{9,... | collective-permute-start | bytes 350216 | tf_op jit(solution)/shard_map/ppermute | solution.py:43
  13.3 27.1 %collective-permute-start.9 = (bf16[10752,512]{1,0:T(8,128)(2,1)S(1)}, bf16[10752,512]{1,0:T(8,128)(2,1)S(1)}, u32[]{:S(2)}, u32[]{:S(2)}) collective-permute-start(bf16[10752,512]{1,0:T(8,128)(2,1)S(1)} %join.1.refs_2_), channel_id=1, source_target_pairs={{0,16},{16,0},{1,17},{17,1},{2,18},{18,2},{3,19},{19,3},{4,20},{20... | collective-permute-start | bytes 33030152 | tf_op jit(solution)/shard_map/ppermute | solution.py:59
  13.4 9.8 %collective-permute-start.4 = (bf16[32,7296]{1,0:T(8,128)(2,1)S(1)}, bf16[32,7296]{1,0:T(8,128)(2,1)S(1)}, u32[]{:S(2)}, u32[]{:S(2)}) collective-permute-start(bf16[32,7296]{1,0:T(8,128)(2,1)S(1)} %pad_maximum_fusion), channel_id=1, source_target_pairs={{0,1},{1,2},{2,3},{3,0},{4,5},{5,6},{6,7},{7,4},{8,9},{9,10},{10,1... | collective-permute-start | bytes 1400840 | tf_op jit(solution)/shard_map/ppermute | solution.py:43
  15.0 8.6 %collective-permute-start.3 = (bf16[32,7296]{1,0:T(8,128)(2,1)S(1)}, bf16[32,7296]{1,0:T(8,128)(2,1)S(1)}, u32[]{:S(2)}, u32[]{:S(2)}) collective-permute-start(bf16[32,7296]{1,0:T(8,128)(2,1)S(1)} %pad_maximum_fusion), channel_id=1, source_target_pairs={{0,3},{1,0},{2,1},{3,2},{4,7},{5,4},{6,5},{7,6},{8,11},{9,8},{10,9... | collective-permute-start | bytes 1400840 | tf_op jit(solution)/shard_map/ppermute | solution.py:43
  23.6 9.9 %collective-permute-start.5 = (bf16[16,7296]{1,0:T(8,128)(2,1)S(1)}, bf16[16,7296]{1,0:T(8,128)(2,1)S(1)}, u32[]{:S(2)}, u32[]{:S(2)}) collective-permute-start(bf16[16,7296]{1,0:T(8,128)(2,1)S(1)} %slice.75), channel_id=1, source_target_pairs={{0,1},{1,2},{2,3},{3,0},{4,5},{5,6},{6,7},{7,4},{8,9},{9,10},{10,1... | collective-permute-start | bytes 700424 | tf_op jit(solution)/shard_map/ppermute | solution.py:43
  25.3 14.8 %collective-permute-start.7 = (bf16[64,7296]{1,0:T(8,128)(2,1)S(1)}, bf16[64,7296]{1,0:T(8,128)(2,1)S(1)}, u32[]{:S(2)}, u32[]{:S(2)}) collective-permute-start(bf16[64,7296]{1,0:T(8,128)(2,1)S(1)} %constant_dynamic-update-slice_fusion.refs_0_), channel_id=1, source_target_pairs={{0,4},{1,5},{2,6},{3,7},{4,8},{5,9},{6,10},{7,11},{8,12},{9,13},{1... | collective-permute-start | bytes 2801672 | tf_op jit(solution)/shard_map/ppermute | solution.py:43
  26.8 13.6 %collective-permute-start.8 = (bf16[64,7296]{1,0:T(8,128)(2,1)S(1)}, bf16[64,7296]{1,0:T(8,128)(2,1)S(1)}, u32[]{:S(2)}, u32[]{:S(2)}) collective-permute-start(bf16[64,7296]{1,0:T(8,128)(2,1)S(1)} %constant_dynamic-update-slice_fusion.refs_0_), channel_id=1, source_target_pairs={{0,12},{1,13},{2,14},{3,15},{4,0},{5,1},{6,2},{7,3},{8,4},{9,5},{1... | collective-permute-start | bytes 2801672 | tf_op jit(solution)/shard_map/ppermute | solution.py:43
  28.6 8.6 %collective-permute-start.6 = (bf16[16,7296]{1,0:T(8,128)(2,1)S(1)}, bf16[16,7296]{1,0:T(8,128)(2,1)S(1)}, u32[]{:S(2)}, u32[]{:S(2)}) collective-permute-start(bf16[16,7296]{1,0:T(8,128)(2,1)S(1)} %slice.76), channel_id=1, source_target_pairs={{0,3},{1,0},{2,1},{3,2},{4,7},{5,4},{6,5},{7,6},{8,11},{9,8},{10,9... | collective-permute-start | bytes 700424 | tf_op jit(solution)/shard_map/ppermute | solution.py:43
  37.3 13.6 %collective-permute-start.10 = (bf16[64,7296]{1,0:T(8,128)(2,1)S(1)}, bf16[64,7296]{1,0:T(8,128)(2,1)S(1)}, u32[]{:S(2)}, u32[]{:S(2)}) collective-permute-start(bf16[64,7296]{1,0:T(8,128)(2,1)S(1)} %constant_dynamic-update-slice_fusion.2.refs_1_), channel_id=1, source_target_pairs={{0,12},{1,13},{2,14},{3,15},{4,0},{5,1},{6,2},{7,3},{8,4},{9,5},{1... | collective-permute-start | bytes 2801672 | tf_op jit(solution)/shard_map/ppermute | solution.py:43
  38.9 15.3 %collective-permute-start.13 = (bf16[64,7296]{1,0:T(8,128)(2,1)S(1)}, bf16[64,7296]{1,0:T(8,128)(2,1)S(1)}, u32[]{:S(2)}, u32[]{:S(2)}) collective-permute-start(bf16[64,7296]{1,0:T(8,128)(2,1)S(1)} %constant_dynamic-update-slice_fusion.2.refs_1_), channel_id=1, source_target_pairs={{0,4},{1,5},{2,6},{3,7},{4,8},{5,9},{6,10},{7,11},{8,12},{9,13},{1... | collective-permute-start | bytes 2801672 | tf_op jit(solution)/shard_map/ppermute | solution.py:43
  50.9 14.8 %collective-permute-start.11 = (bf16[64,7296]{1,0:T(8,128)(2,1)S(1)}, bf16[64,7296]{1,0:T(8,128)(2,1)S(1)}, u32[]{:S(2)}, u32[]{:S(2)}) collective-permute-start(bf16[64,7296]{1,0:T(8,128)(2,1)S(1)} %collective-permute-done.7.refs_1_), channel_id=1, source_target_pairs={{0,4},{1,5},{2,6},{3,7},{4,8},{5,9},{6,10},{7,11},{8,12},{9,13},{1... | collective-permute-start | bytes 2801672 | tf_op jit(solution)/shard_map/ppermute | solution.py:43
  51.9 13.8 %collective-permute-start.12 = (bf16[64,7296]{1,0:T(8,128)(2,1)S(1)}, bf16[64,7296]{1,0:T(8,128)(2,1)S(1)}, u32[]{:S(2)}, u32[]{:S(2)}) collective-permute-start(bf16[64,7296]{1,0:T(8,128)(2,1)S(1)} %collective-permute-done.10.refs_0_), channel_id=1, source_target_pairs={{0,12},{1,13},{2,14},{3,15},{4,0},{5,1},{6,2},{7,3},{8,4},{9,5},{1... | collective-permute-start | bytes 2801672 | tf_op jit(solution)/shard_map/ppermute | solution.py:43
  57.8 14.9 %copy-start = (bf16[8,128,512]{2,1,0:T(8,128)(2,1)S(1)}, bf16[8,128,512]{2,1,0:T(8,128)(2,1)}, u32[]{:S(2)}) copy-start(bf16[8,128,512]{2,1,0:T(8,128)(2,1)} %key_up_ref.3) | copy-start | bytes 3145732
  57.9 14.9 %copy-start.1 = (bf16[8,512,128]{2,1,0:T(8,128)(2,1)S(1)}, bf16[8,512,128]{2,1,0:T(8,128)(2,1)}, u32[]{:S(2)}) copy-start(bf16[8,512,128]{2,1,0:T(8,128)(2,1)} %value_up_ref.3) | copy-start | bytes 3145732
  57.9 14.9 %copy-start.2 = (bf16[2,4096,64]{1,2,0:T(8,128)(2,1)S(1)}, bf16[2,4096,64]{1,2,0:T(8,128)(2,1)}, u32[]{:S(2)}) copy-start(bf16[2,4096,64]{1,2,0:T(8,128)(2,1)} %param.26) | copy-start | bytes 3145732
  57.9 14.9 %copy-start.3 = (bf16[128,1024]{1,0:T(8,128)(2,1)S(1)}, bf16[128,1024]{1,0:T(8,128)(2,1)}, u32[]{:S(2)}) copy-start(bf16[128,1024]{1,0:T(8,128)(2,1)} %nope_ref.3) | copy-start | bytes 786436
  57.9 14.9 %copy-start.4 = (bf16[128,512]{1,0:T(8,128)(2,1)S(1)}, bf16[128,512]{1,0:T(8,128)(2,1)}, u32[]{:S(2)}) copy-start(bf16[128,512]{1,0:T(8,128)(2,1)} %rope_ref.3) | copy-start | bytes 393220
  57.9 14.9 %copy-start.5 = (bf16[128,512]{1,0:T(8,128)(2,1)S(1)}, bf16[128,512]{1,0:T(8,128)(2,1)}, u32[]{:S(2)}) copy-start(bf16[128,512]{1,0:T(8,128)(2,1)} %new_latent_ref.3) | copy-start | bytes 393220
  57.9 14.9 %copy-start.6 = (bf16[128,64]{0,1:T(8,128)(2,1)S(1)}, bf16[128,64]{0,1:T(8,128)(2,1)}, u32[]{:S(2)}) copy-start(bf16[128,64]{0,1:T(8,128)(2,1)} %param.28) | copy-start | bytes 49156
  57.9 14.9 %copy-start.7 = (s32[2]{0:T(128)S(1)}, s32[2]{0:T(128)}, u32[]{:S(2)}) copy-start(s32[2]{0:T(128)} %length_ref.1) | copy-start | bytes 28
  57.9 22.0 %collective-permute-start.16 = (bf16[64,7168]{1,0:T(8,128)(2,1)S(1)}, bf16[64,7168]{1,0:T(8,128)(2,1)S(1)}, u32[]{:S(2)}, u32[]{:S(2)}) collective-permute-start(bf16[64,7168]{1,0:T(8,128)(2,1)S(1)} %get-tuple-element.67), channel_id=1, source_target_pairs={{0,4},{1,5},{2,6},{3,7},{4,8},{5,9},{6,10},{7,11},{8,12},{9,13},{1... | collective-permute-start | bytes 2752520 | tf_op jit(solution)/shard_map/ppermute | solution.py:43
  58.0 21.9 %collective-permute-start.17 = (bf16[64,7168]{1,0:T(8,128)(2,1)S(1)}, bf16[64,7168]{1,0:T(8,128)(2,1)S(1)}, u32[]{:S(2)}, u32[]{:S(2)}) collective-permute-start(bf16[64,7168]{1,0:T(8,128)(2,1)S(1)} %get-tuple-element.68), channel_id=1, source_target_pairs={{0,12},{1,13},{2,14},{3,15},{4,0},{5,1},{6,2},{7,3},{8,4},{9,5},{1... | collective-permute-start | bytes 2752520 | tf_op jit(solution)/shard_map/ppermute | solution.py:43
  69.4 16.0 %collective-permute-start.14 = (bf16[64,7168]{1,0:T(8,128)(2,1)S(1)}, bf16[64,7168]{1,0:T(8,128)(2,1)S(1)}, u32[]{:S(2)}, u32[]{:S(2)}) collective-permute-start(bf16[64,7168]{1,0:T(8,128)(2,1)S(1)} %get-tuple-element.71), channel_id=1, source_target_pairs={{0,4},{1,5},{2,6},{3,7},{4,8},{5,9},{6,10},{7,11},{8,12},{9,13},{1... | collective-permute-start | bytes 2752520 | tf_op jit(solution)/shard_map/ppermute | solution.py:43
  70.4 14.9 %collective-permute-start.15 = (bf16[64,7168]{1,0:T(8,128)(2,1)S(1)}, bf16[64,7168]{1,0:T(8,128)(2,1)S(1)}, u32[]{:S(2)}, u32[]{:S(2)}) collective-permute-start(bf16[64,7168]{1,0:T(8,128)(2,1)S(1)} %get-tuple-element.72), channel_id=1, source_target_pairs={{0,12},{1,13},{2,14},{3,15},{4,0},{5,1},{6,2},{7,3},{8,4},{9,5},{1... | collective-permute-start | bytes 2752520 | tf_op jit(solution)/shard_map/ppermute | solution.py:43
  85.6 14.2 %collective-permute-start.19 = (bf16[64,7168]{1,0:T(8,128)(2,1)S(1)}, bf16[64,7168]{1,0:T(8,128)(2,1)S(1)}, u32[]{:S(2)}, u32[]{:S(2)}) collective-permute-start(bf16[64,7168]{1,0:T(8,128)(2,1)S(1)} %add_convert_fusion), channel_id=1, source_target_pairs={{0,12},{1,13},{2,14},{3,15},{4,0},{5,1},{6,2},{7,3},{8,4},{9,5},{1... | collective-permute-start | bytes 2752520 | tf_op jit(solution)/shard_map/ppermute | solution.py:43
  89.1 14.9 %collective-permute-start.18 = (bf16[64,7168]{1,0:T(8,128)(2,1)S(1)}, bf16[64,7168]{1,0:T(8,128)(2,1)S(1)}, u32[]{:S(2)}, u32[]{:S(2)}) collective-permute-start(bf16[64,7168]{1,0:T(8,128)(2,1)S(1)} %add_convert_fusion.1), channel_id=1, source_target_pairs={{0,4},{1,5},{2,6},{3,7},{4,8},{5,9},{6,10},{7,11},{8,12},{9,13},{1... | collective-permute-start | bytes 2752520 | tf_op jit(solution)/shard_map/ppermute | solution.py:43
  104.8 9.8 %collective-permute-start.20 = (bf16[32,7168]{1,0:T(8,128)(2,1)S(1)}, bf16[32,7168]{1,0:T(8,128)(2,1)S(1)}, u32[]{:S(2)}, u32[]{:S(2)}) collective-permute-start(bf16[32,7168]{1,0:T(8,128)(2,1)S(1)} %pad_maximum_fusion.1), channel_id=1, source_target_pairs={{0,1},{1,2},{2,3},{3,0},{4,5},{5,6},{6,7},{7,4},{8,9},{9,10},{10,1... | collective-permute-start | bytes 1376264 | tf_op jit(solution)/shard_map/ppermute | solution.py:43
  106.1 8.5 %collective-permute-start.21 = (bf16[32,7168]{1,0:T(8,128)(2,1)S(1)}, bf16[32,7168]{1,0:T(8,128)(2,1)S(1)}, u32[]{:S(2)}, u32[]{:S(2)}) collective-permute-start(bf16[32,7168]{1,0:T(8,128)(2,1)S(1)} %concatenate.29), channel_id=1, source_target_pairs={{0,3},{1,0},{2,1},{3,2},{4,7},{5,4},{6,5},{7,6},{8,11},{9,8},{10,9... | collective-permute-start | bytes 1376264 | tf_op jit(solution)/shard_map/ppermute | solution.py:43
  114.7 7.3 %collective-permute-start.22 = (bf16[16,7168]{1,0:T(8,128)(2,1)S(1)}, bf16[16,7168]{1,0:T(8,128)(2,1)S(1)}, u32[]{:S(2)}, u32[]{:S(2)}) collective-permute-start(bf16[16,7168]{1,0:T(8,128)(2,1)S(1)} %fusion.2), channel_id=1, source_target_pairs={{0,1},{1,2},{2,3},{3,0},{4,5},{5,6},{6,7},{7,4},{8,9},{9,10},{10,1... | collective-permute-start | bytes 688136 | tf_op jit(solution)/shard_map/ppermute | solution.py:43
  116.2 6.0 %collective-permute-start.23 = (bf16[16,7168]{1,0:T(8,128)(2,1)S(1)}, bf16[16,7168]{1,0:T(8,128)(2,1)S(1)}, u32[]{:S(2)}, u32[]{:S(2)}) collective-permute-start(bf16[16,7168]{1,0:T(8,128)(2,1)S(1)} %fusion.1), channel_id=1, source_target_pairs={{0,3},{1,0},{2,1},{3,2},{4,7},{5,4},{6,5},{7,6},{8,11},{9,8},{10,9... | collective-permute-start | bytes 688136 | tf_op jit(solution)/shard_map/ppermute | solution.py:43
  122.5 7.3 %collective-permute-start.24 = (bf16[8,7168]{1,0:T(8,128)(2,1)S(1)}, bf16[8,7168]{1,0:T(8,128)(2,1)S(1)}, u32[]{:S(2)}, u32[]{:S(2)}) collective-permute-start(bf16[8,7168]{1,0:T(8,128)(2,1)S(1)} %get-tuple-element.90), channel_id=1, source_target_pairs={{0,32},{1,33},{2,34},{3,35},{4,36},{5,37},{6,38},{7,39},{8,40},{9,... | collective-permute-start | bytes 344072 | tf_op jit(solution)/shard_map/ppermute | solution.py:43
  123.0 6.8 %collective-permute-start.25 = (bf16[8,7168]{1,0:T(8,128)(2,1)S(1)}, bf16[8,7168]{1,0:T(8,128)(2,1)S(1)}, u32[]{:S(2)}, u32[]{:S(2)}) collective-permute-start(bf16[8,7168]{1,0:T(8,128)(2,1)S(1)} %get-tuple-element.92), channel_id=1, source_target_pairs={{0,64},{1,65},{2,66},{3,67},{4,68},{5,69},{6,70},{7,71},{8,72},{9,... | collective-permute-start | bytes 344072 | tf_op jit(solution)/shard_map/ppermute | solution.py:43
  125.4 5.3 %collective-permute-start.26 = (bf16[8,7168]{1,0:T(8,128)(2,1)S(1)}, bf16[8,7168]{1,0:T(8,128)(2,1)S(1)}, u32[]{:S(2)}, u32[]{:S(2)}) collective-permute-start(bf16[8,7168]{1,0:T(8,128)(2,1)S(1)} %get-tuple-element.91), channel_id=1, source_target_pairs={{0,96},{1,97},{2,98},{3,99},{4,100},{5,101},{6,102},{7,103},{8,104... | collective-permute-start | bytes 344072 | tf_op jit(solution)/shard_map/ppermute | solution.py:43

commit v10 on v9

--- a/solution.py
+++ b/solution.py
@@ -328,8 +328,9 @@
     own_terms = expert_terms([own_low, own_high], weights)
     above_low, relayed, own_terms = lax.optimization_barrier((above_low, below_low, own_terms))
     above_low, below_low = expert_terms([above_low, relayed], weights)
-    relayed, above_high, above_low, below_low = lax.optimization_barrier((relayed, above_high, above_low, below_low))
-    far_low, far_high = shift(relayed, 2, 1), shift(above_high, 2, -1)
+    far_low = shift(relayed, 2, 1)
+    above_high, above_low, below_low = lax.optimization_barrier((above_high, above_low, below_low))
+    far_high = shift(above_high, 2, -1)
     above_high, below_high = expert_terms([above_high, below_high], weights)
     above_high, below_low = lax.optimization_barrier((above_high, below_low))
     near_high, near_low = shift(above_high, 2, 1), shift(below_low, 2, -1)

time: 132 us -> 133 us (level)
  Pallas kernels: 34.3 us -> 41 us
  waiting for transfers between devices: 51.1 us -> 47.8 us
  starting transfers between devices: 41.7 us -> 39.8 us
    pallas_call x2, Pallas kernels: 14.3 us -> 21 us  [attend(): pl.pallas_call(functools.partial(attention_kernel, sequence), grid_spec=p...]
    ppermute x26, waiting for transfers between devices: 51.1 us -> 47.8 us  [shift(): return lax.ppermute(value, AXES, pairs)]
    ppermute x26, starting transfers between devices: 41.6 us -> 39.7 us  [shift(): return lax.ppermute(value, AXES, pairs)]
  transfers between devices with their start and end apart: 27 -> 27, of which waited for: 19 -> 20; matrix products, arithmetic and copies ran while one was open for 1% -> 1% of each run, Pallas kernels for 25% -> 30%
where the time goes in v10:
time: 133 us
  waiting for transfers between devices  47.8 us (36%)
  Pallas kernels  41 us (31%)
  starting transfers between devices  39.8 us (30%)
  other arithmetic  2.85 us (2%)
    ppermute x26, waiting for transfers between devices, shift(): return lax.ppermute(value, AXES, pairs)  47.8 us
    ppermute x26, starting transfers between devices, shift(): return lax.ppermute(value, AXES, pairs)  39.7 us
    pallas_call x2, Pallas kernels, attend(): pl.pallas_call(functools.partial(attention_kernel, sequence), grid_spec=p...  21 us
    pallas_call x4, Pallas kernels, expert_terms(): pl.pallas_call(functools.partial(expert_kernel, sources=len(pieces), outp...  14.7 us
    pallas_call x1, Pallas kernels, joined(): pl.pallas_call(join_kernel, in_specs=[pl.BlockSpec(memory_space=pl.ANY)]...  4.23 us
  transfers between devices with their start and end apart: 27, of which 20 were waited for; matrix products, arithmetic and copies ran while one was open for 1% of the time, Pallas kernels for 30%

profile of v10, /device:TPU:0, one launch (start us, length us, event | category | flops | bytes accessed | tf_op | source)
XLA Modules:
  0.0 132.7 jit_solution(13467166595064335318)
XLA Ops:
  0.6 1.1 pack.1
  1.7 4.2 %collective-permute-start = (bf16[8,7296]{1,0:T(8,128)(2,1)S(1)}, bf16[8,7296]{1,0:T(8,128)(2,1)S(1)}, u32[]{:S(2)}, u32[]{:S(2)}) collective-permute-start(bf16[8,7296]{1,0:T(8,128)(2,1)S(1)} %pack.1), channel_id=1, source_target_pairs={{0,96},{1,97},{2,98},{3,99},{4,100},{5,101},{6,102},{7,103},{8,104... | collective-permute-start | bytes 350216 | tf_op jit(solution)/shard_map/ppermute | solution.py:43
  5.9 1.3 collective-permute-start.2
  7.2 4.2 %join.1.refs_2_ = bf16[10752,512]{1,0:T(8,128)(2,1)S(1)} custom-call(bf16[7168,256]{1,0:T(8,128)(2,1)} %bitcast.9, bf16[7168,256]{1,0:T(8,128)(2,1)} %bitcast.10, bf16[256,7168]{1,0:T(8,128)(2,1)} %bitcast.11), custom_call_target="tpu_custom_call" | custom-call | bytes 22020096 | tf_op jit(solution)/shard_map/join/pallas_call | solution.py:142
  11.4 0.9 collective-permute-done.1
  12.4 0.9 collective-permute-done.2
  13.2 0.1 pad_maximum_fusion
  13.3 0.1 collective-permute-start.9
  13.4 1.6 %collective-permute-start.4 = (bf16[32,7296]{1,0:T(8,128)(2,1)S(1)}, bf16[32,7296]{1,0:T(8,128)(2,1)S(1)}, u32[]{:S(2)}, u32[]{:S(2)}) collective-permute-start(bf16[32,7296]{1,0:T(8,128)(2,1)S(1)} %pad_maximum_fusion), channel_id=1, source_target_pairs={{0,1},{1,2},{2,3},{3,0},{4,5},{5,6},{6,7},{7,4},{8,9},{9,10},{10,1... | collective-permute-start | bytes 1400840 | tf_op jit(solution)/shard_map/ppermute | solution.py:43
  15.0 1.7 %collective-permute-start.3 = (bf16[32,7296]{1,0:T(8,128)(2,1)S(1)}, bf16[32,7296]{1,0:T(8,128)(2,1)S(1)}, u32[]{:S(2)}, u32[]{:S(2)}) collective-permute-start(bf16[32,7296]{1,0:T(8,128)(2,1)S(1)} %pad_maximum_fusion), channel_id=1, source_target_pairs={{0,3},{1,0},{2,1},{3,2},{4,7},{5,4},{6,5},{7,6},{8,11},{9,8},{10,9... | collective-permute-start | bytes 1400840 | tf_op jit(solution)/shard_map/ppermute | solution.py:43
  16.7 6.5 %collective-permute-done.4 = bf16[32,7296]{1,0:T(8,128)(2,1)S(1)} collective-permute-done((bf16[32,7296]{1,0:T(8,128)(2,1)S(1)}, bf16[32,7296]{1,0:T(8,128)(2,1)S(1)}, u32[]{:S(2)}, u32[]{:S(2)}) %collective-permute-start.4) | collective-permute-done | bytes 466976 | tf_op jit(solution)/shard_map/ppermute | solution.py:43
  23.2 0.3 collective-permute-done.3
  23.6 1.6 %collective-permute-start.5 = (bf16[16,7296]{1,0:T(8,128)(2,1)S(1)}, bf16[16,7296]{1,0:T(8,128)(2,1)S(1)}, u32[]{:S(2)}, u32[]{:S(2)}) collective-permute-start(bf16[16,7296]{1,0:T(8,128)(2,1)S(1)} %slice.75), channel_id=1, source_target_pairs={{0,1},{1,2},{2,3},{3,0},{4,5},{5,6},{6,7},{7,4},{8,9},{9,10},{10,1... | collective-permute-start | bytes 700424 | tf_op jit(solution)/shard_map/ppermute | solution.py:43
  25.3 1.6 %collective-permute-start.7 = (bf16[64,7296]{1,0:T(8,128)(2,1)S(1)}, bf16[64,7296]{1,0:T(8,128)(2,1)S(1)}, u32[]{:S(2)}, u32[]{:S(2)}) collective-permute-start(bf16[64,7296]{1,0:T(8,128)(2,1)S(1)} %constant_dynamic-update-slice_fusion.refs_0_), channel_id=1, source_target_pairs={{0,4},{1,5},{2,6},{3,7},{4,8},{5,9},{6,10},{7,11},{8,12},{9,13},{1... | collective-permute-start | bytes 2801672 | tf_op jit(solution)/shard_map/ppermute | solution.py:43
  26.8 1.7 %collective-permute-start.8 = (bf16[64,7296]{1,0:T(8,128)(2,1)S(1)}, bf16[64,7296]{1,0:T(8,128)(2,1)S(1)}, u32[]{:S(2)}, u32[]{:S(2)}) collective-permute-start(bf16[64,7296]{1,0:T(8,128)(2,1)S(1)} %constant_dynamic-update-slice_fusion.refs_0_), channel_id=1, source_target_pairs={{0,12},{1,13},{2,14},{3,15},{4,0},{5,1},{6,2},{7,3},{8,4},{9,5},{1... | collective-permute-start | bytes 2801672 | tf_op jit(solution)/shard_map/ppermute | solution.py:43
  28.6 1.7 %collective-permute-start.6 = (bf16[16,7296]{1,0:T(8,128)(2,1)S(1)}, bf16[16,7296]{1,0:T(8,128)(2,1)S(1)}, u32[]{:S(2)}, u32[]{:S(2)}) collective-permute-start(bf16[16,7296]{1,0:T(8,128)(2,1)S(1)} %slice.76), channel_id=1, source_target_pairs={{0,3},{1,0},{2,1},{3,2},{4,7},{5,4},{6,5},{7,6},{8,11},{9,8},{10,9... | collective-permute-start | bytes 700424 | tf_op jit(solution)/shard_map/ppermute | solution.py:43
  30.2 3.3 %collective-permute-done.5 = bf16[16,7296]{1,0:T(8,128)(2,1)S(1)} collective-permute-done((bf16[16,7296]{1,0:T(8,128)(2,1)S(1)}, bf16[16,7296]{1,0:T(8,128)(2,1)S(1)}, u32[]{:S(2)}, u32[]{:S(2)}) %collective-permute-start.5) | collective-permute-done | bytes 233504 | tf_op jit(solution)/shard_map/ppermute | solution.py:43
  33.5 3.7 %collective-permute-done.6 = bf16[16,7296]{1,0:T(8,128)(2,1)S(1)} collective-permute-done((bf16[16,7296]{1,0:T(8,128)(2,1)S(1)}, bf16[16,7296]{1,0:T(8,128)(2,1)S(1)}, u32[]{:S(2)}, u32[]{:S(2)}) %collective-permute-start.6) | collective-permute-done | bytes 233504 | tf_op jit(solution)/shard_map/ppermute | solution.py:43
  37.3 1.6 %collective-permute-start.11 = (bf16[64,7296]{1,0:T(8,128)(2,1)S(1)}, bf16[64,7296]{1,0:T(8,128)(2,1)S(1)}, u32[]{:S(2)}, u32[]{:S(2)}) collective-permute-start(bf16[64,7296]{1,0:T(8,128)(2,1)S(1)} %constant_dynamic-update-slice_fusion.2.refs_1_), channel_id=1, source_target_pairs={{0,12},{1,13},{2,14},{3,15},{4,0},{5,1},{6,2},{7,3},{8,4},{9,5},{1... | collective-permute-start | bytes 2801672 | tf_op jit(solution)/shard_map/ppermute | solution.py:43
  38.9 0.5 collective-permute-start.13
  39.4 0.7 collective-permute-done.7.refs_1_
  40.1 0.3 collective-permute-done.8.refs_0_
  40.4 3.7 %expert.4 = (bf16[64,7168]{1,0:T(8,128)(2,1)S(1)}, bf16[64,7168]{1,0:T(8,128)(2,1)S(1)}) custom-call(bf16[64,7296]{1,0:T(8,128)(2,1)S(1)} %constant_dynamic-update-slice_fusion.refs_0_, bf16[64,7296]{1,0:T(8,128)(2,1)S(1)} %constant_dynamic-update-slice_fusion.2.refs_1_, bf16[10752,512]{1,0:T(8,128)(2,1)S(1)} %join.1.refs_2_, ...), custom_call_target="tpu_custom_call" | custom-call | flops 2818572288 | bytes 3670016 | tf_op jit(solution)/shard_map/expert/pallas_call | solution.py:104
  44.1 3.7 %expert.5 = (bf16[64,7168]{1,0:T(8,128)(2,1)S(1)}, bf16[64,7168]{1,0:T(8,128)(2,1)S(1)}) custom-call(bf16[64,7296]{1,0:T(8,128)(2,1)S(1)} %collective-permute-done.8.refs_0_, bf16[64,7296]{1,0:T(8,128)(2,1)S(1)} %collective-permute-done.7.refs_1_, bf16[10752,512]{1,0:T(8,128)(2,1)S(1)} %join.1.refs_2_, bf16[10752,512]{1,0:T(8,128)(2,1)S(1)} %collective-permute-done.9.refs_3_), custom_call_target="tpu_custom_call" | custom-call | flops 2818572288 | bytes 3670016 | tf_op jit(solution)/shard_map/expert/pallas_call | solution.py:104
  47.8 3.1 %collective-permute-done.11.refs_0_ = bf16[64,7296]{1,0:T(8,128)(2,1)S(1)} collective-permute-done((bf16[64,7296]{1,0:T(8,128)(2,1)S(1)}, bf16[64,7296]{1,0:T(8,128)(2,1)S(1)}, u32[]{:S(2)}, u32[]{:S(2)}) %collective-permute-start.11) | collective-permute-done | bytes 933920 | tf_op jit(solution)/shard_map/ppermute | solution.py:43
  50.9 2.8 %collective-permute-start.12 = (bf16[64,7296]{1,0:T(8,128)(2,1)S(1)}, bf16[64,7296]{1,0:T(8,128)(2,1)S(1)}, u32[]{:S(2)}, u32[]{:S(2)}) collective-permute-start(bf16[64,7296]{1,0:T(8,128)(2,1)S(1)} %collective-permute-done.11.refs_0_), channel_id=1, source_target_pairs={{0,12},{1,13},{2,14},{3,15},{4,0},{5,1},{6,2},{7,3},{8,4},{9,5},{1... | collective-permute-start | bytes 2801672 | tf_op jit(solution)/shard_map/ppermute | solution.py:43
  53.7 3.7 %expert.6 = (bf16[64,7168]{1,0:T(8,128)(2,1)S(1)}, bf16[64,7168]{1,0:T(8,128)(2,1)S(1)}) custom-call(bf16[64,7296]{1,0:T(8,128)(2,1)S(1)} %collective-permute-done.11.refs_0_, bf16[64,7296]{1,0:T(8,128)(2,1)S(1)} %collective-permute-done.13.refs_1_, bf16[10752,512]{1,0:T(8,128)(2,1)S(1)} %join.1.refs_2_, bf16[10752,512]{1,0:T(8,128)(2,1)S(1)} %collective-permute-done.9.refs_3_), custom_call_target="tpu_custom_call" | custom-call | flops 2818572288 | bytes 3670016 | tf_op jit(solution)/shard_map/expert/pallas_call | solution.py:104
  57.4 0.0 copy-start
  57.5 0.3 collective-permute-start.16
  57.8 3.1 %collective-permute-start.17 = (bf16[64,7168]{1,0:T(8,128)(2,1)S(1)}, bf16[64,7168]{1,0:T(8,128)(2,1)S(1)}, u32[]{:S(2)}, u32[]{:S(2)}) collective-permute-start(bf16[64,7168]{1,0:T(8,128)(2,1)S(1)} %get-tuple-element.66), channel_id=1, source_target_pairs={{0,12},{1,13},{2,14},{3,15},{4,0},{5,1},{6,2},{7,3},{8,4},{9,5},{1... | collective-permute-start | bytes 2752520 | tf_op jit(solution)/shard_map/ppermute | solution.py:43
  60.9 3.9 %collective-permute-done.12.refs_1_ = bf16[64,7296]{1,0:T(8,128)(2,1)S(1)} collective-permute-done((bf16[64,7296]{1,0:T(8,128)(2,1)S(1)}, bf16[64,7296]{1,0:T(8,128)(2,1)S(1)}, u32[]{:S(2)}, u32[]{:S(2)}) %collective-permute-start.12) | collective-permute-done | bytes 933920 | tf_op jit(solution)/shard_map/ppermute | solution.py:43
  64.8 3.7 %collective-permute-done.10.refs_0_ = bf16[64,7296]{1,0:T(8,128)(2,1)S(1)} collective-permute-done((bf16[64,7296]{1,0:T(8,128)(2,1)S(1)}, bf16[64,7296]{1,0:T(8,128)(2,1)S(1)}, u32[]{:S(2)}, u32[]{:S(2)}) %collective-permute-start.10) | collective-permute-done | bytes 933920 | tf_op jit(solution)/shard_map/ppermute | solution.py:43
  68.5 3.7 %expert.7 = (bf16[64,7168]{1,0:T(8,128)(2,1)S(1)}, bf16[64,7168]{1,0:T(8,128)(2,1)S(1)}) custom-call(bf16[64,7296]{1,0:T(8,128)(2,1)S(1)} %collective-permute-done.10.refs_0_, bf16[64,7296]{1,0:T(8,128)(2,1)S(1)} %collective-permute-done.12.refs_1_, bf16[10752,512]{1,0:T(8,128)(2,1)S(1)} %join.1.refs_2_, bf16[10752,512]{1,0:T(8,128)(2,1)S(1)} %collective-permute-done.9.refs_3_), custom_call_target="tpu_custom_call" | custom-call | flops 2818572288 | bytes 3670016 | tf_op jit(solution)/shard_map/expert/pallas_call | solution.py:104
  72.1 0.1 collective-permute-start.14
  72.2 3.2 %collective-permute-start.15 = (bf16[64,7168]{1,0:T(8,128)(2,1)S(1)}, bf16[64,7168]{1,0:T(8,128)(2,1)S(1)}, u32[]{:S(2)}, u32[]{:S(2)}) collective-permute-start(bf16[64,7168]{1,0:T(8,128)(2,1)S(1)} %get-tuple-element.70), channel_id=1, source_target_pairs={{0,12},{1,13},{2,14},{3,15},{4,0},{5,1},{6,2},{7,3},{8,4},{9,5},{1... | collective-permute-start | bytes 2752520 | tf_op jit(solution)/shard_map/ppermute | solution.py:43
  75.5 10.5 %attend.2 = bf16[64,1024]{1,0:T(8,128)(2,1)S(1)} custom-call(s32[2]{0:T(128)S(1)} %copy-done.7, bf16[128,1024]{1,0:T(8,128)(2,1)S(1)} %copy-done.3, bf16[128,512]{1,0:T(8,128)(2,1)S(1)} %copy-done.4, bf16[8,128,512]{2,1,0:T(8,128)(2,1)S(1)} %copy-done, bf16[8,512,128]{2,1,0:T(8,128)(2,1)S(1)} %copy-done.1, bf16[2,4096,512]{2,1,0:T(8,128)(2,1)} %latent_ref.3, ...), custom_call_target="tpu_custom_call" | custom-call | flops 100000000 | bytes 133333 | tf_op jit(solution)/shard_map/attend/pallas_call | solution.py:254
  86.0 2.1 %collective-permute-done.14 = bf16[64,7168]{1,0:T(8,128)(2,1)S(1)} collective-permute-done((bf16[64,7168]{1,0:T(8,128)(2,1)S(1)}, bf16[64,7168]{1,0:T(8,128)(2,1)S(1)}, u32[]{:S(2)}, u32[]{:S(2)}) %collective-permute-start.14) | collective-permute-done | bytes 917536 | tf_op jit(solution)/shard_map/ppermute | solution.py:43
  88.1 0.2 add_convert_fusion
  88.3 2.0 %collective-permute-start.19 = (bf16[64,7168]{1,0:T(8,128)(2,1)S(1)}, bf16[64,7168]{1,0:T(8,128)(2,1)S(1)}, u32[]{:S(2)}, u32[]{:S(2)}) collective-permute-start(bf16[64,7168]{1,0:T(8,128)(2,1)S(1)} %add_convert_fusion), channel_id=1, source_target_pairs={{0,12},{1,13},{2,14},{3,15},{4,0},{5,1},{6,2},{7,3},{8,4},{9,5},{1... | collective-permute-start | bytes 2752520 | tf_op jit(solution)/shard_map/ppermute | solution.py:43
  90.3 0.2 add_convert_fusion.1
  90.6 0.4 collective-permute-start.18
  90.9 10.5 %attend.3 = bf16[64,1024]{1,0:T(8,128)(2,1)S(1)} custom-call(s32[2]{0:T(128)S(1)} %copy-done.7, bf16[128,1024]{1,0:T(8,128)(2,1)S(1)} %copy-done.3, bf16[128,512]{1,0:T(8,128)(2,1)S(1)} %copy-done.4, bf16[8,128,512]{2,1,0:T(8,128)(2,1)S(1)} %copy-done, bf16[8,512,128]{2,1,0:T(8,128)(2,1)S(1)} %copy-done.1, bf16[2,4096,512]{2,1,0:T(8,128)(2,1)} %latent_ref.3, ...), custom_call_target="tpu_custom_call" | custom-call | flops 6000000000 | bytes 8000000 | tf_op jit(solution)/shard_map/attend/pallas_call | solution.py:254
  101.4 0.4 collective-permute-done.19
  101.8 3.6 %collective-permute-done.18 = bf16[64,7168]{1,0:T(8,128)(2,1)S(1)} collective-permute-done((bf16[64,7168]{1,0:T(8,128)(2,1)S(1)}, bf16[64,7168]{1,0:T(8,128)(2,1)S(1)}, u32[]{:S(2)}, u32[]{:S(2)}) %collective-permute-start.18) | collective-permute-done | bytes 917536 | tf_op jit(solution)/shard_map/ppermute | solution.py:43
  105.4 0.3 fusion.3
  105.8 0.3 convert_add_fusion.1
  106.2 1.3 %collective-permute-start.20 = (bf16[32,7168]{1,0:T(8,128)(2,1)S(1)}, bf16[32,7168]{1,0:T(8,128)(2,1)S(1)}, u32[]{:S(2)}, u32[]{:S(2)}) collective-permute-start(bf16[32,7168]{1,0:T(8,128)(2,1)S(1)} %pad_maximum_fusion.1), channel_id=1, source_target_pairs={{0,1},{1,2},{2,3},{3,0},{4,5},{5,6},{6,7},{7,4},{8,9},{9,10},{10,1... | collective-permute-start | bytes 1376264 | tf_op jit(solution)/shard_map/ppermute | solution.py:43
  107.6 2.0 %collective-permute-start.21 = (bf16[32,7168]{1,0:T(8,128)(2,1)S(1)}, bf16[32,7168]{1,0:T(8,128)(2,1)S(1)}, u32[]{:S(2)}, u32[]{:S(2)}) collective-permute-start(bf16[32,7168]{1,0:T(8,128)(2,1)S(1)} %concatenate.29), channel_id=1, source_target_pairs={{0,3},{1,0},{2,1},{3,2},{4,7},{5,4},{6,5},{7,6},{8,11},{9,8},{10,9... | collective-permute-start | bytes 1376264 | tf_op jit(solution)/shard_map/ppermute | solution.py:43
  109.6 6.3 %collective-permute-done.20 = bf16[32,7168]{1,0:T(8,128)(2,1)S(1)} collective-permute-done((bf16[32,7168]{1,0:T(8,128)(2,1)S(1)}, bf16[32,7168]{1,0:T(8,128)(2,1)S(1)}, u32[]{:S(2)}, u32[]{:S(2)}) %collective-permute-start.20) | collective-permute-done | bytes 458784 | tf_op jit(solution)/shard_map/ppermute | solution.py:43
  116.0 0.1 collective-permute-done.21
  116.2 1.5 %collective-permute-start.22 = (bf16[16,7168]{1,0:T(8,128)(2,1)S(1)}, bf16[16,7168]{1,0:T(8,128)(2,1)S(1)}, u32[]{:S(2)}, u32[]{:S(2)}) collective-permute-start(bf16[16,7168]{1,0:T(8,128)(2,1)S(1)} %fusion.2), channel_id=1, source_target_pairs={{0,1},{1,2},{2,3},{3,0},{4,5},{5,6},{6,7},{7,4},{8,9},{9,10},{10,1... | collective-permute-start | bytes 688136 | tf_op jit(solution)/shard_map/ppermute | solution.py:43
  117.7 1.8 %collective-permute-start.23 = (bf16[16,7168]{1,0:T(8,128)(2,1)S(1)}, bf16[16,7168]{1,0:T(8,128)(2,1)S(1)}, u32[]{:S(2)}, u32[]{:S(2)}) collective-permute-start(bf16[16,7168]{1,0:T(8,128)(2,1)S(1)} %fusion.1), channel_id=1, source_target_pairs={{0,3},{1,0},{2,1},{3,2},{4,7},{5,4},{6,5},{7,6},{8,11},{9,8},{10,9... | collective-permute-start | bytes 688136 | tf_op jit(solution)/shard_map/ppermute | solution.py:43
  119.5 4.0 %collective-permute-done.22 = bf16[16,7168]{1,0:T(8,128)(2,1)S(1)} collective-permute-done((bf16[16,7168]{1,0:T(8,128)(2,1)S(1)}, bf16[16,7168]{1,0:T(8,128)(2,1)S(1)}, u32[]{:S(2)}, u32[]{:S(2)}) %collective-permute-start.22) | collective-permute-done | bytes 229408 | tf_op jit(solution)/shard_map/ppermute | solution.py:43
  123.5 0.1 convert_add_fusion.3
  123.5 0.2 collective-permute-done.23
  123.7 0.1 convert_add_fusion.2
  123.8 0.1 fusion
  123.9 0.5 collective-permute-start.24
  124.4 2.0 %collective-permute-start.25 = (bf16[8,7168]{1,0:T(8,128)(2,1)S(1)}, bf16[8,7168]{1,0:T(8,128)(2,1)S(1)}, u32[]{:S(2)}, u32[]{:S(2)}) collective-permute-start(bf16[8,7168]{1,0:T(8,128)(2,1)S(1)} %get-tuple-element.90), channel_id=1, source_target_pairs={{0,64},{1,65},{2,66},{3,67},{4,68},{5,69},{6,70},{7,71},{8,72},{9,... | collective-permute-start | bytes 344072 | tf_op jit(solution)/shard_map/ppermute | solution.py:43
  126.5 1.1 collective-permute-start.26
  127.6 0.7 pad_maximum_fusion.2
  128.3 2.9 %collective-permute-done.24 = bf16[8,7168]{1,0:T(8,128)(2,1)S(1)} collective-permute-done((bf16[8,7168]{1,0:T(8,128)(2,1)S(1)}, bf16[8,7168]{1,0:T(8,128)(2,1)S(1)}, u32[]{:S(2)}, u32[]{:S(2)}) %collective-permute-start.24) | collective-permute-done | bytes 114720 | tf_op jit(solution)/shard_map/ppermute | solution.py:43
  131.2 0.9 collective-permute-done.26
  132.0 0.7 add_convert_fusion.2
  (38 shorter events, 0.5 us)
Async XLA Ops:
  1.7 9.7 %collective-permute-start = (bf16[8,7296]{1,0:T(8,128)(2,1)S(1)}, bf16[8,7296]{1,0:T(8,128)(2,1)S(1)}, u32[]{:S(2)}, u32[]{:S(2)}) collective-permute-start(bf16[8,7296]{1,0:T(8,128)(2,1)S(1)} %pack.1), channel_id=1, source_target_pairs={{0,96},{1,97},{2,98},{3,99},{4,100},{5,101},{6,102},{7,103},{8,104... | collective-permute-start | bytes 350216 | tf_op jit(solution)/shard_map/ppermute | solution.py:43
  5.9 6.4 %collective-permute-start.1 = (bf16[8,7296]{1,0:T(8,128)(2,1)S(1)}, bf16[8,7296]{1,0:T(8,128)(2,1)S(1)}, u32[]{:S(2)}, u32[]{:S(2)}) collective-permute-start(bf16[8,7296]{1,0:T(8,128)(2,1)S(1)} %pack.1), channel_id=1, source_target_pairs={{0,64},{1,65},{2,66},{3,67},{4,68},{5,69},{6,70},{7,71},{8,72},{9,... | collective-permute-start | bytes 350216 | tf_op jit(solution)/shard_map/ppermute | solution.py:43
  5.9 7.3 %collective-permute-start.2 = (bf16[8,7296]{1,0:T(8,128)(2,1)S(1)}, bf16[8,7296]{1,0:T(8,128)(2,1)S(1)}, u32[]{:S(2)}, u32[]{:S(2)}) collective-permute-start(bf16[8,7296]{1,0:T(8,128)(2,1)S(1)} %pack.1), channel_id=1, source_target_pairs={{0,32},{1,33},{2,34},{3,35},{4,36},{5,37},{6,38},{7,39},{8,40},{9,... | collective-permute-start | bytes 350216 | tf_op jit(solution)/shard_map/ppermute | solution.py:43
  13.3 27.1 %collective-permute-start.9 = (bf16[10752,512]{1,0:T(8,128)(2,1)S(1)}, bf16[10752,512]{1,0:T(8,128)(2,1)S(1)}, u32[]{:S(2)}, u32[]{:S(2)}) collective-permute-start(bf16[10752,512]{1,0:T(8,128)(2,1)S(1)} %join.1.refs_2_), channel_id=1, source_target_pairs={{0,16},{16,0},{1,17},{17,1},{2,18},{18,2},{3,19},{19,3},{4,20},{20... | collective-permute-start | bytes 33030152 | tf_op jit(solution)/shard_map/ppermute | solution.py:59
  13.4 9.8 %collective-permute-start.4 = (bf16[32,7296]{1,0:T(8,128)(2,1)S(1)}, bf16[32,7296]{1,0:T(8,128)(2,1)S(1)}, u32[]{:S(2)}, u32[]{:S(2)}) collective-permute-start(bf16[32,7296]{1,0:T(8,128)(2,1)S(1)} %pad_maximum_fusion), channel_id=1, source_target_pairs={{0,1},{1,2},{2,3},{3,0},{4,5},{5,6},{6,7},{7,4},{8,9},{9,10},{10,1... | collective-permute-start | bytes 1400840 | tf_op jit(solution)/shard_map/ppermute | solution.py:43
  15.0 8.6 %collective-permute-start.3 = (bf16[32,7296]{1,0:T(8,128)(2,1)S(1)}, bf16[32,7296]{1,0:T(8,128)(2,1)S(1)}, u32[]{:S(2)}, u32[]{:S(2)}) collective-permute-start(bf16[32,7296]{1,0:T(8,128)(2,1)S(1)} %pad_maximum_fusion), channel_id=1, source_target_pairs={{0,3},{1,0},{2,1},{3,2},{4,7},{5,4},{6,5},{7,6},{8,11},{9,8},{10,9... | collective-permute-start | bytes 1400840 | tf_op jit(solution)/shard_map/ppermute | solution.py:43
  23.6 9.9 %collective-permute-start.5 = (bf16[16,7296]{1,0:T(8,128)(2,1)S(1)}, bf16[16,7296]{1,0:T(8,128)(2,1)S(1)}, u32[]{:S(2)}, u32[]{:S(2)}) collective-permute-start(bf16[16,7296]{1,0:T(8,128)(2,1)S(1)} %slice.75), channel_id=1, source_target_pairs={{0,1},{1,2},{2,3},{3,0},{4,5},{5,6},{6,7},{7,4},{8,9},{9,10},{10,1... | collective-permute-start | bytes 700424 | tf_op jit(solution)/shard_map/ppermute | solution.py:43
  25.3 14.8 %collective-permute-start.7 = (bf16[64,7296]{1,0:T(8,128)(2,1)S(1)}, bf16[64,7296]{1,0:T(8,128)(2,1)S(1)}, u32[]{:S(2)}, u32[]{:S(2)}) collective-permute-start(bf16[64,7296]{1,0:T(8,128)(2,1)S(1)} %constant_dynamic-update-slice_fusion.refs_0_), channel_id=1, source_target_pairs={{0,4},{1,5},{2,6},{3,7},{4,8},{5,9},{6,10},{7,11},{8,12},{9,13},{1... | collective-permute-start | bytes 2801672 | tf_op jit(solution)/shard_map/ppermute | solution.py:43
  26.8 13.6 %collective-permute-start.8 = (bf16[64,7296]{1,0:T(8,128)(2,1)S(1)}, bf16[64,7296]{1,0:T(8,128)(2,1)S(1)}, u32[]{:S(2)}, u32[]{:S(2)}) collective-permute-start(bf16[64,7296]{1,0:T(8,128)(2,1)S(1)} %constant_dynamic-update-slice_fusion.refs_0_), channel_id=1, source_target_pairs={{0,12},{1,13},{2,14},{3,15},{4,0},{5,1},{6,2},{7,3},{8,4},{9,5},{1... | collective-permute-start | bytes 2801672 | tf_op jit(solution)/shard_map/ppermute | solution.py:43
  28.6 8.6 %collective-permute-start.6 = (bf16[16,7296]{1,0:T(8,128)(2,1)S(1)}, bf16[16,7296]{1,0:T(8,128)(2,1)S(1)}, u32[]{:S(2)}, u32[]{:S(2)}) collective-permute-start(bf16[16,7296]{1,0:T(8,128)(2,1)S(1)} %slice.76), channel_id=1, source_target_pairs={{0,3},{1,0},{2,1},{3,2},{4,7},{5,4},{6,5},{7,6},{8,11},{9,8},{10,9... | collective-permute-start | bytes 700424 | tf_op jit(solution)/shard_map/ppermute | solution.py:43
  37.3 13.6 %collective-permute-start.11 = (bf16[64,7296]{1,0:T(8,128)(2,1)S(1)}, bf16[64,7296]{1,0:T(8,128)(2,1)S(1)}, u32[]{:S(2)}, u32[]{:S(2)}) collective-permute-start(bf16[64,7296]{1,0:T(8,128)(2,1)S(1)} %constant_dynamic-update-slice_fusion.2.refs_1_), channel_id=1, source_target_pairs={{0,12},{1,13},{2,14},{3,15},{4,0},{5,1},{6,2},{7,3},{8,4},{9,5},{1... | collective-permute-start | bytes 2801672 | tf_op jit(solution)/shard_map/ppermute | solution.py:43
  38.9 14.8 %collective-permute-start.13 = (bf16[64,7296]{1,0:T(8,128)(2,1)S(1)}, bf16[64,7296]{1,0:T(8,128)(2,1)S(1)}, u32[]{:S(2)}, u32[]{:S(2)}) collective-permute-start(bf16[64,7296]{1,0:T(8,128)(2,1)S(1)} %constant_dynamic-update-slice_fusion.2.refs_1_), channel_id=1, source_target_pairs={{0,4},{1,5},{2,6},{3,7},{4,8},{5,9},{6,10},{7,11},{8,12},{9,13},{1... | collective-permute-start | bytes 2801672 | tf_op jit(solution)/shard_map/ppermute | solution.py:43
  50.9 13.8 %collective-permute-start.12 = (bf16[64,7296]{1,0:T(8,128)(2,1)S(1)}, bf16[64,7296]{1,0:T(8,128)(2,1)S(1)}, u32[]{:S(2)}, u32[]{:S(2)}) collective-permute-start(bf16[64,7296]{1,0:T(8,128)(2,1)S(1)} %collective-permute-done.11.refs_0_), channel_id=1, source_target_pairs={{0,12},{1,13},{2,14},{3,15},{4,0},{5,1},{6,2},{7,3},{8,4},{9,5},{1... | collective-permute-start | bytes 2801672 | tf_op jit(solution)/shard_map/ppermute | solution.py:43
  53.7 14.8 %collective-permute-start.10 = (bf16[64,7296]{1,0:T(8,128)(2,1)S(1)}, bf16[64,7296]{1,0:T(8,128)(2,1)S(1)}, u32[]{:S(2)}, u32[]{:S(2)}) collective-permute-start(bf16[64,7296]{1,0:T(8,128)(2,1)S(1)} %collective-permute-done.7.refs_1_), channel_id=1, source_target_pairs={{0,4},{1,5},{2,6},{3,7},{4,8},{5,9},{6,10},{7,11},{8,12},{9,13},{1... | collective-permute-start | bytes 2801672 | tf_op jit(solution)/shard_map/ppermute | solution.py:43
  57.4 18.1 %copy-start = (bf16[8,128,512]{2,1,0:T(8,128)(2,1)S(1)}, bf16[8,128,512]{2,1,0:T(8,128)(2,1)}, u32[]{:S(2)}) copy-start(bf16[8,128,512]{2,1,0:T(8,128)(2,1)} %key_up_ref.3) | copy-start | bytes 3145732
  57.4 18.1 %copy-start.1 = (bf16[8,512,128]{2,1,0:T(8,128)(2,1)S(1)}, bf16[8,512,128]{2,1,0:T(8,128)(2,1)}, u32[]{:S(2)}) copy-start(bf16[8,512,128]{2,1,0:T(8,128)(2,1)} %value_up_ref.3) | copy-start | bytes 3145732
  57.4 18.1 %copy-start.2 = (bf16[2,4096,64]{1,2,0:T(8,128)(2,1)S(1)}, bf16[2,4096,64]{1,2,0:T(8,128)(2,1)}, u32[]{:S(2)}) copy-start(bf16[2,4096,64]{1,2,0:T(8,128)(2,1)} %param.26) | copy-start | bytes 3145732
  57.4 18.1 %copy-start.3 = (bf16[128,1024]{1,0:T(8,128)(2,1)S(1)}, bf16[128,1024]{1,0:T(8,128)(2,1)}, u32[]{:S(2)}) copy-start(bf16[128,1024]{1,0:T(8,128)(2,1)} %nope_ref.3) | copy-start | bytes 786436
  57.4 18.1 %copy-start.4 = (bf16[128,512]{1,0:T(8,128)(2,1)S(1)}, bf16[128,512]{1,0:T(8,128)(2,1)}, u32[]{:S(2)}) copy-start(bf16[128,512]{1,0:T(8,128)(2,1)} %rope_ref.3) | copy-start | bytes 393220
  57.4 18.1 %copy-start.5 = (bf16[128,512]{1,0:T(8,128)(2,1)S(1)}, bf16[128,512]{1,0:T(8,128)(2,1)}, u32[]{:S(2)}) copy-start(bf16[128,512]{1,0:T(8,128)(2,1)} %new_latent_ref.3) | copy-start | bytes 393220
  57.4 18.1 %copy-start.6 = (bf16[128,64]{0,1:T(8,128)(2,1)S(1)}, bf16[128,64]{0,1:T(8,128)(2,1)}, u32[]{:S(2)}) copy-start(bf16[128,64]{0,1:T(8,128)(2,1)} %param.28) | copy-start | bytes 49156
  57.4 18.0 %copy-start.7 = (s32[2]{0:T(128)S(1)}, s32[2]{0:T(128)}, u32[]{:S(2)}) copy-start(s32[2]{0:T(128)} %length_ref.1) | copy-start | bytes 28
  57.5 28.5 %collective-permute-start.16 = (bf16[64,7168]{1,0:T(8,128)(2,1)S(1)}, bf16[64,7168]{1,0:T(8,128)(2,1)S(1)}, u32[]{:S(2)}, u32[]{:S(2)}) collective-permute-start(bf16[64,7168]{1,0:T(8,128)(2,1)S(1)} %get-tuple-element.65), channel_id=1, source_target_pairs={{0,4},{1,5},{2,6},{3,7},{4,8},{5,9},{6,10},{7,11},{8,12},{9,13},{1... | collective-permute-start | bytes 2752520 | tf_op jit(solution)/shard_map/ppermute | solution.py:43
  57.8 28.2 %collective-permute-start.17 = (bf16[64,7168]{1,0:T(8,128)(2,1)S(1)}, bf16[64,7168]{1,0:T(8,128)(2,1)S(1)}, u32[]{:S(2)}, u32[]{:S(2)}) collective-permute-start(bf16[64,7168]{1,0:T(8,128)(2,1)S(1)} %get-tuple-element.66), channel_id=1, source_target_pairs={{0,12},{1,13},{2,14},{3,15},{4,0},{5,1},{6,2},{7,3},{8,4},{9,5},{1... | collective-permute-start | bytes 2752520 | tf_op jit(solution)/shard_map/ppermute | solution.py:43
  72.1 16.0 %collective-permute-start.14 = (bf16[64,7168]{1,0:T(8,128)(2,1)S(1)}, bf16[64,7168]{1,0:T(8,128)(2,1)S(1)}, u32[]{:S(2)}, u32[]{:S(2)}) collective-permute-start(bf16[64,7168]{1,0:T(8,128)(2,1)S(1)} %get-tuple-element.69), channel_id=1, source_target_pairs={{0,4},{1,5},{2,6},{3,7},{4,8},{5,9},{6,10},{7,11},{8,12},{9,13},{1... | collective-permute-start | bytes 2752520 | tf_op jit(solution)/shard_map/ppermute | solution.py:43
  72.2 15.9 %collective-permute-start.15 = (bf16[64,7168]{1,0:T(8,128)(2,1)S(1)}, bf16[64,7168]{1,0:T(8,128)(2,1)S(1)}, u32[]{:S(2)}, u32[]{:S(2)}) collective-permute-start(bf16[64,7168]{1,0:T(8,128)(2,1)S(1)} %get-tuple-element.70), channel_id=1, source_target_pairs={{0,12},{1,13},{2,14},{3,15},{4,0},{5,1},{6,2},{7,3},{8,4},{9,5},{1... | collective-permute-start | bytes 2752520 | tf_op jit(solution)/shard_map/ppermute | solution.py:43
  88.3 13.5 %collective-permute-start.19 = (bf16[64,7168]{1,0:T(8,128)(2,1)S(1)}, bf16[64,7168]{1,0:T(8,128)(2,1)S(1)}, u32[]{:S(2)}, u32[]{:S(2)}) collective-permute-start(bf16[64,7168]{1,0:T(8,128)(2,1)S(1)} %add_convert_fusion), channel_id=1, source_target_pairs={{0,12},{1,13},{2,14},{3,15},{4,0},{5,1},{6,2},{7,3},{8,4},{9,5},{1... | collective-permute-start | bytes 2752520 | tf_op jit(solution)/shard_map/ppermute | solution.py:43
  90.6 14.9 %collective-permute-start.18 = (bf16[64,7168]{1,0:T(8,128)(2,1)S(1)}, bf16[64,7168]{1,0:T(8,128)(2,1)S(1)}, u32[]{:S(2)}, u32[]{:S(2)}) collective-permute-start(bf16[64,7168]{1,0:T(8,128)(2,1)S(1)} %add_convert_fusion.1), channel_id=1, source_target_pairs={{0,4},{1,5},{2,6},{3,7},{4,8},{5,9},{6,10},{7,11},{8,12},{9,13},{1... | collective-permute-start | bytes 2752520 | tf_op jit(solution)/shard_map/ppermute | solution.py:43
  106.2 9.8 %collective-permute-start.20 = (bf16[32,7168]{1,0:T(8,128)(2,1)S(1)}, bf16[32,7168]{1,0:T(8,128)(2,1)S(1)}, u32[]{:S(2)}, u32[]{:S(2)}) collective-permute-start(bf16[32,7168]{1,0:T(8,128)(2,1)S(1)} %pad_maximum_fusion.1), channel_id=1, source_target_pairs={{0,1},{1,2},{2,3},{3,0},{4,5},{5,6},{6,7},{7,4},{8,9},{9,10},{10,1... | collective-permute-start | bytes 1376264 | tf_op jit(solution)/shard_map/ppermute | solution.py:43
  107.6 8.5 %collective-permute-start.21 = (bf16[32,7168]{1,0:T(8,128)(2,1)S(1)}, bf16[32,7168]{1,0:T(8,128)(2,1)S(1)}, u32[]{:S(2)}, u32[]{:S(2)}) collective-permute-start(bf16[32,7168]{1,0:T(8,128)(2,1)S(1)} %concatenate.29), channel_id=1, source_target_pairs={{0,3},{1,0},{2,1},{3,2},{4,7},{5,4},{6,5},{7,6},{8,11},{9,8},{10,9... | collective-permute-start | bytes 1376264 | tf_op jit(solution)/shard_map/ppermute | solution.py:43
  116.2 7.3 %collective-permute-start.22 = (bf16[16,7168]{1,0:T(8,128)(2,1)S(1)}, bf16[16,7168]{1,0:T(8,128)(2,1)S(1)}, u32[]{:S(2)}, u32[]{:S(2)}) collective-permute-start(bf16[16,7168]{1,0:T(8,128)(2,1)S(1)} %fusion.2), channel_id=1, source_target_pairs={{0,1},{1,2},{2,3},{3,0},{4,5},{5,6},{6,7},{7,4},{8,9},{9,10},{10,1... | collective-permute-start | bytes 688136 | tf_op jit(solution)/shard_map/ppermute | solution.py:43
  117.7 6.0 %collective-permute-start.23 = (bf16[16,7168]{1,0:T(8,128)(2,1)S(1)}, bf16[16,7168]{1,0:T(8,128)(2,1)S(1)}, u32[]{:S(2)}, u32[]{:S(2)}) collective-permute-start(bf16[16,7168]{1,0:T(8,128)(2,1)S(1)} %fusion.1), channel_id=1, source_target_pairs={{0,3},{1,0},{2,1},{3,2},{4,7},{5,4},{6,5},{7,6},{8,11},{9,8},{10,9... | collective-permute-start | bytes 688136 | tf_op jit(solution)/shard_map/ppermute | solution.py:43
  123.9 7.3 %collective-permute-start.24 = (bf16[8,7168]{1,0:T(8,128)(2,1)S(1)}, bf16[8,7168]{1,0:T(8,128)(2,1)S(1)}, u32[]{:S(2)}, u32[]{:S(2)}) collective-permute-start(bf16[8,7168]{1,0:T(8,128)(2,1)S(1)} %get-tuple-element.88), channel_id=1, source_target_pairs={{0,32},{1,33},{2,34},{3,35},{4,36},{5,37},{6,38},{7,39},{8,40},{9,... | collective-permute-start | bytes 344072 | tf_op jit(solution)/shard_map/ppermute | solution.py:43
  124.4 6.8 %collective-permute-start.25 = (bf16[8,7168]{1,0:T(8,128)(2,1)S(1)}, bf16[8,7168]{1,0:T(8,128)(2,1)S(1)}, u32[]{:S(2)}, u32[]{:S(2)}) collective-permute-start(bf16[8,7168]{1,0:T(8,128)(2,1)S(1)} %get-tuple-element.90), channel_id=1, source_target_pairs={{0,64},{1,65},{2,66},{3,67},{4,68},{5,69},{6,70},{7,71},{8,72},{9,... | collective-permute-start | bytes 344072 | tf_op jit(solution)/shard_map/ppermute | solution.py:43
  126.5 5.6 %collective-permute-start.26 = (bf16[8,7168]{1,0:T(8,128)(2,1)S(1)}, bf16[8,7168]{1,0:T(8,128)(2,1)S(1)}, u32[]{:S(2)}, u32[]{:S(2)}) collective-permute-start(bf16[8,7168]{1,0:T(8,128)(2,1)S(1)} %get-tuple-element.89), channel_id=1, source_target_pairs={{0,96},{1,97},{2,98},{3,99},{4,100},{5,101},{6,102},{7,103},{8,104... | collective-permute-start | bytes 344072 | tf_op jit(solution)/shard_map/ppermute | solution.py:43

commit v11 on v9

--- a/solution.py
+++ b/solution.py
@@ -18,7 +18,7 @@
 AXES = ("z", "core", "x", "y")
 SIZES = (4, 2, 4, 4)
 RING = 4
-ORDERS = ((0, 3, 2), (2, 0, 3))
+ORDERS = ((3, 0, 2), (2, 0, 3))
 KERNEL_VMEM = 12 * 1024 * 1024
 EXPERT_VMEM = 10 * 1024 * 1024
 PACK = 128

time: 132 us -> 138 us (1.045)
  waiting for transfers between devices: 51.1 us -> 56.8 us
    ppermute x26, waiting for transfers between devices: 51.1 us -> 56.8 us  [shift(): return lax.ppermute(value, AXES, pairs)]
  transfers between devices with their start and end apart: 27 -> 27, of which waited for: 19 -> 20; matrix products, arithmetic and copies ran while one was open for 1% -> 1% of each run, Pallas kernels for 25% -> 24%
where the time goes in v11:
time: 138 us
  waiting for transfers between devices  56.8 us (41%)
  starting transfers between devices  42.1 us (31%)
  Pallas kernels  34.3 us (25%)
  other arithmetic  2.92 us (2%)
    ppermute x26, waiting for transfers between devices, shift(): return lax.ppermute(value, AXES, pairs)  56.8 us
    ppermute x26, starting transfers between devices, shift(): return lax.ppermute(value, AXES, pairs)  42.1 us
    pallas_call x4, Pallas kernels, expert_terms(): pl.pallas_call(functools.partial(expert_kernel, sources=len(pieces), outp...  14.7 us
    pallas_call x2, Pallas kernels, attend(): pl.pallas_call(functools.partial(attention_kernel, sequence), grid_spec=p...  14.3 us
    pallas_call x1, Pallas kernels, joined(): pl.pallas_call(join_kernel, in_specs=[pl.BlockSpec(memory_space=pl.ANY)]...  4.23 us
  transfers between devices with their start and end apart: 27, of which 20 were waited for; matrix products, arithmetic and copies ran while one was open for 1% of the time, Pallas kernels for 24%

profile of v11, /device:TPU:0, one launch (start us, length us, event | category | flops | bytes accessed | tf_op | source)
XLA Modules:
  0.0 137.5 jit_solution(423354573291867783)
XLA Ops:
  0.6 1.1 pack.1
  1.7 3.2 %collective-permute-start = (bf16[8,7296]{1,0:T(8,128)(2,1)S(1)}, bf16[8,7296]{1,0:T(8,128)(2,1)S(1)}, u32[]{:S(2)}, u32[]{:S(2)}) collective-permute-start(bf16[8,7296]{1,0:T(8,128)(2,1)S(1)} %pack.1), channel_id=1, source_target_pairs={{0,3},{1,0},{2,1},{3,2},{4,7},{5,4},{6,5},{7,6},{8,11},{9,8},{10,9... | collective-permute-start | bytes 350216 | tf_op jit(solution)/shard_map/ppermute | solution.py:43
  4.9 0.6 collective-permute-start.1
  5.5 1.0 collective-permute-start.2
  6.5 4.2 %join.1.refs_2_ = bf16[10752,512]{1,0:T(8,128)(2,1)S(1)} custom-call(bf16[7168,256]{1,0:T(8,128)(2,1)} %bitcast.9, bf16[7168,256]{1,0:T(8,128)(2,1)} %bitcast.10, bf16[256,7168]{1,0:T(8,128)(2,1)} %bitcast.11), custom_call_target="tpu_custom_call" | custom-call | bytes 22020096 | tf_op jit(solution)/shard_map/join/pallas_call | solution.py:142
  10.8 0.6 collective-permute-done.1
  11.3 1.2 collective-permute-done.2
  12.5 0.1 collective-permute-start.9
  12.6 2.0 %collective-permute-start.4 = (bf16[32,7296]{1,0:T(8,128)(2,1)S(1)}, bf16[32,7296]{1,0:T(8,128)(2,1)S(1)}, u32[]{:S(2)}, u32[]{:S(2)}) collective-permute-start(bf16[32,7296]{1,0:T(8,128)(2,1)S(1)} %pad_maximum_fusion), channel_id=1, source_target_pairs={{0,32},{1,33},{2,34},{3,35},{4,36},{5,37},{6,38},{7,39},{8,40},{9,... | collective-permute-start | bytes 1400840 | tf_op jit(solution)/shard_map/ppermute | solution.py:43
  14.6 2.2 %collective-permute-start.3 = (bf16[32,7296]{1,0:T(8,128)(2,1)S(1)}, bf16[32,7296]{1,0:T(8,128)(2,1)S(1)}, u32[]{:S(2)}, u32[]{:S(2)}) collective-permute-start(bf16[32,7296]{1,0:T(8,128)(2,1)S(1)} %pad_maximum_fusion), channel_id=1, source_target_pairs={{0,96},{1,97},{2,98},{3,99},{4,100},{5,101},{6,102},{7,103},{8,104... | collective-permute-start | bytes 1400840 | tf_op jit(solution)/shard_map/ppermute | solution.py:43
  16.8 11.2 %collective-permute-done.4 = bf16[32,7296]{1,0:T(8,128)(2,1)S(1)} collective-permute-done((bf16[32,7296]{1,0:T(8,128)(2,1)S(1)}, bf16[32,7296]{1,0:T(8,128)(2,1)S(1)}, u32[]{:S(2)}, u32[]{:S(2)}) %collective-permute-start.4) | collective-permute-done | bytes 466976 | tf_op jit(solution)/shard_map/ppermute | solution.py:43
  28.1 1.3 collective-permute-start.5
  29.4 1.6 %collective-permute-start.7 = (bf16[64,7296]{1,0:T(8,128)(2,1)S(1)}, bf16[64,7296]{1,0:T(8,128)(2,1)S(1)}, u32[]{:S(2)}, u32[]{:S(2)}) collective-permute-start(bf16[64,7296]{1,0:T(8,128)(2,1)S(1)} %constant_dynamic-update-slice_fusion.refs_0_), channel_id=1, source_target_pairs={{0,4},{1,5},{2,6},{3,7},{4,8},{5,9},{6,10},{7,11},{8,12},{9,13},{1... | collective-permute-start | bytes 2801672 | tf_op jit(solution)/shard_map/ppermute | solution.py:43
  31.0 1.7 %collective-permute-start.8 = (bf16[64,7296]{1,0:T(8,128)(2,1)S(1)}, bf16[64,7296]{1,0:T(8,128)(2,1)S(1)}, u32[]{:S(2)}, u32[]{:S(2)}) collective-permute-start(bf16[64,7296]{1,0:T(8,128)(2,1)S(1)} %constant_dynamic-update-slice_fusion.refs_0_), channel_id=1, source_target_pairs={{0,12},{1,13},{2,14},{3,15},{4,0},{5,1},{6,2},{7,3},{8,4},{9,5},{1... | collective-permute-start | bytes 2801672 | tf_op jit(solution)/shard_map/ppermute | solution.py:43
  32.7 2.0 %collective-permute-start.6 = (bf16[16,7296]{1,0:T(8,128)(2,1)S(1)}, bf16[16,7296]{1,0:T(8,128)(2,1)S(1)}, u32[]{:S(2)}, u32[]{:S(2)}) collective-permute-start(bf16[16,7296]{1,0:T(8,128)(2,1)S(1)} %slice.76), channel_id=1, source_target_pairs={{0,96},{1,97},{2,98},{3,99},{4,100},{5,101},{6,102},{7,103},{8,104... | collective-permute-start | bytes 700424 | tf_op jit(solution)/shard_map/ppermute | solution.py:43
  34.7 2.1 %collective-permute-done.5 = bf16[16,7296]{1,0:T(8,128)(2,1)S(1)} collective-permute-done((bf16[16,7296]{1,0:T(8,128)(2,1)S(1)}, bf16[16,7296]{1,0:T(8,128)(2,1)S(1)}, u32[]{:S(2)}, u32[]{:S(2)}) %collective-permute-start.5) | collective-permute-done | bytes 233504 | tf_op jit(solution)/shard_map/ppermute | solution.py:43
  36.8 2.0 %collective-permute-done.6 = bf16[16,7296]{1,0:T(8,128)(2,1)S(1)} collective-permute-done((bf16[16,7296]{1,0:T(8,128)(2,1)S(1)}, bf16[16,7296]{1,0:T(8,128)(2,1)S(1)}, u32[]{:S(2)}, u32[]{:S(2)}) %collective-permute-start.6) | collective-permute-done | bytes 233504 | tf_op jit(solution)/shard_map/ppermute | solution.py:43
  38.9 2.8 %collective-permute-start.10 = (bf16[64,7296]{1,0:T(8,128)(2,1)S(1)}, bf16[64,7296]{1,0:T(8,128)(2,1)S(1)}, u32[]{:S(2)}, u32[]{:S(2)}) collective-permute-start(bf16[64,7296]{1,0:T(8,128)(2,1)S(1)} %constant_dynamic-update-slice_fusion.2.refs_1_), channel_id=1, source_target_pairs={{0,12},{1,13},{2,14},{3,15},{4,0},{5,1},{6,2},{7,3},{8,4},{9,5},{1... | collective-permute-start | bytes 2801672 | tf_op jit(solution)/shard_map/ppermute | solution.py:43
  41.7 2.5 %collective-permute-done.7.refs_1_ = bf16[64,7296]{1,0:T(8,128)(2,1)S(1)} collective-permute-done((bf16[64,7296]{1,0:T(8,128)(2,1)S(1)}, bf16[64,7296]{1,0:T(8,128)(2,1)S(1)}, u32[]{:S(2)}, u32[]{:S(2)}) %collective-permute-start.7) | collective-permute-done | bytes 933920 | tf_op jit(solution)/shard_map/ppermute | solution.py:43
  44.3 0.3 collective-permute-done.8.refs_0_
  44.5 3.7 %expert.4 = (bf16[64,7168]{1,0:T(8,128)(2,1)S(1)}, bf16[64,7168]{1,0:T(8,128)(2,1)S(1)}) custom-call(bf16[64,7296]{1,0:T(8,128)(2,1)S(1)} %constant_dynamic-update-slice_fusion.refs_0_, bf16[64,7296]{1,0:T(8,128)(2,1)S(1)} %constant_dynamic-update-slice_fusion.2.refs_1_, bf16[10752,512]{1,0:T(8,128)(2,1)S(1)} %join.1.refs_2_, ...), custom_call_target="tpu_custom_call" | custom-call | flops 2818572288 | bytes 3670016 | tf_op jit(solution)/shard_map/expert/pallas_call | solution.py:104
  48.2 3.7 %expert.5 = (bf16[64,7168]{1,0:T(8,128)(2,1)S(1)}, bf16[64,7168]{1,0:T(8,128)(2,1)S(1)}) custom-call(bf16[64,7296]{1,0:T(8,128)(2,1)S(1)} %collective-permute-done.8.refs_0_, bf16[64,7296]{1,0:T(8,128)(2,1)S(1)} %collective-permute-done.7.refs_1_, bf16[10752,512]{1,0:T(8,128)(2,1)S(1)} %join.1.refs_2_, bf16[10752,512]{1,0:T(8,128)(2,1)S(1)} %collective-permute-done.9.refs_3_), custom_call_target="tpu_custom_call" | custom-call | flops 2818572288 | bytes 3670016 | tf_op jit(solution)/shard_map/expert/pallas_call | solution.py:104
  51.9 2.6 %collective-permute-done.10.refs_0_ = bf16[64,7296]{1,0:T(8,128)(2,1)S(1)} collective-permute-done((bf16[64,7296]{1,0:T(8,128)(2,1)S(1)}, bf16[64,7296]{1,0:T(8,128)(2,1)S(1)}, u32[]{:S(2)}, u32[]{:S(2)}) %collective-permute-start.10) | collective-permute-done | bytes 933920 | tf_op jit(solution)/shard_map/ppermute | solution.py:43
  54.6 1.5 %collective-permute-start.11 = (bf16[64,7296]{1,0:T(8,128)(2,1)S(1)}, bf16[64,7296]{1,0:T(8,128)(2,1)S(1)}, u32[]{:S(2)}, u32[]{:S(2)}) collective-permute-start(bf16[64,7296]{1,0:T(8,128)(2,1)S(1)} %collective-permute-done.7.refs_1_), channel_id=1, source_target_pairs={{0,4},{1,5},{2,6},{3,7},{4,8},{5,9},{6,10},{7,11},{8,12},{9,13},{1... | collective-permute-start | bytes 2801672 | tf_op jit(solution)/shard_map/ppermute | solution.py:43
  56.0 1.7 %collective-permute-start.12 = (bf16[64,7296]{1,0:T(8,128)(2,1)S(1)}, bf16[64,7296]{1,0:T(8,128)(2,1)S(1)}, u32[]{:S(2)}, u32[]{:S(2)}) collective-permute-start(bf16[64,7296]{1,0:T(8,128)(2,1)S(1)} %collective-permute-done.10.refs_0_), channel_id=1, source_target_pairs={{0,12},{1,13},{2,14},{3,15},{4,0},{5,1},{6,2},{7,3},{8,4},{9,5},{1... | collective-permute-start | bytes 2801672 | tf_op jit(solution)/shard_map/ppermute | solution.py:43
  57.8 3.7 %expert.6 = (bf16[64,7168]{1,0:T(8,128)(2,1)S(1)}, bf16[64,7168]{1,0:T(8,128)(2,1)S(1)}) custom-call(bf16[64,7296]{1,0:T(8,128)(2,1)S(1)} %collective-permute-done.10.refs_0_, bf16[64,7296]{1,0:T(8,128)(2,1)S(1)} %collective-permute-done.13.refs_1_, bf16[10752,512]{1,0:T(8,128)(2,1)S(1)} %join.1.refs_2_, bf16[10752,512]{1,0:T(8,128)(2,1)S(1)} %collective-permute-done.9.refs_3_), custom_call_target="tpu_custom_call" | custom-call | flops 2818572288 | bytes 3670016 | tf_op jit(solution)/shard_map/expert/pallas_call | solution.py:104
  61.6 0.3 collective-permute-start.16
  61.9 3.0 %collective-permute-start.17 = (bf16[64,7168]{1,0:T(8,128)(2,1)S(1)}, bf16[64,7168]{1,0:T(8,128)(2,1)S(1)}, u32[]{:S(2)}, u32[]{:S(2)}) collective-permute-start(bf16[64,7168]{1,0:T(8,128)(2,1)S(1)} %get-tuple-element.68), channel_id=1, source_target_pairs={{0,12},{1,13},{2,14},{3,15},{4,0},{5,1},{6,2},{7,3},{8,4},{9,5},{1... | collective-permute-start | bytes 2752520 | tf_op jit(solution)/shard_map/ppermute | solution.py:43
  64.9 4.5 %collective-permute-done.11.refs_0_ = bf16[64,7296]{1,0:T(8,128)(2,1)S(1)} collective-permute-done((bf16[64,7296]{1,0:T(8,128)(2,1)S(1)}, bf16[64,7296]{1,0:T(8,128)(2,1)S(1)}, u32[]{:S(2)}, u32[]{:S(2)}) %collective-permute-start.11) | collective-permute-done | bytes 933920 | tf_op jit(solution)/shard_map/ppermute | solution.py:43
  69.3 0.3 collective-permute-done.12.refs_1_
  69.6 3.7 %expert.7 = (bf16[64,7168]{1,0:T(8,128)(2,1)S(1)}, bf16[64,7168]{1,0:T(8,128)(2,1)S(1)}) custom-call(bf16[64,7296]{1,0:T(8,128)(2,1)S(1)} %collective-permute-done.11.refs_0_, bf16[64,7296]{1,0:T(8,128)(2,1)S(1)} %collective-permute-done.12.refs_1_, bf16[10752,512]{1,0:T(8,128)(2,1)S(1)} %join.1.refs_2_, bf16[10752,512]{1,0:T(8,128)(2,1)S(1)} %collective-permute-done.9.refs_3_), custom_call_target="tpu_custom_call" | custom-call | flops 2818572288 | bytes 3670016 | tf_op jit(solution)/shard_map/expert/pallas_call | solution.py:104
  73.3 1.3 collective-permute-start.14
  74.6 2.0 %collective-permute-start.15 = (bf16[64,7168]{1,0:T(8,128)(2,1)S(1)}, bf16[64,7168]{1,0:T(8,128)(2,1)S(1)}, u32[]{:S(2)}, u32[]{:S(2)}) collective-permute-start(bf16[64,7168]{1,0:T(8,128)(2,1)S(1)} %get-tuple-element.72), channel_id=1, source_target_pairs={{0,12},{1,13},{2,14},{3,15},{4,0},{5,1},{6,2},{7,3},{8,4},{9,5},{1... | collective-permute-start | bytes 2752520 | tf_op jit(solution)/shard_map/ppermute | solution.py:43
  76.7 7.1 %attend.2 = bf16[64,1024]{1,0:T(8,128)(2,1)S(1)} custom-call(s32[2]{0:T(128)S(1)} %copy-done.7, bf16[128,1024]{1,0:T(8,128)(2,1)S(1)} %copy-done.3, bf16[128,512]{1,0:T(8,128)(2,1)S(1)} %copy-done.4, bf16[8,128,512]{2,1,0:T(8,128)(2,1)S(1)} %copy-done, bf16[8,512,128]{2,1,0:T(8,128)(2,1)S(1)} %copy-done.1, bf16[2,4096,512]{2,1,0:T(8,128)(2,1)} %latent_ref.3, ...), custom_call_target="tpu_custom_call" | custom-call | flops 100000000 | bytes 133333 | tf_op jit(solution)/shard_map/attend/pallas_call | solution.py:254
  83.8 5.2 %collective-permute-done.14 = bf16[64,7168]{1,0:T(8,128)(2,1)S(1)} collective-permute-done((bf16[64,7168]{1,0:T(8,128)(2,1)S(1)}, bf16[64,7168]{1,0:T(8,128)(2,1)S(1)}, u32[]{:S(2)}, u32[]{:S(2)}) %collective-permute-start.14) | collective-permute-done | bytes 917536 | tf_op jit(solution)/shard_map/ppermute | solution.py:43
  89.0 0.3 collective-permute-done.15
  89.3 0.2 add_convert_fusion
  89.5 3.0 %collective-permute-start.19 = (bf16[64,7168]{1,0:T(8,128)(2,1)S(1)}, bf16[64,7168]{1,0:T(8,128)(2,1)S(1)}, u32[]{:S(2)}, u32[]{:S(2)}) collective-permute-start(bf16[64,7168]{1,0:T(8,128)(2,1)S(1)} %add_convert_fusion), channel_id=1, source_target_pairs={{0,12},{1,13},{2,14},{3,15},{4,0},{5,1},{6,2},{7,3},{8,4},{9,5},{1... | collective-permute-start | bytes 2752520 | tf_op jit(solution)/shard_map/ppermute | solution.py:43
  92.5 0.2 add_convert_fusion.1
  92.7 0.3 collective-permute-start.18
  93.1 7.2 %attend.3 = bf16[64,1024]{1,0:T(8,128)(2,1)S(1)} custom-call(s32[2]{0:T(128)S(1)} %copy-done.7, bf16[128,1024]{1,0:T(8,128)(2,1)S(1)} %copy-done.3, bf16[128,512]{1,0:T(8,128)(2,1)S(1)} %copy-done.4, bf16[8,128,512]{2,1,0:T(8,128)(2,1)S(1)} %copy-done, bf16[8,512,128]{2,1,0:T(8,128)(2,1)S(1)} %copy-done.1, bf16[2,4096,512]{2,1,0:T(8,128)(2,1)} %latent_ref.3, ...), custom_call_target="tpu_custom_call" | custom-call | flops 6000000000 | bytes 8000000 | tf_op jit(solution)/shard_map/attend/pallas_call | solution.py:254
  100.2 3.2 %collective-permute-done.19 = bf16[64,7168]{1,0:T(8,128)(2,1)S(1)} collective-permute-done((bf16[64,7168]{1,0:T(8,128)(2,1)S(1)}, bf16[64,7168]{1,0:T(8,128)(2,1)S(1)}, u32[]{:S(2)}, u32[]{:S(2)}) %collective-permute-start.19) | collective-permute-done | bytes 917536 | tf_op jit(solution)/shard_map/ppermute | solution.py:43
  103.4 4.2 %collective-permute-done.18 = bf16[64,7168]{1,0:T(8,128)(2,1)S(1)} collective-permute-done((bf16[64,7168]{1,0:T(8,128)(2,1)S(1)}, bf16[64,7168]{1,0:T(8,128)(2,1)S(1)}, u32[]{:S(2)}, u32[]{:S(2)}) %collective-permute-start.18) | collective-permute-done | bytes 917536 | tf_op jit(solution)/shard_map/ppermute | solution.py:43
  107.6 0.3 fusion.3
  108.0 0.3 convert_add_fusion.1
  108.4 1.7 %collective-permute-start.20 = (bf16[32,7168]{1,0:T(8,128)(2,1)S(1)}, bf16[32,7168]{1,0:T(8,128)(2,1)S(1)}, u32[]{:S(2)}, u32[]{:S(2)}) collective-permute-start(bf16[32,7168]{1,0:T(8,128)(2,1)S(1)} %pad_maximum_fusion.1), channel_id=1, source_target_pairs={{0,32},{1,33},{2,34},{3,35},{4,36},{5,37},{6,38},{7,39},{8,40},{9,... | collective-permute-start | bytes 1376264 | tf_op jit(solution)/shard_map/ppermute | solution.py:43
  110.1 1.7 %collective-permute-start.21 = (bf16[32,7168]{1,0:T(8,128)(2,1)S(1)}, bf16[32,7168]{1,0:T(8,128)(2,1)S(1)}, u32[]{:S(2)}, u32[]{:S(2)}) collective-permute-start(bf16[32,7168]{1,0:T(8,128)(2,1)S(1)} %concatenate.29), channel_id=1, source_target_pairs={{0,96},{1,97},{2,98},{3,99},{4,100},{5,101},{6,102},{7,103},{8,104... | collective-permute-start | bytes 1376264 | tf_op jit(solution)/shard_map/ppermute | solution.py:43
  111.8 7.6 %collective-permute-done.20 = bf16[32,7168]{1,0:T(8,128)(2,1)S(1)} collective-permute-done((bf16[32,7168]{1,0:T(8,128)(2,1)S(1)}, bf16[32,7168]{1,0:T(8,128)(2,1)S(1)}, u32[]{:S(2)}, u32[]{:S(2)}) %collective-permute-start.20) | collective-permute-done | bytes 458784 | tf_op jit(solution)/shard_map/ppermute | solution.py:43
  119.4 0.1 fusion.2
  119.5 0.5 collective-permute-done.21
  120.0 2.4 %collective-permute-start.22 = (bf16[16,7168]{1,0:T(8,128)(2,1)S(1)}, bf16[16,7168]{1,0:T(8,128)(2,1)S(1)}, u32[]{:S(2)}, u32[]{:S(2)}) collective-permute-start(bf16[16,7168]{1,0:T(8,128)(2,1)S(1)} %fusion.2), channel_id=1, source_target_pairs={{0,32},{1,33},{2,34},{3,35},{4,36},{5,37},{6,38},{7,39},{8,40},{9,... | collective-permute-start | bytes 688136 | tf_op jit(solution)/shard_map/ppermute | solution.py:43
  122.4 0.9 collective-permute-start.23
  123.3 4.0 %collective-permute-done.22 = bf16[16,7168]{1,0:T(8,128)(2,1)S(1)} collective-permute-done((bf16[16,7168]{1,0:T(8,128)(2,1)S(1)}, bf16[16,7168]{1,0:T(8,128)(2,1)S(1)}, u32[]{:S(2)}, u32[]{:S(2)}) %collective-permute-start.22) | collective-permute-done | bytes 229408 | tf_op jit(solution)/shard_map/ppermute | solution.py:43
  127.3 0.1 convert_add_fusion.3
  127.4 1.1 collective-permute-done.23
  128.4 0.1 convert_add_fusion.2
  128.5 0.1 fusion
  128.6 0.6 collective-permute-start.24
  129.2 1.8 %collective-permute-start.25 = (bf16[8,7168]{1,0:T(8,128)(2,1)S(1)}, bf16[8,7168]{1,0:T(8,128)(2,1)S(1)}, u32[]{:S(2)}, u32[]{:S(2)}) collective-permute-start(bf16[8,7168]{1,0:T(8,128)(2,1)S(1)} %get-tuple-element.92), channel_id=1, source_target_pairs={{0,2},{1,3},{2,0},{3,1},{4,6},{5,7},{6,4},{7,5},{8,10},{9,11},{10,... | collective-permute-start | bytes 344072 | tf_op jit(solution)/shard_map/ppermute | solution.py:43
  131.1 1.4 collective-permute-start.26
  132.4 0.7 pad_maximum_fusion.2
  133.2 2.8 %collective-permute-done.24 = bf16[8,7168]{1,0:T(8,128)(2,1)S(1)} collective-permute-done((bf16[8,7168]{1,0:T(8,128)(2,1)S(1)}, bf16[8,7168]{1,0:T(8,128)(2,1)S(1)}, u32[]{:S(2)}, u32[]{:S(2)}) %collective-permute-start.24) | collective-permute-done | bytes 114720 | tf_op jit(solution)/shard_map/ppermute | solution.py:43
  135.9 0.9 collective-permute-done.26
  136.8 0.7 add_convert_fusion.2
  (38 shorter events, 0.5 us)
Async XLA Ops:
  1.7 9.0 %collective-permute-start = (bf16[8,7296]{1,0:T(8,128)(2,1)S(1)}, bf16[8,7296]{1,0:T(8,128)(2,1)S(1)}, u32[]{:S(2)}, u32[]{:S(2)}) collective-permute-start(bf16[8,7296]{1,0:T(8,128)(2,1)S(1)} %pack.1), channel_id=1, source_target_pairs={{0,3},{1,0},{2,1},{3,2},{4,7},{5,4},{6,5},{7,6},{8,11},{9,8},{10,9... | collective-permute-start | bytes 350216 | tf_op jit(solution)/shard_map/ppermute | solution.py:43
  4.9 6.4 %collective-permute-start.1 = (bf16[8,7296]{1,0:T(8,128)(2,1)S(1)}, bf16[8,7296]{1,0:T(8,128)(2,1)S(1)}, u32[]{:S(2)}, u32[]{:S(2)}) collective-permute-start(bf16[8,7296]{1,0:T(8,128)(2,1)S(1)} %pack.1), channel_id=1, source_target_pairs={{0,2},{1,3},{2,0},{3,1},{4,6},{5,7},{6,4},{7,5},{8,10},{9,11},{10,... | collective-permute-start | bytes 350216 | tf_op jit(solution)/shard_map/ppermute | solution.py:43
  5.5 6.9 %collective-permute-start.2 = (bf16[8,7296]{1,0:T(8,128)(2,1)S(1)}, bf16[8,7296]{1,0:T(8,128)(2,1)S(1)}, u32[]{:S(2)}, u32[]{:S(2)}) collective-permute-start(bf16[8,7296]{1,0:T(8,128)(2,1)S(1)} %pack.1), channel_id=1, source_target_pairs={{0,1},{1,2},{2,3},{3,0},{4,5},{5,6},{6,7},{7,4},{8,9},{9,10},{10,1... | collective-permute-start | bytes 350216 | tf_op jit(solution)/shard_map/ppermute | solution.py:43
  12.5 32.0 %collective-permute-start.9 = (bf16[10752,512]{1,0:T(8,128)(2,1)S(1)}, bf16[10752,512]{1,0:T(8,128)(2,1)S(1)}, u32[]{:S(2)}, u32[]{:S(2)}) collective-permute-start(bf16[10752,512]{1,0:T(8,128)(2,1)S(1)} %join.1.refs_2_), channel_id=1, source_target_pairs={{0,16},{16,0},{1,17},{17,1},{2,18},{18,2},{3,19},{19,3},{4,20},{20... | collective-permute-start | bytes 33030152 | tf_op jit(solution)/shard_map/ppermute | solution.py:59
  12.6 15.4 %collective-permute-start.4 = (bf16[32,7296]{1,0:T(8,128)(2,1)S(1)}, bf16[32,7296]{1,0:T(8,128)(2,1)S(1)}, u32[]{:S(2)}, u32[]{:S(2)}) collective-permute-start(bf16[32,7296]{1,0:T(8,128)(2,1)S(1)} %pad_maximum_fusion), channel_id=1, source_target_pairs={{0,32},{1,33},{2,34},{3,35},{4,36},{5,37},{6,38},{7,39},{8,40},{9,... | collective-permute-start | bytes 1400840 | tf_op jit(solution)/shard_map/ppermute | solution.py:43
  14.6 13.4 %collective-permute-start.3 = (bf16[32,7296]{1,0:T(8,128)(2,1)S(1)}, bf16[32,7296]{1,0:T(8,128)(2,1)S(1)}, u32[]{:S(2)}, u32[]{:S(2)}) collective-permute-start(bf16[32,7296]{1,0:T(8,128)(2,1)S(1)} %pad_maximum_fusion), channel_id=1, source_target_pairs={{0,96},{1,97},{2,98},{3,99},{4,100},{5,101},{6,102},{7,103},{8,104... | collective-permute-start | bytes 1400840 | tf_op jit(solution)/shard_map/ppermute | solution.py:43
  28.1 8.7 %collective-permute-start.5 = (bf16[16,7296]{1,0:T(8,128)(2,1)S(1)}, bf16[16,7296]{1,0:T(8,128)(2,1)S(1)}, u32[]{:S(2)}, u32[]{:S(2)}) collective-permute-start(bf16[16,7296]{1,0:T(8,128)(2,1)S(1)} %slice.75), channel_id=1, source_target_pairs={{0,32},{1,33},{2,34},{3,35},{4,36},{5,37},{6,38},{7,39},{8,40},{9,... | collective-permute-start | bytes 700424 | tf_op jit(solution)/shard_map/ppermute | solution.py:43
  29.4 14.8 %collective-permute-start.7 = (bf16[64,7296]{1,0:T(8,128)(2,1)S(1)}, bf16[64,7296]{1,0:T(8,128)(2,1)S(1)}, u32[]{:S(2)}, u32[]{:S(2)}) collective-permute-start(bf16[64,7296]{1,0:T(8,128)(2,1)S(1)} %constant_dynamic-update-slice_fusion.refs_0_), channel_id=1, source_target_pairs={{0,4},{1,5},{2,6},{3,7},{4,8},{5,9},{6,10},{7,11},{8,12},{9,13},{1... | collective-permute-start | bytes 2801672 | tf_op jit(solution)/shard_map/ppermute | solution.py:43
  31.0 13.6 %collective-permute-start.8 = (bf16[64,7296]{1,0:T(8,128)(2,1)S(1)}, bf16[64,7296]{1,0:T(8,128)(2,1)S(1)}, u32[]{:S(2)}, u32[]{:S(2)}) collective-permute-start(bf16[64,7296]{1,0:T(8,128)(2,1)S(1)} %constant_dynamic-update-slice_fusion.refs_0_), channel_id=1, source_target_pairs={{0,12},{1,13},{2,14},{3,15},{4,0},{5,1},{6,2},{7,3},{8,4},{9,5},{1... | collective-permute-start | bytes 2801672 | tf_op jit(solution)/shard_map/ppermute | solution.py:43
  32.7 6.1 %collective-permute-start.6 = (bf16[16,7296]{1,0:T(8,128)(2,1)S(1)}, bf16[16,7296]{1,0:T(8,128)(2,1)S(1)}, u32[]{:S(2)}, u32[]{:S(2)}) collective-permute-start(bf16[16,7296]{1,0:T(8,128)(2,1)S(1)} %slice.76), channel_id=1, source_target_pairs={{0,96},{1,97},{2,98},{3,99},{4,100},{5,101},{6,102},{7,103},{8,104... | collective-permute-start | bytes 700424 | tf_op jit(solution)/shard_map/ppermute | solution.py:43
  38.9 15.6 %collective-permute-start.10 = (bf16[64,7296]{1,0:T(8,128)(2,1)S(1)}, bf16[64,7296]{1,0:T(8,128)(2,1)S(1)}, u32[]{:S(2)}, u32[]{:S(2)}) collective-permute-start(bf16[64,7296]{1,0:T(8,128)(2,1)S(1)} %constant_dynamic-update-slice_fusion.2.refs_1_), channel_id=1, source_target_pairs={{0,12},{1,13},{2,14},{3,15},{4,0},{5,1},{6,2},{7,3},{8,4},{9,5},{1... | collective-permute-start | bytes 2801672 | tf_op jit(solution)/shard_map/ppermute | solution.py:43
  41.7 16.1 %collective-permute-start.13 = (bf16[64,7296]{1,0:T(8,128)(2,1)S(1)}, bf16[64,7296]{1,0:T(8,128)(2,1)S(1)}, u32[]{:S(2)}, u32[]{:S(2)}) collective-permute-start(bf16[64,7296]{1,0:T(8,128)(2,1)S(1)} %constant_dynamic-update-slice_fusion.2.refs_1_), channel_id=1, source_target_pairs={{0,4},{1,5},{2,6},{3,7},{4,8},{5,9},{6,10},{7,11},{8,12},{9,13},{1... | collective-permute-start | bytes 2801672 | tf_op jit(solution)/shard_map/ppermute | solution.py:43
  54.6 14.8 %collective-permute-start.11 = (bf16[64,7296]{1,0:T(8,128)(2,1)S(1)}, bf16[64,7296]{1,0:T(8,128)(2,1)S(1)}, u32[]{:S(2)}, u32[]{:S(2)}) collective-permute-start(bf16[64,7296]{1,0:T(8,128)(2,1)S(1)} %collective-permute-done.7.refs_1_), channel_id=1, source_target_pairs={{0,4},{1,5},{2,6},{3,7},{4,8},{5,9},{6,10},{7,11},{8,12},{9,13},{1... | collective-permute-start | bytes 2801672 | tf_op jit(solution)/shard_map/ppermute | solution.py:43
  56.0 13.6 %collective-permute-start.12 = (bf16[64,7296]{1,0:T(8,128)(2,1)S(1)}, bf16[64,7296]{1,0:T(8,128)(2,1)S(1)}, u32[]{:S(2)}, u32[]{:S(2)}) collective-permute-start(bf16[64,7296]{1,0:T(8,128)(2,1)S(1)} %collective-permute-done.10.refs_0_), channel_id=1, source_target_pairs={{0,12},{1,13},{2,14},{3,15},{4,0},{5,1},{6,2},{7,3},{8,4},{9,5},{1... | collective-permute-start | bytes 2801672 | tf_op jit(solution)/shard_map/ppermute | solution.py:43
  61.5 15.1 %copy-start = (bf16[8,128,512]{2,1,0:T(8,128)(2,1)S(1)}, bf16[8,128,512]{2,1,0:T(8,128)(2,1)}, u32[]{:S(2)}) copy-start(bf16[8,128,512]{2,1,0:T(8,128)(2,1)} %key_up_ref.3) | copy-start | bytes 3145732
  61.5 15.1 %copy-start.1 = (bf16[8,512,128]{2,1,0:T(8,128)(2,1)S(1)}, bf16[8,512,128]{2,1,0:T(8,128)(2,1)}, u32[]{:S(2)}) copy-start(bf16[8,512,128]{2,1,0:T(8,128)(2,1)} %value_up_ref.3) | copy-start | bytes 3145732
  61.5 15.1 %copy-start.2 = (bf16[2,4096,64]{1,2,0:T(8,128)(2,1)S(1)}, bf16[2,4096,64]{1,2,0:T(8,128)(2,1)}, u32[]{:S(2)}) copy-start(bf16[2,4096,64]{1,2,0:T(8,128)(2,1)} %param.26) | copy-start | bytes 3145732
  61.5 15.1 %copy-start.3 = (bf16[128,1024]{1,0:T(8,128)(2,1)S(1)}, bf16[128,1024]{1,0:T(8,128)(2,1)}, u32[]{:S(2)}) copy-start(bf16[128,1024]{1,0:T(8,128)(2,1)} %nope_ref.3) | copy-start | bytes 786436
  61.5 15.1 %copy-start.4 = (bf16[128,512]{1,0:T(8,128)(2,1)S(1)}, bf16[128,512]{1,0:T(8,128)(2,1)}, u32[]{:S(2)}) copy-start(bf16[128,512]{1,0:T(8,128)(2,1)} %rope_ref.3) | copy-start | bytes 393220
  61.5 15.1 %copy-start.5 = (bf16[128,512]{1,0:T(8,128)(2,1)S(1)}, bf16[128,512]{1,0:T(8,128)(2,1)}, u32[]{:S(2)}) copy-start(bf16[128,512]{1,0:T(8,128)(2,1)} %new_latent_ref.3) | copy-start | bytes 393220
  61.5 15.1 %copy-start.6 = (bf16[128,64]{0,1:T(8,128)(2,1)S(1)}, bf16[128,64]{0,1:T(8,128)(2,1)}, u32[]{:S(2)}) copy-start(bf16[128,64]{0,1:T(8,128)(2,1)} %param.28) | copy-start | bytes 49156
  61.6 15.1 %copy-start.7 = (s32[2]{0:T(128)S(1)}, s32[2]{0:T(128)}, u32[]{:S(2)}) copy-start(s32[2]{0:T(128)} %length_ref.1) | copy-start | bytes 28
  61.6 22.2 %collective-permute-start.16 = (bf16[64,7168]{1,0:T(8,128)(2,1)S(1)}, bf16[64,7168]{1,0:T(8,128)(2,1)S(1)}, u32[]{:S(2)}, u32[]{:S(2)}) collective-permute-start(bf16[64,7168]{1,0:T(8,128)(2,1)S(1)} %get-tuple-element.67), channel_id=1, source_target_pairs={{0,4},{1,5},{2,6},{3,7},{4,8},{5,9},{6,10},{7,11},{8,12},{9,13},{1... | collective-permute-start | bytes 2752520 | tf_op jit(solution)/shard_map/ppermute | solution.py:43
  61.9 21.9 %collective-permute-start.17 = (bf16[64,7168]{1,0:T(8,128)(2,1)S(1)}, bf16[64,7168]{1,0:T(8,128)(2,1)S(1)}, u32[]{:S(2)}, u32[]{:S(2)}) collective-permute-start(bf16[64,7168]{1,0:T(8,128)(2,1)S(1)} %get-tuple-element.68), channel_id=1, source_target_pairs={{0,12},{1,13},{2,14},{3,15},{4,0},{5,1},{6,2},{7,3},{8,4},{9,5},{1... | collective-permute-start | bytes 2752520 | tf_op jit(solution)/shard_map/ppermute | solution.py:43
  73.3 15.7 %collective-permute-start.14 = (bf16[64,7168]{1,0:T(8,128)(2,1)S(1)}, bf16[64,7168]{1,0:T(8,128)(2,1)S(1)}, u32[]{:S(2)}, u32[]{:S(2)}) collective-permute-start(bf16[64,7168]{1,0:T(8,128)(2,1)S(1)} %get-tuple-element.71), channel_id=1, source_target_pairs={{0,4},{1,5},{2,6},{3,7},{4,8},{5,9},{6,10},{7,11},{8,12},{9,13},{1... | collective-permute-start | bytes 2752520 | tf_op jit(solution)/shard_map/ppermute | solution.py:43
  74.6 14.7 %collective-permute-start.15 = (bf16[64,7168]{1,0:T(8,128)(2,1)S(1)}, bf16[64,7168]{1,0:T(8,128)(2,1)S(1)}, u32[]{:S(2)}, u32[]{:S(2)}) collective-permute-start(bf16[64,7168]{1,0:T(8,128)(2,1)S(1)} %get-tuple-element.72), channel_id=1, source_target_pairs={{0,12},{1,13},{2,14},{3,15},{4,0},{5,1},{6,2},{7,3},{8,4},{9,5},{1... | collective-permute-start | bytes 2752520 | tf_op jit(solution)/shard_map/ppermute | solution.py:43
  89.5 13.9 %collective-permute-start.19 = (bf16[64,7168]{1,0:T(8,128)(2,1)S(1)}, bf16[64,7168]{1,0:T(8,128)(2,1)S(1)}, u32[]{:S(2)}, u32[]{:S(2)}) collective-permute-start(bf16[64,7168]{1,0:T(8,128)(2,1)S(1)} %add_convert_fusion), channel_id=1, source_target_pairs={{0,12},{1,13},{2,14},{3,15},{4,0},{5,1},{6,2},{7,3},{8,4},{9,5},{1... | collective-permute-start | bytes 2752520 | tf_op jit(solution)/shard_map/ppermute | solution.py:43
  92.7 14.9 %collective-permute-start.18 = (bf16[64,7168]{1,0:T(8,128)(2,1)S(1)}, bf16[64,7168]{1,0:T(8,128)(2,1)S(1)}, u32[]{:S(2)}, u32[]{:S(2)}) collective-permute-start(bf16[64,7168]{1,0:T(8,128)(2,1)S(1)} %add_convert_fusion.1), channel_id=1, source_target_pairs={{0,4},{1,5},{2,6},{3,7},{4,8},{5,9},{6,10},{7,11},{8,12},{9,13},{1... | collective-permute-start | bytes 2752520 | tf_op jit(solution)/shard_map/ppermute | solution.py:43
  108.4 11.0 %collective-permute-start.20 = (bf16[32,7168]{1,0:T(8,128)(2,1)S(1)}, bf16[32,7168]{1,0:T(8,128)(2,1)S(1)}, u32[]{:S(2)}, u32[]{:S(2)}) collective-permute-start(bf16[32,7168]{1,0:T(8,128)(2,1)S(1)} %pad_maximum_fusion.1), channel_id=1, source_target_pairs={{0,32},{1,33},{2,34},{3,35},{4,36},{5,37},{6,38},{7,39},{8,40},{9,... | collective-permute-start | bytes 1376264 | tf_op jit(solution)/shard_map/ppermute | solution.py:43
  110.1 9.8 %collective-permute-start.21 = (bf16[32,7168]{1,0:T(8,128)(2,1)S(1)}, bf16[32,7168]{1,0:T(8,128)(2,1)S(1)}, u32[]{:S(2)}, u32[]{:S(2)}) collective-permute-start(bf16[32,7168]{1,0:T(8,128)(2,1)S(1)} %concatenate.29), channel_id=1, source_target_pairs={{0,96},{1,97},{2,98},{3,99},{4,100},{5,101},{6,102},{7,103},{8,104... | collective-permute-start | bytes 1376264 | tf_op jit(solution)/shard_map/ppermute | solution.py:43
  120.0 7.3 %collective-permute-start.22 = (bf16[16,7168]{1,0:T(8,128)(2,1)S(1)}, bf16[16,7168]{1,0:T(8,128)(2,1)S(1)}, u32[]{:S(2)}, u32[]{:S(2)}) collective-permute-start(bf16[16,7168]{1,0:T(8,128)(2,1)S(1)} %fusion.2), channel_id=1, source_target_pairs={{0,32},{1,33},{2,34},{3,35},{4,36},{5,37},{6,38},{7,39},{8,40},{9,... | collective-permute-start | bytes 688136 | tf_op jit(solution)/shard_map/ppermute | solution.py:43
  122.4 6.0 %collective-permute-start.23 = (bf16[16,7168]{1,0:T(8,128)(2,1)S(1)}, bf16[16,7168]{1,0:T(8,128)(2,1)S(1)}, u32[]{:S(2)}, u32[]{:S(2)}) collective-permute-start(bf16[16,7168]{1,0:T(8,128)(2,1)S(1)} %fusion.1), channel_id=1, source_target_pairs={{0,96},{1,97},{2,98},{3,99},{4,100},{5,101},{6,102},{7,103},{8,104... | collective-permute-start | bytes 688136 | tf_op jit(solution)/shard_map/ppermute | solution.py:43
  128.6 7.3 %collective-permute-start.24 = (bf16[8,7168]{1,0:T(8,128)(2,1)S(1)}, bf16[8,7168]{1,0:T(8,128)(2,1)S(1)}, u32[]{:S(2)}, u32[]{:S(2)}) collective-permute-start(bf16[8,7168]{1,0:T(8,128)(2,1)S(1)} %get-tuple-element.90), channel_id=1, source_target_pairs={{0,1},{1,2},{2,3},{3,0},{4,5},{5,6},{6,7},{7,4},{8,9},{9,10},{10,1... | collective-permute-start | bytes 344072 | tf_op jit(solution)/shard_map/ppermute | solution.py:43
  129.2 6.7 %collective-permute-start.25 = (bf16[8,7168]{1,0:T(8,128)(2,1)S(1)}, bf16[8,7168]{1,0:T(8,128)(2,1)S(1)}, u32[]{:S(2)}, u32[]{:S(2)}) collective-permute-start(bf16[8,7168]{1,0:T(8,128)(2,1)S(1)} %get-tuple-element.92), channel_id=1, source_target_pairs={{0,2},{1,3},{2,0},{3,1},{4,6},{5,7},{6,4},{7,5},{8,10},{9,11},{10,... | collective-permute-start | bytes 344072 | tf_op jit(solution)/shard_map/ppermute | solution.py:43
  131.1 5.7 %collective-permute-start.26 = (bf16[8,7168]{1,0:T(8,128)(2,1)S(1)}, bf16[8,7168]{1,0:T(8,128)(2,1)S(1)}, u32[]{:S(2)}, u32[]{:S(2)}) collective-permute-start(bf16[8,7168]{1,0:T(8,128)(2,1)S(1)} %get-tuple-element.91), channel_id=1, source_target_pairs={{0,3},{1,0},{2,1},{3,2},{4,7},{5,4},{6,5},{7,6},{8,11},{9,8},{10,9... | collective-permute-start | bytes 344072 | tf_op jit(solution)/shard_map/ppermute | solution.py:43
